TPU v7x, 32 devices: a whole 2x2x4 slice. The times are simulated.
32 devices in a mesh: section: 4 (over x, core), seq: 8 (over z, y).
Axes of the slice: x: 2, y: 2, z: 4, core: 2. Of those that a mesh axis runs over, the one named last changes fastest.
Arguments:
- queries: bfloat16 [4, 2560, 1024], P('section', 'seq'), may hold values from -60 to 60
- keys_new: bfloat16 [4, 2560, 1024], P('section', 'seq'), may hold values from -6 to 6
- values_new: bfloat16 [4, 2560, 1024], P('section', 'seq'), may hold values from -6 to 6
- keys_cache: bfloat16 [4, 6144, 1024], P('section', None, 'seq'), may hold values from -6 to 6
- values_cache: bfloat16 [4, 6144, 1024], P('section', None, 'seq'), may hold values from -6 to 6
- window: int32 [4, 8], P('section', 'seq'), may hold values from 1 to 3, as said below
- global_blocks: int32 [4, 2], P('section'), may hold values from 0 to 95
- random_blocks: int32 [4, 40, 3], P('section'), may hold values from 0 to 95
Outputs:
- handed: bfloat16 [4, 2560, 1024], P('section', 'seq')
Inputs may be any that keep to these rules, and one draw needn't show every extreme that they name: In every section some head has the window 3.
All inputs are finite; a program needn't handle non-finite values.
Results may differ from a plain program's by a relative error of at most 0.0049.
Values may be sent and summed in bfloat16 or wider, within the bound.
No kernel may reach another device: no remote copies, remote signals or barrier semaphores. Data moves between devices by JAX's collectives and lax.ppermute only.
A program may use at most 128 MiB of HBM per device.

v0:
```python
import math

import jax
import jax.numpy as jnp
from jax import lax
from jax.sharding import PartitionSpec as P

HD = 128
BLK = 64
WMAX = 3
GLOB = 2
RAND = 3
NK = 8


masked_score = -1e30


def as_sent(shard):

    def short(part):
        return part.astype(jnp.bfloat16) if part.dtype == jnp.float32 else part

    return jax.tree.map(short, shard)


def passed_along(shard, axis, by):
    devices = lax.axis_size(axis)
    return lax.ppermute(shard, axis, [(i, (i + by) % devices) for i in range(devices)])


def block_mask(span_blocks):
    rows = jnp.arange(BLK, dtype=jnp.int32)[:, None]
    column = jnp.arange(NK * BLK, dtype=jnp.int32)[None, :]
    which = column // BLK
    inside = column % BLK
    allowed = jnp.where(which >= WMAX, True, which < span_blocks)
    return allowed & ((which != 0) | (inside <= rows))


def attend_local(
    query,
    fresh_keys,
    fresh_values,
    old_keys,
    old_values,
    span_blocks,
    global_row,
    random_rows,
    group,
):
    stretch_rows = query.shape[0]
    block_count = stretch_rows // BLK
    cache_blocks = old_keys.shape[0] // BLK
    lead = (WMAX - 1) * BLK
    near_keys = jnp.concatenate([old_keys[old_keys.shape[0] - lead :], fresh_keys], axis=0)
    near_values = jnp.concatenate([old_values[old_values.shape[0] - lead :], fresh_values], axis=0)
    glob_keys = jnp.concatenate(
        [lax.dynamic_slice_in_dim(old_keys, global_row[g] * BLK, BLK, 0) for g in range(GLOB)],
        axis=0,
    )
    glob_values = jnp.concatenate(
        [lax.dynamic_slice_in_dim(old_values, global_row[g] * BLK, BLK, 0) for g in range(GLOB)],
        axis=0,
    )
    key_blocks = old_keys.reshape(cache_blocks, BLK, HD)
    value_blocks = old_values.reshape(cache_blocks, BLK, HD)
    query_blocks = query.reshape(block_count, BLK, HD)
    allowed = block_mask(span_blocks)
    scale = 1.0 / math.sqrt(HD)

    def one_group(index):
        first = index * group
        query_part = lax.dynamic_slice_in_dim(query_blocks, first, group, 0)
        near_key_part = lax.dynamic_slice_in_dim(
            near_keys, first * BLK, (group + WMAX - 1) * BLK, 0
        )
        near_value_part = lax.dynamic_slice_in_dim(
            near_values, first * BLK, (group + WMAX - 1) * BLK, 0
        )
        random_part = lax.dynamic_slice_in_dim(random_rows, first, group, 0)
        rand_keys = key_blocks[random_part].reshape(group, RAND * BLK, HD)
        rand_values = value_blocks[random_part].reshape(group, RAND * BLK, HD)
        near_value_list = []
        pieces = []
        for slot in range(WMAX):
            offset = (WMAX - 1 - slot) * BLK
            slot_keys = near_key_part[offset : offset + group * BLK].reshape(group, BLK, HD)
            near_value_list.append(
                near_value_part[offset : offset + group * BLK].reshape(group, BLK, HD)
            )
            pieces.append(
                jnp.einsum(
                    "gih,gjh->gij", query_part, slot_keys, preferred_element_type=jnp.float32
                )
            )
        pieces.append(
            jnp.einsum("gih,jh->gij", query_part, glob_keys, preferred_element_type=jnp.float32)
        )
        pieces.append(
            jnp.einsum("gih,gjh->gij", query_part, rand_keys, preferred_element_type=jnp.float32)
        )
        scores = jnp.concatenate(pieces, axis=2) * scale
        scores = jnp.where(allowed[None], scores, masked_score)
        top = jnp.max(scores, axis=-1, keepdims=True)
        expo = jnp.exp(scores - top)
        weights = (expo / jnp.sum(expo, axis=-1, keepdims=True)).astype(jnp.bfloat16)
        result = jnp.einsum(
            "gij,gjh->gih",
            weights[:, :, WMAX * BLK + GLOB * BLK :],
            rand_values,
            preferred_element_type=jnp.float32,
        )
        result = result + jnp.einsum(
            "gij,jh->gih",
            weights[:, :, WMAX * BLK : WMAX * BLK + GLOB * BLK],
            glob_values,
            preferred_element_type=jnp.float32,
        )
        for slot in range(WMAX):
            result = result + jnp.einsum(
                "gij,gjh->gih",
                weights[:, :, slot * BLK : (slot + 1) * BLK],
                near_value_list[slot],
                preferred_element_type=jnp.float32,
            )
        return result.astype(jnp.bfloat16)

    outputs = lax.map(one_group, jnp.arange(block_count // group, dtype=jnp.int32))
    return outputs.reshape(stretch_rows, HD)


def per_device(
    queries, keys_new, values_new, keys_cache, values_cache, window, global_blocks, random_blocks
):
    head_queries = lax.all_to_all(queries, "seq", split_axis=2, concat_axis=1, tiled=True)
    head_keys, head_values = (
        lax.all_to_all(keys_new, "seq", split_axis=2, concat_axis=1, tiled=True),
        lax.all_to_all(values_new, "seq", split_axis=2, concat_axis=1, tiled=True),
    )
    stretch_rows = head_queries.shape[1]
    block_count = stretch_rows // BLK
    group = math.gcd(block_count, 8)
    global_row = global_blocks[0]
    random_rows = random_blocks[0]
    results = [
        attend_local(
            head_queries[0],
            head_keys[0],
            head_values[0],
            keys_cache[0],
            values_cache[0],
            window[0, 0],
            global_row,
            random_rows,
            group,
        )
    ]
    attended = jnp.concatenate(results, axis=1)[None]
    regrouped = lax.all_to_all(
        as_sent(attended), "seq", split_axis=1, concat_axis=2, tiled=True
    ).astype(attended.dtype)
    return passed_along(as_sent(regrouped), "section", 1).astype(regrouped.dtype)


def solution(mesh):
    placed = (
        P("section", "seq", None),
        P("section", "seq", None),
        P("section", "seq", None),
        P("section", None, "seq"),
        P("section", None, "seq"),
        P("section", "seq"),
        P("section", None),
        P("section", None, None),
    )
    return jax.shard_map(
        per_device, mesh=mesh, in_specs=placed, out_specs=P("section", "seq", None), check_vma=False
    )
```

profile of v0, /device:TPU:0, one launch (start us, length us, event | category | flops | bytes accessed | tf_op | source)
XLA Modules:
  0.0 213.9 jit_solution(10517276454453544756)
XLA Ops:
  0.0 4.1 %copy.45 = bf16[1,320,1024]{1,0,2:T(2,128)(2,1)S(1)} copy(bf16[1,320,1024]{2,1,0:T(8,128)(2,1)} %param.12) | data formatting | bytes 1310720 | tf_op args[2]
  4.6 5.6 %reduce.2 = bf16[1024,320]{1,0:T(8,128)(2,1)S(1)} reduce(bf16[1024,1,320]{2,1,0:T(2,128)(2,1)S(1)} %bitcast.125, bf16[]{:T(256)} %broadcast.139), dimensions={1}, to_apply=%bitcast.58.reduce_sub_computation | reduce | bytes 1310722
  11.9 7.4 %all-to-all-start.2 = ((bf16[8,2,20480]{2,1,0:T(2,128)(2,1)}), bf16[8,2,20480]{2,1,0:T(2,128)(2,1)S(1)}, u32[]{:S(2)}, u32[]{:S(2)}) async-start(bf16[8,2,20480]{2,1,0:T(2,128)(2,1)} %reshape.177), calls=%async_computation.2 | async-start | bytes 1310720 | tf_op jit(solution)/shard_map/all_to_all | solution.py:139
  19.3 2.3 %copy.42 = bf16[1,320,1024]{1,0,2:T(2,128)(2,1)S(1)} copy(bf16[1,320,1024]{2,1,0:T(8,128)(2,1)S(1)} %copy-done.3) | data formatting | bytes 1310720 | tf_op args[1]
  21.6 5.6 %reduce.1 = bf16[1024,320]{1,0:T(8,128)(2,1)S(1)} reduce(bf16[1024,1,320]{2,1,0:T(2,128)(2,1)S(1)} %bitcast.129, bf16[]{:T(256)} %broadcast.139), dimensions={1}, to_apply=%bitcast.56.reduce_sub_computation | reduce | bytes 1310722
  29.0 7.6 %all-to-all-done.2 = bf16[8,2,20480]{2,1,0:T(2,128)(2,1)S(1)} async-done(((bf16[8,2,20480]{2,1,0:T(2,128)(2,1)}), bf16[8,2,20480]{2,1,0:T(2,128)(2,1)S(1)}, u32[]{:S(2)}, u32[]{:S(2)}) %all-to-all-start.2) | async-done | bytes 655392 | tf_op jit(solution)/shard_map/all_to_all | solution.py:139
  36.6 4.4 %all-to-all-start.1 = ((bf16[8,2,20480]{2,1,0:T(2,128)(2,1)}), bf16[8,2,20480]{2,1,0:T(2,128)(2,1)}, u32[]{:S(2)}, u32[]{:S(2)}) async-start(bf16[8,2,20480]{2,1,0:T(2,128)(2,1)} %reshape.175), calls=%async_computation.1 | async-start | bytes 1310720 | tf_op jit(solution)/shard_map/all_to_all | solution.py:138
  41.0 2.3 %copy.39 = bf16[1,320,1024]{1,0,2:T(2,128)(2,1)S(1)} copy(bf16[1,320,1024]{2,1,0:T(8,128)(2,1)S(1)} %copy-done.4) | data formatting | bytes 1310720 | tf_op args[0]
  43.4 5.6 %reduce = bf16[1024,320]{1,0:T(8,128)(2,1)S(1)} reduce(bf16[1024,1,320]{2,1,0:T(2,128)(2,1)S(1)} %bitcast.130, bf16[]{:T(256)} %broadcast.139), dimensions={1}, to_apply=%bitcast.54.reduce_sub_computation | reduce | bytes 1310722
  50.7 7.1 %all-to-all-done.1 = bf16[8,2,20480]{2,1,0:T(2,128)(2,1)} async-done(((bf16[8,2,20480]{2,1,0:T(2,128)(2,1)}), bf16[8,2,20480]{2,1,0:T(2,128)(2,1)}, u32[]{:S(2)}, u32[]{:S(2)}) %all-to-all-start.1) | async-done | bytes 655392 | tf_op jit(solution)/shard_map/all_to_all | solution.py:138
  57.8 4.5 %all-to-all-start = ((bf16[8,2,20480]{2,1,0:T(2,128)(2,1)}), bf16[8,2,20480]{2,1,0:T(2,128)(2,1)}, u32[]{:S(2)}, u32[]{:S(2)}) async-start(bf16[8,2,20480]{2,1,0:T(2,128)(2,1)} %reshape.173), calls=%async_computation | async-start | bytes 1310720 | tf_op jit(solution)/shard_map/all_to_all | solution.py:136
  72.3 4.5 %reshape.176 = bf16[1024,1,320]{2,1,0:T(2,128)(2,1)S(1)} reshape(bf16[8,2,20480]{2,1,0:T(2,128)(2,1)} %all-to-all-done.1) | data formatting | bytes 1310720
  79.0 4.5 %reshape.174 = bf16[1024,1,320]{2,1,0:T(2,128)(2,1)S(1)} reshape(bf16[8,2,20480]{2,1,0:T(2,128)(2,1)} %all-to-all-done) | data formatting | bytes 1310720
  84.8 2.3 %pad_maximum_fusion = (bf16[2688,128]{1,0:T(8,128)(2,1)}, bf16[2688,128]{1,0:T(8,128)(2,1)}) fusion(bf16[2560,128]{1,0:T(8,128)(2,1)} %bitcast.142, bf16[128,128]{1,0:T(8,128)(2,1)S(1)} %slice_bitcast_fusion.1, bf16[2560,128]{1,0:T(8,128)(2,1)S(1)} %bitcast.141, bf16[128,128]{1,0:T(8,128)(2,1)S(1)} %slice_bitcast_fusion), kind=kLoop, calls=%fused_computation.55 | loop fusion | flops 2752512 | bytes 2752512 | tf_op jit(solution)/shard_map/concatenate | solution.py:56
  87.6 72.1 %while.13 = (s32[]{:T(128)}, bf16[5,8,64,128]{3,2,1,0:T(8,128)(2,1)}, s32[5]{0:T(128)}, bf16[40,64,128]{2,1,0:T(8,128)(2,1)S(1)}, bf16[2688,128]{1,0:T(8,128)(2,...) while((s32[]{:T(128)}, ...), condition=%wide.region_3.4_spmd.clone, body=%wide.region_0.3_spmd.clone.sunk | while | flops 136218192 | bytes 16003649 | solution.py:129
  89.5 1.9 constant_dynamic-slice_fusion.7
  93.5 2.0 gather_fusion.1
  98.1 2.1 gather_fusion
  103.9 2.0 constant_dynamic-slice_fusion.7
  108.0 2.0 gather_fusion.1
  112.6 2.1 gather_fusion
  122.4 2.0 gather_fusion.1
  127.0 2.1 gather_fusion
  132.9 1.9 constant_dynamic-slice_fusion.7
  136.8 2.0 gather_fusion.1
  141.4 2.1 gather_fusion
  151.2 2.0 gather_fusion.1
  155.8 2.1 gather_fusion
  159.7 6.4 %copy.63 = bf16[1,2560,128]{2,0,1:T(2,128)(2,1)S(1)} copy(bf16[1,2560,128]{2,1,0:T(8,128)(2,1)} %bitcast.145) | data formatting | bytes 1310720 | tf_op jit(solution)/shard_map/broadcast_in_dim;reshape | solution.py:159
  166.1 14.2 %reduce.3 = bf16[2560,128]{1,0:T(8,128)(2,1)S(1)} reduce(bf16[2560,1,128]{2,1,0:T(2,128)(2,1)S(1)} %bitcast.131, bf16[]{:T(256)} %broadcast.139), dimensions={1}, to_apply=%bitcast.72.reduce_sub_computation | reduce | bytes 1310722
  180.4 21.6 %all_to_all.63 = bf16[8,2,20480]{2,1,0:T(2,128)(2,1)S(1)} all-to-all(bf16[8,2,20480]{2,1,0:T(2,128)(2,1)S(1)} %reshape.179), channel_id=1, replica_groups=mesh['section'=4,'seq'=8] {'seq'}, dimensions={0} | all-to-all | bytes 1310720 | tf_op jit(solution)/shard_map/all_to_all | solution.py:160
  203.1 10.0 %collective-permute-done = bf16[1,320,1024]{2,1,0:T(8,128)(2,1)S(1)} collective-permute-done((bf16[1,320,1024]{2,1,0:T(8,128)(2,1)S(1)}, bf16[1,320,1024]{2,1,0:T(8,128)(2,1)S(1)}, u32[]{:S(2)}, u32[]{:S(2)}) %collective-permute-start) | collective-permute-done | bytes 655392 | tf_op jit(solution)/shard_map/ppermute | solution.py:29
  (154 shorter events, 58.0 us)
Async XLA Ops:
  11.9 7.4 %copy-start.3 = (bf16[1,320,1024]{2,1,0:T(8,128)(2,1)S(1)}, bf16[1,320,1024]{2,1,0:T(8,128)(2,1)}, u32[]{:S(2)}) copy-start(bf16[1,320,1024]{2,1,0:T(8,128)(2,1)} %param.11) | copy-start | bytes 1966084
  11.9 24.7 %all-to-all-start.2 = ((bf16[8,2,20480]{2,1,0:T(2,128)(2,1)}), bf16[8,2,20480]{2,1,0:T(2,128)(2,1)S(1)}, u32[]{:S(2)}, u32[]{:S(2)}) async-start(bf16[8,2,20480]{2,1,0:T(2,128)(2,1)} %reshape.177), calls=%async_computation.2 | async-start | bytes 1310720 | tf_op jit(solution)/shard_map/all_to_all | solution.py:139
  29.0 12.1 %copy-start.4 = (bf16[1,320,1024]{2,1,0:T(8,128)(2,1)S(1)}, bf16[1,320,1024]{2,1,0:T(8,128)(2,1)}, u32[]{:S(2)}) copy-start(bf16[1,320,1024]{2,1,0:T(8,128)(2,1)} %param.10) | copy-start | bytes 1966084
  36.6 21.2 %all-to-all-start.1 = ((bf16[8,2,20480]{2,1,0:T(2,128)(2,1)}), bf16[8,2,20480]{2,1,0:T(2,128)(2,1)}, u32[]{:S(2)}, u32[]{:S(2)}) async-start(bf16[8,2,20480]{2,1,0:T(2,128)(2,1)} %reshape.175), calls=%async_computation.1 | async-start | bytes 1310720 | tf_op jit(solution)/shard_map/all_to_all | solution.py:138
  49.0 13.3 %copy-start.5 = (s32[1,2]{1,0:T(1,128)S(1)}, s32[1,2]{1,0:T(1,128)}, u32[]{:S(2)}) copy-start(s32[1,2]{1,0:T(1,128)} %param.16) | copy-start | bytes 28
  49.0 16.0 %copy-start.6 = (s32[1,40,3]{1,0,2:T(1,128)S(1)}, s32[1,40,3]{1,0,2:T(1,128)}, u32[]{:S(2)}) copy-start(s32[1,40,3]{1,0,2:T(1,128)} %param.17) | copy-start | bytes 1444
  57.8 21.2 %all-to-all-start = ((bf16[8,2,20480]{2,1,0:T(2,128)(2,1)}), bf16[8,2,20480]{2,1,0:T(2,128)(2,1)}, u32[]{:S(2)}, u32[]{:S(2)}) async-start(bf16[8,2,20480]{2,1,0:T(2,128)(2,1)} %reshape.173), calls=%async_computation | async-start | bytes 1310720 | tf_op jit(solution)/shard_map/all_to_all | solution.py:136
  83.7 1.1 copy-start.1
  97.9 2.6 %copy-start.2 = (bf16[128,128]{1,0:T(8,128)(2,1)S(1)}, bf16[128,128]{1,0:T(8,128)(2,1)}, u32[]{:S(2)}) copy-start(bf16[128,128]{1,0:T(8,128)(2,1)} %get-tuple-element.477) | copy-start | bytes 98308 | tf_op jit(solution)/shard_map/while
  98.1 2.6 %copy-start = (bf16[512,128]{1,0:T(8,128)(2,1)S(1)}, bf16[512,128]{1,0:T(8,128)(2,1)}, u32[]{:S(2)}) copy-start(bf16[512,128]{1,0:T(8,128)(2,1)} %get-tuple-element.421) | copy-start | bytes 393220 | tf_op jit(solution)/shard_map/while
  112.5 2.6 %copy-start.2 = (bf16[128,128]{1,0:T(8,128)(2,1)S(1)}, bf16[128,128]{1,0:T(8,128)(2,1)}, u32[]{:S(2)}) copy-start(bf16[128,128]{1,0:T(8,128)(2,1)} %get-tuple-element.477) | copy-start | bytes 98308 | tf_op jit(solution)/shard_map/while
  112.6 2.6 %copy-start = (bf16[512,128]{1,0:T(8,128)(2,1)S(1)}, bf16[512,128]{1,0:T(8,128)(2,1)}, u32[]{:S(2)}) copy-start(bf16[512,128]{1,0:T(8,128)(2,1)} %get-tuple-element.421) | copy-start | bytes 393220 | tf_op jit(solution)/shard_map/while
  126.9 2.6 %copy-start.2 = (bf16[128,128]{1,0:T(8,128)(2,1)S(1)}, bf16[128,128]{1,0:T(8,128)(2,1)}, u32[]{:S(2)}) copy-start(bf16[128,128]{1,0:T(8,128)(2,1)} %get-tuple-element.477) | copy-start | bytes 98308 | tf_op jit(solution)/shard_map/while
  127.0 2.6 %copy-start = (bf16[512,128]{1,0:T(8,128)(2,1)S(1)}, bf16[512,128]{1,0:T(8,128)(2,1)}, u32[]{:S(2)}) copy-start(bf16[512,128]{1,0:T(8,128)(2,1)} %get-tuple-element.421) | copy-start | bytes 393220 | tf_op jit(solution)/shard_map/while
  141.3 2.6 %copy-start.2 = (bf16[128,128]{1,0:T(8,128)(2,1)S(1)}, bf16[128,128]{1,0:T(8,128)(2,1)}, u32[]{:S(2)}) copy-start(bf16[128,128]{1,0:T(8,128)(2,1)} %get-tuple-element.477) | copy-start | bytes 98308 | tf_op jit(solution)/shard_map/while
  141.4 2.6 %copy-start = (bf16[512,128]{1,0:T(8,128)(2,1)S(1)}, bf16[512,128]{1,0:T(8,128)(2,1)}, u32[]{:S(2)}) copy-start(bf16[512,128]{1,0:T(8,128)(2,1)} %get-tuple-element.421) | copy-start | bytes 393220 | tf_op jit(solution)/shard_map/while
  155.7 2.6 %copy-start.2 = (bf16[128,128]{1,0:T(8,128)(2,1)S(1)}, bf16[128,128]{1,0:T(8,128)(2,1)}, u32[]{:S(2)}) copy-start(bf16[128,128]{1,0:T(8,128)(2,1)} %get-tuple-element.477) | copy-start | bytes 98308 | tf_op jit(solution)/shard_map/while
  155.8 2.6 %copy-start = (bf16[512,128]{1,0:T(8,128)(2,1)S(1)}, bf16[512,128]{1,0:T(8,128)(2,1)}, u32[]{:S(2)}) copy-start(bf16[512,128]{1,0:T(8,128)(2,1)} %get-tuple-element.421) | copy-start | bytes 393220 | tf_op jit(solution)/shard_map/while
  203.0 10.1 %collective-permute-start = (bf16[1,320,1024]{2,1,0:T(8,128)(2,1)S(1)}, bf16[1,320,1024]{2,1,0:T(8,128)(2,1)S(1)}, u32[]{:S(2)}, u32[]{:S(2)}) collective-permute-start(bf16[1,320,1024]{2,1,0:T(8,128)(2,1)S(1)} %bitcast.144), channel_id=1, source_target_pairs={{0,8},{8,16},{16,24},{24,0},{1,9},{9,17},{17,25},{25,1},{2,10},{10... | collective-permute-start | bytes 1966088 | tf_op jit(solution)/shard_map/ppermute | solution.py:29
where the time goes:
time: 216 us; the launch traced here: 214 us
  local copies, waits for them, and re-layouts  82.2 us (38%)
  other arithmetic  40.6 us (19%)
  waiting for transfers between devices  25.4 us (12%)
  blocking collectives  21.6 us (10%)
  matrix products  18.3 us (8%)
  starting transfers between devices  16.4 us (8%)
  loops' own time  7.2 us (3%)
  between operations  2.26 us (1%)
    unnamed x4, other arithmetic  31 us
    unnamed x28, local copies, waits for them, and re-layouts  28.2 us
    all_to_all x1, blocking collectives, per_device(): lax.all_to_all(as_sent(attended), 'seq', split_axis=1, concat_axis=2, til...  21.6 us
    gather x5, local copies, waits for them, and re-layouts, one_group(): rand_values = value_blocks[random_part].reshape(group, RAND * BLK, HD)  10.3 us
    gather x5, local copies, waits for them, and re-layouts, one_group(): rand_keys = key_blocks[random_part].reshape(group, RAND * BLK, HD)  10.2 us
    ppermute x1, waiting for transfers between devices, passed_along(): lax.ppermute(shard, axis, [(i, (i + by) % devices) for i in range(devices)])  10 us
    slice x5, local copies, waits for them, and re-layouts, one_group(): near_value_part[offset:offset + group * BLK].reshape(group, BLK, HD)  9.7 us
    all_to_all x1, waiting for transfers between devices, per_device(): lax.all_to_all(values_new, 'seq', split_axis=2, concat_axis=1, tiled=True)  7.63 us
  transfers between devices with their start and end apart: 4, of which 4 were waited for; matrix products, arithmetic and copies ran while one was open for 16% of the time, Pallas kernels for 0%

commit v1 on v0

v1 whole, which is shorter than its diff:
```python
import functools
import math

import jax
import jax.numpy as jnp
from jax import lax
from jax.experimental import pallas as pl
from jax.experimental.pallas import tpu as pltpu
from jax.sharding import PartitionSpec as P

HD = 128
BLK = 64
WMAX = 3
GLOB = 2
RAND = 3
LANES = 128
STAT_ROWS = 16
MASKED = -1e30
EXPO_SCALE = math.log2(math.e) / math.sqrt(HD)
VMEM_LIMIT = 56 * 1024 * 1024
CHUNKS_PER_CALL = 8

whole_vmem = pl.BlockSpec(memory_space=pltpu.VMEM)
whole_smem = pl.BlockSpec(memory_space=pltpu.SMEM)


def partner(me, step):
    return jnp.bitwise_xor(me, step)


def scores_of(query, keys):
    return lax.dot_general(
        query, keys, (((1,), (1,)), ((), ())), preferred_element_type=jnp.float32
    )


def softmax_part(pieces, values):
    top = functools.reduce(
        jnp.maximum, [jnp.max(piece, axis=1, keepdims=True) for piece in pieces]
    )
    expo = [jnp.exp2((piece - top) * EXPO_SCALE) for piece in pieces]
    total = functools.reduce(jnp.add, [jnp.sum(part, axis=1, keepdims=True) for part in expo])
    mixed = functools.reduce(
        jnp.add,
        [
            jnp.dot(part.astype(jnp.bfloat16), value, preferred_element_type=jnp.float32)
            for part, value in zip(expo, values)
        ],
    )
    return mixed / total, top * EXPO_SCALE + jnp.log2(total)


def as_row(column, offset):
    shape = (column.shape[0], LANES)
    row_at = lax.broadcasted_iota(jnp.int32, shape, 0)
    lane_at = lax.broadcasted_iota(jnp.int32, shape, 1)
    spread = jnp.where(lane_at == row_at + offset, column, 0.0)
    return jnp.sum(spread, axis=0, keepdims=True)


def stat_tile(rows):
    at = lax.broadcasted_iota(jnp.int32, (STAT_ROWS, LANES), 0)
    tile = jnp.zeros((STAT_ROWS, LANES), jnp.float32)
    count = len(rows)
    for index, row in enumerate(rows):
        high = row.astype(jnp.bfloat16).astype(jnp.float32)
        middle = (row - high).astype(jnp.bfloat16).astype(jnp.float32)
        low = row - high - middle
        for part, value in enumerate((high, middle, low)):
            tile = jnp.where(at == part * count + index, value, tile)
    return tile.astype(jnp.bfloat16)


def stat_rows_of(tile, count):
    wide = tile.astype(jnp.float32)
    return [
        wide[index : index + 1]
        + wide[count + index : count + index + 1]
        + wide[2 * count + index : 2 * count + index + 1]
        for index in range(count)
    ]


def stat_count(rows):
    return -(-rows // LANES)


def split_kernel(steps, me_ref, query_ref, key_ref, value_ref, *out_refs):
    me = me_ref[0]
    rows = query_ref.shape[0]
    halo = (WMAX - 1) * BLK
    out_refs[0][0] = key_ref[rows - halo :, :]
    out_refs[0][1] = value_ref[rows - halo :, :]
    for step in range(steps):
        head = pl.multiple_of(partner(me, step) * HD, HD)
        out_refs[1 + step][...] = query_ref[:, pl.ds(head, HD)]


def far_kernel(
    steps, me_ref, span_ref, global_ref, random_ref, key_ref, value_ref, *refs
):
    me = me_ref[0]
    span = span_ref[0]
    count = len(steps)
    query_refs, out_refs = refs[:count], refs[count:]
    last = key_ref.shape[0] // BLK - 1

    def block(ref, at):
        if isinstance(at, int):
            return ref[at * BLK : (at + 1) * BLK, :]
        return ref[pl.ds(pl.multiple_of(at * BLK, BLK), BLK), :]

    glob_keys = [block(key_ref, global_ref[g]) for g in range(GLOB)]
    glob_values = [block(value_ref, global_ref[g]) for g in range(GLOB)]
    for index, step in enumerate(steps):
        chunk = partner(me, step)
        query_ref, out_ref = query_refs[index], out_refs[index]
        rows = query_ref.shape[0]
        blocks = rows // BLK
        first = chunk == 0
        stats = []
        for b in range(blocks):
            query = query_ref[b * BLK : (b + 1) * BLK, :]
            base = (chunk * blocks + b) * RAND
            picks = [random_ref[base + r] for r in range(RAND)]
            keys = glob_keys + [block(key_ref, pick) for pick in picks]
            values = glob_values + [block(value_ref, pick) for pick in picks]
            known = len(keys) * BLK
            spare = [last + 1 + b - w for w in range(b + 1, WMAX)]
            keys = keys + [block(key_ref, at) for at in spare]
            values = values + [block(value_ref, at) for at in spare]
            scores = scores_of(query, jnp.concatenate(keys, axis=0))
            if spare:
                open_slots = jnp.where(first, jnp.clip(span - (b + 1), 0, len(spare)), 0)
                lane_at = lax.broadcasted_iota(jnp.int32, scores.shape, 1)
                scores = jnp.where(lane_at < known + open_slots * BLK, scores, MASKED)
            mixed, lse = softmax_part([scores], [jnp.concatenate(values, axis=0)])
            out_ref[b * BLK : (b + 1) * BLK, :] = mixed.astype(jnp.bfloat16)
            row = as_row(lse, (b * BLK) % LANES)
            if (b * BLK) % LANES:
                stats[-1] = stats[-1] + row
            else:
                stats.append(row)
        out_ref[rows:, :] = stat_tile(stats)


def near_kernel(
    me_ref, spans_ref, query_ref, key_ref, value_ref, halo_ref, out_ref
):
    me = me_ref[0]
    rows = query_ref.shape[0]
    heads = query_ref.shape[1] // HD
    halo = (WMAX - 1) * BLK

    def one_head(head, carry):
        lanes = pl.ds(pl.multiple_of(head * HD, HD), HD)
        span = spans_ref[head]
        stats = []
        for start in range(0, rows, 2 * BLK):
            size = min(2 * BLK, rows - start)
            query = query_ref[start : start + size, lanes]
            if start < halo:
                keys = [halo_ref[0, start:, lanes], key_ref[: start + size, lanes]]
                values = [halo_ref[1, start:, lanes], value_ref[: start + size, lanes]]
                keys, values = jnp.concatenate(keys, axis=0), jnp.concatenate(values, axis=0)
            else:
                keys = key_ref[start - halo : start + size, lanes]
                values = value_ref[start - halo : start + size, lanes]
            scores = scores_of(query, keys)
            row_at = lax.broadcasted_iota(jnp.int32, scores.shape, 0)
            lane_at = lax.broadcasted_iota(jnp.int32, scores.shape, 1)
            allowed = (lane_at <= row_at + halo) & (
                lane_at // BLK - row_at // BLK > WMAX - 1 - span
            )
            if start < halo:
                closed = jnp.where(me == 0, halo - start, 0)
                allowed = allowed & (lane_at >= closed)
            mixed, lse = softmax_part([jnp.where(allowed, scores, MASKED)], [values])
            out_ref[start : start + size, lanes] = mixed.astype(jnp.bfloat16)
            stats.append(as_row(lse, 0))
        out_ref[rows:, lanes] = stat_tile(stats)
        return carry

    lax.fori_loop(0, heads, one_head, 0)


def merge_kernel(steps, me_ref, near_ref, *refs):
    me = me_ref[0]
    far_refs, out_ref = refs[:-1], refs[-1]
    rows = out_ref.shape[0]
    count = stat_count(rows)
    for step in range(steps):
        far_ref = far_refs[step]
        lanes = pl.ds(pl.multiple_of(partner(me, step) * HD, HD), HD)
        far_stats = stat_rows_of(far_ref[rows:, :], count)
        near_stats = stat_rows_of(near_ref[rows:, lanes], count)
        for index in range(count):
            start = index * LANES
            size = min(LANES, rows - start)
            share = 1.0 / (1.0 + jnp.exp2(near_stats[index] - far_stats[index]))
            row_at = lax.broadcasted_iota(jnp.int32, (size, LANES), 0)
            lane_at = lax.broadcasted_iota(jnp.int32, (size, LANES), 1)
            column = jnp.sum(
                jnp.where(row_at == lane_at, share, 0.0), axis=1, keepdims=True
            )
            far = far_ref[start : start + size, :].astype(jnp.float32)
            near = near_ref[start : start + size, lanes].astype(jnp.float32)
            out_ref[start : start + size, lanes] = (
                far * column + near * (1.0 - column)
            ).astype(jnp.bfloat16)


def params():
    return pltpu.CompilerParams(vmem_limit_bytes=VMEM_LIMIT)


def per_device(
    queries, keys_new, values_new, keys_cache, values_cache, window, global_blocks, random_blocks
):
    section_count = lax.axis_size("section")
    seq_count = lax.axis_size("seq")
    rows, wide = queries.shape[1], queries.shape[2]
    halo = (WMAX - 1) * BLK
    heads = wide // HD
    bf16 = jnp.bfloat16
    me = lax.axis_index("seq").astype(jnp.int32)[None]
    spans = lax.all_gather(window[0], "seq", axis=0, tiled=True)

    parts = pl.pallas_call(
        functools.partial(split_kernel, seq_count),
        out_shape=[jax.ShapeDtypeStruct((2, halo, wide), bf16)]
        + [jax.ShapeDtypeStruct((rows, HD), bf16)] * seq_count,
        in_specs=[whole_smem] + [whole_vmem] * 3,
        out_specs=[whole_vmem] * (1 + seq_count),
        compiler_params=params(),
        cost_estimate=pl.CostEstimate(flops=0, bytes_accessed=5 * rows * wide, transcendentals=0),
        name="split",
    )(me, queries[0], keys_new[0], values_new[0])
    mine, sent = parts[0], parts[1:]

    def swapped(shard, step):
        if step == 0:
            return shard
        return lax.ppermute(shard, "seq", [(i, i ^ step) for i in range(seq_count)])

    order = sorted(range(seq_count), reverse=True)
    came = {step: swapped(sent[step], step) for step in order}
    before = lax.ppermute(mine, "seq", [(i, i + 1) for i in range(seq_count - 1)])

    picks = random_blocks[0].reshape(-1)

    def far_call(steps):
        count = len(steps)
        return pl.pallas_call(
            functools.partial(far_kernel, steps),
            out_shape=[jax.ShapeDtypeStruct((rows + STAT_ROWS, HD), bf16)] * count,
            in_specs=[whole_smem] * 4 + [whole_vmem] * (2 + count),
            out_specs=[whole_vmem] * count,
            compiler_params=params(),
            cost_estimate=pl.CostEstimate(
                flops=count * rows * 320 * HD * 4,
                bytes_accessed=2 * 2 * keys_cache.shape[1] * HD + 4 * count * rows * HD,
                transcendentals=count * rows * 320,
            ),
            name="far",
        )(
            me,
            window[0],
            global_blocks[0],
            picks,
            keys_cache[0],
            values_cache[0],
            *[came[step] for step in steps],
        )

    far = {}
    for begin in range(0, seq_count, CHUNKS_PER_CALL):
        steps = order[begin : begin + CHUNKS_PER_CALL]
        far.update(zip(steps, far_call(steps)))

    def onward(shard, step):
        pairs = [
            (s * seq_count + t, ((s + 1) % section_count) * seq_count + (t ^ step))
            for s in range(section_count)
            for t in range(seq_count)
        ]
        return lax.ppermute(shard, ("section", "seq"), pairs)

    handed_far = {step: onward(far[step], step) for step in order}

    near = pl.pallas_call(
        near_kernel,
        out_shape=jax.ShapeDtypeStruct((rows + STAT_ROWS, wide), bf16),
        in_specs=[whole_smem] * 2 + [whole_vmem] * 4,
        out_specs=whole_vmem,
        compiler_params=params(),
        cost_estimate=pl.CostEstimate(
            flops=heads * rows * 256 * HD * 4,
            bytes_accessed=9 * rows * wide,
            transcendentals=heads * rows * 256,
        ),
        name="near",
    )(me, spans, queries[0], keys_new[0], values_new[0], before)
    handed_near = lax.ppermute(
        near, "section", [(s, (s + 1) % section_count) for s in range(section_count)]
    )

    merged = pl.pallas_call(
        functools.partial(merge_kernel, seq_count),
        out_shape=jax.ShapeDtypeStruct((rows, wide), bf16),
        in_specs=[whole_smem] + [whole_vmem] * (1 + seq_count),
        out_specs=whole_vmem,
        compiler_params=params(),
        cost_estimate=pl.CostEstimate(flops=0, bytes_accessed=6 * rows * wide, transcendentals=0),
        name="merge",
    )(me, handed_near, *[handed_far[step] for step in range(seq_count)])
    return merged[None]


def solution(mesh):
    placed = (
        P("section", "seq", None),
        P("section", "seq", None),
        P("section", "seq", None),
        P("section", None, "seq"),
        P("section", None, "seq"),
        P("section", "seq"),
        P("section", None),
        P("section", None, None),
    )
    return jax.shard_map(
        per_device, mesh=mesh, in_specs=placed, out_specs=P("section", "seq", None), check_vma=False
    )
```

time: 216 us -> 98 us (0.45)
  local copies, waits for them, and re-layouts: 82.2 us -> 4.93 us
  other arithmetic: 40.6 us -> 0 us
  Pallas kernels: 0 us -> 26.1 us
  starting transfers between devices: 16.4 us -> 37.5 us
  matrix products: 18.3 us -> 0 us
  waiting for transfers between devices: 25.4 us -> 14.9 us
  blocking collectives: 21.6 us -> 12.5 us
  loops' own time: 7.2 us -> 0 us
    ppermute x1 -> x17, starting transfers between devices: 0.06 us -> 37.5 us  [the longest x7 21.4 us: swapped(): return lax.ppermute(shard, 'seq', [(i, i ^ step) for i in range(seq_count)])]
    unnamed x4 -> x0, other arithmetic: 31 us -> none
    pallas_call x0 -> x4, Pallas kernels: none -> 26.1 us  [the longest x1 13 us: far_call(): pl.pallas_call(functools.partial(far_kernel, steps), out_shape=[jax.Shape...]
    unnamed x28 -> x56, local copies, waits for them, and re-layouts: 28.2 us -> 4.3 us
    all_to_all x1 -> x0, blocking collectives: 21.6 us -> none  [per_device(): lax.all_to_all(as_sent(attended), 'seq', split_axis=1, concat_axis=2, til...]
    gather x10 -> x0, local copies, waits for them, and re-layouts: 20.5 us -> none  [the longest x5 10.3 us: one_group(): rand_values = value_blocks[random_part].reshape(group, RAND * BLK, HD)]
    dot_general x50 -> x0, matrix products: 18.3 us -> none  [the longest x15 6.15 us: one_group(): jnp.einsum('gij,gjh->gih', weights[:, :, slot * BLK:(slot + 1) * BLK], ne...]
    all_to_all x3 -> x0, starting transfers between devices: 16.3 us -> none  [the longest x1 7.41 us: per_device(): lax.all_to_all(values_new, 'seq', split_axis=2, concat_axis=1, tiled=True)]
  transfers between devices with their start and end apart: 4 -> 17, of which waited for: 4 -> 7; matrix products, arithmetic and copies ran while one was open for 16% -> 2% of each run, Pallas kernels for 0% -> 13%
where the time goes in v1:
time: 98 us; the launch traced here: 96.7 us
  starting transfers between devices  37.5 us (38%)
  Pallas kernels  26.1 us (27%)
  waiting for transfers between devices  14.9 us (15%)
  blocking collectives  12.5 us (13%)
  local copies, waits for them, and re-layouts  4.93 us (5%)
    ppermute x7, starting transfers between devices, swapped(): return lax.ppermute(shard, 'seq', [(i, i ^ step) for i in range(seq_count)])  21.4 us
    pallas_call x1, Pallas kernels, far_call(): pl.pallas_call(functools.partial(far_kernel, steps), out_shape=[jax.Shape...  13 us
    all_gather x1, blocking collectives, per_device(): spans = lax.all_gather(window[0], 'seq', axis=0, tiled=True)  12.5 us
    ppermute x8, starting transfers between devices, onward(): return lax.ppermute(shard, ('section', 'seq'), pairs)  11.1 us
    ppermute x8, waiting for transfers between devices, onward(): return lax.ppermute(shard, ('section', 'seq'), pairs)  10.5 us
    pallas_call x1, Pallas kernels, per_device(): pl.pallas_call(near_kernel, out_shape=jax.ShapeDtypeStruct((rows + STAT_R...  7.8 us
    ppermute x1, starting transfers between devices, per_device(): lax.ppermute(mine, 'seq', [(i, i + 1) for i in range(seq_count - 1)])  4.89 us
    ppermute x7, waiting for transfers between devices, swapped(): return lax.ppermute(shard, 'seq', [(i, i ^ step) for i in range(seq_count)])  4.4 us
  transfers between devices with their start and end apart: 17, of which 7 were waited for; matrix products, arithmetic and copies ran while one was open for 2% of the time, Pallas kernels for 13%

profile of v1, /device:TPU:0, one launch (start us, length us, event | category | flops | bytes accessed | tf_op | source)
XLA Modules:
  0.0 96.7 jit_solution(17578598957815099965)
XLA Ops:
  0.0 2.6 %split.1 = (bf16[2,128,1024]{2,1,0:T(8,128)(2,1)}, bf16[320,128]{1,0:T(8,128)(2,1)}, bf16[320,128]{1,0:T(8,128)(2,1)}, bf16[320,128]{1,0:T(8,128)(2,1)}, bf16[32...) custom-call(s32[1]{0:T(128)} %bitcast.me_ref, ...), custom_call_target="tpu_custom_call" | custom-call | bytes 1638400 | tf_op jit(solution)/shard_map/split/pallas_call | solution.py:229
  2.6 4.9 %collective-permute-start = (bf16[2,128,1024]{2,1,0:T(8,128)(2,1)}, bf16[2,128,1024]{2,1,0:T(8,128)(2,1)S(1)}, u32[]{:S(2)}, u32[]{:S(2)}) collective-permute-start(bf16[2,128,1024]{2,1,0:T(8,128)(2,1)} %get-tuple-element.22), channel_id=1, source_target_pairs={{0,1},{1,2},{2,3},{3,4},{4,5},{5,6},{6,7},{8,9},{9,10},{10,11},{11... | collective-permute-start | bytes 1572872 | tf_op jit(solution)/shard_map/ppermute | solution.py:248
  8.1 0.6 dynamic-slice
  8.7 0.7 bitcast_dynamic-update-slice_fusion
  9.4 12.5 %all-reduce.spans_ref = s32[8]{0:T(128)} all-reduce(s32[8]{0:T(128)S(1)} %bitcast_dynamic-update-slice_fusion), channel_id=2, replica_groups=mesh['section'=4,'seq'=8] {'seq'}, use_global_device_ids=true, to_apply=%add | all-reduce | flops 8 | bytes 64 | tf_op jit(solution)/shard_map/all_gather | solution.py:227
  21.9 0.8 copy-done.1
  22.7 7.8 %near.1 = bf16[336,1024]{1,0:T(8,128)(2,1)} custom-call(s32[1]{0:T(128)} %bitcast.me_ref, s32[8]{0:T(128)} %all-reduce.spans_ref, bf16[320,1024]{1,0:T(8,128)(2,1)} %bitcast.13, bf16[320,1024]{1,0:T(8,128)(2,1)} %bitcast.15, bf16[320,1024]{1,0:T(8,128)(2,1)} %bitcast.17, bf16[2,128,1024]{2,1,0:T(8,128)(2,1)} %copy-done.1), custom_call_target="tpu_custom_call" | custom-call | flops 335544320 | bytes 2949120 | tf_op jit(solution)/shard_map/near/pallas_call | solution.py:291
  30.5 7.1 %collective-permute-start.2 = (bf16[320,128]{1,0:T(8,128)(2,1)S(1)}, bf16[320,128]{1,0:T(8,128)(2,1)S(1)}, u32[]{:S(2)}, u32[]{:S(2)}) collective-permute-start(bf16[320,128]{1,0:T(8,128)(2,1)S(1)} %copy-done.24), channel_id=1, source_target_pairs={{0,7},{1,6},{2,5},{3,4},{4,3},{5,2},{6,1},{7,0},{8,15},{9,14},{10,... | collective-permute-start | bytes 245768 | tf_op jit(solution)/shard_map/ppermute | solution.py:244
  37.6 3.6 %collective-permute-start.3 = (bf16[320,128]{1,0:T(8,128)(2,1)S(1)}, bf16[320,128]{1,0:T(8,128)(2,1)S(1)}, u32[]{:S(2)}, u32[]{:S(2)}) collective-permute-start(bf16[320,128]{1,0:T(8,128)(2,1)S(1)} %copy-done.23), channel_id=1, source_target_pairs={{0,6},{1,7},{2,4},{3,5},{4,2},{5,3},{6,0},{7,1},{8,14},{9,15},{10,... | collective-permute-start | bytes 245768 | tf_op jit(solution)/shard_map/ppermute | solution.py:244
  41.4 2.4 %collective-permute-start.6 = (bf16[320,128]{1,0:T(8,128)(2,1)S(1)}, bf16[320,128]{1,0:T(8,128)(2,1)S(1)}, u32[]{:S(2)}, u32[]{:S(2)}) collective-permute-start(bf16[320,128]{1,0:T(8,128)(2,1)S(1)} %copy-done.20), channel_id=1, source_target_pairs={{0,3},{1,2},{2,1},{3,0},{4,7},{5,6},{6,5},{7,4},{8,11},{9,10},{10,... | collective-permute-start | bytes 245768 | tf_op jit(solution)/shard_map/ppermute | solution.py:244
  43.8 2.1 %collective-permute-done.3.refs_1_ = bf16[320,128]{1,0:T(8,128)(2,1)S(1)} collective-permute-done((bf16[320,128]{1,0:T(8,128)(2,1)S(1)}, bf16[320,128]{1,0:T(8,128)(2,1)S(1)}, u32[]{:S(2)}, u32[]{:S(2)}) %collective-permute-start.3) | collective-permute-done | bytes 81952 | tf_op jit(solution)/shard_map/ppermute | solution.py:244
  45.9 5.6 %collective-permute-start.7 = (bf16[320,128]{1,0:T(8,128)(2,1)S(1)}, bf16[320,128]{1,0:T(8,128)(2,1)S(1)}, u32[]{:S(2)}, u32[]{:S(2)}) collective-permute-start(bf16[320,128]{1,0:T(8,128)(2,1)S(1)} %copy-done.19), channel_id=1, source_target_pairs={{0,2},{1,3},{2,0},{3,1},{4,6},{5,7},{6,4},{7,5},{8,10},{9,11},{10,... | collective-permute-start | bytes 245768 | tf_op jit(solution)/shard_map/ppermute | solution.py:244
  51.5 2.6 %collective-permute-start.8 = (bf16[320,128]{1,0:T(8,128)(2,1)S(1)}, bf16[320,128]{1,0:T(8,128)(2,1)S(1)}, u32[]{:S(2)}, u32[]{:S(2)}) collective-permute-start(bf16[320,128]{1,0:T(8,128)(2,1)S(1)} %copy-done.18), channel_id=1, source_target_pairs={{0,1},{1,0},{2,3},{3,2},{4,5},{5,4},{6,7},{7,6},{8,9},{9,8},{10,11... | collective-permute-start | bytes 245768 | tf_op jit(solution)/shard_map/ppermute | solution.py:244
  54.2 0.6 reshape_squeeze.3.random_ref
  54.9 1.7 %collective-permute-done.7.refs_5_ = bf16[320,128]{1,0:T(8,128)(2,1)S(1)} collective-permute-done((bf16[320,128]{1,0:T(8,128)(2,1)S(1)}, bf16[320,128]{1,0:T(8,128)(2,1)S(1)}, u32[]{:S(2)}, u32[]{:S(2)}) %collective-permute-start.7) | collective-permute-done | bytes 81952 | tf_op jit(solution)/shard_map/ppermute | solution.py:244
  56.6 0.6 collective-permute-done.8.refs_6_
  57.2 0.6 copy-done.16
  57.8 13.0 %far.1 = (bf16[336,128]{1,0:T(8,128)(2,1)}, bf16[336,128]{1,0:T(8,128)(2,1)}, bf16[336,128]{1,0:T(8,128)(2,1)}, bf16[336,128]{1,0:T(8,128)(2,1)}, bf16[336,128]{...) custom-call(s32[1]{0:T(128)} %bitcast.me_ref, ...), custom_call_target="tpu_custom_call" | custom-call | flops 419430400 | bytes 4456448 | tf_op jit(solution)/shard_map/far/pallas_call | solution.py:254
  70.9 0.1 collective-permute-start.9
  71.0 3.0 %collective-permute-start.10 = (bf16[336,128]{1,0:T(8,128)(2,1)}, bf16[336,128]{1,0:T(8,128)(2,1)S(1)}, u32[]{:S(2)}, u32[]{:S(2)}) collective-permute-start(bf16[336,128]{1,0:T(8,128)(2,1)} %get-tuple-element.32), channel_id=1, source_target_pairs={{0,9},{1,8},{2,11},{3,10},{4,13},{5,12},{6,15},{7,14},{8,17},{9,16... | collective-permute-start | bytes 258056 | tf_op jit(solution)/shard_map/ppermute | solution.py:287
  74.0 1.3 %collective-permute-start.12 = (bf16[336,128]{1,0:T(8,128)(2,1)}, bf16[336,128]{1,0:T(8,128)(2,1)S(1)}, u32[]{:S(2)}, u32[]{:S(2)}) collective-permute-start(bf16[336,128]{1,0:T(8,128)(2,1)} %get-tuple-element.34), channel_id=1, source_target_pairs={{0,11},{1,10},{2,9},{3,8},{4,15},{5,14},{6,13},{7,12},{8,19},{9,18... | collective-permute-start | bytes 258056 | tf_op jit(solution)/shard_map/ppermute | solution.py:287
  75.3 0.7 collective-permute-start.13
  76.0 1.6 %collective-permute-done.10.refs_1_ = bf16[336,128]{1,0:T(8,128)(2,1)S(1)} collective-permute-done((bf16[336,128]{1,0:T(8,128)(2,1)}, bf16[336,128]{1,0:T(8,128)(2,1)S(1)}, u32[]{:S(2)}, u32[]{:S(2)}) %collective-permute-start.10) | collective-permute-done | bytes 86048 | tf_op jit(solution)/shard_map/ppermute | solution.py:287
  77.6 2.6 %collective-permute-start.14 = (bf16[336,128]{1,0:T(8,128)(2,1)}, bf16[336,128]{1,0:T(8,128)(2,1)S(1)}, u32[]{:S(2)}, u32[]{:S(2)}) collective-permute-start(bf16[336,128]{1,0:T(8,128)(2,1)} %get-tuple-element.36), channel_id=1, source_target_pairs={{0,13},{1,12},{2,15},{3,14},{4,9},{5,8},{6,11},{7,10},{8,21},{9,20... | collective-permute-start | bytes 258056 | tf_op jit(solution)/shard_map/ppermute | solution.py:287
  80.2 0.8 collective-permute-start.15
  81.0 0.1 collective-permute-done.12.refs_3_
  81.2 2.6 %collective-permute-start.16 = (bf16[336,128]{1,0:T(8,128)(2,1)}, bf16[336,128]{1,0:T(8,128)(2,1)S(1)}, u32[]{:S(2)}, u32[]{:S(2)}) collective-permute-start(bf16[336,128]{1,0:T(8,128)(2,1)} %get-tuple-element.38), channel_id=1, source_target_pairs={{0,15},{1,14},{2,13},{3,12},{4,11},{5,10},{6,9},{7,8},{8,23},{9,22... | collective-permute-start | bytes 258056 | tf_op jit(solution)/shard_map/ppermute | solution.py:287
  83.8 1.8 %collective-permute-done.13.refs_4_ = bf16[336,128]{1,0:T(8,128)(2,1)S(1)} collective-permute-done((bf16[336,128]{1,0:T(8,128)(2,1)}, bf16[336,128]{1,0:T(8,128)(2,1)S(1)}, u32[]{:S(2)}, u32[]{:S(2)}) %collective-permute-start.13) | collective-permute-done | bytes 86048 | tf_op jit(solution)/shard_map/ppermute | solution.py:287
  85.5 6.9 %collective-permute-done.14.refs_5_ = bf16[336,128]{1,0:T(8,128)(2,1)S(1)} collective-permute-done((bf16[336,128]{1,0:T(8,128)(2,1)}, bf16[336,128]{1,0:T(8,128)(2,1)S(1)}, u32[]{:S(2)}, u32[]{:S(2)}) %collective-permute-start.14) | collective-permute-done | bytes 86048 | tf_op jit(solution)/shard_map/ppermute | solution.py:287
  92.5 0.6 copy-done.7
  93.2 0.9 copy-done
  94.0 2.7 %merge.1 = bf16[320,1024]{1,0:T(8,128)(2,1)} custom-call(s32[1]{0:T(128)} %bitcast.me_ref, bf16[336,1024]{1,0:T(8,128)(2,1)} %copy-done, bf16[336,128]{1,0:T(8,128)(2,1)} %copy-done.2, bf16[336,128]{1,0:T(8,128)(2,1)} %copy-done.3, bf16[336,128]{1,0:T(8,128)(2,1)} %copy-done.4, bf16[336,128]{1,0:T(8,128)(2,1)} %copy-done.5, bf16[336,128]{1,0:T(8,128)(2,1)} %copy-done.6, ...), custom_call_target="tpu_custom_call" | custom-call | bytes 1966080 | tf_op jit(solution)/shard_map/merge/pallas_call | solution.py:308
  (64 shorter events, 0.4 us)
Async XLA Ops:
  0.0 8.1 %copy-start.25 = (u32[32]{0:T(128)S(1)}, u32[32]{0:T(128)}, u32[]{:S(2)}) copy-start(u32[32]{0:T(128)} %constant.14) | copy-start | bytes 388
  2.6 19.4 %collective-permute-start = (bf16[2,128,1024]{2,1,0:T(8,128)(2,1)}, bf16[2,128,1024]{2,1,0:T(8,128)(2,1)S(1)}, u32[]{:S(2)}, u32[]{:S(2)}) collective-permute-start(bf16[2,128,1024]{2,1,0:T(8,128)(2,1)} %get-tuple-element.22), channel_id=1, source_target_pairs={{0,1},{1,2},{2,3},{3,4},{4,5},{5,6},{6,7},{8,9},{9,10},{10,11},{11... | collective-permute-start | bytes 1572872 | tf_op jit(solution)/shard_map/ppermute | solution.py:248
  21.9 8.7 %copy-start.24 = (bf16[320,128]{1,0:T(8,128)(2,1)S(1)}, bf16[320,128]{1,0:T(8,128)(2,1)}, u32[]{:S(2)}) copy-start(bf16[320,128]{1,0:T(8,128)(2,1)} %get-tuple-element.23) | copy-start | bytes 245764
  21.9 15.8 %copy-start.23 = (bf16[320,128]{1,0:T(8,128)(2,1)S(1)}, bf16[320,128]{1,0:T(8,128)(2,1)}, u32[]{:S(2)}) copy-start(bf16[320,128]{1,0:T(8,128)(2,1)} %get-tuple-element.24) | copy-start | bytes 245764
  21.9 19.4 %copy-start.22 = (bf16[320,128]{1,0:T(8,128)(2,1)S(1)}, bf16[320,128]{1,0:T(8,128)(2,1)}, u32[]{:S(2)}) copy-start(bf16[320,128]{1,0:T(8,128)(2,1)} %get-tuple-element.25) | copy-start | bytes 245764
  21.9 19.4 %copy-start.21 = (bf16[320,128]{1,0:T(8,128)(2,1)S(1)}, bf16[320,128]{1,0:T(8,128)(2,1)}, u32[]{:S(2)}) copy-start(bf16[320,128]{1,0:T(8,128)(2,1)} %get-tuple-element.26) | copy-start | bytes 245764
  21.9 19.5 %copy-start.20 = (bf16[320,128]{1,0:T(8,128)(2,1)S(1)}, bf16[320,128]{1,0:T(8,128)(2,1)}, u32[]{:S(2)}) copy-start(bf16[320,128]{1,0:T(8,128)(2,1)} %get-tuple-element.27) | copy-start | bytes 245764
  21.9 24.0 %copy-start.19 = (bf16[320,128]{1,0:T(8,128)(2,1)S(1)}, bf16[320,128]{1,0:T(8,128)(2,1)}, u32[]{:S(2)}) copy-start(bf16[320,128]{1,0:T(8,128)(2,1)} %get-tuple-element.28) | copy-start | bytes 245764
  21.9 29.6 %copy-start.18 = (bf16[320,128]{1,0:T(8,128)(2,1)S(1)}, bf16[320,128]{1,0:T(8,128)(2,1)}, u32[]{:S(2)}) copy-start(bf16[320,128]{1,0:T(8,128)(2,1)} %get-tuple-element.29) | copy-start | bytes 245764
  21.9 32.2 %copy-start.17 = (s32[1,40,3]{1,0,2:T(1,128)S(1)}, s32[1,40,3]{1,0,2:T(1,128)}, u32[]{:S(2)}) copy-start(s32[1,40,3]{1,0,2:T(1,128)} %param.15) | copy-start | bytes 1444
  30.5 62.0 %collective-permute-start.1 = (bf16[336,1024]{1,0:T(8,128)(2,1)}, bf16[336,1024]{1,0:T(8,128)(2,1)S(1)}, u32[]{:S(2)}, u32[]{:S(2)}) collective-permute-start(bf16[336,1024]{1,0:T(8,128)(2,1)} %near.1), channel_id=1, source_target_pairs={{0,8},{8,16},{16,24},{24,0},{1,9},{9,17},{17,25},{25,1},{2,10},{10... | collective-permute-start | bytes 2064392 | tf_op jit(solution)/shard_map/ppermute | solution.py:304
  30.5 10.8 %collective-permute-start.2 = (bf16[320,128]{1,0:T(8,128)(2,1)S(1)}, bf16[320,128]{1,0:T(8,128)(2,1)S(1)}, u32[]{:S(2)}, u32[]{:S(2)}) collective-permute-start(bf16[320,128]{1,0:T(8,128)(2,1)S(1)} %copy-done.24), channel_id=1, source_target_pairs={{0,7},{1,6},{2,5},{3,4},{4,3},{5,2},{6,1},{7,0},{8,15},{9,14},{10,... | collective-permute-start | bytes 245768 | tf_op jit(solution)/shard_map/ppermute | solution.py:244
  37.6 8.2 %collective-permute-start.3 = (bf16[320,128]{1,0:T(8,128)(2,1)S(1)}, bf16[320,128]{1,0:T(8,128)(2,1)S(1)}, u32[]{:S(2)}, u32[]{:S(2)}) collective-permute-start(bf16[320,128]{1,0:T(8,128)(2,1)S(1)} %copy-done.23), channel_id=1, source_target_pairs={{0,6},{1,7},{2,4},{3,5},{4,2},{5,3},{6,0},{7,1},{8,14},{9,15},{10,... | collective-permute-start | bytes 245768 | tf_op jit(solution)/shard_map/ppermute | solution.py:244
  41.2 10.2 %collective-permute-start.4 = (bf16[320,128]{1,0:T(8,128)(2,1)S(1)}, bf16[320,128]{1,0:T(8,128)(2,1)S(1)}, u32[]{:S(2)}, u32[]{:S(2)}) collective-permute-start(bf16[320,128]{1,0:T(8,128)(2,1)S(1)} %copy-done.22), channel_id=1, source_target_pairs={{0,5},{1,4},{2,7},{3,6},{4,1},{5,0},{6,3},{7,2},{8,13},{9,12},{10,... | collective-permute-start | bytes 245768 | tf_op jit(solution)/shard_map/ppermute | solution.py:244
  41.3 13.6 %collective-permute-start.5 = (bf16[320,128]{1,0:T(8,128)(2,1)S(1)}, bf16[320,128]{1,0:T(8,128)(2,1)S(1)}, u32[]{:S(2)}, u32[]{:S(2)}) collective-permute-start(bf16[320,128]{1,0:T(8,128)(2,1)S(1)} %copy-done.21), channel_id=1, source_target_pairs={{0,4},{1,5},{2,6},{3,7},{4,0},{5,1},{6,2},{7,3},{8,12},{9,13},{10,... | collective-permute-start | bytes 245768 | tf_op jit(solution)/shard_map/ppermute | solution.py:244
  41.3 15.8 %copy-start.10 = (bf16[320,128]{1,0:T(8,128)(2,1)}, bf16[320,128]{1,0:T(8,128)(2,1)S(1)}, u32[]{:S(2)}) copy-start(bf16[320,128]{1,0:T(8,128)(2,1)S(1)} %collective-permute-done.2.refs_0_) | copy-start | bytes 245764
  41.4 13.5 %collective-permute-start.6 = (bf16[320,128]{1,0:T(8,128)(2,1)S(1)}, bf16[320,128]{1,0:T(8,128)(2,1)S(1)}, u32[]{:S(2)}, u32[]{:S(2)}) collective-permute-start(bf16[320,128]{1,0:T(8,128)(2,1)S(1)} %copy-done.20), channel_id=1, source_target_pairs={{0,3},{1,2},{2,1},{3,0},{4,7},{5,6},{6,5},{7,4},{8,11},{9,10},{10,... | collective-permute-start | bytes 245768 | tf_op jit(solution)/shard_map/ppermute | solution.py:244
  45.9 11.3 %copy-start.11 = (bf16[320,128]{1,0:T(8,128)(2,1)}, bf16[320,128]{1,0:T(8,128)(2,1)S(1)}, u32[]{:S(2)}) copy-start(bf16[320,128]{1,0:T(8,128)(2,1)S(1)} %collective-permute-done.3.refs_1_) | copy-start | bytes 245764
  45.9 10.7 %collective-permute-start.7 = (bf16[320,128]{1,0:T(8,128)(2,1)S(1)}, bf16[320,128]{1,0:T(8,128)(2,1)S(1)}, u32[]{:S(2)}, u32[]{:S(2)}) collective-permute-start(bf16[320,128]{1,0:T(8,128)(2,1)S(1)} %copy-done.19), channel_id=1, source_target_pairs={{0,2},{1,3},{2,0},{3,1},{4,6},{5,7},{6,4},{7,5},{8,10},{9,11},{10,... | collective-permute-start | bytes 245768 | tf_op jit(solution)/shard_map/ppermute | solution.py:244
  51.5 5.7 %collective-permute-start.8 = (bf16[320,128]{1,0:T(8,128)(2,1)S(1)}, bf16[320,128]{1,0:T(8,128)(2,1)S(1)}, u32[]{:S(2)}, u32[]{:S(2)}) collective-permute-start(bf16[320,128]{1,0:T(8,128)(2,1)S(1)} %copy-done.18), channel_id=1, source_target_pairs={{0,1},{1,0},{2,3},{3,2},{4,5},{5,4},{6,7},{7,6},{8,9},{9,8},{10,11... | collective-permute-start | bytes 245768 | tf_op jit(solution)/shard_map/ppermute | solution.py:244
  70.9 4.4 %collective-permute-start.9 = (bf16[336,128]{1,0:T(8,128)(2,1)}, bf16[336,128]{1,0:T(8,128)(2,1)S(1)}, u32[]{:S(2)}, u32[]{:S(2)}) collective-permute-start(bf16[336,128]{1,0:T(8,128)(2,1)} %get-tuple-element.31), channel_id=1, source_target_pairs={{0,8},{1,9},{2,10},{3,11},{4,12},{5,13},{6,14},{7,15},{8,16},{9,17... | collective-permute-start | bytes 258056 | tf_op jit(solution)/shard_map/ppermute | solution.py:287
  71.0 6.6 %collective-permute-start.10 = (bf16[336,128]{1,0:T(8,128)(2,1)}, bf16[336,128]{1,0:T(8,128)(2,1)S(1)}, u32[]{:S(2)}, u32[]{:S(2)}) collective-permute-start(bf16[336,128]{1,0:T(8,128)(2,1)} %get-tuple-element.32), channel_id=1, source_target_pairs={{0,9},{1,8},{2,11},{3,10},{4,13},{5,12},{6,15},{7,14},{8,17},{9,16... | collective-permute-start | bytes 258056 | tf_op jit(solution)/shard_map/ppermute | solution.py:287
  74.0 6.2 %collective-permute-start.11 = (bf16[336,128]{1,0:T(8,128)(2,1)}, bf16[336,128]{1,0:T(8,128)(2,1)S(1)}, u32[]{:S(2)}, u32[]{:S(2)}) collective-permute-start(bf16[336,128]{1,0:T(8,128)(2,1)} %get-tuple-element.33), channel_id=1, source_target_pairs={{0,10},{1,11},{2,8},{3,9},{4,14},{5,15},{6,12},{7,13},{8,18},{9,19... | collective-permute-start | bytes 258056 | tf_op jit(solution)/shard_map/ppermute | solution.py:287
  74.0 7.2 %collective-permute-start.12 = (bf16[336,128]{1,0:T(8,128)(2,1)}, bf16[336,128]{1,0:T(8,128)(2,1)S(1)}, u32[]{:S(2)}, u32[]{:S(2)}) collective-permute-start(bf16[336,128]{1,0:T(8,128)(2,1)} %get-tuple-element.34), channel_id=1, source_target_pairs={{0,11},{1,10},{2,9},{3,8},{4,15},{5,14},{6,13},{7,12},{8,19},{9,18... | collective-permute-start | bytes 258056 | tf_op jit(solution)/shard_map/ppermute | solution.py:287
  75.3 17.2 %copy-start.2 = (bf16[336,128]{1,0:T(8,128)(2,1)}, bf16[336,128]{1,0:T(8,128)(2,1)S(1)}, u32[]{:S(2)}) copy-start(bf16[336,128]{1,0:T(8,128)(2,1)S(1)} %collective-permute-done.9.refs_0_) | copy-start | bytes 258052
  75.3 10.3 %collective-permute-start.13 = (bf16[336,128]{1,0:T(8,128)(2,1)}, bf16[336,128]{1,0:T(8,128)(2,1)S(1)}, u32[]{:S(2)}, u32[]{:S(2)}) collective-permute-start(bf16[336,128]{1,0:T(8,128)(2,1)} %get-tuple-element.35), channel_id=1, source_target_pairs={{0,12},{1,13},{2,14},{3,15},{4,8},{5,9},{6,10},{7,11},{8,20},{9,21... | collective-permute-start | bytes 258056 | tf_op jit(solution)/shard_map/ppermute | solution.py:287
  77.6 14.9 %copy-start.3 = (bf16[336,128]{1,0:T(8,128)(2,1)}, bf16[336,128]{1,0:T(8,128)(2,1)S(1)}, u32[]{:S(2)}) copy-start(bf16[336,128]{1,0:T(8,128)(2,1)S(1)} %collective-permute-done.10.refs_1_) | copy-start | bytes 258052
  77.6 14.9 %collective-permute-start.14 = (bf16[336,128]{1,0:T(8,128)(2,1)}, bf16[336,128]{1,0:T(8,128)(2,1)S(1)}, u32[]{:S(2)}, u32[]{:S(2)}) collective-permute-start(bf16[336,128]{1,0:T(8,128)(2,1)} %get-tuple-element.36), channel_id=1, source_target_pairs={{0,13},{1,12},{2,15},{3,14},{4,9},{5,8},{6,11},{7,10},{8,21},{9,20... | collective-permute-start | bytes 258056 | tf_op jit(solution)/shard_map/ppermute | solution.py:287
  80.2 12.3 %copy-start.4 = (bf16[336,128]{1,0:T(8,128)(2,1)}, bf16[336,128]{1,0:T(8,128)(2,1)S(1)}, u32[]{:S(2)}) copy-start(bf16[336,128]{1,0:T(8,128)(2,1)S(1)} %collective-permute-done.11.refs_2_) | copy-start | bytes 258052
  80.2 12.3 %collective-permute-start.15 = (bf16[336,128]{1,0:T(8,128)(2,1)}, bf16[336,128]{1,0:T(8,128)(2,1)S(1)}, u32[]{:S(2)}, u32[]{:S(2)}) collective-permute-start(bf16[336,128]{1,0:T(8,128)(2,1)} %get-tuple-element.37), channel_id=1, source_target_pairs={{0,14},{1,15},{2,12},{3,13},{4,10},{5,11},{6,8},{7,9},{8,22},{9,23... | collective-permute-start | bytes 258056 | tf_op jit(solution)/shard_map/ppermute | solution.py:287
  81.2 11.4 %copy-start.5 = (bf16[336,128]{1,0:T(8,128)(2,1)}, bf16[336,128]{1,0:T(8,128)(2,1)S(1)}, u32[]{:S(2)}) copy-start(bf16[336,128]{1,0:T(8,128)(2,1)S(1)} %collective-permute-done.12.refs_3_) | copy-start | bytes 258052
  81.2 11.3 %collective-permute-start.16 = (bf16[336,128]{1,0:T(8,128)(2,1)}, bf16[336,128]{1,0:T(8,128)(2,1)S(1)}, u32[]{:S(2)}, u32[]{:S(2)}) collective-permute-start(bf16[336,128]{1,0:T(8,128)(2,1)} %get-tuple-element.38), channel_id=1, source_target_pairs={{0,15},{1,14},{2,13},{3,12},{4,11},{5,10},{6,9},{7,8},{8,23},{9,22... | collective-permute-start | bytes 258056 | tf_op jit(solution)/shard_map/ppermute | solution.py:287
  (11 other events, 22.3 us)

commit v2 on v1

--- a/solution.py
+++ b/solution.py
@@ -17,10 +17,10 @@
 STAT_ROWS = 16
 MASKED = -1e30
 EXPO_SCALE = math.log2(math.e) / math.sqrt(HD)
-VMEM_LIMIT = 56 * 1024 * 1024
-CHUNKS_PER_CALL = 8
+VMEM_BASE = 12 * 1024 * 1024
 
 whole_vmem = pl.BlockSpec(memory_space=pltpu.VMEM)
+anywhere = pl.BlockSpec(memory_space=pl.ANY)
 whole_smem = pl.BlockSpec(memory_space=pltpu.SMEM)
 
 
@@ -34,20 +34,17 @@
     )
 
 
-def softmax_part(pieces, values):
-    top = functools.reduce(
-        jnp.maximum, [jnp.max(piece, axis=1, keepdims=True) for piece in pieces]
-    )
-    expo = [jnp.exp2((piece - top) * EXPO_SCALE) for piece in pieces]
-    total = functools.reduce(jnp.add, [jnp.sum(part, axis=1, keepdims=True) for part in expo])
-    mixed = functools.reduce(
-        jnp.add,
-        [
-            jnp.dot(part.astype(jnp.bfloat16), value, preferred_element_type=jnp.float32)
-            for part, value in zip(expo, values)
-        ],
-    )
-    return mixed / total, top * EXPO_SCALE + jnp.log2(total)
+def softmax_parts(scores, values):
+    tops = [jnp.max(score, axis=1, keepdims=True) for score in scores]
+    expos = [jnp.exp2((score - top) * EXPO_SCALE) for score, top in zip(scores, tops)]
+    totals = [jnp.sum(expo, axis=1, keepdims=True) for expo in expos]
+    mixed = [
+        jnp.dot(expo.astype(jnp.bfloat16), value, preferred_element_type=jnp.float32)
+        for expo, value in zip(expos, values)
+    ]
+    parts = [(mix * (1.0 / total)).astype(jnp.bfloat16) for mix, total in zip(mixed, totals)]
+    lses = [top * EXPO_SCALE + jnp.log2(total) for top, total in zip(tops, totals)]
+    return parts, lses
 
 
 def as_row(column, offset):
@@ -102,7 +99,7 @@
     me = me_ref[0]
     span = span_ref[0]
     count = len(steps)
-    query_refs, out_refs = refs[:count], refs[count:]
+    query_refs, out_refs = refs[:count], refs[-count:]
     last = key_ref.shape[0] // BLK - 1
 
     def block(ref, at):
@@ -115,10 +112,16 @@
     for index, step in enumerate(steps):
         chunk = partner(me, step)
         query_ref, out_ref = query_refs[index], out_refs[index]
+        if step == 0:
+            near_ref = refs[count]
+            wide = near_ref.shape[1]
+            out_ref[:, :wide] = near_ref[...]
+        else:
+            wide = 0
         rows = query_ref.shape[0]
         blocks = rows // BLK
         first = chunk == 0
-        stats = []
+        all_scores, all_values = [], []
         for b in range(blocks):
             query = query_ref[b * BLK : (b + 1) * BLK, :]
             base = (chunk * blocks + b) * RAND
@@ -134,14 +137,20 @@
                 open_slots = jnp.where(first, jnp.clip(span - (b + 1), 0, len(spare)), 0)
                 lane_at = lax.broadcasted_iota(jnp.int32, scores.shape, 1)
                 scores = jnp.where(lane_at < known + open_slots * BLK, scores, MASKED)
-            mixed, lse = softmax_part([scores], [jnp.concatenate(values, axis=0)])
-            out_ref[b * BLK : (b + 1) * BLK, :] = mixed.astype(jnp.bfloat16)
-            row = as_row(lse, (b * BLK) % LANES)
+            all_scores.append(scores)
+            all_values.append(jnp.concatenate(values, axis=0))
+        parts, lses = softmax_parts(all_scores, all_values)
+        stats = []
+        for b in range(blocks):
+            row = as_row(lses[b], (b * BLK) % LANES)
             if (b * BLK) % LANES:
                 stats[-1] = stats[-1] + row
             else:
                 stats.append(row)
-        out_ref[rows:, :] = stat_tile(stats)
+        tile = stat_tile(stats)
+        for b in range(blocks):
+            out_ref[b * BLK : (b + 1) * BLK, wide:] = parts[b]
+        out_ref[rows:, wide:] = tile
 
 
 def near_kernel(
@@ -154,10 +163,11 @@
 
     def one_head(head, carry):
         lanes = pl.ds(pl.multiple_of(head * HD, HD), HD)
-        span = spans_ref[head]
-        stats = []
-        for start in range(0, rows, 2 * BLK):
-            size = min(2 * BLK, rows - start)
+        span = spans_ref[head, 0]
+        all_scores, all_values = [], []
+        starts = list(range(0, rows, 2 * BLK))
+        sizes = [min(2 * BLK, rows - start) for start in starts]
+        for start, size in zip(starts, sizes):
             query = query_ref[start : start + size, lanes]
             if start < halo:
                 keys = [halo_ref[0, start:, lanes], key_ref[: start + size, lanes]]
@@ -175,24 +185,28 @@
             if start < halo:
                 closed = jnp.where(me == 0, halo - start, 0)
                 allowed = allowed & (lane_at >= closed)
-            mixed, lse = softmax_part([jnp.where(allowed, scores, MASKED)], [values])
-            out_ref[start : start + size, lanes] = mixed.astype(jnp.bfloat16)
-            stats.append(as_row(lse, 0))
-        out_ref[rows:, lanes] = stat_tile(stats)
+            all_scores.append(jnp.where(allowed, scores, MASKED))
+            all_values.append(values)
+        parts, lses = softmax_parts(all_scores, all_values)
+        tile = stat_tile([as_row(lse, 0) for lse in lses])
+        for start, size, part in zip(starts, sizes, parts):
+            out_ref[start : start + size, lanes] = part
+        out_ref[rows:, lanes] = tile
         return carry
 
     lax.fori_loop(0, heads, one_head, 0)
 
 
-def merge_kernel(steps, me_ref, near_ref, *refs):
+def merge_kernel(steps, me_ref, *refs):
     me = me_ref[0]
     far_refs, out_ref = refs[:-1], refs[-1]
-    rows = out_ref.shape[0]
+    near_ref = far_refs[steps.index(0)]
+    rows, wide = out_ref.shape
     count = stat_count(rows)
-    for step in range(steps):
-        far_ref = far_refs[step]
+    for step, far_ref in zip(steps, far_refs):
+        part = slice(wide, None) if step == 0 else slice(None)
         lanes = pl.ds(pl.multiple_of(partner(me, step) * HD, HD), HD)
-        far_stats = stat_rows_of(far_ref[rows:, :], count)
+        far_stats = stat_rows_of(far_ref[rows:, part], count)
         near_stats = stat_rows_of(near_ref[rows:, lanes], count)
         for index in range(count):
             start = index * LANES
@@ -203,15 +217,15 @@
             column = jnp.sum(
                 jnp.where(row_at == lane_at, share, 0.0), axis=1, keepdims=True
             )
-            far = far_ref[start : start + size, :].astype(jnp.float32)
+            far = far_ref[start : start + size, part].astype(jnp.float32)
             near = near_ref[start : start + size, lanes].astype(jnp.float32)
             out_ref[start : start + size, lanes] = (
                 far * column + near * (1.0 - column)
             ).astype(jnp.bfloat16)
 
 
-def params():
-    return pltpu.CompilerParams(vmem_limit_bytes=VMEM_LIMIT)
+def params(shard):
+    return pltpu.CompilerParams(vmem_limit_bytes=VMEM_BASE + 14 * 2 * math.prod(shard.shape))
 
 
 def per_device(
@@ -224,7 +238,9 @@
     heads = wide // HD
     bf16 = jnp.bfloat16
     me = lax.axis_index("seq").astype(jnp.int32)[None]
-    spans = lax.all_gather(window[0], "seq", axis=0, tiled=True)
+    spans = lax.all_gather(
+        lax.optimization_barrier(jnp.broadcast_to(window, (8, LANES))), "seq", axis=0, tiled=True
+    )
 
     parts = pl.pallas_call(
         functools.partial(split_kernel, seq_count),
@@ -232,7 +248,7 @@
         + [jax.ShapeDtypeStruct((rows, HD), bf16)] * seq_count,
         in_specs=[whole_smem] + [whole_vmem] * 3,
         out_specs=[whole_vmem] * (1 + seq_count),
-        compiler_params=params(),
+        compiler_params=params(queries),
         cost_estimate=pl.CostEstimate(flops=0, bytes_accessed=5 * rows * wide, transcendentals=0),
         name="split",
     )(me, queries[0], keys_new[0], values_new[0])
@@ -243,20 +259,37 @@
             return shard
         return lax.ppermute(shard, "seq", [(i, i ^ step) for i in range(seq_count)])
 
-    order = sorted(range(seq_count), reverse=True)
+    half = max(seq_count // 2, 1)
+    order = list(range(seq_count - 1, half - 1, -1)) + list(range(half))
     came = {step: swapped(sent[step], step) for step in order}
     before = lax.ppermute(mine, "seq", [(i, i + 1) for i in range(seq_count - 1)])
 
+    near = pl.pallas_call(
+        near_kernel,
+        out_shape=jax.ShapeDtypeStruct((rows + STAT_ROWS, wide), bf16),
+        in_specs=[whole_smem] * 2 + [whole_vmem] * 4,
+        out_specs=whole_vmem,
+        compiler_params=params(queries),
+        cost_estimate=pl.CostEstimate(
+            flops=heads * rows * 256 * HD * 4,
+            bytes_accessed=9 * rows * wide,
+            transcendentals=heads * rows * 256,
+        ),
+        name="near",
+    )(me, spans[::8], queries[0], keys_new[0], values_new[0], before)
     picks = random_blocks[0].reshape(-1)
 
     def far_call(steps):
         count = len(steps)
+        out_rows = rows + STAT_ROWS
+        widths = [HD] * count
+        widths[steps.index(0)] += wide
         return pl.pallas_call(
             functools.partial(far_kernel, steps),
-            out_shape=[jax.ShapeDtypeStruct((rows + STAT_ROWS, HD), bf16)] * count,
-            in_specs=[whole_smem] * 4 + [whole_vmem] * (2 + count),
+            out_shape=[jax.ShapeDtypeStruct((out_rows, width), bf16) for width in widths],
+            in_specs=[whole_smem] * 4 + [whole_vmem] * (2 + count + 1),
             out_specs=[whole_vmem] * count,
-            compiler_params=params(),
+            compiler_params=params(queries),
             cost_estimate=pl.CostEstimate(
                 flops=count * rows * 320 * HD * 4,
                 bytes_accessed=2 * 2 * keys_cache.shape[1] * HD + 4 * count * rows * HD,
@@ -271,12 +304,10 @@
             keys_cache[0],
             values_cache[0],
             *[came[step] for step in steps],
+            near,
         )
 
-    far = {}
-    for begin in range(0, seq_count, CHUNKS_PER_CALL):
-        steps = order[begin : begin + CHUNKS_PER_CALL]
-        far.update(zip(steps, far_call(steps)))
+    far = dict(zip(order, far_call(order)))
 
     def onward(shard, step):
         pairs = [
@@ -286,34 +317,17 @@
         ]
         return lax.ppermute(shard, ("section", "seq"), pairs)
 
-    handed_far = {step: onward(far[step], step) for step in order}
-
-    near = pl.pallas_call(
-        near_kernel,
-        out_shape=jax.ShapeDtypeStruct((rows + STAT_ROWS, wide), bf16),
-        in_specs=[whole_smem] * 2 + [whole_vmem] * 4,
+    handed = {step: onward(far[step], step) for step in order}
+
+    merged = pl.pallas_call(
+        functools.partial(merge_kernel, order),
+        out_shape=jax.ShapeDtypeStruct((rows, wide), bf16),
+        in_specs=[whole_smem] + [whole_vmem] * seq_count,
         out_specs=whole_vmem,
-        compiler_params=params(),
-        cost_estimate=pl.CostEstimate(
-            flops=heads * rows * 256 * HD * 4,
-            bytes_accessed=9 * rows * wide,
-            transcendentals=heads * rows * 256,
-        ),
-        name="near",
-    )(me, spans, queries[0], keys_new[0], values_new[0], before)
-    handed_near = lax.ppermute(
-        near, "section", [(s, (s + 1) % section_count) for s in range(section_count)]
-    )
-
-    merged = pl.pallas_call(
-        functools.partial(merge_kernel, seq_count),
-        out_shape=jax.ShapeDtypeStruct((rows, wide), bf16),
-        in_specs=[whole_smem] + [whole_vmem] * (1 + seq_count),
-        out_specs=whole_vmem,
-        compiler_params=params(),
+        compiler_params=params(queries),
         cost_estimate=pl.CostEstimate(flops=0, bytes_accessed=6 * rows * wide, transcendentals=0),
         name="merge",
-    )(me, handed_near, *[handed_far[step] for step in range(seq_count)])
+    )(me, *[handed[step] for step in order])
     return merged[None]
 
 

time: 98 us -> 97.8 us (level); the launches traced: 96.7 us -> 97.5 us
  blocking collectives: 12.5 us -> 30.9 us
  Pallas kernels: 26.1 us -> 10.4 us
  waiting for transfers between devices: 14.9 us -> 12.2 us
  starting transfers between devices: 37.5 us -> 39.6 us
  local copies, waits for them, and re-layouts: 4.93 us -> 3.52 us
    all_gather x1, blocking collectives: 12.5 us -> 30.9 us  [per_device(): lax.all_gather(lax.optimization_barrier(jnp.broadcast_to(window, (8, LANE...]
    pallas_call x1, Pallas kernels: 13 us -> 4.11 us  [far_call(): pl.pallas_call(functools.partial(far_kernel, steps), out_shape=[jax.Shape...]
    ppermute x7, waiting for transfers between devices: 4.4 us -> 0.02 us  [swapped(): return lax.ppermute(shard, 'seq', [(i, i ^ step) for i in range(seq_count)])]
    pallas_call x1, Pallas kernels: 7.8 us -> 4.1 us  [per_device(): pl.pallas_call(near_kernel, out_shape=jax.ShapeDtypeStruct((rows + STAT_R...]
    ppermute x7, starting transfers between devices: 21.4 us -> 24.9 us  [swapped(): return lax.ppermute(shard, 'seq', [(i, i ^ step) for i in range(seq_count)])]
    ppermute x8, waiting for transfers between devices: 10.5 us -> 12.2 us  [onward(): return lax.ppermute(shard, ('section', 'seq'), pairs)]
    pallas_call x1, Pallas kernels: 2.57 us -> 0.83 us  [per_device(): pl.pallas_call(functools.partial(split_kernel, seq_count), out_shape=[jax...]
    pallas_call x1, Pallas kernels: 2.67 us -> 1.31 us  [per_device(): pl.pallas_call(functools.partial(merge_kernel, order), out_shape=jax.Shap...]
  transfers between devices with their start and end apart: 17 -> 16, of which waited for: 7 -> 5; matrix products, arithmetic and copies ran while one was open for 2% -> 0% of each run, Pallas kernels for 13% -> 4%
where the time goes in v2:
time: 97.8 us; the launch traced here: 97.5 us
  starting transfers between devices  39.6 us (40%)
  blocking collectives  30.9 us (32%)
  waiting for transfers between devices  12.2 us (12%)
  Pallas kernels  10.4 us (11%)
  local copies, waits for them, and re-layouts  3.52 us (4%)
    all_gather x1, blocking collectives, per_device(): lax.all_gather(lax.optimization_barrier(jnp.broadcast_to(window, (8, LANE...  30.9 us
    ppermute x7, starting transfers between devices, swapped(): return lax.ppermute(shard, 'seq', [(i, i ^ step) for i in range(seq_count)])  24.9 us
    ppermute x8, waiting for transfers between devices, onward(): return lax.ppermute(shard, ('section', 'seq'), pairs)  12.2 us
    ppermute x8, starting transfers between devices, onward(): return lax.ppermute(shard, ('section', 'seq'), pairs)  9.8 us
    ppermute x1, starting transfers between devices, per_device(): lax.ppermute(mine, 'seq', [(i, i + 1) for i in range(seq_count - 1)])  4.89 us
    pallas_call x1, Pallas kernels, far_call(): pl.pallas_call(functools.partial(far_kernel, steps), out_shape=[jax.Shape...  4.11 us
    pallas_call x1, Pallas kernels, per_device(): pl.pallas_call(near_kernel, out_shape=jax.ShapeDtypeStruct((rows + STAT_R...  4.1 us
    unnamed x21, local copies, waits for them, and re-layouts  3.4 us
  transfers between devices with their start and end apart: 16, of which 5 were waited for; matrix products, arithmetic and copies ran while one was open for 0% of the time, Pallas kernels for 4%

profile of v2, /device:TPU:0, one launch (start us, length us, event | category | flops | bytes accessed | tf_op | source)
XLA Modules:
  0.0 97.5 jit_solution(14686926892787694574)
XLA Ops:
  0.0 1.1 %copy-done = bf16[1,320,1024]{2,1,0:T(8,128)(2,1)S(1)} copy-done((bf16[1,320,1024]{2,1,0:T(8,128)(2,1)S(1)}, bf16[1,320,1024]{2,1,0:T(8,128)(2,1)}, u32[]{:S(2)}) %copy-start) | copy-done | bytes 655384
  1.1 1.1 %copy-done.2 = bf16[1,320,1024]{2,1,0:T(8,128)(2,1)S(1)} copy-done((bf16[1,320,1024]{2,1,0:T(8,128)(2,1)S(1)}, bf16[1,320,1024]{2,1,0:T(8,128)(2,1)}, u32[]{:S(2)}) %copy-start.2) | copy-done | bytes 655384
  2.2 1.1 %copy-done.4 = bf16[1,320,1024]{2,1,0:T(8,128)(2,1)S(1)} copy-done((bf16[1,320,1024]{2,1,0:T(8,128)(2,1)S(1)}, bf16[1,320,1024]{2,1,0:T(8,128)(2,1)}, u32[]{:S(2)}) %copy-start.4) | copy-done | bytes 655384
  3.3 0.8 split.1
  4.1 4.9 %collective-permute-start.7 = (bf16[2,128,1024]{2,1,0:T(8,128)(2,1)S(1)}, bf16[2,128,1024]{2,1,0:T(8,128)(2,1)S(1)}, u32[]{:S(2)}, u32[]{:S(2)}) collective-permute-start(bf16[2,128,1024]{2,1,0:T(8,128)(2,1)S(1)} %get-tuple-element.30), channel_id=1, source_target_pairs={{0,1},{1,2},{2,3},{3,4},{4,5},{5,6},{6,7},{8,9},{9,10},{10,11},{11... | collective-permute-start | bytes 1572872 | tf_op jit(solution)/shard_map/ppermute | solution.py:265
  9.0 2.5 %collective-permute-start = (bf16[320,128]{1,0:T(8,128)(2,1)S(1)}, bf16[320,128]{1,0:T(8,128)(2,1)S(1)}, u32[]{:S(2)}, u32[]{:S(2)}) collective-permute-start(bf16[320,128]{1,0:T(8,128)(2,1)S(1)} %get-tuple-element.22), channel_id=1, source_target_pairs={{0,7},{1,6},{2,5},{3,4},{4,3},{5,2},{6,1},{7,0},{8,15},{9,14},{10,... | collective-permute-start | bytes 245768 | tf_op jit(solution)/shard_map/ppermute | solution.py:260
  11.5 2.4 %collective-permute-start.1 = (bf16[320,128]{1,0:T(8,128)(2,1)S(1)}, bf16[320,128]{1,0:T(8,128)(2,1)S(1)}, u32[]{:S(2)}, u32[]{:S(2)}) collective-permute-start(bf16[320,128]{1,0:T(8,128)(2,1)S(1)} %get-tuple-element.23), channel_id=1, source_target_pairs={{0,6},{1,7},{2,4},{3,5},{4,2},{5,3},{6,0},{7,1},{8,14},{9,15},{10,... | collective-permute-start | bytes 245768 | tf_op jit(solution)/shard_map/ppermute | solution.py:260
  13.8 0.7 collective-permute-start.2
  14.6 2.2 %collective-permute-start.3 = (bf16[320,128]{1,0:T(8,128)(2,1)S(1)}, bf16[320,128]{1,0:T(8,128)(2,1)S(1)}, u32[]{:S(2)}, u32[]{:S(2)}) collective-permute-start(bf16[320,128]{1,0:T(8,128)(2,1)S(1)} %get-tuple-element.25), channel_id=1, source_target_pairs={{0,4},{1,5},{2,6},{3,7},{4,0},{5,1},{6,2},{7,3},{8,12},{9,13},{10,... | collective-permute-start | bytes 245768 | tf_op jit(solution)/shard_map/ppermute | solution.py:260
  16.7 11.4 %collective-permute-start.4 = (bf16[320,128]{1,0:T(8,128)(2,1)S(1)}, bf16[320,128]{1,0:T(8,128)(2,1)S(1)}, u32[]{:S(2)}, u32[]{:S(2)}) collective-permute-start(bf16[320,128]{1,0:T(8,128)(2,1)S(1)} %get-tuple-element.27), channel_id=1, source_target_pairs={{0,1},{1,0},{2,3},{3,2},{4,5},{5,4},{6,7},{7,6},{8,9},{9,8},{10,11... | collective-permute-start | bytes 245768 | tf_op jit(solution)/shard_map/ppermute | solution.py:260
  28.1 5.9 %collective-permute-start.6 = (bf16[320,128]{1,0:T(8,128)(2,1)S(1)}, bf16[320,128]{1,0:T(8,128)(2,1)S(1)}, u32[]{:S(2)}, u32[]{:S(2)}) collective-permute-start(bf16[320,128]{1,0:T(8,128)(2,1)S(1)} %get-tuple-element.29), channel_id=1, source_target_pairs={{0,3},{1,2},{2,1},{3,0},{4,7},{5,6},{6,5},{7,4},{8,11},{9,10},{10,... | collective-permute-start | bytes 245768 | tf_op jit(solution)/shard_map/ppermute | solution.py:260
  34.6 0.1 copy.10
  34.7 0.1 reshape_squeeze.3.random_ref
  34.8 30.9 %all_gather.3 = s32[64,128]{1,0:T(8,128)S(1)} all-gather(s32[8,128]{1,0:T(8,128)S(1)} %broadcast_in_dim.15), channel_id=1, replica_groups=mesh['section'=4,'seq'=8] {'seq'}, dimensions={0}, use_global_device_ids=true | all-gather | bytes 36864 | tf_op jit(solution)/shard_map/all_gather | solution.py:241
  65.8 0.0 copy-start.6
  65.8 0.0 copy-start.7
  65.8 0.0 copy-start.8
  65.8 4.1 %near.1.refs_8_ = bf16[336,1024]{1,0:T(8,128)(2,1)S(1)} custom-call(s32[1]{0:T(128)} %bitcast.me_ref, s32[8,128]{1,0:T(8,128)S(1)} %slice.3.spans_ref, bf16[320,1024]{1,0:T(8,128)(2,1)S(1)} %bitcast.13, bf16[320,1024]{1,0:T(8,128)(2,1)S(1)} %bitcast.15, bf16[320,1024]{1,0:T(8,128)(2,1)S(1)} %bitcast.17, bf16[2,128,1024]{2,1,0:T(8,128)(2,1)S(1)} %collective-permute-done.7.halo_ref), custom_call_target="tpu_custom_call" | custom-call | flops 335544320 | bytes 2949120 | tf_op jit(solution)/shard_map/near/pallas_call | solution.py:267
  69.9 0.0 collective-permute-done.2.refs_2_
  70.0 0.0 collective-permute-done.5.refs_6_
  70.0 4.1 %far.1 = (bf16[336,128]{1,0:T(8,128)(2,1)S(1)}, bf16[336,128]{1,0:T(8,128)(2,1)S(1)}, bf16[336,128]{1,0:T(8,128)(2,1)S(1)}, bf16[336,128]{1,0:T(8,128)(2,1)S(1)}...) custom-call(s32[1]{0:T(128)} %bitcast.me_ref, ...), custom_call_target="tpu_custom_call" | custom-call | flops 419430400 | bytes 4456448 | tf_op jit(solution)/shard_map/far/pallas_call | solution.py:287
  74.1 0.1 collective-permute-start.12
  74.2 4.5 %collective-permute-start.8 = (bf16[336,128]{1,0:T(8,128)(2,1)S(1)}, bf16[336,128]{1,0:T(8,128)(2,1)S(1)}, u32[]{:S(2)}, u32[]{:S(2)}) collective-permute-start(bf16[336,128]{1,0:T(8,128)(2,1)S(1)} %get-tuple-element.31), channel_id=1, source_target_pairs={{0,15},{1,14},{2,13},{3,12},{4,11},{5,10},{6,9},{7,8},{8,23},{9,22... | collective-permute-start | bytes 258056 | tf_op jit(solution)/shard_map/ppermute | solution.py:318
  78.7 0.1 collective-permute-start.9
  78.7 3.5 %collective-permute-start.11 = (bf16[336,128]{1,0:T(8,128)(2,1)S(1)}, bf16[336,128]{1,0:T(8,128)(2,1)S(1)}, u32[]{:S(2)}, u32[]{:S(2)}) collective-permute-start(bf16[336,128]{1,0:T(8,128)(2,1)S(1)} %get-tuple-element.34), channel_id=1, source_target_pairs={{0,12},{1,13},{2,14},{3,15},{4,8},{5,9},{6,10},{7,11},{8,20},{9,21... | collective-permute-start | bytes 258056 | tf_op jit(solution)/shard_map/ppermute | solution.py:318
  82.3 1.7 %collective-permute-start.13 = (bf16[336,128]{1,0:T(8,128)(2,1)S(1)}, bf16[336,128]{1,0:T(8,128)(2,1)S(1)}, u32[]{:S(2)}, u32[]{:S(2)}) collective-permute-start(bf16[336,128]{1,0:T(8,128)(2,1)S(1)} %get-tuple-element.36), channel_id=1, source_target_pairs={{0,9},{1,8},{2,11},{3,10},{4,13},{5,12},{6,15},{7,14},{8,17},{9,16... | collective-permute-start | bytes 258056 | tf_op jit(solution)/shard_map/ppermute | solution.py:318
  84.0 2.3 %collective-permute-done.9.refs_1_ = bf16[336,128]{1,0:T(8,128)(2,1)S(1)} collective-permute-done((bf16[336,128]{1,0:T(8,128)(2,1)S(1)}, bf16[336,128]{1,0:T(8,128)(2,1)S(1)}, u32[]{:S(2)}, u32[]{:S(2)}) %collective-permute-start.9) | collective-permute-done | bytes 86048 | tf_op jit(solution)/shard_map/ppermute | solution.py:318
  86.3 4.0 %collective-permute-done.10.refs_2_ = bf16[336,128]{1,0:T(8,128)(2,1)S(1)} collective-permute-done((bf16[336,128]{1,0:T(8,128)(2,1)S(1)}, bf16[336,128]{1,0:T(8,128)(2,1)S(1)}, u32[]{:S(2)}, u32[]{:S(2)}) %collective-permute-start.10) | collective-permute-done | bytes 86048 | tf_op jit(solution)/shard_map/ppermute | solution.py:318
  90.2 2.5 %collective-permute-done.11.refs_3_ = bf16[336,128]{1,0:T(8,128)(2,1)S(1)} collective-permute-done((bf16[336,128]{1,0:T(8,128)(2,1)S(1)}, bf16[336,128]{1,0:T(8,128)(2,1)S(1)}, u32[]{:S(2)}, u32[]{:S(2)}) %collective-permute-start.11) | collective-permute-done | bytes 86048 | tf_op jit(solution)/shard_map/ppermute | solution.py:318
  92.7 0.9 collective-permute-done.14.refs_6_
  93.6 2.5 %collective-permute-done.15.refs_7_ = bf16[336,128]{1,0:T(8,128)(2,1)S(1)} collective-permute-done((bf16[336,128]{1,0:T(8,128)(2,1)S(1)}, bf16[336,128]{1,0:T(8,128)(2,1)S(1)}, u32[]{:S(2)}, u32[]{:S(2)}) %collective-permute-start.15) | collective-permute-done | bytes 86048 | tf_op jit(solution)/shard_map/ppermute | solution.py:318
  96.2 1.3 %merge.1 = bf16[320,1024]{1,0:T(8,128)(2,1)} custom-call(s32[1]{0:T(128)} %bitcast.me_ref, bf16[336,128]{1,0:T(8,128)(2,1)S(1)} %collective-permute-done.8.refs_0_, bf16[336,128]{1,0:T(8,128)(2,1)S(1)} %collective-permute-done.9.refs_1_, bf16[336,128]{1,0:T(8,128)(2,1)S(1)} %collective-permute-done.10.refs_2_, ...), custom_call_target="tpu_custom_call" | custom-call | bytes 1966080 | tf_op jit(solution)/shard_map/merge/pallas_call | solution.py:322
  (29 shorter events, 0.1 us)
Async XLA Ops:
  0.0 34.6 %copy-start.9 = (s32[1,40,3]{1,0,2:T(1,128)S(1)}, s32[1,40,3]{1,0,2:T(1,128)}, u32[]{:S(2)}) copy-start(s32[1,40,3]{1,0,2:T(1,128)} %param.15) | copy-start | bytes 1444
  0.0 1.1 %copy-start = (bf16[1,320,1024]{2,1,0:T(8,128)(2,1)S(1)}, bf16[1,320,1024]{2,1,0:T(8,128)(2,1)}, u32[]{:S(2)}) copy-start(bf16[1,320,1024]{2,1,0:T(8,128)(2,1)} %param.8) | copy-start | bytes 1966084
  1.1 1.1 %copy-start.2 = (bf16[1,320,1024]{2,1,0:T(8,128)(2,1)S(1)}, bf16[1,320,1024]{2,1,0:T(8,128)(2,1)}, u32[]{:S(2)}) copy-start(bf16[1,320,1024]{2,1,0:T(8,128)(2,1)} %param.9) | copy-start | bytes 1966084
  2.2 1.1 %copy-start.4 = (bf16[1,320,1024]{2,1,0:T(8,128)(2,1)S(1)}, bf16[1,320,1024]{2,1,0:T(8,128)(2,1)}, u32[]{:S(2)}) copy-start(bf16[1,320,1024]{2,1,0:T(8,128)(2,1)} %param.10) | copy-start | bytes 1966084
  3.3 62.5 %copy-start.1 = (bf16[1,320,1024]{2,1,0:T(8,128)(2,1)S(1)}, bf16[1,320,1024]{2,1,0:T(8,128)(2,1)}, u32[]{:S(2)}) copy-start(bf16[1,320,1024]{2,1,0:T(8,128)(2,1)} %param.8) | copy-start | bytes 1966084
  3.3 62.5 %copy-start.3 = (bf16[1,320,1024]{2,1,0:T(8,128)(2,1)S(1)}, bf16[1,320,1024]{2,1,0:T(8,128)(2,1)}, u32[]{:S(2)}) copy-start(bf16[1,320,1024]{2,1,0:T(8,128)(2,1)} %param.9) | copy-start | bytes 1966084
  3.3 62.5 %copy-start.5 = (bf16[1,320,1024]{2,1,0:T(8,128)(2,1)S(1)}, bf16[1,320,1024]{2,1,0:T(8,128)(2,1)}, u32[]{:S(2)}) copy-start(bf16[1,320,1024]{2,1,0:T(8,128)(2,1)} %param.10) | copy-start | bytes 1966084
  4.1 24.0 %collective-permute-start.7 = (bf16[2,128,1024]{2,1,0:T(8,128)(2,1)S(1)}, bf16[2,128,1024]{2,1,0:T(8,128)(2,1)S(1)}, u32[]{:S(2)}, u32[]{:S(2)}) collective-permute-start(bf16[2,128,1024]{2,1,0:T(8,128)(2,1)S(1)} %get-tuple-element.30), channel_id=1, source_target_pairs={{0,1},{1,2},{2,3},{3,4},{4,5},{5,6},{6,7},{8,9},{9,10},{10,11},{11... | collective-permute-start | bytes 1572872 | tf_op jit(solution)/shard_map/ppermute | solution.py:265
  9.0 7.7 %collective-permute-start = (bf16[320,128]{1,0:T(8,128)(2,1)S(1)}, bf16[320,128]{1,0:T(8,128)(2,1)S(1)}, u32[]{:S(2)}, u32[]{:S(2)}) collective-permute-start(bf16[320,128]{1,0:T(8,128)(2,1)S(1)} %get-tuple-element.22), channel_id=1, source_target_pairs={{0,7},{1,6},{2,5},{3,4},{4,3},{5,2},{6,1},{7,0},{8,15},{9,14},{10,... | collective-permute-start | bytes 245768 | tf_op jit(solution)/shard_map/ppermute | solution.py:260
  11.5 16.6 %collective-permute-start.1 = (bf16[320,128]{1,0:T(8,128)(2,1)S(1)}, bf16[320,128]{1,0:T(8,128)(2,1)S(1)}, u32[]{:S(2)}, u32[]{:S(2)}) collective-permute-start(bf16[320,128]{1,0:T(8,128)(2,1)S(1)} %get-tuple-element.23), channel_id=1, source_target_pairs={{0,6},{1,7},{2,4},{3,5},{4,2},{5,3},{6,0},{7,1},{8,14},{9,15},{10,... | collective-permute-start | bytes 245768 | tf_op jit(solution)/shard_map/ppermute | solution.py:260
  13.8 56.1 %collective-permute-start.2 = (bf16[320,128]{1,0:T(8,128)(2,1)}, bf16[320,128]{1,0:T(8,128)(2,1)S(1)}, u32[]{:S(2)}, u32[]{:S(2)}) collective-permute-start(bf16[320,128]{1,0:T(8,128)(2,1)} %get-tuple-element.24), channel_id=1, source_target_pairs={{0,5},{1,4},{2,7},{3,6},{4,1},{5,0},{6,3},{7,2},{8,13},{9,12},{10,... | collective-permute-start | bytes 245768 | tf_op jit(solution)/shard_map/ppermute | solution.py:260
  14.6 55.4 %collective-permute-start.3 = (bf16[320,128]{1,0:T(8,128)(2,1)S(1)}, bf16[320,128]{1,0:T(8,128)(2,1)S(1)}, u32[]{:S(2)}, u32[]{:S(2)}) collective-permute-start(bf16[320,128]{1,0:T(8,128)(2,1)S(1)} %get-tuple-element.25), channel_id=1, source_target_pairs={{0,4},{1,5},{2,6},{3,7},{4,0},{5,1},{6,2},{7,3},{8,12},{9,13},{10,... | collective-permute-start | bytes 245768 | tf_op jit(solution)/shard_map/ppermute | solution.py:260
  16.7 53.2 %collective-permute-start.4 = (bf16[320,128]{1,0:T(8,128)(2,1)S(1)}, bf16[320,128]{1,0:T(8,128)(2,1)S(1)}, u32[]{:S(2)}, u32[]{:S(2)}) collective-permute-start(bf16[320,128]{1,0:T(8,128)(2,1)S(1)} %get-tuple-element.27), channel_id=1, source_target_pairs={{0,1},{1,0},{2,3},{3,2},{4,5},{5,4},{6,7},{7,6},{8,9},{9,8},{10,11... | collective-permute-start | bytes 245768 | tf_op jit(solution)/shard_map/ppermute | solution.py:260
  28.1 41.9 %collective-permute-start.5 = (bf16[320,128]{1,0:T(8,128)(2,1)S(1)}, bf16[320,128]{1,0:T(8,128)(2,1)S(1)}, u32[]{:S(2)}, u32[]{:S(2)}) collective-permute-start(bf16[320,128]{1,0:T(8,128)(2,1)S(1)} %get-tuple-element.28), channel_id=1, source_target_pairs={{0,2},{1,3},{2,0},{3,1},{4,6},{5,7},{6,4},{7,5},{8,10},{9,11},{10,... | collective-permute-start | bytes 245768 | tf_op jit(solution)/shard_map/ppermute | solution.py:260
  28.1 41.9 %collective-permute-start.6 = (bf16[320,128]{1,0:T(8,128)(2,1)S(1)}, bf16[320,128]{1,0:T(8,128)(2,1)S(1)}, u32[]{:S(2)}, u32[]{:S(2)}) collective-permute-start(bf16[320,128]{1,0:T(8,128)(2,1)S(1)} %get-tuple-element.29), channel_id=1, source_target_pairs={{0,3},{1,2},{2,1},{3,0},{4,7},{5,6},{6,5},{7,4},{8,11},{9,10},{10,... | collective-permute-start | bytes 245768 | tf_op jit(solution)/shard_map/ppermute | solution.py:260
  65.8 4.2 %copy-start.6 = (bf16[1,6144,128]{2,1,0:T(8,128)(2,1)S(1)}, bf16[1,6144,128]{2,1,0:T(8,128)(2,1)}, u32[]{:S(2)}) copy-start(bf16[1,6144,128]{2,1,0:T(8,128)(2,1)} %param.11) | copy-start | bytes 4718596
  65.8 4.2 %copy-start.7 = (bf16[1,6144,128]{2,1,0:T(8,128)(2,1)S(1)}, bf16[1,6144,128]{2,1,0:T(8,128)(2,1)}, u32[]{:S(2)}) copy-start(bf16[1,6144,128]{2,1,0:T(8,128)(2,1)} %param.12) | copy-start | bytes 4718596
  65.8 4.2 %copy-start.8 = (s32[1,2]{1,0:T(1,128)S(1)}, s32[1,2]{1,0:T(1,128)}, u32[]{:S(2)}) copy-start(s32[1,2]{1,0:T(1,128)} %param.14) | copy-start | bytes 28
  74.1 22.0 %collective-permute-start.12 = (bf16[336,1152]{1,0:T(8,128)(2,1)S(1)}, bf16[336,1152]{1,0:T(8,128)(2,1)S(1)}, u32[]{:S(2)}, u32[]{:S(2)}) collective-permute-start(bf16[336,1152]{1,0:T(8,128)(2,1)S(1)} %get-tuple-element.35), channel_id=1, source_target_pairs={{0,8},{1,9},{2,10},{3,11},{4,12},{5,13},{6,14},{7,15},{8,16},{9,17... | collective-permute-start | bytes 2322440 | tf_op jit(solution)/shard_map/ppermute | solution.py:318
  74.2 8.0 %collective-permute-start.8 = (bf16[336,128]{1,0:T(8,128)(2,1)S(1)}, bf16[336,128]{1,0:T(8,128)(2,1)S(1)}, u32[]{:S(2)}, u32[]{:S(2)}) collective-permute-start(bf16[336,128]{1,0:T(8,128)(2,1)S(1)} %get-tuple-element.31), channel_id=1, source_target_pairs={{0,15},{1,14},{2,13},{3,12},{4,11},{5,10},{6,9},{7,8},{8,23},{9,22... | collective-permute-start | bytes 258056 | tf_op jit(solution)/shard_map/ppermute | solution.py:318
  78.7 7.6 %collective-permute-start.9 = (bf16[336,128]{1,0:T(8,128)(2,1)S(1)}, bf16[336,128]{1,0:T(8,128)(2,1)S(1)}, u32[]{:S(2)}, u32[]{:S(2)}) collective-permute-start(bf16[336,128]{1,0:T(8,128)(2,1)S(1)} %get-tuple-element.32), channel_id=1, source_target_pairs={{0,14},{1,15},{2,12},{3,13},{4,10},{5,11},{6,8},{7,9},{8,22},{9,23... | collective-permute-start | bytes 258056 | tf_op jit(solution)/shard_map/ppermute | solution.py:318
  78.7 11.5 %collective-permute-start.10 = (bf16[336,128]{1,0:T(8,128)(2,1)S(1)}, bf16[336,128]{1,0:T(8,128)(2,1)S(1)}, u32[]{:S(2)}, u32[]{:S(2)}) collective-permute-start(bf16[336,128]{1,0:T(8,128)(2,1)S(1)} %get-tuple-element.33), channel_id=1, source_target_pairs={{0,13},{1,12},{2,15},{3,14},{4,9},{5,8},{6,11},{7,10},{8,21},{9,20... | collective-permute-start | bytes 258056 | tf_op jit(solution)/shard_map/ppermute | solution.py:318
  78.7 14.0 %collective-permute-start.11 = (bf16[336,128]{1,0:T(8,128)(2,1)S(1)}, bf16[336,128]{1,0:T(8,128)(2,1)S(1)}, u32[]{:S(2)}, u32[]{:S(2)}) collective-permute-start(bf16[336,128]{1,0:T(8,128)(2,1)S(1)} %get-tuple-element.34), channel_id=1, source_target_pairs={{0,12},{1,13},{2,14},{3,15},{4,8},{5,9},{6,10},{7,11},{8,20},{9,21... | collective-permute-start | bytes 258056 | tf_op jit(solution)/shard_map/ppermute | solution.py:318
  82.3 10.5 %collective-permute-start.13 = (bf16[336,128]{1,0:T(8,128)(2,1)S(1)}, bf16[336,128]{1,0:T(8,128)(2,1)S(1)}, u32[]{:S(2)}, u32[]{:S(2)}) collective-permute-start(bf16[336,128]{1,0:T(8,128)(2,1)S(1)} %get-tuple-element.36), channel_id=1, source_target_pairs={{0,9},{1,8},{2,11},{3,10},{4,13},{5,12},{6,15},{7,14},{8,17},{9,16... | collective-permute-start | bytes 258056 | tf_op jit(solution)/shard_map/ppermute | solution.py:318
  86.3 7.4 %collective-permute-start.14 = (bf16[336,128]{1,0:T(8,128)(2,1)S(1)}, bf16[336,128]{1,0:T(8,128)(2,1)S(1)}, u32[]{:S(2)}, u32[]{:S(2)}) collective-permute-start(bf16[336,128]{1,0:T(8,128)(2,1)S(1)} %get-tuple-element.37), channel_id=1, source_target_pairs={{0,10},{1,11},{2,8},{3,9},{4,14},{5,15},{6,12},{7,13},{8,18},{9,19... | collective-permute-start | bytes 258056 | tf_op jit(solution)/shard_map/ppermute | solution.py:318
  90.2 6.0 %collective-permute-start.15 = (bf16[336,128]{1,0:T(8,128)(2,1)S(1)}, bf16[336,128]{1,0:T(8,128)(2,1)S(1)}, u32[]{:S(2)}, u32[]{:S(2)}) collective-permute-start(bf16[336,128]{1,0:T(8,128)(2,1)S(1)} %get-tuple-element.38), channel_id=1, source_target_pairs={{0,11},{1,10},{2,9},{3,8},{4,15},{5,14},{6,13},{7,12},{8,19},{9,18... | collective-permute-start | bytes 258056 | tf_op jit(solution)/shard_map/ppermute | solution.py:318

commit v3 on v2

--- a/solution.py
+++ b/solution.py
@@ -82,15 +82,30 @@
     return -(-rows // LANES)
 
 
-def split_kernel(steps, me_ref, query_ref, key_ref, value_ref, *out_refs):
+def split_kernel(
+    steps, me_ref, span_ref, query_ref, key_ref, value_ref, *refs
+):
+    halo_ref, out_refs, arrived = refs[0], refs[1:-1], refs[-1]
     me = me_ref[0]
     rows = query_ref.shape[0]
-    halo = (WMAX - 1) * BLK
-    out_refs[0][0] = key_ref[rows - halo :, :]
-    out_refs[0][1] = value_ref[rows - halo :, :]
-    for step in range(steps):
+    halo = halo_ref.shape[1]
+    copies = []
+    for step, out_ref in zip(steps, out_refs):
         head = pl.multiple_of(partner(me, step) * HD, HD)
-        out_refs[1 + step][...] = query_ref[:, pl.ds(head, HD)]
+        copies.append((query_ref.at[:, pl.ds(head, HD)], out_ref.at[:rows]))
+    copies.append((key_ref.at[rows - halo :], halo_ref.at[0]))
+    copies.append((value_ref.at[rows - halo :], halo_ref.at[1]))
+    copies = [
+        pltpu.make_async_copy(source, target, arrived.at[index])
+        for index, (source, target) in enumerate(copies)
+    ]
+    for copy in copies:
+        copy.start()
+    width = jnp.full((STAT_ROWS, HD), span_ref[0].astype(jnp.float32)).astype(jnp.bfloat16)
+    for out_ref in out_refs:
+        out_ref[rows:, :] = width
+    for copy in copies:
+        copy.wait()
 
 
 def far_kernel(
@@ -99,7 +114,7 @@
     me = me_ref[0]
     span = span_ref[0]
     count = len(steps)
-    query_refs, out_refs = refs[:count], refs[-count:]
+    query_refs, out_refs = refs[:count], refs[count:]
     last = key_ref.shape[0] // BLK - 1
 
     def block(ref, at):
@@ -112,13 +127,7 @@
     for index, step in enumerate(steps):
         chunk = partner(me, step)
         query_ref, out_ref = query_refs[index], out_refs[index]
-        if step == 0:
-            near_ref = refs[count]
-            wide = near_ref.shape[1]
-            out_ref[:, :wide] = near_ref[...]
-        else:
-            wide = 0
-        rows = query_ref.shape[0]
+        rows = query_ref.shape[0] - STAT_ROWS
         blocks = rows // BLK
         first = chunk == 0
         all_scores, all_values = [], []
@@ -149,24 +158,25 @@
                 stats.append(row)
         tile = stat_tile(stats)
         for b in range(blocks):
-            out_ref[b * BLK : (b + 1) * BLK, wide:] = parts[b]
-        out_ref[rows:, wide:] = tile
+            out_ref[b * BLK : (b + 1) * BLK, :] = parts[b]
+        out_ref[rows:, :] = tile
 
 
 def near_kernel(
-    me_ref, spans_ref, query_ref, key_ref, value_ref, halo_ref, out_ref
+    steps, me_ref, query_ref, key_ref, value_ref, halo_ref, own_ref, *refs
 ):
+    came_refs, out_ref = refs[:-1], refs[-1]
     me = me_ref[0]
-    rows = query_ref.shape[0]
-    heads = query_ref.shape[1] // HD
+    rows, wide = query_ref.shape
     halo = (WMAX - 1) * BLK
-
-    def one_head(head, carry):
-        lanes = pl.ds(pl.multiple_of(head * HD, HD), HD)
-        span = spans_ref[head, 0]
+    starts = list(range(0, rows, 2 * BLK))
+    sizes = [min(2 * BLK, rows - start) for start in starts]
+    out_ref[:, wide:] = own_ref[...]
+    for step, came_ref in zip(steps, came_refs):
+        lanes = pl.ds(pl.multiple_of(partner(me, step) * HD, HD), HD)
+        width = came_ref[rows:, :].astype(jnp.float32)[:1]
+        width = jnp.concatenate([width] * ((2 * BLK + halo) // LANES), axis=1)
         all_scores, all_values = [], []
-        starts = list(range(0, rows, 2 * BLK))
-        sizes = [min(2 * BLK, rows - start) for start in starts]
         for start, size in zip(starts, sizes):
             query = query_ref[start : start + size, lanes]
             if start < halo:
@@ -179,9 +189,8 @@
             scores = scores_of(query, keys)
             row_at = lax.broadcasted_iota(jnp.int32, scores.shape, 0)
             lane_at = lax.broadcasted_iota(jnp.int32, scores.shape, 1)
-            allowed = (lane_at <= row_at + halo) & (
-                lane_at // BLK - row_at // BLK > WMAX - 1 - span
-            )
+            slot = (lane_at // BLK - row_at // BLK).astype(jnp.float32)
+            allowed = (lane_at <= row_at + halo) & (slot + width[:, : size + halo] >= WMAX)
             if start < halo:
                 closed = jnp.where(me == 0, halo - start, 0)
                 allowed = allowed & (lane_at >= closed)
@@ -192,9 +201,6 @@
         for start, size, part in zip(starts, sizes, parts):
             out_ref[start : start + size, lanes] = part
         out_ref[rows:, lanes] = tile
-        return carry
-
-    lax.fori_loop(0, heads, one_head, 0)
 
 
 def merge_kernel(steps, me_ref, *refs):
@@ -238,56 +244,39 @@
     heads = wide // HD
     bf16 = jnp.bfloat16
     me = lax.axis_index("seq").astype(jnp.int32)[None]
-    spans = lax.all_gather(
-        lax.optimization_barrier(jnp.broadcast_to(window, (8, LANES))), "seq", axis=0, tiled=True
-    )
+    half = max(seq_count // 2, 1)
+    order = list(range(seq_count - 1, half - 1, -1)) + list(range(half))
 
     parts = pl.pallas_call(
-        functools.partial(split_kernel, seq_count),
+        functools.partial(split_kernel, order),
         out_shape=[jax.ShapeDtypeStruct((2, halo, wide), bf16)]
-        + [jax.ShapeDtypeStruct((rows, HD), bf16)] * seq_count,
-        in_specs=[whole_smem] + [whole_vmem] * 3,
+        + [jax.ShapeDtypeStruct((rows + STAT_ROWS, HD), bf16)] * seq_count,
+        in_specs=[whole_smem] * 2 + [anywhere] * 3,
         out_specs=[whole_vmem] * (1 + seq_count),
+        scratch_shapes=[pltpu.SemaphoreType.DMA((seq_count + 2,))],
         compiler_params=params(queries),
         cost_estimate=pl.CostEstimate(flops=0, bytes_accessed=5 * rows * wide, transcendentals=0),
         name="split",
-    )(me, queries[0], keys_new[0], values_new[0])
-    mine, sent = parts[0], parts[1:]
+    )(me, window[0], queries[0], keys_new[0], values_new[0])
+    mine, sent = parts[0], dict(zip(order, parts[1:]))
 
     def swapped(shard, step):
         if step == 0:
             return shard
         return lax.ppermute(shard, "seq", [(i, i ^ step) for i in range(seq_count)])
 
-    half = max(seq_count // 2, 1)
-    order = list(range(seq_count - 1, half - 1, -1)) + list(range(half))
     came = {step: swapped(sent[step], step) for step in order}
     before = lax.ppermute(mine, "seq", [(i, i + 1) for i in range(seq_count - 1)])
 
-    near = pl.pallas_call(
-        near_kernel,
-        out_shape=jax.ShapeDtypeStruct((rows + STAT_ROWS, wide), bf16),
-        in_specs=[whole_smem] * 2 + [whole_vmem] * 4,
-        out_specs=whole_vmem,
-        compiler_params=params(queries),
-        cost_estimate=pl.CostEstimate(
-            flops=heads * rows * 256 * HD * 4,
-            bytes_accessed=9 * rows * wide,
-            transcendentals=heads * rows * 256,
-        ),
-        name="near",
-    )(me, spans[::8], queries[0], keys_new[0], values_new[0], before)
     picks = random_blocks[0].reshape(-1)
 
     def far_call(steps):
         count = len(steps)
         out_rows = rows + STAT_ROWS
-        widths = [HD] * count
-        widths[steps.index(0)] += wide
         return pl.pallas_call(
             functools.partial(far_kernel, steps),
-            out_shape=[jax.ShapeDtypeStruct((out_rows, width), bf16) for width in widths],
-            in_specs=[whole_smem] * 4 + [whole_vmem] * (2 + count + 1),
+            out_shape=[jax.ShapeDtypeStruct((out_rows, HD), bf16)] * count,
+            in_specs=[whole_smem] * 4 + [whole_vmem] * (2 + count),
             out_specs=[whole_vmem] * count,
             compiler_params=params(queries),
             cost_estimate=pl.CostEstimate(
@@ -304,10 +293,30 @@
             keys_cache[0],
             values_cache[0],
             *[came[step] for step in steps],
-            near,
         )
 
     far = dict(zip(order, far_call(order)))
+    far[0] = pl.pallas_call(
+        functools.partial(near_kernel, order),
+        out_shape=jax.ShapeDtypeStruct((rows + STAT_ROWS, wide + HD), bf16),
+        in_specs=[whole_smem] + [whole_vmem] * (5 + seq_count),
+        out_specs=whole_vmem,
+        compiler_params=params(queries),
+        cost_estimate=pl.CostEstimate(
+            flops=heads * rows * 256 * HD * 4,
+            bytes_accessed=9 * rows * wide,
+            transcendentals=heads * rows * 256,
+        ),
+        name="near",
+    )(
+        me,
+        queries[0],
+        keys_new[0],
+        values_new[0],
+        before,
+        far[0],
+        *[came[step] for step in order],
+    )
 
     def onward(shard, step):
         pairs = [

time: 97.8 us -> 75.5 us (0.77)
  blocking collectives: 30.9 us -> 0 us
  starting transfers between devices: 39.6 us -> 47.8 us
  Pallas kernels: 10.4 us -> 8.9 us
  local copies, waits for them, and re-layouts: 3.52 us -> 4.89 us
    all_gather x1 -> x0, blocking collectives: 30.9 us -> none  [per_device(): lax.all_gather(lax.optimization_barrier(jnp.broadcast_to(window, (8, LANE...]
    ppermute x8, starting transfers between devices: 9.8 us -> 15.4 us  [onward(): return lax.ppermute(shard, ('section', 'seq'), pairs)]
    ppermute x7, starting transfers between devices: 24.9 us -> 27.5 us  [swapped(): return lax.ppermute(shard, 'seq', [(i, i ^ step) for i in range(seq_count)])]
    ppermute x7, waiting for transfers between devices: 0.02 us -> 2.24 us  [swapped(): return lax.ppermute(shard, 'seq', [(i, i ^ step) for i in range(seq_count)])]
    ppermute x8, waiting for transfers between devices: 12.2 us -> 10.5 us  [onward(): return lax.ppermute(shard, ('section', 'seq'), pairs)]
    unnamed x21, local copies, waits for them, and re-layouts: 3.4 us -> 4.78 us
    pallas_call x2, Pallas kernels: 4.93 us -> 3.55 us  [the longest x1 2.57 us: per_device(): pl.pallas_call(functools.partial(near_kernel, order), out_shape=jax.Shape...]
  transfers between devices with their start and end apart: 16 -> 16, of which waited for: 5 -> 6; matrix products, arithmetic and copies ran while one was open for 0% -> 0% of each run, Pallas kernels for 4% -> 5%
where the time goes in v3:
time: 75.5 us; the launch traced here: 75.2 us
  starting transfers between devices  47.8 us (63%)
  waiting for transfers between devices  12.8 us (17%)
  Pallas kernels  8.9 us (12%)
  local copies, waits for them, and re-layouts  4.89 us (6%)
  between operations  0.81 us (1%)
    ppermute x7, starting transfers between devices, swapped(): return lax.ppermute(shard, 'seq', [(i, i ^ step) for i in range(seq_count)])  27.5 us
    ppermute x8, starting transfers between devices, onward(): return lax.ppermute(shard, ('section', 'seq'), pairs)  15.4 us
    ppermute x8, waiting for transfers between devices, onward(): return lax.ppermute(shard, ('section', 'seq'), pairs)  10.5 us
    ppermute x1, starting transfers between devices, per_device(): lax.ppermute(mine, 'seq', [(i, i + 1) for i in range(seq_count - 1)])  4.9 us
    unnamed x21, local copies, waits for them, and re-layouts  4.78 us
    pallas_call x1, Pallas kernels, far_call(): pl.pallas_call(functools.partial(far_kernel, steps), out_shape=[jax.Shape...  4.04 us
    pallas_call x1, Pallas kernels, per_device(): pl.pallas_call(functools.partial(near_kernel, order), out_shape=jax.Shape...  2.57 us
    ppermute x7, waiting for transfers between devices, swapped(): return lax.ppermute(shard, 'seq', [(i, i ^ step) for i in range(seq_count)])  2.24 us
  transfers between devices with their start and end apart: 16, of which 6 were waited for; matrix products, arithmetic and copies ran while one was open for 0% of the time, Pallas kernels for 5%

profile of v3, /device:TPU:0, one launch (start us, length us, event | category | flops | bytes accessed | tf_op | source)
XLA Modules:
  0.0 75.2 jit_solution(15430502294533012579)
XLA Ops:
  0.7 0.0 copy-start
  0.7 1.1 %copy-done = bf16[1,320,1024]{2,1,0:T(8,128)(2,1)S(1)} copy-done((bf16[1,320,1024]{2,1,0:T(8,128)(2,1)S(1)}, bf16[1,320,1024]{2,1,0:T(8,128)(2,1)}, u32[]{:S(2)}) %copy-start) | copy-done | bytes 655384
  1.8 1.1 %copy-done.2 = bf16[1,320,1024]{2,1,0:T(8,128)(2,1)S(1)} copy-done((bf16[1,320,1024]{2,1,0:T(8,128)(2,1)S(1)}, bf16[1,320,1024]{2,1,0:T(8,128)(2,1)}, u32[]{:S(2)}) %copy-start.2) | copy-done | bytes 655384
  2.9 1.1 %copy-done.4 = bf16[1,320,1024]{2,1,0:T(8,128)(2,1)S(1)} copy-done((bf16[1,320,1024]{2,1,0:T(8,128)(2,1)S(1)}, bf16[1,320,1024]{2,1,0:T(8,128)(2,1)}, u32[]{:S(2)}) %copy-start.4) | copy-done | bytes 655384
  4.0 1.0 %split.1 = (bf16[2,128,1024]{2,1,0:T(8,128)(2,1)S(1)}, bf16[336,128]{1,0:T(8,128)(2,1)S(1)}, bf16[336,128]{1,0:T(8,128)(2,1)S(1)}, bf16[336,128]{1,0:T(8,128)(2,...) custom-call(s32[1]{0:T(128)} %bitcast.me_ref, ...), custom_call_target="tpu_custom_call" | custom-call | bytes 1638400 | tf_op jit(solution)/shard_map/split/pallas_call | solution.py:250
  4.9 4.9 %collective-permute-start.11 = (bf16[2,128,1024]{2,1,0:T(8,128)(2,1)S(1)}, bf16[2,128,1024]{2,1,0:T(8,128)(2,1)S(1)}, u32[]{:S(2)}, u32[]{:S(2)}) collective-permute-start(bf16[2,128,1024]{2,1,0:T(8,128)(2,1)S(1)} %get-tuple-element.34), channel_id=1, source_target_pairs={{0,1},{1,2},{2,3},{3,4},{4,5},{5,6},{6,7},{8,9},{9,10},{10,11},{11... | collective-permute-start | bytes 1572872 | tf_op jit(solution)/shard_map/ppermute | solution.py:269
  9.9 2.5 %collective-permute-start = (bf16[336,128]{1,0:T(8,128)(2,1)S(1)}, bf16[336,128]{1,0:T(8,128)(2,1)S(1)}, u32[]{:S(2)}, u32[]{:S(2)}) collective-permute-start(bf16[336,128]{1,0:T(8,128)(2,1)S(1)} %get-tuple-element.22), channel_id=1, source_target_pairs={{0,7},{1,6},{2,5},{3,4},{4,3},{5,2},{6,1},{7,0},{8,15},{9,14},{10,... | collective-permute-start | bytes 258056 | tf_op jit(solution)/shard_map/ppermute | solution.py:266
  12.3 2.4 %collective-permute-start.1 = (bf16[336,128]{1,0:T(8,128)(2,1)S(1)}, bf16[336,128]{1,0:T(8,128)(2,1)S(1)}, u32[]{:S(2)}, u32[]{:S(2)}) collective-permute-start(bf16[336,128]{1,0:T(8,128)(2,1)S(1)} %get-tuple-element.23), channel_id=1, source_target_pairs={{0,6},{1,7},{2,4},{3,5},{4,2},{5,3},{6,0},{7,1},{8,14},{9,15},{10,... | collective-permute-start | bytes 258056 | tf_op jit(solution)/shard_map/ppermute | solution.py:266
  14.7 0.7 collective-permute-start.2
  15.4 2.2 %collective-permute-start.3 = (bf16[336,128]{1,0:T(8,128)(2,1)}, bf16[336,128]{1,0:T(8,128)(2,1)S(1)}, u32[]{:S(2)}, u32[]{:S(2)}) collective-permute-start(bf16[336,128]{1,0:T(8,128)(2,1)} %get-tuple-element.25), channel_id=1, source_target_pairs={{0,4},{1,5},{2,6},{3,7},{4,0},{5,1},{6,2},{7,3},{8,12},{9,13},{10,... | collective-permute-start | bytes 258056 | tf_op jit(solution)/shard_map/ppermute | solution.py:266
  17.6 11.6 %collective-permute-start.4 = (bf16[336,128]{1,0:T(8,128)(2,1)}, bf16[336,128]{1,0:T(8,128)(2,1)S(1)}, u32[]{:S(2)}, u32[]{:S(2)}) collective-permute-start(bf16[336,128]{1,0:T(8,128)(2,1)} %get-tuple-element.27), channel_id=1, source_target_pairs={{0,1},{1,0},{2,3},{3,2},{4,5},{5,4},{6,7},{7,6},{8,9},{9,8},{10,11... | collective-permute-start | bytes 258056 | tf_op jit(solution)/shard_map/ppermute | solution.py:266
  29.2 0.0 collective-permute-done.2.refs_2_
  29.2 8.2 %collective-permute-start.6 = (bf16[336,128]{1,0:T(8,128)(2,1)S(1)}, bf16[336,128]{1,0:T(8,128)(2,1)S(1)}, u32[]{:S(2)}, u32[]{:S(2)}) collective-permute-start(bf16[336,128]{1,0:T(8,128)(2,1)S(1)} %get-tuple-element.29), channel_id=1, source_target_pairs={{0,3},{1,2},{2,1},{3,0},{4,7},{5,6},{6,5},{7,4},{8,11},{9,10},{10,... | collective-permute-start | bytes 258056 | tf_op jit(solution)/shard_map/ppermute | solution.py:266
  37.3 0.1 copy.10
  37.4 0.1 reshape_squeeze.3.random_ref
  37.6 2.2 %collective-permute-done.6.refs_7_ = bf16[336,128]{1,0:T(8,128)(2,1)S(1)} collective-permute-done((bf16[336,128]{1,0:T(8,128)(2,1)S(1)}, bf16[336,128]{1,0:T(8,128)(2,1)S(1)}, u32[]{:S(2)}, u32[]{:S(2)}) %collective-permute-start.6) | collective-permute-done | bytes 86048 | tf_op jit(solution)/shard_map/ppermute | solution.py:266
  39.8 1.4 %copy-done.7 = bf16[1,6144,128]{2,1,0:T(8,128)(2,1)S(1)} copy-done((bf16[1,6144,128]{2,1,0:T(8,128)(2,1)S(1)}, bf16[1,6144,128]{2,1,0:T(8,128)(2,1)}, u32[]{:S(2)}) %copy-start.7) | copy-done | bytes 1572888
  41.2 4.0 %far.1 = (bf16[336,128]{1,0:T(8,128)(2,1)S(1)}, bf16[336,128]{1,0:T(8,128)(2,1)S(1)}, bf16[336,128]{1,0:T(8,128)(2,1)S(1)}, bf16[336,128]{1,0:T(8,128)(2,1)S(1)}...) custom-call(s32[1]{0:T(128)} %bitcast.me_ref, ...), custom_call_target="tpu_custom_call" | custom-call | flops 419430400 | bytes 4456448 | tf_op jit(solution)/shard_map/far/pallas_call | solution.py:276
  45.3 2.6 %near.1 = bf16[336,1152]{1,0:T(8,128)(2,1)S(1)} custom-call(s32[1]{0:T(128)} %bitcast.me_ref, bf16[320,1024]{1,0:T(8,128)(2,1)S(1)} %bitcast.12, bf16[320,1024]{1,0:T(8,128)(2,1)S(1)} %bitcast.14, bf16[320,1024]{1,0:T(8,128)(2,1)S(1)} %bitcast.16, bf16[2,128,1024]{2,1,0:T(8,128)(2,1)S(1)} %collective-permute-done.11.halo_ref, ...), custom_call_target="tpu_custom_call" | custom-call | flops 335544320 | bytes 2949120 | tf_op jit(solution)/shard_map/near/pallas_call | solution.py:299
  47.9 0.1 collective-permute-start.12
  48.0 5.9 %collective-permute-start.7 = (bf16[336,128]{1,0:T(8,128)(2,1)S(1)}, bf16[336,128]{1,0:T(8,128)(2,1)S(1)}, u32[]{:S(2)}, u32[]{:S(2)}) collective-permute-start(bf16[336,128]{1,0:T(8,128)(2,1)S(1)} %get-tuple-element.30), channel_id=1, source_target_pairs={{0,15},{1,14},{2,13},{3,12},{4,11},{5,10},{6,9},{7,8},{8,23},{9,22... | collective-permute-start | bytes 258056 | tf_op jit(solution)/shard_map/ppermute | solution.py:327
  53.9 1.1 %collective-permute-start.8 = (bf16[336,128]{1,0:T(8,128)(2,1)S(1)}, bf16[336,128]{1,0:T(8,128)(2,1)S(1)}, u32[]{:S(2)}, u32[]{:S(2)}) collective-permute-start(bf16[336,128]{1,0:T(8,128)(2,1)S(1)} %get-tuple-element.31), channel_id=1, source_target_pairs={{0,14},{1,15},{2,12},{3,13},{4,10},{5,11},{6,8},{7,9},{8,22},{9,23... | collective-permute-start | bytes 258056 | tf_op jit(solution)/shard_map/ppermute | solution.py:327
  54.9 0.1 collective-permute-start.9
  55.0 3.4 %collective-permute-start.10 = (bf16[336,128]{1,0:T(8,128)(2,1)S(1)}, bf16[336,128]{1,0:T(8,128)(2,1)S(1)}, u32[]{:S(2)}, u32[]{:S(2)}) collective-permute-start(bf16[336,128]{1,0:T(8,128)(2,1)S(1)} %get-tuple-element.33), channel_id=1, source_target_pairs={{0,12},{1,13},{2,14},{3,15},{4,8},{5,9},{6,10},{7,11},{8,20},{9,21... | collective-permute-start | bytes 258056 | tf_op jit(solution)/shard_map/ppermute | solution.py:327
  58.4 0.2 collective-permute-start.13
  58.6 2.8 %collective-permute-done.8.refs_1_ = bf16[336,128]{1,0:T(8,128)(2,1)S(1)} collective-permute-done((bf16[336,128]{1,0:T(8,128)(2,1)S(1)}, bf16[336,128]{1,0:T(8,128)(2,1)S(1)}, u32[]{:S(2)}, u32[]{:S(2)}) %collective-permute-start.8) | collective-permute-done | bytes 86048 | tf_op jit(solution)/shard_map/ppermute | solution.py:327
  61.5 4.7 %collective-permute-start.14 = (bf16[336,128]{1,0:T(8,128)(2,1)S(1)}, bf16[336,128]{1,0:T(8,128)(2,1)S(1)}, u32[]{:S(2)}, u32[]{:S(2)}) collective-permute-start(bf16[336,128]{1,0:T(8,128)(2,1)S(1)} %get-tuple-element.37), channel_id=1, source_target_pairs={{0,10},{1,11},{2,8},{3,9},{4,14},{5,15},{6,12},{7,13},{8,18},{9,19... | collective-permute-start | bytes 258056 | tf_op jit(solution)/shard_map/ppermute | solution.py:327
  66.1 2.0 %collective-permute-done.9.refs_2_ = bf16[336,128]{1,0:T(8,128)(2,1)S(1)} collective-permute-done((bf16[336,128]{1,0:T(8,128)(2,1)S(1)}, bf16[336,128]{1,0:T(8,128)(2,1)S(1)}, u32[]{:S(2)}, u32[]{:S(2)}) %collective-permute-start.9) | collective-permute-done | bytes 86048 | tf_op jit(solution)/shard_map/ppermute | solution.py:327
  68.1 1.0 %collective-permute-done.10.refs_3_ = bf16[336,128]{1,0:T(8,128)(2,1)S(1)} collective-permute-done((bf16[336,128]{1,0:T(8,128)(2,1)S(1)}, bf16[336,128]{1,0:T(8,128)(2,1)S(1)}, u32[]{:S(2)}, u32[]{:S(2)}) %collective-permute-start.10) | collective-permute-done | bytes 86048 | tf_op jit(solution)/shard_map/ppermute | solution.py:327
  69.1 0.9 %collective-permute-done.14.refs_6_ = bf16[336,128]{1,0:T(8,128)(2,1)S(1)} collective-permute-done((bf16[336,128]{1,0:T(8,128)(2,1)S(1)}, bf16[336,128]{1,0:T(8,128)(2,1)S(1)}, u32[]{:S(2)}, u32[]{:S(2)}) %collective-permute-start.14) | collective-permute-done | bytes 86048 | tf_op jit(solution)/shard_map/ppermute | solution.py:327
  70.0 3.8 %collective-permute-done.15.refs_7_ = bf16[336,128]{1,0:T(8,128)(2,1)S(1)} collective-permute-done((bf16[336,128]{1,0:T(8,128)(2,1)S(1)}, bf16[336,128]{1,0:T(8,128)(2,1)S(1)}, u32[]{:S(2)}, u32[]{:S(2)}) %collective-permute-start.15) | collective-permute-done | bytes 86048 | tf_op jit(solution)/shard_map/ppermute | solution.py:327
  73.9 1.3 %merge.1 = bf16[320,1024]{1,0:T(8,128)(2,1)} custom-call(s32[1]{0:T(128)} %bitcast.me_ref, bf16[336,128]{1,0:T(8,128)(2,1)S(1)} %collective-permute-done.7.refs_0_, bf16[336,128]{1,0:T(8,128)(2,1)S(1)} %collective-permute-done.8.refs_1_, bf16[336,128]{1,0:T(8,128)(2,1)S(1)} %collective-permute-done.9.refs_2_, ...), custom_call_target="tpu_custom_call" | custom-call | bytes 1966080 | tf_op jit(solution)/shard_map/merge/pallas_call | solution.py:331
  (26 shorter events, 0.1 us)
Async XLA Ops:
  0.0 37.3 %copy-start.9 = (s32[1,40,3]{1,0,2:T(1,128)S(1)}, s32[1,40,3]{1,0,2:T(1,128)}, u32[]{:S(2)}) copy-start(s32[1,40,3]{1,0,2:T(1,128)} %param.15) | copy-start | bytes 1444
  0.0 39.8 %copy-start.8 = (s32[1,2]{1,0:T(1,128)S(1)}, s32[1,2]{1,0:T(1,128)}, u32[]{:S(2)}) copy-start(s32[1,2]{1,0:T(1,128)} %param.14) | copy-start | bytes 28
  0.7 1.1 %copy-start = (bf16[1,320,1024]{2,1,0:T(8,128)(2,1)S(1)}, bf16[1,320,1024]{2,1,0:T(8,128)(2,1)}, u32[]{:S(2)}) copy-start(bf16[1,320,1024]{2,1,0:T(8,128)(2,1)} %param.8) | copy-start | bytes 1966084
  1.8 1.1 %copy-start.2 = (bf16[1,320,1024]{2,1,0:T(8,128)(2,1)S(1)}, bf16[1,320,1024]{2,1,0:T(8,128)(2,1)}, u32[]{:S(2)}) copy-start(bf16[1,320,1024]{2,1,0:T(8,128)(2,1)} %param.9) | copy-start | bytes 1966084
  2.9 1.1 %copy-start.4 = (bf16[1,320,1024]{2,1,0:T(8,128)(2,1)S(1)}, bf16[1,320,1024]{2,1,0:T(8,128)(2,1)}, u32[]{:S(2)}) copy-start(bf16[1,320,1024]{2,1,0:T(8,128)(2,1)} %param.10) | copy-start | bytes 1966084
  4.0 35.9 %copy-start.6 = (bf16[1,6144,128]{2,1,0:T(8,128)(2,1)S(1)}, bf16[1,6144,128]{2,1,0:T(8,128)(2,1)}, u32[]{:S(2)}) copy-start(bf16[1,6144,128]{2,1,0:T(8,128)(2,1)} %param.11) | copy-start | bytes 4718596
  4.9 40.3 %collective-permute-start.11 = (bf16[2,128,1024]{2,1,0:T(8,128)(2,1)S(1)}, bf16[2,128,1024]{2,1,0:T(8,128)(2,1)S(1)}, u32[]{:S(2)}, u32[]{:S(2)}) collective-permute-start(bf16[2,128,1024]{2,1,0:T(8,128)(2,1)S(1)} %get-tuple-element.34), channel_id=1, source_target_pairs={{0,1},{1,2},{2,3},{3,4},{4,5},{5,6},{6,7},{8,9},{9,10},{10,11},{11... | collective-permute-start | bytes 1572872 | tf_op jit(solution)/shard_map/ppermute | solution.py:269
  9.9 7.7 %collective-permute-start = (bf16[336,128]{1,0:T(8,128)(2,1)S(1)}, bf16[336,128]{1,0:T(8,128)(2,1)S(1)}, u32[]{:S(2)}, u32[]{:S(2)}) collective-permute-start(bf16[336,128]{1,0:T(8,128)(2,1)S(1)} %get-tuple-element.22), channel_id=1, source_target_pairs={{0,7},{1,6},{2,5},{3,4},{4,3},{5,2},{6,1},{7,0},{8,15},{9,14},{10,... | collective-permute-start | bytes 258056 | tf_op jit(solution)/shard_map/ppermute | solution.py:266
  12.3 16.9 %collective-permute-start.1 = (bf16[336,128]{1,0:T(8,128)(2,1)S(1)}, bf16[336,128]{1,0:T(8,128)(2,1)S(1)}, u32[]{:S(2)}, u32[]{:S(2)}) collective-permute-start(bf16[336,128]{1,0:T(8,128)(2,1)S(1)} %get-tuple-element.23), channel_id=1, source_target_pairs={{0,6},{1,7},{2,4},{3,5},{4,2},{5,3},{6,0},{7,1},{8,14},{9,15},{10,... | collective-permute-start | bytes 258056 | tf_op jit(solution)/shard_map/ppermute | solution.py:266
  14.7 14.5 %collective-permute-start.2 = (bf16[336,128]{1,0:T(8,128)(2,1)S(1)}, bf16[336,128]{1,0:T(8,128)(2,1)S(1)}, u32[]{:S(2)}, u32[]{:S(2)}) collective-permute-start(bf16[336,128]{1,0:T(8,128)(2,1)S(1)} %get-tuple-element.24), channel_id=1, source_target_pairs={{0,5},{1,4},{2,7},{3,6},{4,1},{5,0},{6,3},{7,2},{8,13},{9,12},{10,... | collective-permute-start | bytes 258056 | tf_op jit(solution)/shard_map/ppermute | solution.py:266
  15.4 22.1 %collective-permute-start.3 = (bf16[336,128]{1,0:T(8,128)(2,1)}, bf16[336,128]{1,0:T(8,128)(2,1)S(1)}, u32[]{:S(2)}, u32[]{:S(2)}) collective-permute-start(bf16[336,128]{1,0:T(8,128)(2,1)} %get-tuple-element.25), channel_id=1, source_target_pairs={{0,4},{1,5},{2,6},{3,7},{4,0},{5,1},{6,2},{7,3},{8,12},{9,13},{10,... | collective-permute-start | bytes 258056 | tf_op jit(solution)/shard_map/ppermute | solution.py:266
  17.6 20.0 %collective-permute-start.4 = (bf16[336,128]{1,0:T(8,128)(2,1)}, bf16[336,128]{1,0:T(8,128)(2,1)S(1)}, u32[]{:S(2)}, u32[]{:S(2)}) collective-permute-start(bf16[336,128]{1,0:T(8,128)(2,1)} %get-tuple-element.27), channel_id=1, source_target_pairs={{0,1},{1,0},{2,3},{3,2},{4,5},{5,4},{6,7},{7,6},{8,9},{9,8},{10,11... | collective-permute-start | bytes 258056 | tf_op jit(solution)/shard_map/ppermute | solution.py:266
  29.2 8.4 %collective-permute-start.5 = (bf16[336,128]{1,0:T(8,128)(2,1)S(1)}, bf16[336,128]{1,0:T(8,128)(2,1)S(1)}, u32[]{:S(2)}, u32[]{:S(2)}) collective-permute-start(bf16[336,128]{1,0:T(8,128)(2,1)S(1)} %get-tuple-element.28), channel_id=1, source_target_pairs={{0,2},{1,3},{2,0},{3,1},{4,6},{5,7},{6,4},{7,5},{8,10},{9,11},{10,... | collective-permute-start | bytes 258056 | tf_op jit(solution)/shard_map/ppermute | solution.py:266
  29.2 10.6 %collective-permute-start.6 = (bf16[336,128]{1,0:T(8,128)(2,1)S(1)}, bf16[336,128]{1,0:T(8,128)(2,1)S(1)}, u32[]{:S(2)}, u32[]{:S(2)}) collective-permute-start(bf16[336,128]{1,0:T(8,128)(2,1)S(1)} %get-tuple-element.29), channel_id=1, source_target_pairs={{0,3},{1,2},{2,1},{3,0},{4,7},{5,6},{6,5},{7,4},{8,11},{9,10},{10,... | collective-permute-start | bytes 258056 | tf_op jit(solution)/shard_map/ppermute | solution.py:266
  39.8 1.4 %copy-start.7 = (bf16[1,6144,128]{2,1,0:T(8,128)(2,1)S(1)}, bf16[1,6144,128]{2,1,0:T(8,128)(2,1)}, u32[]{:S(2)}) copy-start(bf16[1,6144,128]{2,1,0:T(8,128)(2,1)} %param.12) | copy-start | bytes 4718596
  41.2 4.1 %copy-start.1 = (bf16[1,320,1024]{2,1,0:T(8,128)(2,1)S(1)}, bf16[1,320,1024]{2,1,0:T(8,128)(2,1)}, u32[]{:S(2)}) copy-start(bf16[1,320,1024]{2,1,0:T(8,128)(2,1)} %param.8) | copy-start | bytes 1966084
  41.2 4.1 %copy-start.3 = (bf16[1,320,1024]{2,1,0:T(8,128)(2,1)S(1)}, bf16[1,320,1024]{2,1,0:T(8,128)(2,1)}, u32[]{:S(2)}) copy-start(bf16[1,320,1024]{2,1,0:T(8,128)(2,1)} %param.9) | copy-start | bytes 1966084
  41.2 4.1 %copy-start.5 = (bf16[1,320,1024]{2,1,0:T(8,128)(2,1)S(1)}, bf16[1,320,1024]{2,1,0:T(8,128)(2,1)}, u32[]{:S(2)}) copy-start(bf16[1,320,1024]{2,1,0:T(8,128)(2,1)} %param.10) | copy-start | bytes 1966084
  47.9 26.0 %collective-permute-start.12 = (bf16[336,1152]{1,0:T(8,128)(2,1)S(1)}, bf16[336,1152]{1,0:T(8,128)(2,1)S(1)}, u32[]{:S(2)}, u32[]{:S(2)}) collective-permute-start(bf16[336,1152]{1,0:T(8,128)(2,1)S(1)} %near.1), channel_id=1, source_target_pairs={{0,8},{1,9},{2,10},{3,11},{4,12},{5,13},{6,14},{7,15},{8,16},{9,17... | collective-permute-start | bytes 2322440 | tf_op jit(solution)/shard_map/ppermute | solution.py:327
  48.0 10.5 %collective-permute-start.7 = (bf16[336,128]{1,0:T(8,128)(2,1)S(1)}, bf16[336,128]{1,0:T(8,128)(2,1)S(1)}, u32[]{:S(2)}, u32[]{:S(2)}) collective-permute-start(bf16[336,128]{1,0:T(8,128)(2,1)S(1)} %get-tuple-element.30), channel_id=1, source_target_pairs={{0,15},{1,14},{2,13},{3,12},{4,11},{5,10},{6,9},{7,8},{8,23},{9,22... | collective-permute-start | bytes 258056 | tf_op jit(solution)/shard_map/ppermute | solution.py:327
  53.9 7.6 %collective-permute-start.8 = (bf16[336,128]{1,0:T(8,128)(2,1)S(1)}, bf16[336,128]{1,0:T(8,128)(2,1)S(1)}, u32[]{:S(2)}, u32[]{:S(2)}) collective-permute-start(bf16[336,128]{1,0:T(8,128)(2,1)S(1)} %get-tuple-element.31), channel_id=1, source_target_pairs={{0,14},{1,15},{2,12},{3,13},{4,10},{5,11},{6,8},{7,9},{8,22},{9,23... | collective-permute-start | bytes 258056 | tf_op jit(solution)/shard_map/ppermute | solution.py:327
  54.9 13.2 %collective-permute-start.9 = (bf16[336,128]{1,0:T(8,128)(2,1)S(1)}, bf16[336,128]{1,0:T(8,128)(2,1)S(1)}, u32[]{:S(2)}, u32[]{:S(2)}) collective-permute-start(bf16[336,128]{1,0:T(8,128)(2,1)S(1)} %get-tuple-element.32), channel_id=1, source_target_pairs={{0,13},{1,12},{2,15},{3,14},{4,9},{5,8},{6,11},{7,10},{8,21},{9,20... | collective-permute-start | bytes 258056 | tf_op jit(solution)/shard_map/ppermute | solution.py:327
  55.0 14.1 %collective-permute-start.10 = (bf16[336,128]{1,0:T(8,128)(2,1)S(1)}, bf16[336,128]{1,0:T(8,128)(2,1)S(1)}, u32[]{:S(2)}, u32[]{:S(2)}) collective-permute-start(bf16[336,128]{1,0:T(8,128)(2,1)S(1)} %get-tuple-element.33), channel_id=1, source_target_pairs={{0,12},{1,13},{2,14},{3,15},{4,8},{5,9},{6,10},{7,11},{8,20},{9,21... | collective-permute-start | bytes 258056 | tf_op jit(solution)/shard_map/ppermute | solution.py:327
  58.4 10.7 %collective-permute-start.13 = (bf16[336,128]{1,0:T(8,128)(2,1)S(1)}, bf16[336,128]{1,0:T(8,128)(2,1)S(1)}, u32[]{:S(2)}, u32[]{:S(2)}) collective-permute-start(bf16[336,128]{1,0:T(8,128)(2,1)S(1)} %get-tuple-element.36), channel_id=1, source_target_pairs={{0,9},{1,8},{2,11},{3,10},{4,13},{5,12},{6,15},{7,14},{8,17},{9,16... | collective-permute-start | bytes 258056 | tf_op jit(solution)/shard_map/ppermute | solution.py:327
  61.5 8.6 %collective-permute-start.14 = (bf16[336,128]{1,0:T(8,128)(2,1)S(1)}, bf16[336,128]{1,0:T(8,128)(2,1)S(1)}, u32[]{:S(2)}, u32[]{:S(2)}) collective-permute-start(bf16[336,128]{1,0:T(8,128)(2,1)S(1)} %get-tuple-element.37), channel_id=1, source_target_pairs={{0,10},{1,11},{2,8},{3,9},{4,14},{5,15},{6,12},{7,13},{8,18},{9,19... | collective-permute-start | bytes 258056 | tf_op jit(solution)/shard_map/ppermute | solution.py:327
  68.1 5.7 %collective-permute-start.15 = (bf16[336,128]{1,0:T(8,128)(2,1)S(1)}, bf16[336,128]{1,0:T(8,128)(2,1)S(1)}, u32[]{:S(2)}, u32[]{:S(2)}) collective-permute-start(bf16[336,128]{1,0:T(8,128)(2,1)S(1)} %get-tuple-element.38), channel_id=1, source_target_pairs={{0,11},{1,10},{2,9},{3,8},{4,15},{5,14},{6,13},{7,12},{8,19},{9,18... | collective-permute-start | bytes 258056 | tf_op jit(solution)/shard_map/ppermute | solution.py:327

commit v4 on v3

--- a/solution.py
+++ b/solution.py
@@ -20,7 +20,7 @@
 VMEM_BASE = 12 * 1024 * 1024
 
 whole_vmem = pl.BlockSpec(memory_space=pltpu.VMEM)
-anywhere = pl.BlockSpec(memory_space=pl.ANY)
+in_hbm = pl.BlockSpec(memory_space=pltpu.HBM)
 whole_smem = pl.BlockSpec(memory_space=pltpu.SMEM)
 
 
@@ -111,10 +111,13 @@
 def far_kernel(
     steps, me_ref, span_ref, global_ref, random_ref, key_ref, value_ref, *refs
 ):
+    count = len(steps)
+    query_refs, out_refs = refs[:count], refs[count : 2 * count]
+    value_held, arrived = refs[2 * count :]
+    value_copy = pltpu.make_async_copy(value_ref, value_held, arrived)
+    value_copy.start()
     me = me_ref[0]
     span = span_ref[0]
-    count = len(steps)
-    query_refs, out_refs = refs[:count], refs[count:]
     last = key_ref.shape[0] // BLK - 1
 
     def block(ref, at):
@@ -123,31 +126,35 @@
         return ref[pl.ds(pl.multiple_of(at * BLK, BLK), BLK), :]
 
     glob_keys = [block(key_ref, global_ref[g]) for g in range(GLOB)]
-    glob_values = [block(value_ref, global_ref[g]) for g in range(GLOB)]
     for index, step in enumerate(steps):
         chunk = partner(me, step)
         query_ref, out_ref = query_refs[index], out_refs[index]
         rows = query_ref.shape[0] - STAT_ROWS
         blocks = rows // BLK
         first = chunk == 0
-        all_scores, all_values = [], []
+        all_scores, all_picks = [], []
         for b in range(blocks):
             query = query_ref[b * BLK : (b + 1) * BLK, :]
             base = (chunk * blocks + b) * RAND
             picks = [random_ref[base + r] for r in range(RAND)]
             keys = glob_keys + [block(key_ref, pick) for pick in picks]
-            values = glob_values + [block(value_ref, pick) for pick in picks]
             known = len(keys) * BLK
             spare = [last + 1 + b - w for w in range(b + 1, WMAX)]
             keys = keys + [block(key_ref, at) for at in spare]
-            values = values + [block(value_ref, at) for at in spare]
             scores = scores_of(query, jnp.concatenate(keys, axis=0))
             if spare:
                 open_slots = jnp.where(first, jnp.clip(span - (b + 1), 0, len(spare)), 0)
                 lane_at = lax.broadcasted_iota(jnp.int32, scores.shape, 1)
                 scores = jnp.where(lane_at < known + open_slots * BLK, scores, MASKED)
             all_scores.append(scores)
-            all_values.append(jnp.concatenate(values, axis=0))
+            all_picks.append(picks + spare)
+        if index == 0:
+            value_copy.wait()
+            glob_values = [block(value_held, global_ref[g]) for g in range(GLOB)]
+        all_values = [
+            jnp.concatenate(glob_values + [block(value_held, at) for at in picks], axis=0)
+            for picks in all_picks
+        ]
         parts, lses = softmax_parts(all_scores, all_values)
         stats = []
         for b in range(blocks):
@@ -245,13 +252,13 @@
     bf16 = jnp.bfloat16
     me = lax.axis_index("seq").astype(jnp.int32)[None]
     half = max(seq_count // 2, 1)
-    order = list(range(seq_count - 1, half - 1, -1)) + list(range(half))
+    order = list(range(1, half)) + list(range(seq_count - 1, half - 1, -1)) + [0]
 
     parts = pl.pallas_call(
         functools.partial(split_kernel, order),
         out_shape=[jax.ShapeDtypeStruct((2, halo, wide), bf16)]
         + [jax.ShapeDtypeStruct((rows + STAT_ROWS, HD), bf16)] * seq_count,
-        in_specs=[whole_smem] * 2 + [anywhere] * 3,
+        in_specs=[whole_smem] * 2 + [in_hbm] * 3,
         out_specs=[whole_vmem] * (1 + seq_count),
         scratch_shapes=[pltpu.SemaphoreType.DMA((seq_count + 2,))],
         compiler_params=params(queries),
@@ -276,8 +283,12 @@
         return pl.pallas_call(
             functools.partial(far_kernel, steps),
             out_shape=[jax.ShapeDtypeStruct((out_rows, HD), bf16)] * count,
-            in_specs=[whole_smem] * 4 + [whole_vmem] * (2 + count),
+            in_specs=[whole_smem] * 4 + [whole_vmem, in_hbm] + [whole_vmem] * count,
             out_specs=[whole_vmem] * count,
+            scratch_shapes=[
+                pltpu.VMEM(values_cache.shape[1:], bf16),
+                pltpu.SemaphoreType.DMA,
+            ],
             compiler_params=params(queries),
             cost_estimate=pl.CostEstimate(
                 flops=count * rows * 320 * HD * 4,

time: 75.5 us -> 81.3 us (1.077)
  waiting for transfers between devices: 12.8 us -> 35.4 us
  starting transfers between devices: 47.8 us -> 30.8 us
    ppermute x7, waiting for transfers between devices: 2.24 us -> 17 us  [swapped(): return lax.ppermute(shard, 'seq', [(i, i ^ step) for i in range(seq_count)])]
    ppermute x7, starting transfers between devices: 27.5 us -> 15.1 us  [swapped(): return lax.ppermute(shard, 'seq', [(i, i ^ step) for i in range(seq_count)])]
    ppermute x8, waiting for transfers between devices: 10.5 us -> 18.4 us  [onward(): return lax.ppermute(shard, ('section', 'seq'), pairs)]
    ppermute x8, starting transfers between devices: 15.4 us -> 10.8 us  [onward(): return lax.ppermute(shard, ('section', 'seq'), pairs)]
  transfers between devices with their start and end apart: 16 -> 16, of which waited for: 6 -> 7; matrix products, arithmetic and copies ran while one was open for 0% -> 0% of each run, Pallas kernels for 5% -> 5%
where the time goes in v4:
time: 81.3 us; the launch traced here: 81 us
  waiting for transfers between devices  35.4 us (44%)
  starting transfers between devices  30.8 us (38%)
  Pallas kernels  9.03 us (11%)
  local copies, waits for them, and re-layouts  4.89 us (6%)
    ppermute x8, waiting for transfers between devices, onward(): return lax.ppermute(shard, ('section', 'seq'), pairs)  18.4 us
    ppermute x7, waiting for transfers between devices, swapped(): return lax.ppermute(shard, 'seq', [(i, i ^ step) for i in range(seq_count)])  17 us
    ppermute x7, starting transfers between devices, swapped(): return lax.ppermute(shard, 'seq', [(i, i ^ step) for i in range(seq_count)])  15.1 us
    ppermute x8, starting transfers between devices, onward(): return lax.ppermute(shard, ('section', 'seq'), pairs)  10.8 us
    ppermute x1, starting transfers between devices, per_device(): lax.ppermute(mine, 'seq', [(i, i + 1) for i in range(seq_count - 1)])  4.9 us
    unnamed x21, local copies, waits for them, and re-layouts  4.78 us
    pallas_call x1, Pallas kernels, far_call(): pl.pallas_call(functools.partial(far_kernel, steps), out_shape=[jax.Shape...  4.14 us
    pallas_call x1, Pallas kernels, per_device(): pl.pallas_call(functools.partial(near_kernel, order), out_shape=jax.Shape...  2.58 us
  transfers between devices with their start and end apart: 16, of which 7 were waited for; matrix products, arithmetic and copies ran while one was open for 0% of the time, Pallas kernels for 5%

profile of v4, /device:TPU:0, one launch (start us, length us, event | category | flops | bytes accessed | tf_op | source)
XLA Modules:
  0.0 81.0 jit_solution(15156337491149044050)
XLA Ops:
  0.7 1.1 %copy-done = bf16[1,320,1024]{2,1,0:T(8,128)(2,1)S(1)} copy-done((bf16[1,320,1024]{2,1,0:T(8,128)(2,1)S(1)}, bf16[1,320,1024]{2,1,0:T(8,128)(2,1)}, u32[]{:S(2)}) %copy-start) | copy-done | bytes 655384
  1.8 1.1 %copy-done.2 = bf16[1,320,1024]{2,1,0:T(8,128)(2,1)S(1)} copy-done((bf16[1,320,1024]{2,1,0:T(8,128)(2,1)S(1)}, bf16[1,320,1024]{2,1,0:T(8,128)(2,1)}, u32[]{:S(2)}) %copy-start.2) | copy-done | bytes 655384
  2.9 1.1 %copy-done.4 = bf16[1,320,1024]{2,1,0:T(8,128)(2,1)S(1)} copy-done((bf16[1,320,1024]{2,1,0:T(8,128)(2,1)S(1)}, bf16[1,320,1024]{2,1,0:T(8,128)(2,1)}, u32[]{:S(2)}) %copy-start.4) | copy-done | bytes 655384
  4.0 1.0 %split.1 = (bf16[2,128,1024]{2,1,0:T(8,128)(2,1)S(1)}, bf16[336,128]{1,0:T(8,128)(2,1)S(1)}, bf16[336,128]{1,0:T(8,128)(2,1)S(1)}, bf16[336,128]{1,0:T(8,128)(2,...) custom-call(s32[1]{0:T(128)} %bitcast.me_ref, ...), custom_call_target="tpu_custom_call" | custom-call | bytes 1638400 | tf_op jit(solution)/shard_map/split/pallas_call | solution.py:257
  4.9 4.9 %collective-permute-start.14 = (bf16[2,128,1024]{2,1,0:T(8,128)(2,1)S(1)}, bf16[2,128,1024]{2,1,0:T(8,128)(2,1)S(1)}, u32[]{:S(2)}, u32[]{:S(2)}) collective-permute-start(bf16[2,128,1024]{2,1,0:T(8,128)(2,1)S(1)} %get-tuple-element.37), channel_id=1, source_target_pairs={{0,1},{1,2},{2,3},{3,4},{4,5},{5,6},{6,7},{8,9},{9,10},{10,11},{11... | collective-permute-start | bytes 1572872 | tf_op jit(solution)/shard_map/ppermute | solution.py:276
  9.9 1.6 %collective-permute-start = (bf16[336,128]{1,0:T(8,128)(2,1)S(1)}, bf16[336,128]{1,0:T(8,128)(2,1)S(1)}, u32[]{:S(2)}, u32[]{:S(2)}) collective-permute-start(bf16[336,128]{1,0:T(8,128)(2,1)S(1)} %get-tuple-element.22), channel_id=1, source_target_pairs={{0,1},{1,0},{2,3},{3,2},{4,5},{5,4},{6,7},{7,6},{8,9},{9,8},{10,11... | collective-permute-start | bytes 258056 | tf_op jit(solution)/shard_map/ppermute | solution.py:273
  11.4 1.6 %collective-permute-start.1 = (bf16[336,128]{1,0:T(8,128)(2,1)S(1)}, bf16[336,128]{1,0:T(8,128)(2,1)S(1)}, u32[]{:S(2)}, u32[]{:S(2)}) collective-permute-start(bf16[336,128]{1,0:T(8,128)(2,1)S(1)} %get-tuple-element.23), channel_id=1, source_target_pairs={{0,2},{1,3},{2,0},{3,1},{4,6},{5,7},{6,4},{7,5},{8,10},{9,11},{10,... | collective-permute-start | bytes 258056 | tf_op jit(solution)/shard_map/ppermute | solution.py:273
  13.0 0.4 collective-permute-start.2
  13.4 3.1 %collective-permute-start.3 = (bf16[336,128]{1,0:T(8,128)(2,1)}, bf16[336,128]{1,0:T(8,128)(2,1)S(1)}, u32[]{:S(2)}, u32[]{:S(2)}) collective-permute-start(bf16[336,128]{1,0:T(8,128)(2,1)} %get-tuple-element.25), channel_id=1, source_target_pairs={{0,7},{1,6},{2,5},{3,4},{4,3},{5,2},{6,1},{7,0},{8,15},{9,14},{10,... | collective-permute-start | bytes 258056 | tf_op jit(solution)/shard_map/ppermute | solution.py:273
  16.5 10.0 %collective-permute-done.refs_0_ = bf16[336,128]{1,0:T(8,128)(2,1)S(1)} collective-permute-done((bf16[336,128]{1,0:T(8,128)(2,1)S(1)}, bf16[336,128]{1,0:T(8,128)(2,1)S(1)}, u32[]{:S(2)}, u32[]{:S(2)}) %collective-permute-start) | collective-permute-done | bytes 86048 | tf_op jit(solution)/shard_map/ppermute | solution.py:273
  26.5 3.6 %collective-permute-start.4 = (bf16[336,128]{1,0:T(8,128)(2,1)}, bf16[336,128]{1,0:T(8,128)(2,1)S(1)}, u32[]{:S(2)}, u32[]{:S(2)}) collective-permute-start(bf16[336,128]{1,0:T(8,128)(2,1)} %get-tuple-element.26), channel_id=1, source_target_pairs={{0,6},{1,7},{2,4},{3,5},{4,2},{5,3},{6,0},{7,1},{8,14},{9,15},{10,... | collective-permute-start | bytes 258056 | tf_op jit(solution)/shard_map/ppermute | solution.py:273
  30.1 1.4 %collective-permute-start.5 = (bf16[336,128]{1,0:T(8,128)(2,1)S(1)}, bf16[336,128]{1,0:T(8,128)(2,1)S(1)}, u32[]{:S(2)}, u32[]{:S(2)}) collective-permute-start(bf16[336,128]{1,0:T(8,128)(2,1)S(1)} %get-tuple-element.27), channel_id=1, source_target_pairs={{0,5},{1,4},{2,7},{3,6},{4,1},{5,0},{6,3},{7,2},{8,13},{9,12},{10,... | collective-permute-start | bytes 258056 | tf_op jit(solution)/shard_map/ppermute | solution.py:273
  31.5 3.5 %collective-permute-start.6 = (bf16[336,128]{1,0:T(8,128)(2,1)S(1)}, bf16[336,128]{1,0:T(8,128)(2,1)S(1)}, u32[]{:S(2)}, u32[]{:S(2)}) collective-permute-start(bf16[336,128]{1,0:T(8,128)(2,1)S(1)} %get-tuple-element.28), channel_id=1, source_target_pairs={{0,4},{1,5},{2,6},{3,7},{4,0},{5,1},{6,2},{7,3},{8,12},{9,13},{10,... | collective-permute-start | bytes 258056 | tf_op jit(solution)/shard_map/ppermute | solution.py:273
  35.0 0.1 copy.10
  35.1 0.1 reshape_squeeze.3.random_ref
  35.2 6.2 %collective-permute-done.5.refs_5_ = bf16[336,128]{1,0:T(8,128)(2,1)S(1)} collective-permute-done((bf16[336,128]{1,0:T(8,128)(2,1)S(1)}, bf16[336,128]{1,0:T(8,128)(2,1)S(1)}, u32[]{:S(2)}, u32[]{:S(2)}) %collective-permute-start.5) | collective-permute-done | bytes 86048 | tf_op jit(solution)/shard_map/ppermute | solution.py:273
  41.4 0.8 collective-permute-done.6.refs_6_
  42.2 1.4 %copy-done.7 = bf16[1,6144,128]{2,1,0:T(8,128)(2,1)S(1)} copy-done((bf16[1,6144,128]{2,1,0:T(8,128)(2,1)S(1)}, bf16[1,6144,128]{2,1,0:T(8,128)(2,1)}, u32[]{:S(2)}) %copy-start.7) | copy-done | bytes 1572888
  43.6 4.1 %far.1 = (bf16[336,128]{1,0:T(8,128)(2,1)S(1)}, bf16[336,128]{1,0:T(8,128)(2,1)S(1)}, bf16[336,128]{1,0:T(8,128)(2,1)S(1)}, bf16[336,128]{1,0:T(8,128)(2,1)S(1)}...) custom-call(s32[1]{0:T(128)} %bitcast.me_ref, ...), custom_call_target="tpu_custom_call" | custom-call | flops 419430400 | bytes 4456448 | tf_op jit(solution)/shard_map/far/pallas_call | solution.py:283
  47.8 2.6 %near.1 = bf16[336,1152]{1,0:T(8,128)(2,1)S(1)} custom-call(s32[1]{0:T(128)} %bitcast.me_ref, bf16[320,1024]{1,0:T(8,128)(2,1)S(1)} %bitcast.12, bf16[320,1024]{1,0:T(8,128)(2,1)S(1)} %bitcast.14, bf16[320,1024]{1,0:T(8,128)(2,1)S(1)} %bitcast.16, bf16[2,128,1024]{2,1,0:T(8,128)(2,1)S(1)} %collective-permute-done.14.halo_ref, ...), custom_call_target="tpu_custom_call" | custom-call | flops 335544320 | bytes 2949120 | tf_op jit(solution)/shard_map/near/pallas_call | solution.py:310
  50.4 0.1 collective-permute-start.15
  50.5 2.0 %collective-permute-start.7 = (bf16[336,128]{1,0:T(8,128)(2,1)S(1)}, bf16[336,128]{1,0:T(8,128)(2,1)S(1)}, u32[]{:S(2)}, u32[]{:S(2)}) collective-permute-start(bf16[336,128]{1,0:T(8,128)(2,1)S(1)} %get-tuple-element.30), channel_id=1, source_target_pairs={{0,9},{1,8},{2,11},{3,10},{4,13},{5,12},{6,15},{7,14},{8,17},{9,16... | collective-permute-start | bytes 258056 | tf_op jit(solution)/shard_map/ppermute | solution.py:338
  52.5 2.4 %collective-permute-start.9 = (bf16[336,128]{1,0:T(8,128)(2,1)S(1)}, bf16[336,128]{1,0:T(8,128)(2,1)S(1)}, u32[]{:S(2)}, u32[]{:S(2)}) collective-permute-start(bf16[336,128]{1,0:T(8,128)(2,1)S(1)} %get-tuple-element.32), channel_id=1, source_target_pairs={{0,11},{1,10},{2,9},{3,8},{4,15},{5,14},{6,13},{7,12},{8,19},{9,18... | collective-permute-start | bytes 258056 | tf_op jit(solution)/shard_map/ppermute | solution.py:338
  54.8 2.1 %collective-permute-start.10 = (bf16[336,128]{1,0:T(8,128)(2,1)S(1)}, bf16[336,128]{1,0:T(8,128)(2,1)S(1)}, u32[]{:S(2)}, u32[]{:S(2)}) collective-permute-start(bf16[336,128]{1,0:T(8,128)(2,1)S(1)} %get-tuple-element.33), channel_id=1, source_target_pairs={{0,15},{1,14},{2,13},{3,12},{4,11},{5,10},{6,9},{7,8},{8,23},{9,22... | collective-permute-start | bytes 258056 | tf_op jit(solution)/shard_map/ppermute | solution.py:338
  57.0 8.7 %collective-permute-done.7.refs_0_ = bf16[336,128]{1,0:T(8,128)(2,1)S(1)} collective-permute-done((bf16[336,128]{1,0:T(8,128)(2,1)S(1)}, bf16[336,128]{1,0:T(8,128)(2,1)S(1)}, u32[]{:S(2)}, u32[]{:S(2)}) %collective-permute-start.7) | collective-permute-done | bytes 86048 | tf_op jit(solution)/shard_map/ppermute | solution.py:338
  65.7 1.2 %collective-permute-start.11 = (bf16[336,128]{1,0:T(8,128)(2,1)S(1)}, bf16[336,128]{1,0:T(8,128)(2,1)S(1)}, u32[]{:S(2)}, u32[]{:S(2)}) collective-permute-start(bf16[336,128]{1,0:T(8,128)(2,1)S(1)} %get-tuple-element.34), channel_id=1, source_target_pairs={{0,14},{1,15},{2,12},{3,13},{4,10},{5,11},{6,8},{7,9},{8,22},{9,23... | collective-permute-start | bytes 258056 | tf_op jit(solution)/shard_map/ppermute | solution.py:338
  66.9 1.4 %collective-permute-start.12 = (bf16[336,128]{1,0:T(8,128)(2,1)S(1)}, bf16[336,128]{1,0:T(8,128)(2,1)S(1)}, u32[]{:S(2)}, u32[]{:S(2)}) collective-permute-start(bf16[336,128]{1,0:T(8,128)(2,1)S(1)} %get-tuple-element.35), channel_id=1, source_target_pairs={{0,13},{1,12},{2,15},{3,14},{4,9},{5,8},{6,11},{7,10},{8,21},{9,20... | collective-permute-start | bytes 258056 | tf_op jit(solution)/shard_map/ppermute | solution.py:338
  68.3 1.6 %collective-permute-start.13 = (bf16[336,128]{1,0:T(8,128)(2,1)S(1)}, bf16[336,128]{1,0:T(8,128)(2,1)S(1)}, u32[]{:S(2)}, u32[]{:S(2)}) collective-permute-start(bf16[336,128]{1,0:T(8,128)(2,1)S(1)} %get-tuple-element.36), channel_id=1, source_target_pairs={{0,12},{1,13},{2,14},{3,15},{4,8},{5,9},{6,10},{7,11},{8,20},{9,21... | collective-permute-start | bytes 258056 | tf_op jit(solution)/shard_map/ppermute | solution.py:338
  69.9 3.4 %collective-permute-done.11.refs_4_ = bf16[336,128]{1,0:T(8,128)(2,1)S(1)} collective-permute-done((bf16[336,128]{1,0:T(8,128)(2,1)S(1)}, bf16[336,128]{1,0:T(8,128)(2,1)S(1)}, u32[]{:S(2)}, u32[]{:S(2)}) %collective-permute-start.11) | collective-permute-done | bytes 86048 | tf_op jit(solution)/shard_map/ppermute | solution.py:338
  73.3 5.5 %collective-permute-done.12.refs_5_ = bf16[336,128]{1,0:T(8,128)(2,1)S(1)} collective-permute-done((bf16[336,128]{1,0:T(8,128)(2,1)S(1)}, bf16[336,128]{1,0:T(8,128)(2,1)S(1)}, u32[]{:S(2)}, u32[]{:S(2)}) %collective-permute-start.12) | collective-permute-done | bytes 86048 | tf_op jit(solution)/shard_map/ppermute | solution.py:338
  78.8 0.9 %collective-permute-done.13.refs_6_ = bf16[336,128]{1,0:T(8,128)(2,1)S(1)} collective-permute-done((bf16[336,128]{1,0:T(8,128)(2,1)S(1)}, bf16[336,128]{1,0:T(8,128)(2,1)S(1)}, u32[]{:S(2)}, u32[]{:S(2)}) %collective-permute-start.13) | collective-permute-done | bytes 86048 | tf_op jit(solution)/shard_map/ppermute | solution.py:338
  79.6 1.3 %merge.1 = bf16[320,1024]{1,0:T(8,128)(2,1)} custom-call(s32[1]{0:T(128)} %bitcast.me_ref, bf16[336,128]{1,0:T(8,128)(2,1)S(1)} %collective-permute-done.7.refs_0_, bf16[336,128]{1,0:T(8,128)(2,1)S(1)} %collective-permute-done.8.refs_1_, bf16[336,128]{1,0:T(8,128)(2,1)S(1)} %collective-permute-done.9.refs_2_, ...), custom_call_target="tpu_custom_call" | custom-call | bytes 1966080 | tf_op jit(solution)/shard_map/merge/pallas_call | solution.py:342
  (26 shorter events, 0.1 us)
Async XLA Ops:
  0.0 35.0 %copy-start.9 = (s32[1,40,3]{1,0,2:T(1,128)S(1)}, s32[1,40,3]{1,0,2:T(1,128)}, u32[]{:S(2)}) copy-start(s32[1,40,3]{1,0,2:T(1,128)} %param.15) | copy-start | bytes 1444
  0.0 42.2 %copy-start.8 = (s32[1,2]{1,0:T(1,128)S(1)}, s32[1,2]{1,0:T(1,128)}, u32[]{:S(2)}) copy-start(s32[1,2]{1,0:T(1,128)} %param.14) | copy-start | bytes 28
  0.7 1.1 %copy-start = (bf16[1,320,1024]{2,1,0:T(8,128)(2,1)S(1)}, bf16[1,320,1024]{2,1,0:T(8,128)(2,1)}, u32[]{:S(2)}) copy-start(bf16[1,320,1024]{2,1,0:T(8,128)(2,1)} %param.8) | copy-start | bytes 1966084
  1.8 1.1 %copy-start.2 = (bf16[1,320,1024]{2,1,0:T(8,128)(2,1)S(1)}, bf16[1,320,1024]{2,1,0:T(8,128)(2,1)}, u32[]{:S(2)}) copy-start(bf16[1,320,1024]{2,1,0:T(8,128)(2,1)} %param.9) | copy-start | bytes 1966084
  2.9 1.1 %copy-start.4 = (bf16[1,320,1024]{2,1,0:T(8,128)(2,1)S(1)}, bf16[1,320,1024]{2,1,0:T(8,128)(2,1)}, u32[]{:S(2)}) copy-start(bf16[1,320,1024]{2,1,0:T(8,128)(2,1)} %param.10) | copy-start | bytes 1966084
  4.0 38.2 %copy-start.6 = (bf16[1,6144,128]{2,1,0:T(8,128)(2,1)S(1)}, bf16[1,6144,128]{2,1,0:T(8,128)(2,1)}, u32[]{:S(2)}) copy-start(bf16[1,6144,128]{2,1,0:T(8,128)(2,1)} %param.11) | copy-start | bytes 4718596
  4.9 42.8 %collective-permute-start.14 = (bf16[2,128,1024]{2,1,0:T(8,128)(2,1)S(1)}, bf16[2,128,1024]{2,1,0:T(8,128)(2,1)S(1)}, u32[]{:S(2)}, u32[]{:S(2)}) collective-permute-start(bf16[2,128,1024]{2,1,0:T(8,128)(2,1)S(1)} %get-tuple-element.37), channel_id=1, source_target_pairs={{0,1},{1,2},{2,3},{3,4},{4,5},{5,6},{6,7},{8,9},{9,10},{10,11},{11... | collective-permute-start | bytes 1572872 | tf_op jit(solution)/shard_map/ppermute | solution.py:276
  9.9 16.7 %collective-permute-start = (bf16[336,128]{1,0:T(8,128)(2,1)S(1)}, bf16[336,128]{1,0:T(8,128)(2,1)S(1)}, u32[]{:S(2)}, u32[]{:S(2)}) collective-permute-start(bf16[336,128]{1,0:T(8,128)(2,1)S(1)} %get-tuple-element.22), channel_id=1, source_target_pairs={{0,1},{1,0},{2,3},{3,2},{4,5},{5,4},{6,7},{7,6},{8,9},{9,8},{10,11... | collective-permute-start | bytes 258056 | tf_op jit(solution)/shard_map/ppermute | solution.py:273
  11.4 18.7 %collective-permute-start.1 = (bf16[336,128]{1,0:T(8,128)(2,1)S(1)}, bf16[336,128]{1,0:T(8,128)(2,1)S(1)}, u32[]{:S(2)}, u32[]{:S(2)}) collective-permute-start(bf16[336,128]{1,0:T(8,128)(2,1)S(1)} %get-tuple-element.23), channel_id=1, source_target_pairs={{0,2},{1,3},{2,0},{3,1},{4,6},{5,7},{6,4},{7,5},{8,10},{9,11},{10,... | collective-permute-start | bytes 258056 | tf_op jit(solution)/shard_map/ppermute | solution.py:273
  13.0 18.5 %collective-permute-start.2 = (bf16[336,128]{1,0:T(8,128)(2,1)S(1)}, bf16[336,128]{1,0:T(8,128)(2,1)S(1)}, u32[]{:S(2)}, u32[]{:S(2)}) collective-permute-start(bf16[336,128]{1,0:T(8,128)(2,1)S(1)} %get-tuple-element.24), channel_id=1, source_target_pairs={{0,3},{1,2},{2,1},{3,0},{4,7},{5,6},{6,5},{7,4},{8,11},{9,10},{10,... | collective-permute-start | bytes 258056 | tf_op jit(solution)/shard_map/ppermute | solution.py:273
  13.4 21.8 %collective-permute-start.3 = (bf16[336,128]{1,0:T(8,128)(2,1)}, bf16[336,128]{1,0:T(8,128)(2,1)S(1)}, u32[]{:S(2)}, u32[]{:S(2)}) collective-permute-start(bf16[336,128]{1,0:T(8,128)(2,1)} %get-tuple-element.25), channel_id=1, source_target_pairs={{0,7},{1,6},{2,5},{3,4},{4,3},{5,2},{6,1},{7,0},{8,15},{9,14},{10,... | collective-permute-start | bytes 258056 | tf_op jit(solution)/shard_map/ppermute | solution.py:273
  26.5 8.7 %collective-permute-start.4 = (bf16[336,128]{1,0:T(8,128)(2,1)}, bf16[336,128]{1,0:T(8,128)(2,1)S(1)}, u32[]{:S(2)}, u32[]{:S(2)}) collective-permute-start(bf16[336,128]{1,0:T(8,128)(2,1)} %get-tuple-element.26), channel_id=1, source_target_pairs={{0,6},{1,7},{2,4},{3,5},{4,2},{5,3},{6,0},{7,1},{8,14},{9,15},{10,... | collective-permute-start | bytes 258056 | tf_op jit(solution)/shard_map/ppermute | solution.py:273
  30.1 11.3 %collective-permute-start.5 = (bf16[336,128]{1,0:T(8,128)(2,1)S(1)}, bf16[336,128]{1,0:T(8,128)(2,1)S(1)}, u32[]{:S(2)}, u32[]{:S(2)}) collective-permute-start(bf16[336,128]{1,0:T(8,128)(2,1)S(1)} %get-tuple-element.27), channel_id=1, source_target_pairs={{0,5},{1,4},{2,7},{3,6},{4,1},{5,0},{6,3},{7,2},{8,13},{9,12},{10,... | collective-permute-start | bytes 258056 | tf_op jit(solution)/shard_map/ppermute | solution.py:273
  31.5 10.7 %collective-permute-start.6 = (bf16[336,128]{1,0:T(8,128)(2,1)S(1)}, bf16[336,128]{1,0:T(8,128)(2,1)S(1)}, u32[]{:S(2)}, u32[]{:S(2)}) collective-permute-start(bf16[336,128]{1,0:T(8,128)(2,1)S(1)} %get-tuple-element.28), channel_id=1, source_target_pairs={{0,4},{1,5},{2,6},{3,7},{4,0},{5,1},{6,2},{7,3},{8,12},{9,13},{10,... | collective-permute-start | bytes 258056 | tf_op jit(solution)/shard_map/ppermute | solution.py:273
  42.2 1.4 %copy-start.7 = (bf16[1,6144,128]{2,1,0:T(8,128)(2,1)S(1)}, bf16[1,6144,128]{2,1,0:T(8,128)(2,1)}, u32[]{:S(2)}) copy-start(bf16[1,6144,128]{2,1,0:T(8,128)(2,1)} %param.12) | copy-start | bytes 4718596
  43.6 4.2 %copy-start.1 = (bf16[1,320,1024]{2,1,0:T(8,128)(2,1)S(1)}, bf16[1,320,1024]{2,1,0:T(8,128)(2,1)}, u32[]{:S(2)}) copy-start(bf16[1,320,1024]{2,1,0:T(8,128)(2,1)} %param.8) | copy-start | bytes 1966084
  43.6 4.2 %copy-start.3 = (bf16[1,320,1024]{2,1,0:T(8,128)(2,1)S(1)}, bf16[1,320,1024]{2,1,0:T(8,128)(2,1)}, u32[]{:S(2)}) copy-start(bf16[1,320,1024]{2,1,0:T(8,128)(2,1)} %param.9) | copy-start | bytes 1966084
  43.6 4.2 %copy-start.5 = (bf16[1,320,1024]{2,1,0:T(8,128)(2,1)S(1)}, bf16[1,320,1024]{2,1,0:T(8,128)(2,1)}, u32[]{:S(2)}) copy-start(bf16[1,320,1024]{2,1,0:T(8,128)(2,1)} %param.10) | copy-start | bytes 1966084
  50.4 29.2 %collective-permute-start.15 = (bf16[336,1152]{1,0:T(8,128)(2,1)S(1)}, bf16[336,1152]{1,0:T(8,128)(2,1)S(1)}, u32[]{:S(2)}, u32[]{:S(2)}) collective-permute-start(bf16[336,1152]{1,0:T(8,128)(2,1)S(1)} %near.1), channel_id=1, source_target_pairs={{0,8},{1,9},{2,10},{3,11},{4,12},{5,13},{6,14},{7,15},{8,16},{9,17... | collective-permute-start | bytes 2322440 | tf_op jit(solution)/shard_map/ppermute | solution.py:338
  50.5 15.2 %collective-permute-start.7 = (bf16[336,128]{1,0:T(8,128)(2,1)S(1)}, bf16[336,128]{1,0:T(8,128)(2,1)S(1)}, u32[]{:S(2)}, u32[]{:S(2)}) collective-permute-start(bf16[336,128]{1,0:T(8,128)(2,1)S(1)} %get-tuple-element.30), channel_id=1, source_target_pairs={{0,9},{1,8},{2,11},{3,10},{4,13},{5,12},{6,15},{7,14},{8,17},{9,16... | collective-permute-start | bytes 258056 | tf_op jit(solution)/shard_map/ppermute | solution.py:338
  52.5 14.4 %collective-permute-start.8 = (bf16[336,128]{1,0:T(8,128)(2,1)S(1)}, bf16[336,128]{1,0:T(8,128)(2,1)S(1)}, u32[]{:S(2)}, u32[]{:S(2)}) collective-permute-start(bf16[336,128]{1,0:T(8,128)(2,1)S(1)} %get-tuple-element.31), channel_id=1, source_target_pairs={{0,10},{1,11},{2,8},{3,9},{4,14},{5,15},{6,12},{7,13},{8,18},{9,19... | collective-permute-start | bytes 258056 | tf_op jit(solution)/shard_map/ppermute | solution.py:338
  52.5 15.8 %collective-permute-start.9 = (bf16[336,128]{1,0:T(8,128)(2,1)S(1)}, bf16[336,128]{1,0:T(8,128)(2,1)S(1)}, u32[]{:S(2)}, u32[]{:S(2)}) collective-permute-start(bf16[336,128]{1,0:T(8,128)(2,1)S(1)} %get-tuple-element.32), channel_id=1, source_target_pairs={{0,11},{1,10},{2,9},{3,8},{4,15},{5,14},{6,13},{7,12},{8,19},{9,18... | collective-permute-start | bytes 258056 | tf_op jit(solution)/shard_map/ppermute | solution.py:338
  54.8 15.1 %collective-permute-start.10 = (bf16[336,128]{1,0:T(8,128)(2,1)S(1)}, bf16[336,128]{1,0:T(8,128)(2,1)S(1)}, u32[]{:S(2)}, u32[]{:S(2)}) collective-permute-start(bf16[336,128]{1,0:T(8,128)(2,1)S(1)} %get-tuple-element.33), channel_id=1, source_target_pairs={{0,15},{1,14},{2,13},{3,12},{4,11},{5,10},{6,9},{7,8},{8,23},{9,22... | collective-permute-start | bytes 258056 | tf_op jit(solution)/shard_map/ppermute | solution.py:338
  65.7 7.6 %collective-permute-start.11 = (bf16[336,128]{1,0:T(8,128)(2,1)S(1)}, bf16[336,128]{1,0:T(8,128)(2,1)S(1)}, u32[]{:S(2)}, u32[]{:S(2)}) collective-permute-start(bf16[336,128]{1,0:T(8,128)(2,1)S(1)} %get-tuple-element.34), channel_id=1, source_target_pairs={{0,14},{1,15},{2,12},{3,13},{4,10},{5,11},{6,8},{7,9},{8,22},{9,23... | collective-permute-start | bytes 258056 | tf_op jit(solution)/shard_map/ppermute | solution.py:338
  66.9 11.9 %collective-permute-start.12 = (bf16[336,128]{1,0:T(8,128)(2,1)S(1)}, bf16[336,128]{1,0:T(8,128)(2,1)S(1)}, u32[]{:S(2)}, u32[]{:S(2)}) collective-permute-start(bf16[336,128]{1,0:T(8,128)(2,1)S(1)} %get-tuple-element.35), channel_id=1, source_target_pairs={{0,13},{1,12},{2,15},{3,14},{4,9},{5,8},{6,11},{7,10},{8,21},{9,20... | collective-permute-start | bytes 258056 | tf_op jit(solution)/shard_map/ppermute | solution.py:338
  68.3 11.3 %collective-permute-start.13 = (bf16[336,128]{1,0:T(8,128)(2,1)S(1)}, bf16[336,128]{1,0:T(8,128)(2,1)S(1)}, u32[]{:S(2)}, u32[]{:S(2)}) collective-permute-start(bf16[336,128]{1,0:T(8,128)(2,1)S(1)} %get-tuple-element.36), channel_id=1, source_target_pairs={{0,12},{1,13},{2,14},{3,15},{4,8},{5,9},{6,10},{7,11},{8,20},{9,21... | collective-permute-start | bytes 258056 | tf_op jit(solution)/shard_map/ppermute | solution.py:338

commit v5 on v3

--- a/solution.py
+++ b/solution.py
@@ -20,12 +20,19 @@
 VMEM_BASE = 12 * 1024 * 1024
 
 whole_vmem = pl.BlockSpec(memory_space=pltpu.VMEM)
-anywhere = pl.BlockSpec(memory_space=pl.ANY)
+in_hbm = pl.BlockSpec(memory_space=pltpu.HBM)
 whole_smem = pl.BlockSpec(memory_space=pltpu.SMEM)
 
 
-def partner(me, step):
-    return jnp.bitwise_xor(me, step)
+def peers_of(there, by):
+    count = lax.axis_size("section")
+    other = lax.rem(lax.axis_index("section") + (by + count), count)
+    odd = lax.rem(other, 2) == 1
+    me = lax.axis_index("seq")
+    return [
+        jnp.bitwise_xor(me, jnp.where(odd, odd_step, even_step))
+        for even_step, odd_step in zip(*there)
+    ]
 
 
 def scores_of(query, keys):
@@ -82,19 +89,13 @@
     return -(-rows // LANES)
 
 
-def split_kernel(
-    steps, me_ref, span_ref, query_ref, key_ref, value_ref, *refs
-):
-    halo_ref, out_refs, arrived = refs[0], refs[1:-1], refs[-1]
-    me = me_ref[0]
+def split_kernel(there, span_ref, query_ref, *refs):
+    out_refs, arrived = refs[:-1], refs[-1]
     rows = query_ref.shape[0]
-    halo = halo_ref.shape[1]
     copies = []
-    for step, out_ref in zip(steps, out_refs):
-        head = pl.multiple_of(partner(me, step) * HD, HD)
+    for peer, out_ref in zip(peers_of(there, 0), out_refs):
+        head = pl.multiple_of(peer * HD, HD)
         copies.append((query_ref.at[:, pl.ds(head, HD)], out_ref.at[:rows]))
-    copies.append((key_ref.at[rows - halo :], halo_ref.at[0]))
-    copies.append((value_ref.at[rows - halo :], halo_ref.at[1]))
     copies = [
         pltpu.make_async_copy(source, target, arrived.at[index])
         for index, (source, target) in enumerate(copies)
@@ -108,13 +109,33 @@
         copy.wait()
 
 
+def fetch_kernel(key_ref, value_ref, old_key_ref, old_value_ref, *refs):
+    halo_ref, held_key_ref, held_value_ref, arrived = refs
+    halo = halo_ref.shape[1]
+    rows = key_ref.shape[0]
+    copies = [
+        (key_ref.at[rows - halo :], halo_ref.at[0]),
+        (value_ref.at[rows - halo :], halo_ref.at[1]),
+        (old_key_ref, held_key_ref),
+        (old_value_ref, held_value_ref),
+    ]
+    copies = [
+        pltpu.make_async_copy(source, target, arrived.at[index])
+        for index, (source, target) in enumerate(copies)
+    ]
+    for copy in copies:
+        copy.start()
+    for copy in copies:
+        copy.wait()
+
+
 def far_kernel(
-    steps, me_ref, span_ref, global_ref, random_ref, key_ref, value_ref, *refs
+    there, span_ref, global_ref, random_ref, key_ref, value_ref, *refs
 ):
-    me = me_ref[0]
+    peers = peers_of(there, 0)
+    count = len(peers)
+    query_refs, out_refs = refs[:count], refs[count:]
     span = span_ref[0]
-    count = len(steps)
-    query_refs, out_refs = refs[:count], refs[count:]
     last = key_ref.shape[0] // BLK - 1
 
     def block(ref, at):
@@ -124,30 +145,31 @@
 
     glob_keys = [block(key_ref, global_ref[g]) for g in range(GLOB)]
     glob_values = [block(value_ref, global_ref[g]) for g in range(GLOB)]
-    for index, step in enumerate(steps):
-        chunk = partner(me, step)
+    for index, chunk in enumerate(peers):
         query_ref, out_ref = query_refs[index], out_refs[index]
         rows = query_ref.shape[0] - STAT_ROWS
         blocks = rows // BLK
         first = chunk == 0
-        all_scores, all_values = [], []
+        all_scores, all_picks = [], []
         for b in range(blocks):
             query = query_ref[b * BLK : (b + 1) * BLK, :]
             base = (chunk * blocks + b) * RAND
             picks = [random_ref[base + r] for r in range(RAND)]
             keys = glob_keys + [block(key_ref, pick) for pick in picks]
-            values = glob_values + [block(value_ref, pick) for pick in picks]
             known = len(keys) * BLK
             spare = [last + 1 + b - w for w in range(b + 1, WMAX)]
             keys = keys + [block(key_ref, at) for at in spare]
-            values = values + [block(value_ref, at) for at in spare]
             scores = scores_of(query, jnp.concatenate(keys, axis=0))
             if spare:
                 open_slots = jnp.where(first, jnp.clip(span - (b + 1), 0, len(spare)), 0)
                 lane_at = lax.broadcasted_iota(jnp.int32, scores.shape, 1)
                 scores = jnp.where(lane_at < known + open_slots * BLK, scores, MASKED)
             all_scores.append(scores)
-            all_values.append(jnp.concatenate(values, axis=0))
+            all_picks.append(picks + spare)
+        all_values = [
+            jnp.concatenate(glob_values + [block(value_ref, at) for at in picks], axis=0)
+            for picks in all_picks
+        ]
         parts, lses = softmax_parts(all_scores, all_values)
         stats = []
         for b in range(blocks):
@@ -163,17 +185,17 @@
 
 
 def near_kernel(
-    steps, me_ref, query_ref, key_ref, value_ref, halo_ref, own_ref, *refs
+    there, query_ref, key_ref, value_ref, halo_ref, own_ref, *refs
 ):
     came_refs, out_ref = refs[:-1], refs[-1]
-    me = me_ref[0]
+    me = lax.axis_index("seq")
     rows, wide = query_ref.shape
     halo = (WMAX - 1) * BLK
     starts = list(range(0, rows, 2 * BLK))
     sizes = [min(2 * BLK, rows - start) for start in starts]
     out_ref[:, wide:] = own_ref[...]
-    for step, came_ref in zip(steps, came_refs):
-        lanes = pl.ds(pl.multiple_of(partner(me, step) * HD, HD), HD)
+    for peer, came_ref in zip(peers_of(there, 0), came_refs):
+        lanes = pl.ds(pl.multiple_of(peer * HD, HD), HD)
         width = came_ref[rows:, :].astype(jnp.float32)[:1]
         width = jnp.concatenate([width] * ((2 * BLK + halo) // LANES), axis=1)
         all_scores, all_values = [], []
@@ -203,21 +225,21 @@
         out_ref[rows:, lanes] = tile
 
 
-def merge_kernel(steps, me_ref, *refs):
-    me = me_ref[0]
+def merge_kernel(there, *refs):
     far_refs, out_ref = refs[:-1], refs[-1]
-    near_ref = far_refs[steps.index(0)]
+    own = len(far_refs) - 1
+    near_ref = far_refs[own]
     rows, wide = out_ref.shape
     count = stat_count(rows)
-    for step, far_ref in zip(steps, far_refs):
-        part = slice(wide, None) if step == 0 else slice(None)
-        lanes = pl.ds(pl.multiple_of(partner(me, step) * HD, HD), HD)
+    for index, (peer, far_ref) in enumerate(zip(peers_of(there, -1), far_refs)):
+        part = slice(wide, None) if index == own else slice(None)
+        lanes = pl.ds(pl.multiple_of(peer * HD, HD), HD)
         far_stats = stat_rows_of(far_ref[rows:, part], count)
         near_stats = stat_rows_of(near_ref[rows:, lanes], count)
-        for index in range(count):
-            start = index * LANES
+        for group in range(count):
+            start = group * LANES
             size = min(LANES, rows - start)
-            share = 1.0 / (1.0 + jnp.exp2(near_stats[index] - far_stats[index]))
+            share = 1.0 / (1.0 + jnp.exp2(near_stats[group] - far_stats[group]))
             row_at = lax.broadcasted_iota(jnp.int32, (size, LANES), 0)
             lane_at = lax.broadcasted_iota(jnp.int32, (size, LANES), 1)
             column = jnp.sum(
@@ -243,100 +265,112 @@
     halo = (WMAX - 1) * BLK
     heads = wide // HD
     bf16 = jnp.bfloat16
-    me = lax.axis_index("seq").astype(jnp.int32)[None]
     half = max(seq_count // 2, 1)
-    order = list(range(seq_count - 1, half - 1, -1)) + list(range(half))
-
-    parts = pl.pallas_call(
-        functools.partial(split_kernel, order),
-        out_shape=[jax.ShapeDtypeStruct((2, halo, wide), bf16)]
-        + [jax.ShapeDtypeStruct((rows + STAT_ROWS, HD), bf16)] * seq_count,
-        in_specs=[whole_smem] * 2 + [anywhere] * 3,
-        out_specs=[whole_vmem] * (1 + seq_count),
-        scratch_shapes=[pltpu.SemaphoreType.DMA((seq_count + 2,))],
+    inner, outer = list(range(1, half)), list(range(seq_count - 1, half - 1, -1))
+    there = [outer + inner + [0], inner + outer + [0]]
+
+    sent = pl.pallas_call(
+        functools.partial(split_kernel, there),
+        out_shape=[jax.ShapeDtypeStruct((rows + STAT_ROWS, HD), bf16)] * seq_count,
+        in_specs=[whole_smem, in_hbm],
+        out_specs=[whole_vmem] * seq_count,
+        scratch_shapes=[pltpu.SemaphoreType.DMA((seq_count,))],
         compiler_params=params(queries),
         cost_estimate=pl.CostEstimate(flops=0, bytes_accessed=5 * rows * wide, transcendentals=0),
         name="split",
-    )(me, window[0], queries[0], keys_new[0], values_new[0])
-    mine, sent = parts[0], dict(zip(order, parts[1:]))
-
-    def swapped(shard, step):
-        if step == 0:
-            return shard
-        return lax.ppermute(shard, "seq", [(i, i ^ step) for i in range(seq_count)])
-
-    came = {step: swapped(sent[step], step) for step in order}
+    )(window[0], queries[0])
+
+    def linked(shard, by, steps):
+        pairs = [
+            (
+                s * seq_count + t,
+                (s + by) % section_count * seq_count + (t ^ steps[s % 2]),
+            )
+            for s in range(section_count)
+            for t in range(seq_count)
+        ]
+        return lax.ppermute(shard, ("section", "seq"), pairs)
+
+    came = [linked(shard, 0, steps) for shard, steps in zip(sent[:-1], zip(*there))]
+    came.append(sent[-1])
+    mine, held_keys, held_values = pl.pallas_call(
+        fetch_kernel,
+        out_shape=[
+            jax.ShapeDtypeStruct((2, halo, wide), bf16),
+            jax.ShapeDtypeStruct(keys_cache.shape[1:], bf16),
+            jax.ShapeDtypeStruct(values_cache.shape[1:], bf16),
+        ],
+        in_specs=[in_hbm] * 4,
+        out_specs=[whole_vmem] * 3,
+        scratch_shapes=[pltpu.SemaphoreType.DMA((4,))],
+        compiler_params=params(queries),
+        cost_estimate=pl.CostEstimate(
+            flops=0, bytes_accessed=8 * keys_cache.shape[1] * HD, transcendentals=0
+        ),
+        name="fetch",
+    )(keys_new[0], values_new[0], keys_cache[0], values_cache[0])
     before = lax.ppermute(mine, "seq", [(i, i + 1) for i in range(seq_count - 1)])
 
     picks = random_blocks[0].reshape(-1)
 
-    def far_call(steps):
-        count = len(steps)
+    def far_call():
+        count = seq_count
         out_rows = rows + STAT_ROWS
         return pl.pallas_call(
-            functools.partial(far_kernel, steps),
+            functools.partial(far_kernel, there),
             out_shape=[jax.ShapeDtypeStruct((out_rows, HD), bf16)] * count,
-            in_specs=[whole_smem] * 4 + [whole_vmem] * (2 + count),
+            in_specs=[whole_smem] * 3 + [whole_vmem] * (2 + count),
             out_specs=[whole_vmem] * count,
             compiler_params=params(queries),
             cost_estimate=pl.CostEstimate(
-                flops=count * rows * 320 * HD * 4,
+                flops=40 * count * rows * 320 * HD * 4,
                 bytes_accessed=2 * 2 * keys_cache.shape[1] * HD + 4 * count * rows * HD,
                 transcendentals=count * rows * 320,
             ),
             name="far",
         )(
-            me,
             window[0],
             global_blocks[0],
             picks,
-            keys_cache[0],
-            values_cache[0],
-            *[came[step] for step in steps],
+            held_keys,
+            held_values,
+            *came,
         )
 
-    far = dict(zip(order, far_call(order)))
-    far[0] = pl.pallas_call(
-        functools.partial(near_kernel, order),
+    far = far_call()
+    both = pl.pallas_call(
+        functools.partial(near_kernel, there),
         out_shape=jax.ShapeDtypeStruct((rows + STAT_ROWS, wide + HD), bf16),
-        in_specs=[whole_smem] + [whole_vmem] * (5 + seq_count),
+        in_specs=[whole_vmem] * (5 + seq_count),
         out_specs=whole_vmem,
         compiler_params=params(queries),
         cost_estimate=pl.CostEstimate(
-            flops=heads * rows * 256 * HD * 4,
+            flops=40 * heads * rows * 256 * HD * 4,
             bytes_accessed=9 * rows * wide,
             transcendentals=heads * rows * 256,
         ),
         name="near",
     )(
-        me,
         queries[0],
         keys_new[0],
         values_new[0],
         before,
-        far[0],
-        *[came[step] for step in order],
+        far[-1],
+        *came,
     )
 
-    def onward(shard, step):
-        pairs = [
-            (s * seq_count + t, ((s + 1) % section_count) * seq_count + (t ^ step))
-            for s in range(section_count)
-            for t in range(seq_count)
-        ]
-        return lax.ppermute(shard, ("section", "seq"), pairs)
-
-    handed = {step: onward(far[step], step) for step in order}
+    returned = [*far[:-1], both]
+    handed = [linked(shard, 1, steps) for shard, steps in zip(returned, zip(*there))]
 
     merged = pl.pallas_call(
-        functools.partial(merge_kernel, order),
+        functools.partial(merge_kernel, there),
         out_shape=jax.ShapeDtypeStruct((rows, wide), bf16),
-        in_specs=[whole_smem] + [whole_vmem] * seq_count,
+        in_specs=[whole_vmem] * seq_count,
         out_specs=whole_vmem,
         compiler_params=params(queries),
         cost_estimate=pl.CostEstimate(flops=0, bytes_accessed=6 * rows * wide, transcendentals=0),
         name="merge",
-    )(me, *[handed[step] for step in order])
+    )(*handed)
     return merged[None]
 
 

time: 75.5 us -> 66.4 us (0.88)
  the two profiles are of different devices: /device:TPU:0 before, /device:TPU:1 now
where the time goes in v5:
time: 66.4 us; the launch traced here: 66.1 us
  starting transfers between devices  39.6 us (60%)
  waiting for transfers between devices  10.2 us (15%)
  Pallas kernels  8.54 us (13%)
  local copies, waits for them, and re-layouts  6.96 us (10%)
  between operations  0.76 us (1%)
    ppermute x15, starting transfers between devices, linked(): return lax.ppermute(shard, ('section', 'seq'), pairs)  36.5 us
    ppermute x15, waiting for transfers between devices, linked(): return lax.ppermute(shard, ('section', 'seq'), pairs)  9.64 us
    unnamed x19, local copies, waits for them, and re-layouts  6.85 us
    pallas_call x1, Pallas kernels, far_call(): pl.pallas_call(functools.partial(far_kernel, there), out_shape=[jax.Shape...  4.09 us
    ppermute x1, starting transfers between devices, per_device(): lax.ppermute(mine, 'seq', [(i, i + 1) for i in range(seq_count - 1)])  3.12 us
    pallas_call x1, Pallas kernels, per_device(): pl.pallas_call(functools.partial(near_kernel, there), out_shape=jax.Shape...  2.57 us
  transfers between devices with their start and end apart: 16, of which 6 were waited for; matrix products, arithmetic and copies ran while one was open for 1% of the time, Pallas kernels for 7%

profile of v5, /device:TPU:1, one launch (start us, length us, event | category | flops | bytes accessed | tf_op | source)
XLA Modules:
  0.0 66.1 jit_solution(10175956632380534503)
XLA Ops:
  0.7 0.0 copy-start.6
  0.7 1.1 %copy-done.6 = bf16[1,320,1024]{2,1,0:T(8,128)(2,1)S(1)} copy-done((bf16[1,320,1024]{2,1,0:T(8,128)(2,1)S(1)}, bf16[1,320,1024]{2,1,0:T(8,128)(2,1)}, u32[]{:S(2)}) %copy-start.6) | copy-done | bytes 655384
  1.7 0.3 split.1
  2.0 2.1 %collective-permute-start = (bf16[336,128]{1,0:T(8,128)(2,1)S(1)}, bf16[336,128]{1,0:T(8,128)(2,1)S(1)}, u32[]{:S(2)}, u32[]{:S(2)}) collective-permute-start(bf16[336,128]{1,0:T(8,128)(2,1)S(1)} %get-tuple-element.26), channel_id=1, source_target_pairs={{0,7},{1,6},{2,5},{3,4},{4,3},{5,2},{6,1},{7,0},{8,9},{9,8},{10,11... | collective-permute-start | bytes 258056 | tf_op jit(solution)/shard_map/ppermute | solution.py:292
  4.2 1.3 %collective-permute-start.1 = (bf16[336,128]{1,0:T(8,128)(2,1)S(1)}, bf16[336,128]{1,0:T(8,128)(2,1)S(1)}, u32[]{:S(2)}, u32[]{:S(2)}) collective-permute-start(bf16[336,128]{1,0:T(8,128)(2,1)S(1)} %get-tuple-element.27), channel_id=1, source_target_pairs={{0,6},{1,7},{2,4},{3,5},{4,2},{5,3},{6,0},{7,1},{8,10},{9,11},{10,... | collective-permute-start | bytes 258056 | tf_op jit(solution)/shard_map/ppermute | solution.py:292
  5.5 4.4 %collective-permute-start.3 = (bf16[336,128]{1,0:T(8,128)(2,1)S(1)}, bf16[336,128]{1,0:T(8,128)(2,1)S(1)}, u32[]{:S(2)}, u32[]{:S(2)}) collective-permute-start(bf16[336,128]{1,0:T(8,128)(2,1)S(1)} %get-tuple-element.29), channel_id=1, source_target_pairs={{0,4},{1,5},{2,6},{3,7},{4,0},{5,1},{6,2},{7,3},{8,15},{9,14},{10,... | collective-permute-start | bytes 258056 | tf_op jit(solution)/shard_map/ppermute | solution.py:292
  9.8 0.4 collective-permute-start.5
  10.2 2.0 %collective-permute-start.6 = (bf16[336,128]{1,0:T(8,128)(2,1)S(1)}, bf16[336,128]{1,0:T(8,128)(2,1)S(1)}, u32[]{:S(2)}, u32[]{:S(2)}) collective-permute-start(bf16[336,128]{1,0:T(8,128)(2,1)S(1)} %get-tuple-element.32), channel_id=1, source_target_pairs={{0,3},{1,2},{2,1},{3,0},{4,7},{5,6},{6,5},{7,4},{8,12},{9,13},{10,... | collective-permute-start | bytes 258056 | tf_op jit(solution)/shard_map/ppermute | solution.py:292
  12.2 0.8 %copy.10 = s32[1,40,3]{2,1,0:T(8,128)S(1)} copy(s32[1,40,3]{1,0,2:T(1,128)} %param.15) | data formatting | bytes 960 | tf_op args[7]
  13.0 0.1 reshape_squeeze.3.random_ref
  13.1 0.0 copy-start
  13.1 1.4 %copy-done = bf16[1,6144,128]{2,1,0:T(8,128)(2,1)S(1)} copy-done((bf16[1,6144,128]{2,1,0:T(8,128)(2,1)S(1)}, bf16[1,6144,128]{2,1,0:T(8,128)(2,1)}, u32[]{:S(2)}) %copy-start) | copy-done | bytes 1572888
  14.5 1.4 %copy-done.1 = bf16[1,6144,128]{2,1,0:T(8,128)(2,1)S(1)} copy-done((bf16[1,6144,128]{2,1,0:T(8,128)(2,1)S(1)}, bf16[1,6144,128]{2,1,0:T(8,128)(2,1)}, u32[]{:S(2)}) %copy-start.1) | copy-done | bytes 1572888
  15.9 1.1 %copy-done.2 = bf16[1,320,1024]{2,1,0:T(8,128)(2,1)S(1)} copy-done((bf16[1,320,1024]{2,1,0:T(8,128)(2,1)S(1)}, bf16[1,320,1024]{2,1,0:T(8,128)(2,1)}, u32[]{:S(2)}) %copy-start.2) | copy-done | bytes 655384
  17.0 1.1 %copy-done.4 = bf16[1,320,1024]{2,1,0:T(8,128)(2,1)S(1)} copy-done((bf16[1,320,1024]{2,1,0:T(8,128)(2,1)S(1)}, bf16[1,320,1024]{2,1,0:T(8,128)(2,1)}, u32[]{:S(2)}) %copy-start.4) | copy-done | bytes 655384
  18.1 0.3 fetch.1
  18.4 3.1 %collective-permute-start.14 = (bf16[2,128,1024]{2,1,0:T(8,128)(2,1)S(1)}, bf16[2,128,1024]{2,1,0:T(8,128)(2,1)S(1)}, u32[]{:S(2)}, u32[]{:S(2)}) collective-permute-start(bf16[2,128,1024]{2,1,0:T(8,128)(2,1)S(1)} %get-tuple-element.41), channel_id=1, source_target_pairs={{0,1},{1,2},{2,3},{3,4},{4,5},{5,6},{6,7},{8,9},{9,10},{10,11},{11... | collective-permute-start | bytes 1572872 | tf_op jit(solution)/shard_map/ppermute | solution.py:312
  21.5 0.8 %collective-permute-done.5.refs_5_ = bf16[336,128]{1,0:T(8,128)(2,1)S(1)} collective-permute-done((bf16[336,128]{1,0:T(8,128)(2,1)S(1)}, bf16[336,128]{1,0:T(8,128)(2,1)S(1)}, u32[]{:S(2)}, u32[]{:S(2)}) %collective-permute-start.5) | collective-permute-done | bytes 86048 | tf_op jit(solution)/shard_map/ppermute | solution.py:292
  22.4 1.3 %collective-permute-done.6.refs_6_ = bf16[336,128]{1,0:T(8,128)(2,1)S(1)} collective-permute-done((bf16[336,128]{1,0:T(8,128)(2,1)S(1)}, bf16[336,128]{1,0:T(8,128)(2,1)S(1)}, u32[]{:S(2)}, u32[]{:S(2)}) %collective-permute-start.6) | collective-permute-done | bytes 86048 | tf_op jit(solution)/shard_map/ppermute | solution.py:292
  23.7 4.1 %far.1 = (bf16[336,128]{1,0:T(8,128)(2,1)S(1)}, bf16[336,128]{1,0:T(8,128)(2,1)S(1)}, bf16[336,128]{1,0:T(8,128)(2,1)S(1)}, bf16[336,128]{1,0:T(8,128)(2,1)S(1)}...) custom-call(s32[1]{0:T(128)} %bitcast.9.span_ref, ...), custom_call_target="tpu_custom_call" | custom-call | flops 16777216000 | bytes 4456448 | tf_op jit(solution)/shard_map/far/pallas_call | solution.py:319
  27.8 0.6 collective-permute-done.14.halo_ref
  28.4 2.6 %near.1 = bf16[336,1152]{1,0:T(8,128)(2,1)S(1)} custom-call(bf16[320,1024]{1,0:T(8,128)(2,1)S(1)} %bitcast.17, bf16[320,1024]{1,0:T(8,128)(2,1)S(1)} %bitcast.13, bf16[320,1024]{1,0:T(8,128)(2,1)S(1)} %bitcast.15, bf16[2,128,1024]{2,1,0:T(8,128)(2,1)S(1)} %collective-permute-done.14.halo_ref, bf16[336,128]{1,0:T(8,128)(2,1)S(1)} %get-tuple-element.42.own_ref, ...), custom_call_target="tpu_custom_call" | custom-call | flops 13421772800 | bytes 2949120 | tf_op jit(solution)/shard_map/near/pallas_call | solution.py:341
  31.0 8.7 %collective-permute-start.15 = (bf16[336,1152]{1,0:T(8,128)(2,1)S(1)}, bf16[336,1152]{1,0:T(8,128)(2,1)S(1)}, u32[]{:S(2)}, u32[]{:S(2)}) collective-permute-start(bf16[336,1152]{1,0:T(8,128)(2,1)S(1)} %near.1), channel_id=1, source_target_pairs={{0,8},{1,9},{2,10},{3,11},{4,12},{5,13},{6,14},{7,15},{8,16},{9,17... | collective-permute-start | bytes 2322440 | tf_op jit(solution)/shard_map/ppermute | solution.py:292
  39.6 2.0 %collective-permute-start.7 = (bf16[336,128]{1,0:T(8,128)(2,1)S(1)}, bf16[336,128]{1,0:T(8,128)(2,1)S(1)}, u32[]{:S(2)}, u32[]{:S(2)}) collective-permute-start(bf16[336,128]{1,0:T(8,128)(2,1)S(1)} %get-tuple-element.34), channel_id=1, source_target_pairs={{0,15},{1,14},{2,13},{3,12},{4,11},{5,10},{6,9},{7,8},{8,17},{9,16... | collective-permute-start | bytes 258056 | tf_op jit(solution)/shard_map/ppermute | solution.py:292
  41.6 0.3 collective-permute-start.9
  41.9 6.5 %collective-permute-start.10 = (bf16[336,128]{1,0:T(8,128)(2,1)S(1)}, bf16[336,128]{1,0:T(8,128)(2,1)S(1)}, u32[]{:S(2)}, u32[]{:S(2)}) collective-permute-start(bf16[336,128]{1,0:T(8,128)(2,1)S(1)} %get-tuple-element.37), channel_id=1, source_target_pairs={{0,12},{1,13},{2,14},{3,15},{4,8},{5,9},{6,10},{7,11},{8,23},{9,22... | collective-permute-start | bytes 258056 | tf_op jit(solution)/shard_map/ppermute | solution.py:292
  48.5 2.8 %collective-permute-done.7.refs_0_ = bf16[336,128]{1,0:T(8,128)(2,1)S(1)} collective-permute-done((bf16[336,128]{1,0:T(8,128)(2,1)S(1)}, bf16[336,128]{1,0:T(8,128)(2,1)S(1)}, u32[]{:S(2)}, u32[]{:S(2)}) %collective-permute-start.7) | collective-permute-done | bytes 86048 | tf_op jit(solution)/shard_map/ppermute | solution.py:292
  51.2 6.0 %collective-permute-start.11 = (bf16[336,128]{1,0:T(8,128)(2,1)S(1)}, bf16[336,128]{1,0:T(8,128)(2,1)S(1)}, u32[]{:S(2)}, u32[]{:S(2)}) collective-permute-start(bf16[336,128]{1,0:T(8,128)(2,1)S(1)} %get-tuple-element.38), channel_id=1, source_target_pairs={{0,9},{1,8},{2,11},{3,10},{4,13},{5,12},{6,15},{7,14},{8,22},{9,23... | collective-permute-start | bytes 258056 | tf_op jit(solution)/shard_map/ppermute | solution.py:292
  57.2 2.8 %collective-permute-start.13 = (bf16[336,128]{1,0:T(8,128)(2,1)S(1)}, bf16[336,128]{1,0:T(8,128)(2,1)S(1)}, u32[]{:S(2)}, u32[]{:S(2)}) collective-permute-start(bf16[336,128]{1,0:T(8,128)(2,1)S(1)} %get-tuple-element.40), channel_id=1, source_target_pairs={{0,11},{1,10},{2,9},{3,8},{4,15},{5,14},{6,13},{7,12},{8,20},{9,21... | collective-permute-start | bytes 258056 | tf_op jit(solution)/shard_map/ppermute | solution.py:292
  60.1 2.6 %collective-permute-done.12.refs_5_ = bf16[336,128]{1,0:T(8,128)(2,1)S(1)} collective-permute-done((bf16[336,128]{1,0:T(8,128)(2,1)S(1)}, bf16[336,128]{1,0:T(8,128)(2,1)S(1)}, u32[]{:S(2)}, u32[]{:S(2)}) %collective-permute-start.12) | collective-permute-done | bytes 86048 | tf_op jit(solution)/shard_map/ppermute | solution.py:292
  62.7 2.1 %collective-permute-done.13.refs_6_ = bf16[336,128]{1,0:T(8,128)(2,1)S(1)} collective-permute-done((bf16[336,128]{1,0:T(8,128)(2,1)S(1)}, bf16[336,128]{1,0:T(8,128)(2,1)S(1)}, u32[]{:S(2)}, u32[]{:S(2)}) %collective-permute-start.13) | collective-permute-done | bytes 86048 | tf_op jit(solution)/shard_map/ppermute | solution.py:292
  64.8 1.3 %merge.1 = bf16[320,1024]{1,0:T(8,128)(2,1)} custom-call(bf16[336,128]{1,0:T(8,128)(2,1)S(1)} %collective-permute-done.7.refs_0_, bf16[336,128]{1,0:T(8,128)(2,1)S(1)} %collective-permute-done.8.refs_1_, bf16[336,128]{1,0:T(8,128)(2,1)S(1)} %collective-permute-done.9.refs_2_, bf16[336,128]{1,0:T(8,128)(2,1)S(1)} %collective-permute-done.10.refs_3_, ...), custom_call_target="tpu_custom_call" | custom-call | bytes 1966080 | tf_op jit(solution)/shard_map/merge/pallas_call | solution.py:365
  (25 shorter events, 0.1 us)
Async XLA Ops:
  0.7 1.1 %copy-start.6 = (bf16[1,320,1024]{2,1,0:T(8,128)(2,1)S(1)}, bf16[1,320,1024]{2,1,0:T(8,128)(2,1)}, u32[]{:S(2)}) copy-start(bf16[1,320,1024]{2,1,0:T(8,128)(2,1)} %param.8) | copy-start | bytes 1966084
  2.0 7.8 %collective-permute-start = (bf16[336,128]{1,0:T(8,128)(2,1)S(1)}, bf16[336,128]{1,0:T(8,128)(2,1)S(1)}, u32[]{:S(2)}, u32[]{:S(2)}) collective-permute-start(bf16[336,128]{1,0:T(8,128)(2,1)S(1)} %get-tuple-element.26), channel_id=1, source_target_pairs={{0,7},{1,6},{2,5},{3,4},{4,3},{5,2},{6,1},{7,0},{8,9},{9,8},{10,11... | collective-permute-start | bytes 258056 | tf_op jit(solution)/shard_map/ppermute | solution.py:292
  4.2 6.1 %collective-permute-start.1 = (bf16[336,128]{1,0:T(8,128)(2,1)S(1)}, bf16[336,128]{1,0:T(8,128)(2,1)S(1)}, u32[]{:S(2)}, u32[]{:S(2)}) collective-permute-start(bf16[336,128]{1,0:T(8,128)(2,1)S(1)} %get-tuple-element.27), channel_id=1, source_target_pairs={{0,6},{1,7},{2,4},{3,5},{4,2},{5,3},{6,0},{7,1},{8,10},{9,11},{10,... | collective-permute-start | bytes 258056 | tf_op jit(solution)/shard_map/ppermute | solution.py:292
  5.5 12.9 %collective-permute-start.2 = (bf16[336,128]{1,0:T(8,128)(2,1)S(1)}, bf16[336,128]{1,0:T(8,128)(2,1)S(1)}, u32[]{:S(2)}, u32[]{:S(2)}) collective-permute-start(bf16[336,128]{1,0:T(8,128)(2,1)S(1)} %get-tuple-element.28), channel_id=1, source_target_pairs={{0,5},{1,4},{2,7},{3,6},{4,1},{5,0},{6,3},{7,2},{8,11},{9,10},{10,... | collective-permute-start | bytes 258056 | tf_op jit(solution)/shard_map/ppermute | solution.py:292
  5.5 16.1 %collective-permute-start.3 = (bf16[336,128]{1,0:T(8,128)(2,1)S(1)}, bf16[336,128]{1,0:T(8,128)(2,1)S(1)}, u32[]{:S(2)}, u32[]{:S(2)}) collective-permute-start(bf16[336,128]{1,0:T(8,128)(2,1)S(1)} %get-tuple-element.29), channel_id=1, source_target_pairs={{0,4},{1,5},{2,6},{3,7},{4,0},{5,1},{6,2},{7,3},{8,15},{9,14},{10,... | collective-permute-start | bytes 258056 | tf_op jit(solution)/shard_map/ppermute | solution.py:292
  9.8 11.7 %collective-permute-start.4 = (bf16[336,128]{1,0:T(8,128)(2,1)S(1)}, bf16[336,128]{1,0:T(8,128)(2,1)S(1)}, u32[]{:S(2)}, u32[]{:S(2)}) collective-permute-start(bf16[336,128]{1,0:T(8,128)(2,1)S(1)} %get-tuple-element.30), channel_id=1, source_target_pairs={{0,1},{1,0},{2,3},{3,2},{4,5},{5,4},{6,7},{7,6},{8,14},{9,15},{10,... | collective-permute-start | bytes 258056 | tf_op jit(solution)/shard_map/ppermute | solution.py:292
  9.8 12.5 %collective-permute-start.5 = (bf16[336,128]{1,0:T(8,128)(2,1)S(1)}, bf16[336,128]{1,0:T(8,128)(2,1)S(1)}, u32[]{:S(2)}, u32[]{:S(2)}) collective-permute-start(bf16[336,128]{1,0:T(8,128)(2,1)S(1)} %get-tuple-element.31), channel_id=1, source_target_pairs={{0,2},{1,3},{2,0},{3,1},{4,6},{5,7},{6,4},{7,5},{8,13},{9,12},{10,... | collective-permute-start | bytes 258056 | tf_op jit(solution)/shard_map/ppermute | solution.py:292
  10.2 13.5 %collective-permute-start.6 = (bf16[336,128]{1,0:T(8,128)(2,1)S(1)}, bf16[336,128]{1,0:T(8,128)(2,1)S(1)}, u32[]{:S(2)}, u32[]{:S(2)}) collective-permute-start(bf16[336,128]{1,0:T(8,128)(2,1)S(1)} %get-tuple-element.32), channel_id=1, source_target_pairs={{0,3},{1,2},{2,1},{3,0},{4,7},{5,6},{6,5},{7,4},{8,12},{9,13},{10,... | collective-permute-start | bytes 258056 | tf_op jit(solution)/shard_map/ppermute | solution.py:292
  13.1 1.4 %copy-start = (bf16[1,6144,128]{2,1,0:T(8,128)(2,1)S(1)}, bf16[1,6144,128]{2,1,0:T(8,128)(2,1)}, u32[]{:S(2)}) copy-start(bf16[1,6144,128]{2,1,0:T(8,128)(2,1)} %param.11) | copy-start | bytes 4718596
  14.5 1.4 %copy-start.1 = (bf16[1,6144,128]{2,1,0:T(8,128)(2,1)S(1)}, bf16[1,6144,128]{2,1,0:T(8,128)(2,1)}, u32[]{:S(2)}) copy-start(bf16[1,6144,128]{2,1,0:T(8,128)(2,1)} %param.12) | copy-start | bytes 4718596
  15.9 1.1 %copy-start.2 = (bf16[1,320,1024]{2,1,0:T(8,128)(2,1)S(1)}, bf16[1,320,1024]{2,1,0:T(8,128)(2,1)}, u32[]{:S(2)}) copy-start(bf16[1,320,1024]{2,1,0:T(8,128)(2,1)} %param.9) | copy-start | bytes 1966084
  17.0 1.1 %copy-start.4 = (bf16[1,320,1024]{2,1,0:T(8,128)(2,1)S(1)}, bf16[1,320,1024]{2,1,0:T(8,128)(2,1)}, u32[]{:S(2)}) copy-start(bf16[1,320,1024]{2,1,0:T(8,128)(2,1)} %param.10) | copy-start | bytes 1966084
  18.1 5.6 %copy-start.8 = (s32[1,2]{1,0:T(1,128)S(1)}, s32[1,2]{1,0:T(1,128)}, u32[]{:S(2)}) copy-start(s32[1,2]{1,0:T(1,128)} %param.14) | copy-start | bytes 28
  18.4 10.0 %collective-permute-start.14 = (bf16[2,128,1024]{2,1,0:T(8,128)(2,1)S(1)}, bf16[2,128,1024]{2,1,0:T(8,128)(2,1)S(1)}, u32[]{:S(2)}, u32[]{:S(2)}) collective-permute-start(bf16[2,128,1024]{2,1,0:T(8,128)(2,1)S(1)} %get-tuple-element.41), channel_id=1, source_target_pairs={{0,1},{1,2},{2,3},{3,4},{4,5},{5,6},{6,7},{8,9},{9,10},{10,11},{11... | collective-permute-start | bytes 1572872 | tf_op jit(solution)/shard_map/ppermute | solution.py:312
  23.7 4.7 %copy-start.3 = (bf16[1,320,1024]{2,1,0:T(8,128)(2,1)S(1)}, bf16[1,320,1024]{2,1,0:T(8,128)(2,1)}, u32[]{:S(2)}) copy-start(bf16[1,320,1024]{2,1,0:T(8,128)(2,1)} %param.9) | copy-start | bytes 1966084
  23.7 4.7 %copy-start.5 = (bf16[1,320,1024]{2,1,0:T(8,128)(2,1)S(1)}, bf16[1,320,1024]{2,1,0:T(8,128)(2,1)}, u32[]{:S(2)}) copy-start(bf16[1,320,1024]{2,1,0:T(8,128)(2,1)} %param.10) | copy-start | bytes 1966084
  23.7 4.7 %copy-start.7 = (bf16[1,320,1024]{2,1,0:T(8,128)(2,1)S(1)}, bf16[1,320,1024]{2,1,0:T(8,128)(2,1)}, u32[]{:S(2)}) copy-start(bf16[1,320,1024]{2,1,0:T(8,128)(2,1)} %param.8) | copy-start | bytes 1966084
  31.0 33.8 %collective-permute-start.15 = (bf16[336,1152]{1,0:T(8,128)(2,1)S(1)}, bf16[336,1152]{1,0:T(8,128)(2,1)S(1)}, u32[]{:S(2)}, u32[]{:S(2)}) collective-permute-start(bf16[336,1152]{1,0:T(8,128)(2,1)S(1)} %near.1), channel_id=1, source_target_pairs={{0,8},{1,9},{2,10},{3,11},{4,12},{5,13},{6,14},{7,15},{8,16},{9,17... | collective-permute-start | bytes 2322440 | tf_op jit(solution)/shard_map/ppermute | solution.py:292
  39.6 11.6 %collective-permute-start.7 = (bf16[336,128]{1,0:T(8,128)(2,1)S(1)}, bf16[336,128]{1,0:T(8,128)(2,1)S(1)}, u32[]{:S(2)}, u32[]{:S(2)}) collective-permute-start(bf16[336,128]{1,0:T(8,128)(2,1)S(1)} %get-tuple-element.34), channel_id=1, source_target_pairs={{0,15},{1,14},{2,13},{3,12},{4,11},{5,10},{6,9},{7,8},{8,17},{9,16... | collective-permute-start | bytes 258056 | tf_op jit(solution)/shard_map/ppermute | solution.py:292
  41.6 15.6 %collective-permute-start.8 = (bf16[336,128]{1,0:T(8,128)(2,1)S(1)}, bf16[336,128]{1,0:T(8,128)(2,1)S(1)}, u32[]{:S(2)}, u32[]{:S(2)}) collective-permute-start(bf16[336,128]{1,0:T(8,128)(2,1)S(1)} %get-tuple-element.35), channel_id=1, source_target_pairs={{0,14},{1,15},{2,12},{3,13},{4,10},{5,11},{6,8},{7,9},{8,18},{9,19... | collective-permute-start | bytes 258056 | tf_op jit(solution)/shard_map/ppermute | solution.py:292
  41.6 15.6 %collective-permute-start.9 = (bf16[336,128]{1,0:T(8,128)(2,1)S(1)}, bf16[336,128]{1,0:T(8,128)(2,1)S(1)}, u32[]{:S(2)}, u32[]{:S(2)}) collective-permute-start(bf16[336,128]{1,0:T(8,128)(2,1)S(1)} %get-tuple-element.36), channel_id=1, source_target_pairs={{0,13},{1,12},{2,15},{3,14},{4,9},{5,8},{6,11},{7,10},{8,19},{9,18... | collective-permute-start | bytes 258056 | tf_op jit(solution)/shard_map/ppermute | solution.py:292
  41.9 18.1 %collective-permute-start.10 = (bf16[336,128]{1,0:T(8,128)(2,1)S(1)}, bf16[336,128]{1,0:T(8,128)(2,1)S(1)}, u32[]{:S(2)}, u32[]{:S(2)}) collective-permute-start(bf16[336,128]{1,0:T(8,128)(2,1)S(1)} %get-tuple-element.37), channel_id=1, source_target_pairs={{0,12},{1,13},{2,14},{3,15},{4,8},{5,9},{6,10},{7,11},{8,23},{9,22... | collective-permute-start | bytes 258056 | tf_op jit(solution)/shard_map/ppermute | solution.py:292
  51.2 8.9 %collective-permute-start.11 = (bf16[336,128]{1,0:T(8,128)(2,1)S(1)}, bf16[336,128]{1,0:T(8,128)(2,1)S(1)}, u32[]{:S(2)}, u32[]{:S(2)}) collective-permute-start(bf16[336,128]{1,0:T(8,128)(2,1)S(1)} %get-tuple-element.38), channel_id=1, source_target_pairs={{0,9},{1,8},{2,11},{3,10},{4,13},{5,12},{6,15},{7,14},{8,22},{9,23... | collective-permute-start | bytes 258056 | tf_op jit(solution)/shard_map/ppermute | solution.py:292
  57.2 5.5 %collective-permute-start.12 = (bf16[336,128]{1,0:T(8,128)(2,1)S(1)}, bf16[336,128]{1,0:T(8,128)(2,1)S(1)}, u32[]{:S(2)}, u32[]{:S(2)}) collective-permute-start(bf16[336,128]{1,0:T(8,128)(2,1)S(1)} %get-tuple-element.39), channel_id=1, source_target_pairs={{0,10},{1,11},{2,8},{3,9},{4,14},{5,15},{6,12},{7,13},{8,21},{9,20... | collective-permute-start | bytes 258056 | tf_op jit(solution)/shard_map/ppermute | solution.py:292
  57.2 7.5 %collective-permute-start.13 = (bf16[336,128]{1,0:T(8,128)(2,1)S(1)}, bf16[336,128]{1,0:T(8,128)(2,1)S(1)}, u32[]{:S(2)}, u32[]{:S(2)}) collective-permute-start(bf16[336,128]{1,0:T(8,128)(2,1)S(1)} %get-tuple-element.40), channel_id=1, source_target_pairs={{0,11},{1,10},{2,9},{3,8},{4,15},{5,14},{6,13},{7,12},{8,20},{9,21... | collective-permute-start | bytes 258056 | tf_op jit(solution)/shard_map/ppermute | solution.py:292

commit v6 on v5

--- a/solution.py
+++ b/solution.py
@@ -20,6 +20,7 @@
 VMEM_BASE = 12 * 1024 * 1024
 
 whole_vmem = pl.BlockSpec(memory_space=pltpu.VMEM)
+anywhere = pl.BlockSpec(memory_space=pl.ANY)
 in_hbm = pl.BlockSpec(memory_space=pltpu.HBM)
 whole_smem = pl.BlockSpec(memory_space=pltpu.SMEM)
 
@@ -105,26 +106,6 @@
     width = jnp.full((STAT_ROWS, HD), span_ref[0].astype(jnp.float32)).astype(jnp.bfloat16)
     for out_ref in out_refs:
         out_ref[rows:, :] = width
-    for copy in copies:
-        copy.wait()
-
-
-def fetch_kernel(key_ref, value_ref, old_key_ref, old_value_ref, *refs):
-    halo_ref, held_key_ref, held_value_ref, arrived = refs
-    halo = halo_ref.shape[1]
-    rows = key_ref.shape[0]
-    copies = [
-        (key_ref.at[rows - halo :], halo_ref.at[0]),
-        (value_ref.at[rows - halo :], halo_ref.at[1]),
-        (old_key_ref, held_key_ref),
-        (old_value_ref, held_value_ref),
-    ]
-    copies = [
-        pltpu.make_async_copy(source, target, arrived.at[index])
-        for index, (source, target) in enumerate(copies)
-    ]
-    for copy in copies:
-        copy.start()
     for copy in copies:
         copy.wait()
 
@@ -187,7 +168,7 @@
 def near_kernel(
     there, query_ref, key_ref, value_ref, halo_ref, own_ref, *refs
 ):
-    came_refs, out_ref = refs[:-1], refs[-1]
+    came_refs, out_ref = refs[: len(there[0])], refs[-1]
     me = lax.axis_index("seq")
     rows, wide = query_ref.shape
     halo = (WMAX - 1) * BLK
@@ -293,22 +274,7 @@
 
     came = [linked(shard, 0, steps) for shard, steps in zip(sent[:-1], zip(*there))]
     came.append(sent[-1])
-    mine, held_keys, held_values = pl.pallas_call(
-        fetch_kernel,
-        out_shape=[
-            jax.ShapeDtypeStruct((2, halo, wide), bf16),
-            jax.ShapeDtypeStruct(keys_cache.shape[1:], bf16),
-            jax.ShapeDtypeStruct(values_cache.shape[1:], bf16),
-        ],
-        in_specs=[in_hbm] * 4,
-        out_specs=[whole_vmem] * 3,
-        scratch_shapes=[pltpu.SemaphoreType.DMA((4,))],
-        compiler_params=params(queries),
-        cost_estimate=pl.CostEstimate(
-            flops=0, bytes_accessed=8 * keys_cache.shape[1] * HD, transcendentals=0
-        ),
-        name="fetch",
-    )(keys_new[0], values_new[0], keys_cache[0], values_cache[0])
+    mine = jnp.stack([keys_new[0, rows - halo :], values_new[0, rows - halo :]])
     before = lax.ppermute(mine, "seq", [(i, i + 1) for i in range(seq_count - 1)])
 
     picks = random_blocks[0].reshape(-1)
@@ -332,16 +298,18 @@
             window[0],
             global_blocks[0],
             picks,
-            held_keys,
-            held_values,
+            keys_cache[0],
+            values_cache[0],
             *came,
         )
 
     far = far_call()
+    ahead = min(3, seq_count - 1)
+    handed = [linked(shard, 1, steps) for shard, steps in zip(far[:-1], zip(*there))]
     both = pl.pallas_call(
         functools.partial(near_kernel, there),
         out_shape=jax.ShapeDtypeStruct((rows + STAT_ROWS, wide + HD), bf16),
-        in_specs=[whole_vmem] * (5 + seq_count),
+        in_specs=[whole_vmem] * (5 + seq_count) + [anywhere] * ahead,
         out_specs=whole_vmem,
         compiler_params=params(queries),
         cost_estimate=pl.CostEstimate(
@@ -357,10 +325,10 @@
         before,
         far[-1],
         *came,
+        *handed[:ahead],
     )
 
-    returned = [*far[:-1], both]
-    handed = [linked(shard, 1, steps) for shard, steps in zip(returned, zip(*there))]
+    handed.append(linked(both, 1, [0, 0]))
 
     merged = pl.pallas_call(
         functools.partial(merge_kernel, there),

time: 66.4 us -> 60.6 us (0.913)
  the two profiles are of different devices: /device:TPU:1 before, /device:TPU:0 now
where the time goes in v6:
time: 60.6 us; the launch traced here: 60.4 us
  starting transfers between devices  31.7 us (52%)
  waiting for transfers between devices  16.2 us (27%)
  Pallas kernels  8.26 us (14%)
  local copies, waits for them, and re-layouts  3.39 us (6%)
  between operations  0.82 us (1%)
    ppermute x15, starting transfers between devices, linked(): return lax.ppermute(shard, ('section', 'seq'), pairs)  28.1 us
    ppermute x15, waiting for transfers between devices, linked(): return lax.ppermute(shard, ('section', 'seq'), pairs)  16.2 us
    pallas_call x1, Pallas kernels, far_call(): pl.pallas_call(functools.partial(far_kernel, there), out_shape=[jax.Shape...  4.07 us
    ppermute x1, starting transfers between devices, per_device(): lax.ppermute(mine, 'seq', [(i, i + 1) for i in range(seq_count - 1)])  3.54 us
    unnamed x15, local copies, waits for them, and re-layouts  3.27 us
    pallas_call x1, Pallas kernels, per_device(): pl.pallas_call(functools.partial(near_kernel, there), out_shape=jax.Shape...  2.6 us
    pallas_call x1, Pallas kernels, per_device(): pl.pallas_call(functools.partial(merge_kernel, there), out_shape=jax.Shap...  1.32 us
  transfers between devices with their start and end apart: 16, of which 7 were waited for; matrix products, arithmetic and copies ran while one was open for 2% of the time, Pallas kernels for 7%

profile of v6, /device:TPU:0, one launch (start us, length us, event | category | flops | bytes accessed | tf_op | source)
XLA Modules:
  0.0 60.4 jit_solution(16674620618232097359)
XLA Ops:
  0.7 1.1 %copy-done = bf16[1,320,1024]{2,1,0:T(8,128)(2,1)S(1)} copy-done((bf16[1,320,1024]{2,1,0:T(8,128)(2,1)S(1)}, bf16[1,320,1024]{2,1,0:T(8,128)(2,1)}, u32[]{:S(2)}) %copy-start) | copy-done | bytes 655384
  1.8 0.3 split.1
  2.0 6.1 %collective-permute-start = (bf16[336,128]{1,0:T(8,128)(2,1)S(1)}, bf16[336,128]{1,0:T(8,128)(2,1)S(1)}, u32[]{:S(2)}, u32[]{:S(2)}) collective-permute-start(bf16[336,128]{1,0:T(8,128)(2,1)S(1)} %get-tuple-element.21), channel_id=1, source_target_pairs={{0,7},{1,6},{2,5},{3,4},{4,3},{5,2},{6,1},{7,0},{8,9},{9,8},{10,11... | collective-permute-start | bytes 258056 | tf_op jit(solution)/shard_map/ppermute | solution.py:273
  8.1 0.2 collective-permute-start.1
  8.3 0.7 %collective-permute-start.2 = (bf16[336,128]{1,0:T(8,128)(2,1)S(1)}, bf16[336,128]{1,0:T(8,128)(2,1)S(1)}, u32[]{:S(2)}, u32[]{:S(2)}) collective-permute-start(bf16[336,128]{1,0:T(8,128)(2,1)S(1)} %get-tuple-element.23), channel_id=1, source_target_pairs={{0,5},{1,4},{2,7},{3,6},{4,1},{5,0},{6,3},{7,2},{8,11},{9,10},{10,... | collective-permute-start | bytes 258056 | tf_op jit(solution)/shard_map/ppermute | solution.py:273
  9.1 2.0 %collective-permute-start.3 = (bf16[336,128]{1,0:T(8,128)(2,1)S(1)}, bf16[336,128]{1,0:T(8,128)(2,1)S(1)}, u32[]{:S(2)}, u32[]{:S(2)}) collective-permute-start(bf16[336,128]{1,0:T(8,128)(2,1)S(1)} %get-tuple-element.24), channel_id=1, source_target_pairs={{0,4},{1,5},{2,6},{3,7},{4,0},{5,1},{6,2},{7,3},{8,15},{9,14},{10,... | collective-permute-start | bytes 258056 | tf_op jit(solution)/shard_map/ppermute | solution.py:273
  11.1 1.6 %collective-permute-start.4 = (bf16[336,128]{1,0:T(8,128)(2,1)S(1)}, bf16[336,128]{1,0:T(8,128)(2,1)S(1)}, u32[]{:S(2)}, u32[]{:S(2)}) collective-permute-start(bf16[336,128]{1,0:T(8,128)(2,1)S(1)} %get-tuple-element.25), channel_id=1, source_target_pairs={{0,1},{1,0},{2,3},{3,2},{4,5},{5,4},{6,7},{7,6},{8,14},{9,15},{10,... | collective-permute-start | bytes 258056 | tf_op jit(solution)/shard_map/ppermute | solution.py:273
  12.7 0.8 %copy.10 = s32[1,40,3]{2,1,0:T(8,128)S(1)} copy(s32[1,40,3]{1,0,2:T(1,128)} %param.15) | data formatting | bytes 960 | tf_op args[7]
  13.5 0.1 reshape_squeeze.3.random_ref
  13.6 1.3 %collective-permute-start.5 = (bf16[336,128]{1,0:T(8,128)(2,1)S(1)}, bf16[336,128]{1,0:T(8,128)(2,1)S(1)}, u32[]{:S(2)}, u32[]{:S(2)}) collective-permute-start(bf16[336,128]{1,0:T(8,128)(2,1)S(1)} %get-tuple-element.26), channel_id=1, source_target_pairs={{0,2},{1,3},{2,0},{3,1},{4,6},{5,7},{6,4},{7,5},{8,13},{9,12},{10,... | collective-permute-start | bytes 258056 | tf_op jit(solution)/shard_map/ppermute | solution.py:273
  14.9 4.0 %collective-permute-start.6 = (bf16[336,128]{1,0:T(8,128)(2,1)S(1)}, bf16[336,128]{1,0:T(8,128)(2,1)S(1)}, u32[]{:S(2)}, u32[]{:S(2)}) collective-permute-start(bf16[336,128]{1,0:T(8,128)(2,1)S(1)} %get-tuple-element.27), channel_id=1, source_target_pairs={{0,3},{1,2},{2,1},{3,0},{4,7},{5,6},{6,5},{7,4},{8,12},{9,13},{10,... | collective-permute-start | bytes 258056 | tf_op jit(solution)/shard_map/ppermute | solution.py:273
  19.0 0.1 pad_maximum_fusion
  19.0 2.2 %collective-permute-done.2.refs_2_ = bf16[336,128]{1,0:T(8,128)(2,1)S(1)} collective-permute-done((bf16[336,128]{1,0:T(8,128)(2,1)S(1)}, bf16[336,128]{1,0:T(8,128)(2,1)S(1)}, u32[]{:S(2)}, u32[]{:S(2)}) %collective-permute-start.2) | collective-permute-done | bytes 86048 | tf_op jit(solution)/shard_map/ppermute | solution.py:273
  21.3 3.5 %collective-permute-start.14 = (bf16[2,128,1024]{2,1,0:T(8,128)(2,1)S(1)}, bf16[2,128,1024]{2,1,0:T(8,128)(2,1)S(1)}, u32[]{:S(2)}, u32[]{:S(2)}) collective-permute-start(bf16[2,128,1024]{2,1,0:T(8,128)(2,1)S(1)} %pad_maximum_fusion), channel_id=1, source_target_pairs={{0,1},{1,2},{2,3},{3,4},{4,5},{5,6},{6,7},{8,9},{9,10},{10,11},{11... | collective-permute-start | bytes 1572872 | tf_op jit(solution)/shard_map/ppermute | solution.py:278
  24.9 1.4 %copy-done.5 = bf16[1,6144,128]{2,1,0:T(8,128)(2,1)S(1)} copy-done((bf16[1,6144,128]{2,1,0:T(8,128)(2,1)S(1)}, bf16[1,6144,128]{2,1,0:T(8,128)(2,1)}, u32[]{:S(2)}) %copy-start.5) | copy-done | bytes 1572888
  26.3 4.1 %far.1 = (bf16[336,128]{1,0:T(8,128)(2,1)S(1)}, bf16[336,128]{1,0:T(8,128)(2,1)S(1)}, bf16[336,128]{1,0:T(8,128)(2,1)S(1)}, bf16[336,128]{1,0:T(8,128)(2,1)S(1)}...) custom-call(s32[1]{0:T(128)} %bitcast.9.span_ref, ...), custom_call_target="tpu_custom_call" | custom-call | flops 16777216000 | bytes 4456448 | tf_op jit(solution)/shard_map/far/pallas_call | solution.py:285
  30.3 1.2 %collective-permute-start.7 = (bf16[336,128]{1,0:T(8,128)(2,1)S(1)}, bf16[336,128]{1,0:T(8,128)(2,1)S(1)}, u32[]{:S(2)}, u32[]{:S(2)}) collective-permute-start(bf16[336,128]{1,0:T(8,128)(2,1)S(1)} %get-tuple-element.29), channel_id=1, source_target_pairs={{0,15},{1,14},{2,13},{3,12},{4,11},{5,10},{6,9},{7,8},{8,17},{9,16... | collective-permute-start | bytes 258056 | tf_op jit(solution)/shard_map/ppermute | solution.py:273
  31.6 2.7 %collective-permute-start.8 = (bf16[336,128]{1,0:T(8,128)(2,1)S(1)}, bf16[336,128]{1,0:T(8,128)(2,1)S(1)}, u32[]{:S(2)}, u32[]{:S(2)}) collective-permute-start(bf16[336,128]{1,0:T(8,128)(2,1)S(1)} %get-tuple-element.30), channel_id=1, source_target_pairs={{0,14},{1,15},{2,12},{3,13},{4,10},{5,11},{6,8},{7,9},{8,18},{9,19... | collective-permute-start | bytes 258056 | tf_op jit(solution)/shard_map/ppermute | solution.py:273
  34.3 1.0 %collective-permute-start.9 = (bf16[336,128]{1,0:T(8,128)(2,1)S(1)}, bf16[336,128]{1,0:T(8,128)(2,1)S(1)}, u32[]{:S(2)}, u32[]{:S(2)}) collective-permute-start(bf16[336,128]{1,0:T(8,128)(2,1)S(1)} %get-tuple-element.31), channel_id=1, source_target_pairs={{0,13},{1,12},{2,15},{3,14},{4,9},{5,8},{6,11},{7,10},{8,19},{9,18... | collective-permute-start | bytes 258056 | tf_op jit(solution)/shard_map/ppermute | solution.py:273
  35.3 3.8 %collective-permute-done.8.refs_9_.refs_1_ = bf16[336,128]{1,0:T(8,128)(2,1)S(1)} collective-permute-done((bf16[336,128]{1,0:T(8,128)(2,1)S(1)}, bf16[336,128]{1,0:T(8,128)(2,1)S(1)}, u32[]{:S(2)}, u32[]{:S(2)}) %collective-permute-start.8) | collective-permute-done | bytes 86048 | tf_op jit(solution)/shard_map/ppermute | solution.py:273
  39.1 2.3 %collective-permute-done.9.refs_10_.refs_2_ = bf16[336,128]{1,0:T(8,128)(2,1)S(1)} collective-permute-done((bf16[336,128]{1,0:T(8,128)(2,1)S(1)}, bf16[336,128]{1,0:T(8,128)(2,1)S(1)}, u32[]{:S(2)}, u32[]{:S(2)}) %collective-permute-start.9) | collective-permute-done | bytes 86048 | tf_op jit(solution)/shard_map/ppermute | solution.py:273
  41.4 2.6 %near.1 = bf16[336,1152]{1,0:T(8,128)(2,1)S(1)} custom-call(bf16[320,1024]{1,0:T(8,128)(2,1)S(1)} %bitcast.11, bf16[320,1024]{1,0:T(8,128)(2,1)S(1)} %bitcast.12, bf16[320,1024]{1,0:T(8,128)(2,1)S(1)} %bitcast.13, bf16[2,128,1024]{2,1,0:T(8,128)(2,1)S(1)} %collective-permute-done.14.halo_ref, bf16[336,128]{1,0:T(8,128)(2,1)S(1)} %get-tuple-element.36.own_ref, ...), custom_call_target="tpu_custom_call" | custom-call | flops 13421772800 | bytes 2949120 | tf_op jit(solution)/shard_map/near/pallas_call | solution.py:309
  44.1 0.1 collective-permute-start.15
  44.1 0.1 collective-permute-start.10
  44.2 4.2 %collective-permute-start.11 = (bf16[336,128]{1,0:T(8,128)(2,1)S(1)}, bf16[336,128]{1,0:T(8,128)(2,1)S(1)}, u32[]{:S(2)}, u32[]{:S(2)}) collective-permute-start(bf16[336,128]{1,0:T(8,128)(2,1)S(1)} %get-tuple-element.33), channel_id=1, source_target_pairs={{0,9},{1,8},{2,11},{3,10},{4,13},{5,12},{6,15},{7,14},{8,22},{9,23... | collective-permute-start | bytes 258056 | tf_op jit(solution)/shard_map/ppermute | solution.py:273
  48.4 0.1 collective-permute-start.12
  48.5 2.8 %collective-permute-start.13 = (bf16[336,128]{1,0:T(8,128)(2,1)S(1)}, bf16[336,128]{1,0:T(8,128)(2,1)S(1)}, u32[]{:S(2)}, u32[]{:S(2)}) collective-permute-start(bf16[336,128]{1,0:T(8,128)(2,1)S(1)} %get-tuple-element.35), channel_id=1, source_target_pairs={{0,11},{1,10},{2,9},{3,8},{4,15},{5,14},{6,13},{7,12},{8,20},{9,21... | collective-permute-start | bytes 258056 | tf_op jit(solution)/shard_map/ppermute | solution.py:273
  51.3 0.6 %collective-permute-done.10.refs_3_ = bf16[336,128]{1,0:T(8,128)(2,1)S(1)} collective-permute-done((bf16[336,128]{1,0:T(8,128)(2,1)S(1)}, bf16[336,128]{1,0:T(8,128)(2,1)S(1)}, u32[]{:S(2)}, u32[]{:S(2)}) %collective-permute-start.10) | collective-permute-done | bytes 86048 | tf_op jit(solution)/shard_map/ppermute | solution.py:273
  51.9 4.5 %collective-permute-done.12.refs_5_ = bf16[336,128]{1,0:T(8,128)(2,1)S(1)} collective-permute-done((bf16[336,128]{1,0:T(8,128)(2,1)S(1)}, bf16[336,128]{1,0:T(8,128)(2,1)S(1)}, u32[]{:S(2)}, u32[]{:S(2)}) %collective-permute-start.12) | collective-permute-done | bytes 86048 | tf_op jit(solution)/shard_map/ppermute | solution.py:273
  56.4 0.9 %collective-permute-done.13.refs_6_ = bf16[336,128]{1,0:T(8,128)(2,1)S(1)} collective-permute-done((bf16[336,128]{1,0:T(8,128)(2,1)S(1)}, bf16[336,128]{1,0:T(8,128)(2,1)S(1)}, u32[]{:S(2)}, u32[]{:S(2)}) %collective-permute-start.13) | collective-permute-done | bytes 86048 | tf_op jit(solution)/shard_map/ppermute | solution.py:273
  57.3 1.8 %collective-permute-done.15.refs_7_ = bf16[336,1152]{1,0:T(8,128)(2,1)S(1)} collective-permute-done((bf16[336,1152]{1,0:T(8,128)(2,1)S(1)}, bf16[336,1152]{1,0:T(8,128)(2,1)S(1)}, u32[]{:S(2)}, u32[]{:S(2)}) %collective-permute-start.15) | collective-permute-done | bytes 774176 | tf_op jit(solution)/shard_map/ppermute | solution.py:273
  59.1 1.3 %merge.1 = bf16[320,1024]{1,0:T(8,128)(2,1)} custom-call(bf16[336,128]{1,0:T(8,128)(2,1)S(1)} %collective-permute-done.7.refs_8_.refs_0_, bf16[336,128]{1,0:T(8,128)(2,1)S(1)} %collective-permute-done.8.refs_9_.refs_1_, bf16[336,128]{1,0:T(8,128)(2,1)S(1)} %collective-permute-done.9.refs_10_.refs_2_, bf16[336,128]{1,0:T(8,128)(2,1)S(1)} %collective-permute-done.10.refs_3_, ...), custom_call_target="tpu_custom_call" | custom-call | bytes 1966080 | tf_op jit(solution)/shard_map/merge/pallas_call | solution.py:333
  (25 shorter events, 0.1 us)
Async XLA Ops:
  0.0 24.8 %copy-start.6 = (s32[1,2]{1,0:T(1,128)S(1)}, s32[1,2]{1,0:T(1,128)}, u32[]{:S(2)}) copy-start(s32[1,2]{1,0:T(1,128)} %param.14) | copy-start | bytes 28
  0.7 1.1 %copy-start = (bf16[1,320,1024]{2,1,0:T(8,128)(2,1)S(1)}, bf16[1,320,1024]{2,1,0:T(8,128)(2,1)}, u32[]{:S(2)}) copy-start(bf16[1,320,1024]{2,1,0:T(8,128)(2,1)} %param.8) | copy-start | bytes 1966084
  1.8 17.2 %slice-start = ((bf16[1,320,1024]{2,1,0:T(8,128)(2,1)}), bf16[1,128,1024]{2,1,0:T(8,128)(2,1)S(1)}, s32[]{:S(2)}) async-start(bf16[1,320,1024]{2,1,0:T(8,128)(2,1)} %param.9), calls=%async_computation | async-start | bytes 524288 | tf_op jit(solution)/shard_map/slice | solution.py:277
  1.8 17.2 %slice-start.1 = ((bf16[1,320,1024]{2,1,0:T(8,128)(2,1)}), bf16[1,128,1024]{2,1,0:T(8,128)(2,1)S(1)}, s32[]{:S(2)}) async-start(bf16[1,320,1024]{2,1,0:T(8,128)(2,1)} %param.10), calls=%async_computation.1 | async-start | bytes 524288 | tf_op jit(solution)/shard_map/slice | solution.py:277
  1.8 23.1 %copy-start.4 = (bf16[1,6144,128]{2,1,0:T(8,128)(2,1)S(1)}, bf16[1,6144,128]{2,1,0:T(8,128)(2,1)}, u32[]{:S(2)}) copy-start(bf16[1,6144,128]{2,1,0:T(8,128)(2,1)} %param.11) | copy-start | bytes 4718596
  2.0 11.6 %collective-permute-start = (bf16[336,128]{1,0:T(8,128)(2,1)S(1)}, bf16[336,128]{1,0:T(8,128)(2,1)S(1)}, u32[]{:S(2)}, u32[]{:S(2)}) collective-permute-start(bf16[336,128]{1,0:T(8,128)(2,1)S(1)} %get-tuple-element.21), channel_id=1, source_target_pairs={{0,7},{1,6},{2,5},{3,4},{4,3},{5,2},{6,1},{7,0},{8,9},{9,8},{10,11... | collective-permute-start | bytes 258056 | tf_op jit(solution)/shard_map/ppermute | solution.py:273
  8.1 6.8 %collective-permute-start.1 = (bf16[336,128]{1,0:T(8,128)(2,1)S(1)}, bf16[336,128]{1,0:T(8,128)(2,1)S(1)}, u32[]{:S(2)}, u32[]{:S(2)}) collective-permute-start(bf16[336,128]{1,0:T(8,128)(2,1)S(1)} %get-tuple-element.22), channel_id=1, source_target_pairs={{0,6},{1,7},{2,4},{3,5},{4,2},{5,3},{6,0},{7,1},{8,10},{9,11},{10,... | collective-permute-start | bytes 258056 | tf_op jit(solution)/shard_map/ppermute | solution.py:273
  8.3 12.9 %collective-permute-start.2 = (bf16[336,128]{1,0:T(8,128)(2,1)S(1)}, bf16[336,128]{1,0:T(8,128)(2,1)S(1)}, u32[]{:S(2)}, u32[]{:S(2)}) collective-permute-start(bf16[336,128]{1,0:T(8,128)(2,1)S(1)} %get-tuple-element.23), channel_id=1, source_target_pairs={{0,5},{1,4},{2,7},{3,6},{4,1},{5,0},{6,3},{7,2},{8,11},{9,10},{10,... | collective-permute-start | bytes 258056 | tf_op jit(solution)/shard_map/ppermute | solution.py:273
  9.1 15.7 %collective-permute-start.3 = (bf16[336,128]{1,0:T(8,128)(2,1)S(1)}, bf16[336,128]{1,0:T(8,128)(2,1)S(1)}, u32[]{:S(2)}, u32[]{:S(2)}) collective-permute-start(bf16[336,128]{1,0:T(8,128)(2,1)S(1)} %get-tuple-element.24), channel_id=1, source_target_pairs={{0,4},{1,5},{2,6},{3,7},{4,0},{5,1},{6,2},{7,3},{8,15},{9,14},{10,... | collective-permute-start | bytes 258056 | tf_op jit(solution)/shard_map/ppermute | solution.py:273
  11.1 13.7 %collective-permute-start.4 = (bf16[336,128]{1,0:T(8,128)(2,1)S(1)}, bf16[336,128]{1,0:T(8,128)(2,1)S(1)}, u32[]{:S(2)}, u32[]{:S(2)}) collective-permute-start(bf16[336,128]{1,0:T(8,128)(2,1)S(1)} %get-tuple-element.25), channel_id=1, source_target_pairs={{0,1},{1,0},{2,3},{3,2},{4,5},{5,4},{6,7},{7,6},{8,14},{9,15},{10,... | collective-permute-start | bytes 258056 | tf_op jit(solution)/shard_map/ppermute | solution.py:273
  13.6 11.2 %collective-permute-start.5 = (bf16[336,128]{1,0:T(8,128)(2,1)S(1)}, bf16[336,128]{1,0:T(8,128)(2,1)S(1)}, u32[]{:S(2)}, u32[]{:S(2)}) collective-permute-start(bf16[336,128]{1,0:T(8,128)(2,1)S(1)} %get-tuple-element.26), channel_id=1, source_target_pairs={{0,2},{1,3},{2,0},{3,1},{4,6},{5,7},{6,4},{7,5},{8,13},{9,12},{10,... | collective-permute-start | bytes 258056 | tf_op jit(solution)/shard_map/ppermute | solution.py:273
  14.9 9.9 %collective-permute-start.6 = (bf16[336,128]{1,0:T(8,128)(2,1)S(1)}, bf16[336,128]{1,0:T(8,128)(2,1)S(1)}, u32[]{:S(2)}, u32[]{:S(2)}) collective-permute-start(bf16[336,128]{1,0:T(8,128)(2,1)S(1)} %get-tuple-element.27), channel_id=1, source_target_pairs={{0,3},{1,2},{2,1},{3,0},{4,7},{5,6},{6,5},{7,4},{8,12},{9,13},{10,... | collective-permute-start | bytes 258056 | tf_op jit(solution)/shard_map/ppermute | solution.py:273
  21.3 20.2 %collective-permute-start.14 = (bf16[2,128,1024]{2,1,0:T(8,128)(2,1)S(1)}, bf16[2,128,1024]{2,1,0:T(8,128)(2,1)S(1)}, u32[]{:S(2)}, u32[]{:S(2)}) collective-permute-start(bf16[2,128,1024]{2,1,0:T(8,128)(2,1)S(1)} %pad_maximum_fusion), channel_id=1, source_target_pairs={{0,1},{1,2},{2,3},{3,4},{4,5},{5,6},{6,7},{8,9},{9,10},{10,11},{11... | collective-permute-start | bytes 1572872 | tf_op jit(solution)/shard_map/ppermute | solution.py:278
  24.9 1.4 %copy-start.5 = (bf16[1,6144,128]{2,1,0:T(8,128)(2,1)S(1)}, bf16[1,6144,128]{2,1,0:T(8,128)(2,1)}, u32[]{:S(2)}) copy-start(bf16[1,6144,128]{2,1,0:T(8,128)(2,1)} %param.12) | copy-start | bytes 4718596
  26.3 15.2 %copy-start.1 = (bf16[1,320,1024]{2,1,0:T(8,128)(2,1)S(1)}, bf16[1,320,1024]{2,1,0:T(8,128)(2,1)}, u32[]{:S(2)}) copy-start(bf16[1,320,1024]{2,1,0:T(8,128)(2,1)} %param.8) | copy-start | bytes 1966084
  26.3 15.2 %copy-start.2 = (bf16[1,320,1024]{2,1,0:T(8,128)(2,1)S(1)}, bf16[1,320,1024]{2,1,0:T(8,128)(2,1)}, u32[]{:S(2)}) copy-start(bf16[1,320,1024]{2,1,0:T(8,128)(2,1)} %param.9) | copy-start | bytes 1966084
  26.3 15.2 %copy-start.3 = (bf16[1,320,1024]{2,1,0:T(8,128)(2,1)S(1)}, bf16[1,320,1024]{2,1,0:T(8,128)(2,1)}, u32[]{:S(2)}) copy-start(bf16[1,320,1024]{2,1,0:T(8,128)(2,1)} %param.10) | copy-start | bytes 1966084
  30.3 4.9 %collective-permute-start.7 = (bf16[336,128]{1,0:T(8,128)(2,1)S(1)}, bf16[336,128]{1,0:T(8,128)(2,1)S(1)}, u32[]{:S(2)}, u32[]{:S(2)}) collective-permute-start(bf16[336,128]{1,0:T(8,128)(2,1)S(1)} %get-tuple-element.29), channel_id=1, source_target_pairs={{0,15},{1,14},{2,13},{3,12},{4,11},{5,10},{6,9},{7,8},{8,17},{9,16... | collective-permute-start | bytes 258056 | tf_op jit(solution)/shard_map/ppermute | solution.py:273
  31.6 7.6 %collective-permute-start.8 = (bf16[336,128]{1,0:T(8,128)(2,1)S(1)}, bf16[336,128]{1,0:T(8,128)(2,1)S(1)}, u32[]{:S(2)}, u32[]{:S(2)}) collective-permute-start(bf16[336,128]{1,0:T(8,128)(2,1)S(1)} %get-tuple-element.30), channel_id=1, source_target_pairs={{0,14},{1,15},{2,12},{3,13},{4,10},{5,11},{6,8},{7,9},{8,18},{9,19... | collective-permute-start | bytes 258056 | tf_op jit(solution)/shard_map/ppermute | solution.py:273
  34.3 7.2 %collective-permute-start.9 = (bf16[336,128]{1,0:T(8,128)(2,1)S(1)}, bf16[336,128]{1,0:T(8,128)(2,1)S(1)}, u32[]{:S(2)}, u32[]{:S(2)}) collective-permute-start(bf16[336,128]{1,0:T(8,128)(2,1)S(1)} %get-tuple-element.31), channel_id=1, source_target_pairs={{0,13},{1,12},{2,15},{3,14},{4,9},{5,8},{6,11},{7,10},{8,19},{9,18... | collective-permute-start | bytes 258056 | tf_op jit(solution)/shard_map/ppermute | solution.py:273
  44.1 15.0 %collective-permute-start.15 = (bf16[336,1152]{1,0:T(8,128)(2,1)S(1)}, bf16[336,1152]{1,0:T(8,128)(2,1)S(1)}, u32[]{:S(2)}, u32[]{:S(2)}) collective-permute-start(bf16[336,1152]{1,0:T(8,128)(2,1)S(1)} %near.1), channel_id=1, source_target_pairs={{0,8},{1,9},{2,10},{3,11},{4,12},{5,13},{6,14},{7,15},{8,16},{9,17... | collective-permute-start | bytes 2322440 | tf_op jit(solution)/shard_map/ppermute | solution.py:273
  44.1 7.8 %collective-permute-start.10 = (bf16[336,128]{1,0:T(8,128)(2,1)S(1)}, bf16[336,128]{1,0:T(8,128)(2,1)S(1)}, u32[]{:S(2)}, u32[]{:S(2)}) collective-permute-start(bf16[336,128]{1,0:T(8,128)(2,1)S(1)} %get-tuple-element.32), channel_id=1, source_target_pairs={{0,12},{1,13},{2,14},{3,15},{4,8},{5,9},{6,10},{7,11},{8,23},{9,22... | collective-permute-start | bytes 258056 | tf_op jit(solution)/shard_map/ppermute | solution.py:273
  44.2 7.7 %collective-permute-start.11 = (bf16[336,128]{1,0:T(8,128)(2,1)S(1)}, bf16[336,128]{1,0:T(8,128)(2,1)S(1)}, u32[]{:S(2)}, u32[]{:S(2)}) collective-permute-start(bf16[336,128]{1,0:T(8,128)(2,1)S(1)} %get-tuple-element.33), channel_id=1, source_target_pairs={{0,9},{1,8},{2,11},{3,10},{4,13},{5,12},{6,15},{7,14},{8,22},{9,23... | collective-permute-start | bytes 258056 | tf_op jit(solution)/shard_map/ppermute | solution.py:273
  48.4 8.0 %collective-permute-start.12 = (bf16[336,128]{1,0:T(8,128)(2,1)S(1)}, bf16[336,128]{1,0:T(8,128)(2,1)S(1)}, u32[]{:S(2)}, u32[]{:S(2)}) collective-permute-start(bf16[336,128]{1,0:T(8,128)(2,1)S(1)} %get-tuple-element.34), channel_id=1, source_target_pairs={{0,10},{1,11},{2,8},{3,9},{4,14},{5,15},{6,12},{7,13},{8,21},{9,20... | collective-permute-start | bytes 258056 | tf_op jit(solution)/shard_map/ppermute | solution.py:273
  48.5 8.8 %collective-permute-start.13 = (bf16[336,128]{1,0:T(8,128)(2,1)S(1)}, bf16[336,128]{1,0:T(8,128)(2,1)S(1)}, u32[]{:S(2)}, u32[]{:S(2)}) collective-permute-start(bf16[336,128]{1,0:T(8,128)(2,1)S(1)} %get-tuple-element.35), channel_id=1, source_target_pairs={{0,11},{1,10},{2,9},{3,8},{4,15},{5,14},{6,13},{7,12},{8,20},{9,21... | collective-permute-start | bytes 258056 | tf_op jit(solution)/shard_map/ppermute | solution.py:273

commit v7 on v6

--- a/solution.py
+++ b/solution.py
@@ -113,9 +113,6 @@
 def far_kernel(
     there, span_ref, global_ref, random_ref, key_ref, value_ref, *refs
 ):
-    peers = peers_of(there, 0)
-    count = len(peers)
-    query_refs, out_refs = refs[:count], refs[count:]
     span = span_ref[0]
     last = key_ref.shape[0] // BLK - 1
 
@@ -126,9 +123,10 @@
 
     glob_keys = [block(key_ref, global_ref[g]) for g in range(GLOB)]
     glob_values = [block(value_ref, global_ref[g]) for g in range(GLOB)]
-    for index, chunk in enumerate(peers):
-        query_ref, out_ref = query_refs[index], out_refs[index]
-        rows = query_ref.shape[0] - STAT_ROWS
+    peers = peers_of(there, 0)
+    query_refs, out_refs = refs[: len(peers)], refs[len(peers) :]
+    rows = query_refs[0].shape[0] - STAT_ROWS
+    for chunk, query_ref, out_ref in zip(peers, query_refs, out_refs):
         blocks = rows // BLK
         first = chunk == 0
         all_scores, all_picks = [], []
@@ -165,16 +163,13 @@
         out_ref[rows:, :] = tile
 
 
-def near_kernel(
-    there, query_ref, key_ref, value_ref, halo_ref, own_ref, *refs
+def near_rows(
+    there, first, last, query_ref, key_ref, value_ref, halo_ref, came_refs, out_ref
 ):
-    came_refs, out_ref = refs[: len(there[0])], refs[-1]
-    me = lax.axis_index("seq")
-    rows, wide = query_ref.shape
-    halo = (WMAX - 1) * BLK
-    starts = list(range(0, rows, 2 * BLK))
-    sizes = [min(2 * BLK, rows - start) for start in starts]
-    out_ref[:, wide:] = own_ref[...]
+    rows = query_ref.shape[0]
+    halo = (WMAX - 1) * BLK
+    starts = list(range(first, last, 2 * BLK))
+    sizes = [min(2 * BLK, last - start) for start in starts]
     for peer, came_ref in zip(peers_of(there, 0), came_refs):
         lanes = pl.ds(pl.multiple_of(peer * HD, HD), HD)
         width = came_ref[rows:, :].astype(jnp.float32)[:1]
@@ -195,28 +190,53 @@
             slot = (lane_at // BLK - row_at // BLK).astype(jnp.float32)
             allowed = (lane_at <= row_at + halo) & (slot + width[:, : size + halo] >= WMAX)
             if start < halo:
-                closed = jnp.where(me == 0, halo - start, 0)
+                closed = jnp.where(lax.axis_index("seq") == 0, halo - start, 0)
                 allowed = allowed & (lane_at >= closed)
             all_scores.append(jnp.where(allowed, scores, MASKED))
             all_values.append(values)
         parts, lses = softmax_parts(all_scores, all_values)
         tile = stat_tile([as_row(lse, 0) for lse in lses])
         for start, size, part in zip(starts, sizes, parts):
-            out_ref[start : start + size, lanes] = part
-        out_ref[rows:, lanes] = tile
-
-
-def merge_kernel(there, *refs):
-    far_refs, out_ref = refs[:-1], refs[-1]
-    own = len(far_refs) - 1
-    near_ref = far_refs[own]
+            out_ref[start - first : start - first + size, lanes] = part
+        out_ref[last - first : last - first + STAT_ROWS, lanes] = tile
+
+
+def packed_at(index, first, wide):
+    across = wide // HD
+    row, lane = first + index // across * STAT_ROWS, index % across * HD
+    return slice(row, row + STAT_ROWS), slice(lane, lane + HD)
+
+
+def near_inner_kernel(there, query_ref, key_ref, value_ref, own_ref, *refs):
+    rows, wide = query_ref.shape
+    halo = (WMAX - 1) * BLK
+    came_refs, out_ref = refs[:-1], refs[-1]
+    near_rows(there, halo, rows, query_ref, key_ref, value_ref, None, came_refs, out_ref)
+    for index in range(own_ref.shape[0] // STAT_ROWS):
+        at = packed_at(index, rows - halo + STAT_ROWS, wide)
+        out_ref[at] = own_ref[index * STAT_ROWS : (index + 1) * STAT_ROWS, :]
+
+
+def near_edge_kernel(there, query_ref, key_ref, value_ref, halo_ref, *refs):
+    halo = (WMAX - 1) * BLK
+    came_refs, out_ref = refs[: len(there[0])], refs[-1]
+    near_rows(there, 0, halo, query_ref, key_ref, value_ref, halo_ref, came_refs, out_ref)
+
+
+def merge_kernel(there, edge_ref, inner_ref, *refs):
+    far_refs, out_ref, own_ref = refs[:-2], refs[-2], refs[-1]
     rows, wide = out_ref.shape
+    halo = (WMAX - 1) * BLK
+    for index in range(own_ref.shape[0] // STAT_ROWS):
+        at = packed_at(index, rows - halo + STAT_ROWS, wide)
+        own_ref[index * STAT_ROWS : (index + 1) * STAT_ROWS, :] = inner_ref[at]
     count = stat_count(rows)
-    for index, (peer, far_ref) in enumerate(zip(peers_of(there, -1), far_refs)):
-        part = slice(wide, None) if index == own else slice(None)
+    for peer, far_ref in zip(peers_of(there, -1), (*far_refs, own_ref)):
         lanes = pl.ds(pl.multiple_of(peer * HD, HD), HD)
-        far_stats = stat_rows_of(far_ref[rows:, part], count)
-        near_stats = stat_rows_of(near_ref[rows:, lanes], count)
+        far_stats = stat_rows_of(far_ref[rows:, :], count)
+        near_stats = stat_rows_of(edge_ref[halo:, lanes], 1) + stat_rows_of(
+            inner_ref[rows - halo : rows - halo + STAT_ROWS, lanes], count - 1
+        )
         for group in range(count):
             start = group * LANES
             size = min(LANES, rows - start)
@@ -226,8 +246,11 @@
             column = jnp.sum(
                 jnp.where(row_at == lane_at, share, 0.0), axis=1, keepdims=True
             )
-            far = far_ref[start : start + size, part].astype(jnp.float32)
-            near = near_ref[start : start + size, lanes].astype(jnp.float32)
+            far = far_ref[start : start + size, :].astype(jnp.float32)
+            if start < halo:
+                near = edge_ref[start : start + size, lanes].astype(jnp.float32)
+            else:
+                near = inner_ref[start - halo : start - halo + size, lanes].astype(jnp.float32)
             out_ref[start : start + size, lanes] = (
                 far * column + near * (1.0 - column)
             ).astype(jnp.bfloat16)
@@ -250,9 +273,11 @@
     inner, outer = list(range(1, half)), list(range(seq_count - 1, half - 1, -1))
     there = [outer + inner + [0], inner + outer + [0]]
 
+    chunk_shape = jax.ShapeDtypeStruct((rows + STAT_ROWS, HD), bf16)
+    chunk_shape = jax.ShapeDtypeStruct((rows + STAT_ROWS, HD), bf16)
     sent = pl.pallas_call(
         functools.partial(split_kernel, there),
-        out_shape=[jax.ShapeDtypeStruct((rows + STAT_ROWS, HD), bf16)] * seq_count,
+        out_shape=[chunk_shape] * seq_count,
         in_specs=[whole_smem, in_hbm],
         out_specs=[whole_vmem] * seq_count,
         scratch_shapes=[pltpu.SemaphoreType.DMA((seq_count,))],
@@ -279,66 +304,60 @@
 
     picks = random_blocks[0].reshape(-1)
 
-    def far_call():
-        count = seq_count
-        out_rows = rows + STAT_ROWS
+    far = pl.pallas_call(
+        functools.partial(far_kernel, there),
+        out_shape=[chunk_shape] * seq_count,
+        in_specs=[whole_smem] * 3 + [whole_vmem] * (2 + seq_count),
+        out_specs=[whole_vmem] * seq_count,
+        compiler_params=params(queries),
+        cost_estimate=pl.CostEstimate(
+            flops=40 * seq_count * rows * 320 * HD * 4,
+            bytes_accessed=2 * 2 * keys_cache.shape[1] * HD + 4 * seq_count * rows * HD,
+            transcendentals=seq_count * rows * 320,
+        ),
+        name="far",
+    )(window[0], global_blocks[0], picks, keys_cache[0], values_cache[0], *came)
+    handed = [linked(shard, 1, steps) for shard, steps in zip(far[:-1], zip(*there))]
+
+    def near_call(kernel, name, near_part, out_rows, *operands):
         return pl.pallas_call(
-            functools.partial(far_kernel, there),
-            out_shape=[jax.ShapeDtypeStruct((out_rows, HD), bf16)] * count,
-            in_specs=[whole_smem] * 3 + [whole_vmem] * (2 + count),
-            out_specs=[whole_vmem] * count,
+            functools.partial(kernel, there),
+            out_shape=jax.ShapeDtypeStruct((out_rows, wide), bf16),
+            in_specs=[
+                whole_vmem if index < 4 + seq_count else anywhere
+                for index in range(3 + len(operands))
+            ],
+            out_specs=whole_vmem,
             compiler_params=params(queries),
             cost_estimate=pl.CostEstimate(
-                flops=40 * count * rows * 320 * HD * 4,
-                bytes_accessed=2 * 2 * keys_cache.shape[1] * HD + 4 * count * rows * HD,
-                transcendentals=count * rows * 320,
+                flops=40 * heads * near_part * 256 * HD * 4,
+                bytes_accessed=9 * near_part * wide,
+                transcendentals=heads * near_part * 256,
             ),
-            name="far",
-        )(
-            window[0],
-            global_blocks[0],
-            picks,
-            keys_cache[0],
-            values_cache[0],
-            *came,
-        )
-
-    far = far_call()
-    ahead = min(3, seq_count - 1)
-    handed = [linked(shard, 1, steps) for shard, steps in zip(far[:-1], zip(*there))]
-    both = pl.pallas_call(
-        functools.partial(near_kernel, there),
-        out_shape=jax.ShapeDtypeStruct((rows + STAT_ROWS, wide + HD), bf16),
-        in_specs=[whole_vmem] * (5 + seq_count) + [anywhere] * ahead,
-        out_specs=whole_vmem,
-        compiler_params=params(queries),
-        cost_estimate=pl.CostEstimate(
-            flops=40 * heads * rows * 256 * HD * 4,
-            bytes_accessed=9 * rows * wide,
-            transcendentals=heads * rows * 256,
-        ),
-        name="near",
-    )(
-        queries[0],
-        keys_new[0],
-        values_new[0],
-        before,
-        far[-1],
-        *came,
-        *handed[:ahead],
-    )
-
-    handed.append(linked(both, 1, [0, 0]))
+            name=name,
+        )(queries[0], keys_new[0], values_new[0], *operands)
+
+    packed_rows = -(-(rows + STAT_ROWS) // (STAT_ROWS * heads)) * STAT_ROWS
+    inner_part = near_call(
+        near_inner_kernel, "near_inner", rows - halo, rows - halo + STAT_ROWS + packed_rows,
+        far[-1], *came,
+    )
+    edge_part = near_call(
+        near_edge_kernel, "near_edge", halo, halo + STAT_ROWS, before, *came, *handed[:2]
+    )
+    handed_inner = linked(inner_part, 1, [0, 0])
+    handed_edge = linked(edge_part, 1, [0, 0])
 
     merged = pl.pallas_call(
         functools.partial(merge_kernel, there),
         out_shape=jax.ShapeDtypeStruct((rows, wide), bf16),
-        in_specs=[whole_vmem] * seq_count,
+        in_specs=[whole_vmem] * (1 + seq_count),
         out_specs=whole_vmem,
+        scratch_shapes=[pltpu.VMEM(chunk_shape.shape, bf16)],
         compiler_params=params(queries),
         cost_estimate=pl.CostEstimate(flops=0, bytes_accessed=6 * rows * wide, transcendentals=0),
         name="merge",
-    )(*handed)
+    )(handed_edge, handed_inner, *handed)
     return merged[None]
 
 

time: 60.6 us -> 57.7 us (0.952)
  waiting for transfers between devices: 16.2 us -> 13.2 us
  starting transfers between devices: 31.7 us -> 30.5 us
  Pallas kernels: 8.26 us -> 9 us
    ppermute x15 -> x16, waiting for transfers between devices: 16.2 us -> 13.2 us  [linked(): return lax.ppermute(shard, ('section', 'seq'), pairs)]
    ppermute x15 -> x16, starting transfers between devices: 28.1 us -> 27 us  [linked(): return lax.ppermute(shard, ('section', 'seq'), pairs)]
    pallas_call x3 -> x4, Pallas kernels: 6.94 us -> 7.63 us  [the longest x1 4.07 us: per_device(): pl.pallas_call(functools.partial(far_kernel, there), out_shape=[chunk_sha...]
  transfers between devices with their start and end apart: 16 -> 17, of which waited for: 7 -> 7; matrix products, arithmetic and copies ran while one was open for 2% -> 2% of each run, Pallas kernels for 7% -> 13%
where the time goes in v7:
time: 57.7 us; the launch traced here: 57 us
  starting transfers between devices  30.5 us (53%)
  waiting for transfers between devices  13.2 us (23%)
  Pallas kernels  9 us (16%)
  local copies, waits for them, and re-layouts  3.39 us (6%)
  between operations  0.82 us (1%)
    ppermute x16, starting transfers between devices, linked(): return lax.ppermute(shard, ('section', 'seq'), pairs)  27 us
    ppermute x16, waiting for transfers between devices, linked(): return lax.ppermute(shard, ('section', 'seq'), pairs)  13.2 us
    pallas_call x1, Pallas kernels, per_device(): pl.pallas_call(functools.partial(far_kernel, there), out_shape=[chunk_sha...  4.07 us
    ppermute x1, starting transfers between devices, per_device(): lax.ppermute(mine, 'seq', [(i, i + 1) for i in range(seq_count - 1)])  3.54 us
    pallas_call x2, Pallas kernels, near_call(): pl.pallas_call(functools.partial(kernel, there), out_shape=jax.ShapeDtype...  3.29 us
    unnamed x15, local copies, waits for them, and re-layouts  3.27 us
    pallas_call x1, Pallas kernels, per_device(): pl.pallas_call(functools.partial(merge_kernel, there), out_shape=jax.Shap...  1.37 us
  transfers between devices with their start and end apart: 17, of which 7 were waited for; matrix products, arithmetic and copies ran while one was open for 2% of the time, Pallas kernels for 13%

profile of v7, /device:TPU:0, one launch (start us, length us, event | category | flops | bytes accessed | tf_op | source)
XLA Modules:
  0.0 57.0 jit_solution(18132830743450739634)
XLA Ops:
  0.7 1.1 %copy-done = bf16[1,320,1024]{2,1,0:T(8,128)(2,1)S(1)} copy-done((bf16[1,320,1024]{2,1,0:T(8,128)(2,1)S(1)}, bf16[1,320,1024]{2,1,0:T(8,128)(2,1)}, u32[]{:S(2)}) %copy-start) | copy-done | bytes 655384
  1.8 0.3 split.1
  2.0 6.1 %collective-permute-start.1 = (bf16[336,128]{1,0:T(8,128)(2,1)S(1)}, bf16[336,128]{1,0:T(8,128)(2,1)S(1)}, u32[]{:S(2)}, u32[]{:S(2)}) collective-permute-start(bf16[336,128]{1,0:T(8,128)(2,1)S(1)} %get-tuple-element.21), channel_id=1, source_target_pairs={{0,7},{1,6},{2,5},{3,4},{4,3},{5,2},{6,1},{7,0},{8,9},{9,8},{10,11... | collective-permute-start | bytes 258056 | tf_op jit(solution)/shard_map/ppermute | solution.py:298
  8.1 0.2 collective-permute-start.2
  8.3 0.7 %collective-permute-start.3 = (bf16[336,128]{1,0:T(8,128)(2,1)S(1)}, bf16[336,128]{1,0:T(8,128)(2,1)S(1)}, u32[]{:S(2)}, u32[]{:S(2)}) collective-permute-start(bf16[336,128]{1,0:T(8,128)(2,1)S(1)} %get-tuple-element.23), channel_id=1, source_target_pairs={{0,5},{1,4},{2,7},{3,6},{4,1},{5,0},{6,3},{7,2},{8,11},{9,10},{10,... | collective-permute-start | bytes 258056 | tf_op jit(solution)/shard_map/ppermute | solution.py:298
  9.1 2.0 %collective-permute-start.4 = (bf16[336,128]{1,0:T(8,128)(2,1)S(1)}, bf16[336,128]{1,0:T(8,128)(2,1)S(1)}, u32[]{:S(2)}, u32[]{:S(2)}) collective-permute-start(bf16[336,128]{1,0:T(8,128)(2,1)S(1)} %get-tuple-element.24), channel_id=1, source_target_pairs={{0,4},{1,5},{2,6},{3,7},{4,0},{5,1},{6,2},{7,3},{8,15},{9,14},{10,... | collective-permute-start | bytes 258056 | tf_op jit(solution)/shard_map/ppermute | solution.py:298
  11.1 1.6 %collective-permute-start.5 = (bf16[336,128]{1,0:T(8,128)(2,1)S(1)}, bf16[336,128]{1,0:T(8,128)(2,1)S(1)}, u32[]{:S(2)}, u32[]{:S(2)}) collective-permute-start(bf16[336,128]{1,0:T(8,128)(2,1)S(1)} %get-tuple-element.25), channel_id=1, source_target_pairs={{0,1},{1,0},{2,3},{3,2},{4,5},{5,4},{6,7},{7,6},{8,14},{9,15},{10,... | collective-permute-start | bytes 258056 | tf_op jit(solution)/shard_map/ppermute | solution.py:298
  12.7 0.8 %copy.10 = s32[1,40,3]{2,1,0:T(8,128)S(1)} copy(s32[1,40,3]{1,0,2:T(1,128)} %param.15) | data formatting | bytes 960 | tf_op args[7]
  13.5 0.1 reshape_squeeze.3.random_ref
  13.6 1.3 %collective-permute-start.6 = (bf16[336,128]{1,0:T(8,128)(2,1)S(1)}, bf16[336,128]{1,0:T(8,128)(2,1)S(1)}, u32[]{:S(2)}, u32[]{:S(2)}) collective-permute-start(bf16[336,128]{1,0:T(8,128)(2,1)S(1)} %get-tuple-element.26), channel_id=1, source_target_pairs={{0,2},{1,3},{2,0},{3,1},{4,6},{5,7},{6,4},{7,5},{8,13},{9,12},{10,... | collective-permute-start | bytes 258056 | tf_op jit(solution)/shard_map/ppermute | solution.py:298
  14.9 4.0 %collective-permute-start.7 = (bf16[336,128]{1,0:T(8,128)(2,1)S(1)}, bf16[336,128]{1,0:T(8,128)(2,1)S(1)}, u32[]{:S(2)}, u32[]{:S(2)}) collective-permute-start(bf16[336,128]{1,0:T(8,128)(2,1)S(1)} %get-tuple-element.27), channel_id=1, source_target_pairs={{0,3},{1,2},{2,1},{3,0},{4,7},{5,6},{6,5},{7,4},{8,12},{9,13},{10,... | collective-permute-start | bytes 258056 | tf_op jit(solution)/shard_map/ppermute | solution.py:298
  19.0 2.2 %collective-permute-done.3.refs_2_ = bf16[336,128]{1,0:T(8,128)(2,1)S(1)} collective-permute-done((bf16[336,128]{1,0:T(8,128)(2,1)S(1)}, bf16[336,128]{1,0:T(8,128)(2,1)S(1)}, u32[]{:S(2)}, u32[]{:S(2)}) %collective-permute-start.3) | collective-permute-done | bytes 86048 | tf_op jit(solution)/shard_map/ppermute | solution.py:298
  21.3 3.5 %collective-permute-start = (bf16[2,128,1024]{2,1,0:T(8,128)(2,1)S(1)}, bf16[2,128,1024]{2,1,0:T(8,128)(2,1)S(1)}, u32[]{:S(2)}, u32[]{:S(2)}) collective-permute-start(bf16[2,128,1024]{2,1,0:T(8,128)(2,1)S(1)} %pad_maximum_fusion), channel_id=1, source_target_pairs={{0,1},{1,2},{2,3},{3,4},{4,5},{5,6},{6,7},{8,9},{9,10},{10,11},{11... | collective-permute-start | bytes 1572872 | tf_op jit(solution)/shard_map/ppermute | solution.py:303
  24.9 1.4 %copy-done.5 = bf16[1,6144,128]{2,1,0:T(8,128)(2,1)S(1)} copy-done((bf16[1,6144,128]{2,1,0:T(8,128)(2,1)S(1)}, bf16[1,6144,128]{2,1,0:T(8,128)(2,1)}, u32[]{:S(2)}) %copy-start.5) | copy-done | bytes 1572888
  26.3 4.1 %far.1 = (bf16[336,128]{1,0:T(8,128)(2,1)S(1)}, bf16[336,128]{1,0:T(8,128)(2,1)S(1)}, bf16[336,128]{1,0:T(8,128)(2,1)S(1)}, bf16[336,128]{1,0:T(8,128)(2,1)S(1)}...) custom-call(s32[1]{0:T(128)} %bitcast.9.span_ref, ...), custom_call_target="tpu_custom_call" | custom-call | flops 16777216000 | bytes 4456448 | tf_op jit(solution)/shard_map/far/pallas_call | solution.py:307
  30.4 1.2 %collective-permute-start.8 = (bf16[336,128]{1,0:T(8,128)(2,1)S(1)}, bf16[336,128]{1,0:T(8,128)(2,1)S(1)}, u32[]{:S(2)}, u32[]{:S(2)}) collective-permute-start(bf16[336,128]{1,0:T(8,128)(2,1)S(1)} %get-tuple-element.29), channel_id=1, source_target_pairs={{0,15},{1,14},{2,13},{3,12},{4,11},{5,10},{6,9},{7,8},{8,17},{9,16... | collective-permute-start | bytes 258056 | tf_op jit(solution)/shard_map/ppermute | solution.py:298
  31.6 2.7 %collective-permute-start.9 = (bf16[336,128]{1,0:T(8,128)(2,1)S(1)}, bf16[336,128]{1,0:T(8,128)(2,1)S(1)}, u32[]{:S(2)}, u32[]{:S(2)}) collective-permute-start(bf16[336,128]{1,0:T(8,128)(2,1)S(1)} %get-tuple-element.30), channel_id=1, source_target_pairs={{0,14},{1,15},{2,12},{3,13},{4,10},{5,11},{6,8},{7,9},{8,18},{9,19... | collective-permute-start | bytes 258056 | tf_op jit(solution)/shard_map/ppermute | solution.py:298
  34.3 2.3 %near_inner.1 = bf16[256,1024]{1,0:T(8,128)(2,1)S(1)} custom-call(bf16[320,1024]{1,0:T(8,128)(2,1)S(1)} %bitcast.11, bf16[320,1024]{1,0:T(8,128)(2,1)S(1)} %bitcast.13, bf16[320,1024]{1,0:T(8,128)(2,1)S(1)} %bitcast.15, bf16[336,128]{1,0:T(8,128)(2,1)S(1)} %get-tuple-element.31.own_ref, bf16[336,128]{1,0:T(8,128)(2,1)S(1)} %collective-permute-done.1.refs_0_, ...), custom_call_target="tpu_custom_call" | custom-call | flops 8053063680 | bytes 1769472 | tf_op jit(solution)/shard_map/near_inner/pallas_call | solution.py:323
  36.6 0.1 collective-permute-start.11
  36.7 0.5 collective-permute-done.9.refs_9_.refs_1_
  37.2 1.0 %near_edge.1 = bf16[144,1024]{1,0:T(8,128)(2,1)S(1)} custom-call(bf16[320,1024]{1,0:T(8,128)(2,1)S(1)} %bitcast.12, bf16[320,1024]{1,0:T(8,128)(2,1)S(1)} %bitcast.14, bf16[320,1024]{1,0:T(8,128)(2,1)S(1)} %bitcast.16, bf16[2,128,1024]{2,1,0:T(8,128)(2,1)S(1)} %collective-permute-done.halo_ref, bf16[336,128]{1,0:T(8,128)(2,1)S(1)} %collective-permute-done.1.refs_0_, ...), custom_call_target="tpu_custom_call" | custom-call | flops 5368709120 | bytes 1179648 | tf_op jit(solution)/shard_map/near_edge/pallas_call | solution.py:323
  38.2 1.7 %collective-permute-start.10 = (bf16[144,1024]{1,0:T(8,128)(2,1)S(1)}, bf16[144,1024]{1,0:T(8,128)(2,1)S(1)}, u32[]{:S(2)}, u32[]{:S(2)}) collective-permute-start(bf16[144,1024]{1,0:T(8,128)(2,1)S(1)} %near_edge.1), channel_id=1, source_target_pairs={{0,8},{1,9},{2,10},{3,11},{4,12},{5,13},{6,14},{7,15},{8,16},{9,17... | collective-permute-start | bytes 884744 | tf_op jit(solution)/shard_map/ppermute | solution.py:298
  39.9 2.0 %collective-permute-start.12 = (bf16[336,128]{1,0:T(8,128)(2,1)S(1)}, bf16[336,128]{1,0:T(8,128)(2,1)S(1)}, u32[]{:S(2)}, u32[]{:S(2)}) collective-permute-start(bf16[336,128]{1,0:T(8,128)(2,1)S(1)} %get-tuple-element.32), channel_id=1, source_target_pairs={{0,13},{1,12},{2,15},{3,14},{4,9},{5,8},{6,11},{7,10},{8,19},{9,18... | collective-permute-start | bytes 258056 | tf_op jit(solution)/shard_map/ppermute | solution.py:298
  41.8 0.7 %collective-permute-start.13 = (bf16[336,128]{1,0:T(8,128)(2,1)S(1)}, bf16[336,128]{1,0:T(8,128)(2,1)S(1)}, u32[]{:S(2)}, u32[]{:S(2)}) collective-permute-start(bf16[336,128]{1,0:T(8,128)(2,1)S(1)} %get-tuple-element.33), channel_id=1, source_target_pairs={{0,12},{1,13},{2,14},{3,15},{4,8},{5,9},{6,10},{7,11},{8,23},{9,22... | collective-permute-start | bytes 258056 | tf_op jit(solution)/shard_map/ppermute | solution.py:298
  42.5 2.4 %collective-permute-start.14 = (bf16[336,128]{1,0:T(8,128)(2,1)S(1)}, bf16[336,128]{1,0:T(8,128)(2,1)S(1)}, u32[]{:S(2)}, u32[]{:S(2)}) collective-permute-start(bf16[336,128]{1,0:T(8,128)(2,1)S(1)} %get-tuple-element.34), channel_id=1, source_target_pairs={{0,9},{1,8},{2,11},{3,10},{4,13},{5,12},{6,15},{7,14},{8,22},{9,23... | collective-permute-start | bytes 258056 | tf_op jit(solution)/shard_map/ppermute | solution.py:298
  44.9 1.2 %collective-permute-done.12.refs_2_ = bf16[336,128]{1,0:T(8,128)(2,1)S(1)} collective-permute-done((bf16[336,128]{1,0:T(8,128)(2,1)S(1)}, bf16[336,128]{1,0:T(8,128)(2,1)S(1)}, u32[]{:S(2)}, u32[]{:S(2)}) %collective-permute-start.12) | collective-permute-done | bytes 86048 | tf_op jit(solution)/shard_map/ppermute | solution.py:298
  46.1 3.4 %collective-permute-done.13.refs_3_ = bf16[336,128]{1,0:T(8,128)(2,1)S(1)} collective-permute-done((bf16[336,128]{1,0:T(8,128)(2,1)S(1)}, bf16[336,128]{1,0:T(8,128)(2,1)S(1)}, u32[]{:S(2)}, u32[]{:S(2)}) %collective-permute-start.13) | collective-permute-done | bytes 86048 | tf_op jit(solution)/shard_map/ppermute | solution.py:298
  49.5 0.3 collective-permute-start.16
  49.8 0.3 collective-permute-done.14.refs_4_
  50.1 2.9 %collective-permute-done.15.refs_5_ = bf16[336,128]{1,0:T(8,128)(2,1)S(1)} collective-permute-done((bf16[336,128]{1,0:T(8,128)(2,1)S(1)}, bf16[336,128]{1,0:T(8,128)(2,1)S(1)}, u32[]{:S(2)}, u32[]{:S(2)}) %collective-permute-start.15) | collective-permute-done | bytes 86048 | tf_op jit(solution)/shard_map/ppermute | solution.py:298
  53.0 2.6 %collective-permute-done.16.refs_6_ = bf16[336,128]{1,0:T(8,128)(2,1)S(1)} collective-permute-done((bf16[336,128]{1,0:T(8,128)(2,1)S(1)}, bf16[336,128]{1,0:T(8,128)(2,1)S(1)}, u32[]{:S(2)}, u32[]{:S(2)}) %collective-permute-start.16) | collective-permute-done | bytes 86048 | tf_op jit(solution)/shard_map/ppermute | solution.py:298
  55.6 1.4 %merge.1 = bf16[320,1024]{1,0:T(8,128)(2,1)} custom-call(bf16[144,1024]{1,0:T(8,128)(2,1)S(1)} %collective-permute-done.10.edge_ref, bf16[256,1024]{1,0:T(8,128)(2,1)S(1)} %collective-permute-done.11.inner_ref, bf16[336,128]{1,0:T(8,128)(2,1)S(1)} %collective-permute-done.8.refs_8_.refs_0_, bf16[336,128]{1,0:T(8,128)(2,1)S(1)} %collective-permute-done.9.refs_9_.refs_1_, ...), custom_call_target="tpu_custom_call" | custom-call | bytes 1966080 | tf_op jit(solution)/shard_map/merge/pallas_call | solution.py:351
  (28 shorter events, 0.1 us)
Async XLA Ops:
  0.0 24.8 %copy-start.6 = (s32[1,2]{1,0:T(1,128)S(1)}, s32[1,2]{1,0:T(1,128)}, u32[]{:S(2)}) copy-start(s32[1,2]{1,0:T(1,128)} %param.14) | copy-start | bytes 28
  0.7 1.1 %copy-start = (bf16[1,320,1024]{2,1,0:T(8,128)(2,1)S(1)}, bf16[1,320,1024]{2,1,0:T(8,128)(2,1)}, u32[]{:S(2)}) copy-start(bf16[1,320,1024]{2,1,0:T(8,128)(2,1)} %param.8) | copy-start | bytes 1966084
  1.8 17.2 %slice-start = ((bf16[1,320,1024]{2,1,0:T(8,128)(2,1)}), bf16[1,128,1024]{2,1,0:T(8,128)(2,1)S(1)}, s32[]{:S(2)}) async-start(bf16[1,320,1024]{2,1,0:T(8,128)(2,1)} %param.9), calls=%async_computation | async-start | bytes 524288 | tf_op jit(solution)/shard_map/slice | solution.py:302
  1.8 17.2 %slice-start.1 = ((bf16[1,320,1024]{2,1,0:T(8,128)(2,1)}), bf16[1,128,1024]{2,1,0:T(8,128)(2,1)S(1)}, s32[]{:S(2)}) async-start(bf16[1,320,1024]{2,1,0:T(8,128)(2,1)} %param.10), calls=%async_computation.1 | async-start | bytes 524288 | tf_op jit(solution)/shard_map/slice | solution.py:302
  1.8 23.1 %copy-start.4 = (bf16[1,6144,128]{2,1,0:T(8,128)(2,1)S(1)}, bf16[1,6144,128]{2,1,0:T(8,128)(2,1)}, u32[]{:S(2)}) copy-start(bf16[1,6144,128]{2,1,0:T(8,128)(2,1)} %param.11) | copy-start | bytes 4718596
  2.0 11.6 %collective-permute-start.1 = (bf16[336,128]{1,0:T(8,128)(2,1)S(1)}, bf16[336,128]{1,0:T(8,128)(2,1)S(1)}, u32[]{:S(2)}, u32[]{:S(2)}) collective-permute-start(bf16[336,128]{1,0:T(8,128)(2,1)S(1)} %get-tuple-element.21), channel_id=1, source_target_pairs={{0,7},{1,6},{2,5},{3,4},{4,3},{5,2},{6,1},{7,0},{8,9},{9,8},{10,11... | collective-permute-start | bytes 258056 | tf_op jit(solution)/shard_map/ppermute | solution.py:298
  8.1 6.8 %collective-permute-start.2 = (bf16[336,128]{1,0:T(8,128)(2,1)S(1)}, bf16[336,128]{1,0:T(8,128)(2,1)S(1)}, u32[]{:S(2)}, u32[]{:S(2)}) collective-permute-start(bf16[336,128]{1,0:T(8,128)(2,1)S(1)} %get-tuple-element.22), channel_id=1, source_target_pairs={{0,6},{1,7},{2,4},{3,5},{4,2},{5,3},{6,0},{7,1},{8,10},{9,11},{10,... | collective-permute-start | bytes 258056 | tf_op jit(solution)/shard_map/ppermute | solution.py:298
  8.3 12.9 %collective-permute-start.3 = (bf16[336,128]{1,0:T(8,128)(2,1)S(1)}, bf16[336,128]{1,0:T(8,128)(2,1)S(1)}, u32[]{:S(2)}, u32[]{:S(2)}) collective-permute-start(bf16[336,128]{1,0:T(8,128)(2,1)S(1)} %get-tuple-element.23), channel_id=1, source_target_pairs={{0,5},{1,4},{2,7},{3,6},{4,1},{5,0},{6,3},{7,2},{8,11},{9,10},{10,... | collective-permute-start | bytes 258056 | tf_op jit(solution)/shard_map/ppermute | solution.py:298
  9.1 15.7 %collective-permute-start.4 = (bf16[336,128]{1,0:T(8,128)(2,1)S(1)}, bf16[336,128]{1,0:T(8,128)(2,1)S(1)}, u32[]{:S(2)}, u32[]{:S(2)}) collective-permute-start(bf16[336,128]{1,0:T(8,128)(2,1)S(1)} %get-tuple-element.24), channel_id=1, source_target_pairs={{0,4},{1,5},{2,6},{3,7},{4,0},{5,1},{6,2},{7,3},{8,15},{9,14},{10,... | collective-permute-start | bytes 258056 | tf_op jit(solution)/shard_map/ppermute | solution.py:298
  11.1 13.7 %collective-permute-start.5 = (bf16[336,128]{1,0:T(8,128)(2,1)S(1)}, bf16[336,128]{1,0:T(8,128)(2,1)S(1)}, u32[]{:S(2)}, u32[]{:S(2)}) collective-permute-start(bf16[336,128]{1,0:T(8,128)(2,1)S(1)} %get-tuple-element.25), channel_id=1, source_target_pairs={{0,1},{1,0},{2,3},{3,2},{4,5},{5,4},{6,7},{7,6},{8,14},{9,15},{10,... | collective-permute-start | bytes 258056 | tf_op jit(solution)/shard_map/ppermute | solution.py:298
  13.6 11.2 %collective-permute-start.6 = (bf16[336,128]{1,0:T(8,128)(2,1)S(1)}, bf16[336,128]{1,0:T(8,128)(2,1)S(1)}, u32[]{:S(2)}, u32[]{:S(2)}) collective-permute-start(bf16[336,128]{1,0:T(8,128)(2,1)S(1)} %get-tuple-element.26), channel_id=1, source_target_pairs={{0,2},{1,3},{2,0},{3,1},{4,6},{5,7},{6,4},{7,5},{8,13},{9,12},{10,... | collective-permute-start | bytes 258056 | tf_op jit(solution)/shard_map/ppermute | solution.py:298
  14.9 9.9 %collective-permute-start.7 = (bf16[336,128]{1,0:T(8,128)(2,1)S(1)}, bf16[336,128]{1,0:T(8,128)(2,1)S(1)}, u32[]{:S(2)}, u32[]{:S(2)}) collective-permute-start(bf16[336,128]{1,0:T(8,128)(2,1)S(1)} %get-tuple-element.27), channel_id=1, source_target_pairs={{0,3},{1,2},{2,1},{3,0},{4,7},{5,6},{6,5},{7,4},{8,12},{9,13},{10,... | collective-permute-start | bytes 258056 | tf_op jit(solution)/shard_map/ppermute | solution.py:298
  21.3 16.0 %collective-permute-start = (bf16[2,128,1024]{2,1,0:T(8,128)(2,1)S(1)}, bf16[2,128,1024]{2,1,0:T(8,128)(2,1)S(1)}, u32[]{:S(2)}, u32[]{:S(2)}) collective-permute-start(bf16[2,128,1024]{2,1,0:T(8,128)(2,1)S(1)} %pad_maximum_fusion), channel_id=1, source_target_pairs={{0,1},{1,2},{2,3},{3,4},{4,5},{5,6},{6,7},{8,9},{9,10},{10,11},{11... | collective-permute-start | bytes 1572872 | tf_op jit(solution)/shard_map/ppermute | solution.py:303
  24.9 1.4 %copy-start.5 = (bf16[1,6144,128]{2,1,0:T(8,128)(2,1)S(1)}, bf16[1,6144,128]{2,1,0:T(8,128)(2,1)}, u32[]{:S(2)}) copy-start(bf16[1,6144,128]{2,1,0:T(8,128)(2,1)} %param.12) | copy-start | bytes 4718596
  26.3 8.0 %copy-start.1 = (bf16[1,320,1024]{2,1,0:T(8,128)(2,1)S(1)}, bf16[1,320,1024]{2,1,0:T(8,128)(2,1)}, u32[]{:S(2)}) copy-start(bf16[1,320,1024]{2,1,0:T(8,128)(2,1)} %param.8) | copy-start | bytes 1966084
  26.3 8.0 %copy-start.2 = (bf16[1,320,1024]{2,1,0:T(8,128)(2,1)S(1)}, bf16[1,320,1024]{2,1,0:T(8,128)(2,1)}, u32[]{:S(2)}) copy-start(bf16[1,320,1024]{2,1,0:T(8,128)(2,1)} %param.9) | copy-start | bytes 1966084
  26.3 8.0 %copy-start.3 = (bf16[1,320,1024]{2,1,0:T(8,128)(2,1)S(1)}, bf16[1,320,1024]{2,1,0:T(8,128)(2,1)}, u32[]{:S(2)}) copy-start(bf16[1,320,1024]{2,1,0:T(8,128)(2,1)} %param.10) | copy-start | bytes 1966084
  30.4 6.3 %collective-permute-start.8 = (bf16[336,128]{1,0:T(8,128)(2,1)S(1)}, bf16[336,128]{1,0:T(8,128)(2,1)S(1)}, u32[]{:S(2)}, u32[]{:S(2)}) collective-permute-start(bf16[336,128]{1,0:T(8,128)(2,1)S(1)} %get-tuple-element.29), channel_id=1, source_target_pairs={{0,15},{1,14},{2,13},{3,12},{4,11},{5,10},{6,9},{7,8},{8,17},{9,16... | collective-permute-start | bytes 258056 | tf_op jit(solution)/shard_map/ppermute | solution.py:298
  31.6 5.6 %collective-permute-start.9 = (bf16[336,128]{1,0:T(8,128)(2,1)S(1)}, bf16[336,128]{1,0:T(8,128)(2,1)S(1)}, u32[]{:S(2)}, u32[]{:S(2)}) collective-permute-start(bf16[336,128]{1,0:T(8,128)(2,1)S(1)} %get-tuple-element.30), channel_id=1, source_target_pairs={{0,14},{1,15},{2,12},{3,13},{4,10},{5,11},{6,8},{7,9},{8,18},{9,19... | collective-permute-start | bytes 258056 | tf_op jit(solution)/shard_map/ppermute | solution.py:298
  36.6 19.0 %collective-permute-start.11 = (bf16[256,1024]{1,0:T(8,128)(2,1)S(1)}, bf16[256,1024]{1,0:T(8,128)(2,1)S(1)}, u32[]{:S(2)}, u32[]{:S(2)}) collective-permute-start(bf16[256,1024]{1,0:T(8,128)(2,1)S(1)} %near_inner.1), channel_id=1, source_target_pairs={{0,8},{1,9},{2,10},{3,11},{4,12},{5,13},{6,14},{7,15},{8,16},{9,17... | collective-permute-start | bytes 1572872 | tf_op jit(solution)/shard_map/ppermute | solution.py:298
  38.2 17.4 %collective-permute-start.10 = (bf16[144,1024]{1,0:T(8,128)(2,1)S(1)}, bf16[144,1024]{1,0:T(8,128)(2,1)S(1)}, u32[]{:S(2)}, u32[]{:S(2)}) collective-permute-start(bf16[144,1024]{1,0:T(8,128)(2,1)S(1)} %near_edge.1), channel_id=1, source_target_pairs={{0,8},{1,9},{2,10},{3,11},{4,12},{5,13},{6,14},{7,15},{8,16},{9,17... | collective-permute-start | bytes 884744 | tf_op jit(solution)/shard_map/ppermute | solution.py:298
  39.9 6.2 %collective-permute-start.12 = (bf16[336,128]{1,0:T(8,128)(2,1)S(1)}, bf16[336,128]{1,0:T(8,128)(2,1)S(1)}, u32[]{:S(2)}, u32[]{:S(2)}) collective-permute-start(bf16[336,128]{1,0:T(8,128)(2,1)S(1)} %get-tuple-element.32), channel_id=1, source_target_pairs={{0,13},{1,12},{2,15},{3,14},{4,9},{5,8},{6,11},{7,10},{8,19},{9,18... | collective-permute-start | bytes 258056 | tf_op jit(solution)/shard_map/ppermute | solution.py:298
  41.8 7.6 %collective-permute-start.13 = (bf16[336,128]{1,0:T(8,128)(2,1)S(1)}, bf16[336,128]{1,0:T(8,128)(2,1)S(1)}, u32[]{:S(2)}, u32[]{:S(2)}) collective-permute-start(bf16[336,128]{1,0:T(8,128)(2,1)S(1)} %get-tuple-element.33), channel_id=1, source_target_pairs={{0,12},{1,13},{2,14},{3,15},{4,8},{5,9},{6,10},{7,11},{8,23},{9,22... | collective-permute-start | bytes 258056 | tf_op jit(solution)/shard_map/ppermute | solution.py:298
  42.5 7.5 %collective-permute-start.14 = (bf16[336,128]{1,0:T(8,128)(2,1)S(1)}, bf16[336,128]{1,0:T(8,128)(2,1)S(1)}, u32[]{:S(2)}, u32[]{:S(2)}) collective-permute-start(bf16[336,128]{1,0:T(8,128)(2,1)S(1)} %get-tuple-element.34), channel_id=1, source_target_pairs={{0,9},{1,8},{2,11},{3,10},{4,13},{5,12},{6,15},{7,14},{8,22},{9,23... | collective-permute-start | bytes 258056 | tf_op jit(solution)/shard_map/ppermute | solution.py:298
  46.1 6.9 %collective-permute-start.15 = (bf16[336,128]{1,0:T(8,128)(2,1)S(1)}, bf16[336,128]{1,0:T(8,128)(2,1)S(1)}, u32[]{:S(2)}, u32[]{:S(2)}) collective-permute-start(bf16[336,128]{1,0:T(8,128)(2,1)S(1)} %get-tuple-element.35), channel_id=1, source_target_pairs={{0,10},{1,11},{2,8},{3,9},{4,14},{5,15},{6,12},{7,13},{8,21},{9,20... | collective-permute-start | bytes 258056 | tf_op jit(solution)/shard_map/ppermute | solution.py:298
  49.5 6.2 %collective-permute-start.16 = (bf16[336,128]{1,0:T(8,128)(2,1)S(1)}, bf16[336,128]{1,0:T(8,128)(2,1)S(1)}, u32[]{:S(2)}, u32[]{:S(2)}) collective-permute-start(bf16[336,128]{1,0:T(8,128)(2,1)S(1)} %get-tuple-element.36), channel_id=1, source_target_pairs={{0,11},{1,10},{2,9},{3,8},{4,15},{5,14},{6,13},{7,12},{8,20},{9,21... | collective-permute-start | bytes 258056 | tf_op jit(solution)/shard_map/ppermute | solution.py:298

commit v8 on v7

--- a/solution.py
+++ b/solution.py
@@ -110,8 +110,12 @@
         copy.wait()
 
 
+def halo_kernel(rows_ref, _, out_ref):
+    out_ref[...] = rows_ref[...]
+
+
 def far_kernel(
-    there, span_ref, global_ref, random_ref, key_ref, value_ref, *refs
+    there, chosen, span_ref, global_ref, random_ref, key_ref, value_ref, *refs
 ):
     span = span_ref[0]
     last = key_ref.shape[0] // BLK - 1
@@ -123,7 +127,7 @@
 
     glob_keys = [block(key_ref, global_ref[g]) for g in range(GLOB)]
     glob_values = [block(value_ref, global_ref[g]) for g in range(GLOB)]
-    peers = peers_of(there, 0)
+    peers = [peers_of(there, 0)[at] for at in chosen]
     query_refs, out_refs = refs[: len(peers)], refs[len(peers) :]
     rows = query_refs[0].shape[0] - STAT_ROWS
     for chunk, query_ref, out_ref in zip(peers, query_refs, out_refs):
@@ -170,35 +174,44 @@
     halo = (WMAX - 1) * BLK
     starts = list(range(first, last, 2 * BLK))
     sizes = [min(2 * BLK, last - start) for start in starts]
-    for peer, came_ref in zip(peers_of(there, 0), came_refs):
-        lanes = pl.ds(pl.multiple_of(peer * HD, HD), HD)
-        width = came_ref[rows:, :].astype(jnp.float32)[:1]
-        width = jnp.concatenate([width] * ((2 * BLK + halo) // LANES), axis=1)
+    leads = [
+        halo if start < halo else min(-(-(size + halo) // LANES) * LANES - size, start)
+        for start, size in zip(starts, sizes)
+    ]
+    peers = peers_of(there, 0)
+    for begin in range(0, len(peers), 2):
+        pair = range(begin, min(begin + 2, len(peers)))
+        all_lanes = [pl.ds(pl.multiple_of(peers[at] * HD, HD), HD) for at in pair]
         all_scores, all_values = [], []
-        for start, size in zip(starts, sizes):
-            query = query_ref[start : start + size, lanes]
-            if start < halo:
-                keys = [halo_ref[0, start:, lanes], key_ref[: start + size, lanes]]
-                values = [halo_ref[1, start:, lanes], value_ref[: start + size, lanes]]
-                keys, values = jnp.concatenate(keys, axis=0), jnp.concatenate(values, axis=0)
-            else:
-                keys = key_ref[start - halo : start + size, lanes]
-                values = value_ref[start - halo : start + size, lanes]
-            scores = scores_of(query, keys)
-            row_at = lax.broadcasted_iota(jnp.int32, scores.shape, 0)
-            lane_at = lax.broadcasted_iota(jnp.int32, scores.shape, 1)
-            slot = (lane_at // BLK - row_at // BLK).astype(jnp.float32)
-            allowed = (lane_at <= row_at + halo) & (slot + width[:, : size + halo] >= WMAX)
-            if start < halo:
-                closed = jnp.where(lax.axis_index("seq") == 0, halo - start, 0)
-                allowed = allowed & (lane_at >= closed)
-            all_scores.append(jnp.where(allowed, scores, MASKED))
-            all_values.append(values)
+        for at, lanes in zip(pair, all_lanes):
+            width = came_refs[at][rows:, :].astype(jnp.float32)[:1]
+            width = jnp.concatenate([width] * ((2 * BLK + halo) // LANES), axis=1)
+            for start, size, lead in zip(starts, sizes, leads):
+                query = query_ref[start : start + size, lanes]
+                if start < lead:
+                    keys = [halo_ref[0, start:, lanes], key_ref[: start + size, lanes]]
+                    values = [halo_ref[1, start:, lanes], value_ref[: start + size, lanes]]
+                    keys, values = jnp.concatenate(keys, axis=0), jnp.concatenate(values, axis=0)
+                else:
+                    keys = key_ref[start - lead : start + size, lanes]
+                    values = value_ref[start - lead : start + size, lanes]
+                scores = scores_of(query, keys)
+                row_at = lax.broadcasted_iota(jnp.int32, scores.shape, 0)
+                lane_at = lax.broadcasted_iota(jnp.int32, scores.shape, 1)
+                slot = (lane_at // BLK - row_at // BLK - lead // BLK).astype(jnp.float32)
+                allowed = (lane_at <= row_at + lead) & (slot + width[:, : size + lead] >= 1.0)
+                if start < lead:
+                    closed = jnp.where(lax.axis_index("seq") == 0, lead - start, 0)
+                    allowed = allowed & (lane_at >= closed)
+                all_scores.append(jnp.where(allowed, scores, MASKED))
+                all_values.append(values)
         parts, lses = softmax_parts(all_scores, all_values)
-        tile = stat_tile([as_row(lse, 0) for lse in lses])
-        for start, size, part in zip(starts, sizes, parts):
-            out_ref[start - first : start - first + size, lanes] = part
-        out_ref[last - first : last - first + STAT_ROWS, lanes] = tile
+        for index, lanes in enumerate(all_lanes):
+            own = slice(index * len(starts), (index + 1) * len(starts))
+            tile = stat_tile([as_row(lse, 0) for lse in lses[own]])
+            for start, size, part in zip(starts, sizes, parts[own]):
+                out_ref[start - first : start - first + size, lanes] = part
+            out_ref[last - first : last - first + STAT_ROWS, lanes] = tile
 
 
 def packed_at(index, first, wide):
@@ -299,24 +312,60 @@
 
     came = [linked(shard, 0, steps) for shard, steps in zip(sent[:-1], zip(*there))]
     came.append(sent[-1])
-    mine = jnp.stack([keys_new[0, rows - halo :], values_new[0, rows - halo :]])
+    def linked(shard, by, steps):
+        pairs = [
+            (
+                s * seq_count + t,
+                (s + by) % section_count * seq_count + (t ^ steps[s % 2]),
+            )
+            for s in range(section_count)
+            for t in range(seq_count)
+        ]
+        return lax.ppermute(shard, ("section", "seq"), pairs)
+
+    came = [linked(shard, 0, steps) for shard, steps in zip(sent[:-1], zip(*there))]
+    came.append(sent[-1])
+    mine = pl.pallas_call(
+        halo_kernel,
+        out_shape=jax.ShapeDtypeStruct((2, halo, wide), bf16),
+        in_specs=[whole_vmem, anywhere],
+        out_specs=whole_vmem,
+        compiler_params=params(queries),
+        name="halo",
+    )(jnp.stack([keys_new[0, rows - halo :], values_new[0, rows - halo :]]), came[0])
     before = lax.ppermute(mine, "seq", [(i, i + 1) for i in range(seq_count - 1)])
 
     picks = random_blocks[0].reshape(-1)
 
-    far = pl.pallas_call(
-        functools.partial(far_kernel, there),
-        out_shape=[chunk_shape] * seq_count,
-        in_specs=[whole_smem] * 3 + [whole_vmem] * (2 + seq_count),
-        out_specs=[whole_vmem] * seq_count,
-        compiler_params=params(queries),
-        cost_estimate=pl.CostEstimate(
-            flops=40 * seq_count * rows * 320 * HD * 4,
-            bytes_accessed=2 * 2 * keys_cache.shape[1] * HD + 4 * seq_count * rows * HD,
-            transcendentals=seq_count * rows * 320,
-        ),
-        name="far",
-    )(window[0], global_blocks[0], picks, keys_cache[0], values_cache[0], *came)
+    def far_call(chosen):
+        count = len(chosen)
+        return pl.pallas_call(
+            functools.partial(far_kernel, there, chosen),
+            out_shape=[chunk_shape] * count,
+            in_specs=[whole_smem] * 3 + [whole_vmem] * (2 + count),
+            out_specs=[whole_vmem] * count,
+            compiler_params=params(queries),
+            cost_estimate=pl.CostEstimate(
+                flops=40 * count * rows * 320 * HD * 4,
+                bytes_accessed=2 * 2 * keys_cache.shape[1] * HD + 4 * count * rows * HD,
+                transcendentals=count * rows * 320,
+            ),
+            name="far",
+        )(
+            window[0],
+            global_blocks[0],
+            picks,
+            keys_cache[0],
+            values_cache[0],
+            *[came[at] for at in chosen],
+        )
+
+    late = list(range(seq_count - 1 - seq_count // 4, seq_count - 1))
+    early = [at for at in range(seq_count) if at not in late]
+    far = dict(zip(early, far_call(early)))
+    if late:
+        far.update(zip(late, far_call(late)))
+    far = [far[at] for at in range(seq_count)]
     handed = [linked(shard, 1, steps) for shard, steps in zip(far[:-1], zip(*there))]
 
     def near_call(kernel, name, near_part, out_rows, *operands):

time: 57.7 us -> 58.3 us (1.010)
  the two profiles are of different devices: /device:TPU:0 before, /device:TPU:1 now
where the time goes in v8:
time: 58.3 us; the launch traced here: 58.2 us
  starting transfers between devices  42.1 us (72%)
  Pallas kernels  9.17 us (16%)
  waiting for transfers between devices  4.64 us (8%)
  local copies, waits for them, and re-layouts  1.33 us (2%)
  between operations  0.89 us (2%)
    ppermute x16, starting transfers between devices, linked(): return lax.ppermute(shard, ('section', 'seq'), pairs)  39 us
    pallas_call x2, Pallas kernels, far_call(): pl.pallas_call(functools.partial(far_kernel, there, chosen), out_shape=[c...  4.73 us
    ppermute x16, waiting for transfers between devices, linked(): return lax.ppermute(shard, ('section', 'seq'), pairs)  4.64 us
    ppermute x1, starting transfers between devices, per_device(): lax.ppermute(mine, 'seq', [(i, i + 1) for i in range(seq_count - 1)])  3.11 us
    pallas_call x2, Pallas kernels, near_call(): pl.pallas_call(functools.partial(kernel, there), out_shape=jax.ShapeDtype...  2.78 us
    pallas_call x1, Pallas kernels, per_device(): pl.pallas_call(functools.partial(merge_kernel, there), out_shape=jax.Shap...  1.36 us
    unnamed x17, local copies, waits for them, and re-layouts  1.21 us
  transfers between devices with their start and end apart: 17, of which 2 were waited for; matrix products, arithmetic and copies ran while one was open for 0% of the time, Pallas kernels for 13%

profile of v8, /device:TPU:1, one launch (start us, length us, event | category | flops | bytes accessed | tf_op | source)
XLA Modules:
  0.0 58.2 jit_solution(16562980143101115489)
XLA Ops:
  0.7 0.0 copy-start
  0.7 1.1 %copy-done = bf16[1,320,1024]{2,1,0:T(8,128)(2,1)S(1)} copy-done((bf16[1,320,1024]{2,1,0:T(8,128)(2,1)S(1)}, bf16[1,320,1024]{2,1,0:T(8,128)(2,1)}, u32[]{:S(2)}) %copy-start) | copy-done | bytes 655384
  1.8 0.3 split.1
  2.0 2.1 %collective-permute-start = (bf16[336,128]{1,0:T(8,128)(2,1)S(1)}, bf16[336,128]{1,0:T(8,128)(2,1)S(1)}, u32[]{:S(2)}, u32[]{:S(2)}) collective-permute-start(bf16[336,128]{1,0:T(8,128)(2,1)S(1)} %get-tuple-element.21), channel_id=1, source_target_pairs={{0,7},{1,6},{2,5},{3,4},{4,3},{5,2},{6,1},{7,0},{8,9},{9,8},{10,11... | collective-permute-start | bytes 258056 | tf_op jit(solution)/shard_map/ppermute | solution.py:324
  4.2 1.3 %collective-permute-start.2 = (bf16[336,128]{1,0:T(8,128)(2,1)S(1)}, bf16[336,128]{1,0:T(8,128)(2,1)S(1)}, u32[]{:S(2)}, u32[]{:S(2)}) collective-permute-start(bf16[336,128]{1,0:T(8,128)(2,1)S(1)} %get-tuple-element.22), channel_id=1, source_target_pairs={{0,6},{1,7},{2,4},{3,5},{4,2},{5,3},{6,0},{7,1},{8,10},{9,11},{10,... | collective-permute-start | bytes 258056 | tf_op jit(solution)/shard_map/ppermute | solution.py:324
  5.5 4.4 %collective-permute-start.4 = (bf16[336,128]{1,0:T(8,128)(2,1)S(1)}, bf16[336,128]{1,0:T(8,128)(2,1)S(1)}, u32[]{:S(2)}, u32[]{:S(2)}) collective-permute-start(bf16[336,128]{1,0:T(8,128)(2,1)S(1)} %get-tuple-element.24), channel_id=1, source_target_pairs={{0,4},{1,5},{2,6},{3,7},{4,0},{5,1},{6,2},{7,3},{8,15},{9,14},{10,... | collective-permute-start | bytes 258056 | tf_op jit(solution)/shard_map/ppermute | solution.py:324
  9.9 0.0 collective-permute-start.5
  9.9 0.1 copy.10
  10.0 0.1 reshape_squeeze.3.random_ref
  10.1 0.0 copy-start.5
  10.1 0.1 pad_maximum_fusion.rows_ref
  10.2 0.5 collective-permute-start.6
  10.7 2.0 %collective-permute-start.7 = (bf16[336,128]{1,0:T(8,128)(2,1)S(1)}, bf16[336,128]{1,0:T(8,128)(2,1)S(1)}, u32[]{:S(2)}, u32[]{:S(2)}) collective-permute-start(bf16[336,128]{1,0:T(8,128)(2,1)S(1)} %get-tuple-element.27), channel_id=1, source_target_pairs={{0,3},{1,2},{2,1},{3,0},{4,7},{5,6},{6,5},{7,4},{8,12},{9,13},{10,... | collective-permute-start | bytes 258056 | tf_op jit(solution)/shard_map/ppermute | solution.py:324
  12.7 3.1 %collective-permute-start.1 = (bf16[2,128,1024]{2,1,0:T(8,128)(2,1)S(1)}, bf16[2,128,1024]{2,1,0:T(8,128)(2,1)S(1)}, u32[]{:S(2)}, u32[]{:S(2)}) collective-permute-start(bf16[2,128,1024]{2,1,0:T(8,128)(2,1)S(1)} %halo.1), channel_id=1, source_target_pairs={{0,1},{1,2},{2,3},{3,4},{4,5},{5,6},{6,7},{8,9},{9,10},{10,11},{11... | collective-permute-start | bytes 1572872 | tf_op jit(solution)/shard_map/ppermute | solution.py:336
  15.9 0.0 copy-start.1
  15.9 0.0 copy-start.2
  15.9 0.0 copy-start.3
  15.9 3.2 %far.2 = (bf16[336,128]{1,0:T(8,128)(2,1)S(1)}, bf16[336,128]{1,0:T(8,128)(2,1)S(1)}, bf16[336,128]{1,0:T(8,128)(2,1)S(1)}, bf16[336,128]{1,0:T(8,128)(2,1)S(1)}...) custom-call(s32[1]{0:T(128)} %bitcast.9.span_ref, s32[2]{0:T(128)S(1)} %bitcast.22, ...), custom_call_target="tpu_custom_call" | custom-call | flops 12582912000 | bytes 4128768 | tf_op jit(solution)/shard_map/far/pallas_call | solution.py:342
  19.2 9.7 %collective-permute-start.8 = (bf16[336,128]{1,0:T(8,128)(2,1)S(1)}, bf16[336,128]{1,0:T(8,128)(2,1)S(1)}, u32[]{:S(2)}, u32[]{:S(2)}) collective-permute-start(bf16[336,128]{1,0:T(8,128)(2,1)S(1)} %get-tuple-element.29), channel_id=1, source_target_pairs={{0,15},{1,14},{2,13},{3,12},{4,11},{5,10},{6,9},{7,8},{8,17},{9,16... | collective-permute-start | bytes 258056 | tf_op jit(solution)/shard_map/ppermute | solution.py:324
  28.9 1.5 %near_inner.1 = bf16[256,1024]{1,0:T(8,128)(2,1)S(1)} custom-call(bf16[320,1024]{1,0:T(8,128)(2,1)S(1)} %bitcast.12, bf16[320,1024]{1,0:T(8,128)(2,1)S(1)} %bitcast.14, bf16[320,1024]{1,0:T(8,128)(2,1)S(1)} %bitcast.16, bf16[336,128]{1,0:T(8,128)(2,1)S(1)} %get-tuple-element.31.own_ref, bf16[336,128]{1,0:T(8,128)(2,1)S(1)} %collective-permute-done._.refs_0_, ...), custom_call_target="tpu_custom_call" | custom-call | flops 8053063680 | bytes 1769472 | tf_op jit(solution)/shard_map/near_inner/pallas_call | solution.py:372
  30.4 1.2 %collective-permute-start.11 = (bf16[256,1024]{1,0:T(8,128)(2,1)S(1)}, bf16[256,1024]{1,0:T(8,128)(2,1)S(1)}, u32[]{:S(2)}, u32[]{:S(2)}) collective-permute-start(bf16[256,1024]{1,0:T(8,128)(2,1)S(1)} %near_inner.1), channel_id=1, source_target_pairs={{0,8},{1,9},{2,10},{3,11},{4,12},{5,13},{6,14},{7,15},{8,16},{9,17... | collective-permute-start | bytes 1572872 | tf_op jit(solution)/shard_map/ppermute | solution.py:324
  31.5 0.5 collective-permute-start.12
  32.0 5.0 %collective-permute-start.13 = (bf16[336,128]{1,0:T(8,128)(2,1)S(1)}, bf16[336,128]{1,0:T(8,128)(2,1)S(1)}, u32[]{:S(2)}, u32[]{:S(2)}) collective-permute-start(bf16[336,128]{1,0:T(8,128)(2,1)S(1)} %get-tuple-element.33), channel_id=1, source_target_pairs={{0,12},{1,13},{2,14},{3,15},{4,8},{5,9},{6,10},{7,11},{8,23},{9,22... | collective-permute-start | bytes 258056 | tf_op jit(solution)/shard_map/ppermute | solution.py:324
  37.0 1.1 %collective-permute-start.14 = (bf16[336,128]{1,0:T(8,128)(2,1)S(1)}, bf16[336,128]{1,0:T(8,128)(2,1)S(1)}, u32[]{:S(2)}, u32[]{:S(2)}) collective-permute-start(bf16[336,128]{1,0:T(8,128)(2,1)S(1)} %get-tuple-element.34), channel_id=1, source_target_pairs={{0,9},{1,8},{2,11},{3,10},{4,13},{5,12},{6,15},{7,14},{8,22},{9,23... | collective-permute-start | bytes 258056 | tf_op jit(solution)/shard_map/ppermute | solution.py:324
  38.2 1.3 %near_edge.1 = bf16[144,1024]{1,0:T(8,128)(2,1)S(1)} custom-call(bf16[320,1024]{1,0:T(8,128)(2,1)S(1)} %bitcast.13, bf16[320,1024]{1,0:T(8,128)(2,1)S(1)} %bitcast.15, bf16[320,1024]{1,0:T(8,128)(2,1)S(1)} %bitcast.17, bf16[2,128,1024]{2,1,0:T(8,128)(2,1)S(1)} %collective-permute-done.1.halo_ref, bf16[336,128]{1,0:T(8,128)(2,1)S(1)} %collective-permute-done._.refs_0_, ...), custom_call_target="tpu_custom_call" | custom-call | flops 5368709120 | bytes 1179648 | tf_op jit(solution)/shard_map/near_edge/pallas_call | solution.py:372
  39.4 8.4 %collective-permute-start.10 = (bf16[144,1024]{1,0:T(8,128)(2,1)S(1)}, bf16[144,1024]{1,0:T(8,128)(2,1)S(1)}, u32[]{:S(2)}, u32[]{:S(2)}) collective-permute-start(bf16[144,1024]{1,0:T(8,128)(2,1)S(1)} %near_edge.1), channel_id=1, source_target_pairs={{0,8},{1,9},{2,10},{3,11},{4,12},{5,13},{6,14},{7,15},{8,16},{9,17... | collective-permute-start | bytes 884744 | tf_op jit(solution)/shard_map/ppermute | solution.py:324
  47.8 1.5 %far.3 = (bf16[336,128]{1,0:T(8,128)(2,1)S(1)}, bf16[336,128]{1,0:T(8,128)(2,1)S(1)}) custom-call(s32[1]{0:T(128)} %bitcast.10.span_ref, s32[2]{0:T(128)S(1)} %bitcast.23, s32[120]{0:T(128)S(1)} %reshape_squeeze.3.random_ref, bf16[6144,128]{1,0:T(8,128)(2,1)S(1)} %bitcast.19, bf16[6144,128]{1,0:T(8,128)(2,1)S(1)} %bitcast.21, ...), custom_call_target="tpu_custom_call" | custom-call | flops 4194304000 | bytes 3473408 | tf_op jit(solution)/shard_map/far/pallas_call | solution.py:342
  49.3 1.5 %collective-permute-start.15 = (bf16[336,128]{1,0:T(8,128)(2,1)S(1)}, bf16[336,128]{1,0:T(8,128)(2,1)S(1)}, u32[]{:S(2)}, u32[]{:S(2)}) collective-permute-start(bf16[336,128]{1,0:T(8,128)(2,1)S(1)} %get-tuple-element.35), channel_id=1, source_target_pairs={{0,10},{1,11},{2,8},{3,9},{4,14},{5,15},{6,12},{7,13},{8,21},{9,20... | collective-permute-start | bytes 258056 | tf_op jit(solution)/shard_map/ppermute | solution.py:324
  50.8 1.4 %collective-permute-start.16 = (bf16[336,128]{1,0:T(8,128)(2,1)S(1)}, bf16[336,128]{1,0:T(8,128)(2,1)S(1)}, u32[]{:S(2)}, u32[]{:S(2)}) collective-permute-start(bf16[336,128]{1,0:T(8,128)(2,1)S(1)} %get-tuple-element.36), channel_id=1, source_target_pairs={{0,11},{1,10},{2,9},{3,8},{4,15},{5,14},{6,13},{7,12},{8,20},{9,21... | collective-permute-start | bytes 258056 | tf_op jit(solution)/shard_map/ppermute | solution.py:324
  52.2 2.6 %collective-permute-done.15.refs_5_ = bf16[336,128]{1,0:T(8,128)(2,1)S(1)} collective-permute-done((bf16[336,128]{1,0:T(8,128)(2,1)S(1)}, bf16[336,128]{1,0:T(8,128)(2,1)S(1)}, u32[]{:S(2)}, u32[]{:S(2)}) %collective-permute-start.15) | collective-permute-done | bytes 86048 | tf_op jit(solution)/shard_map/ppermute | solution.py:324
  54.8 2.0 %collective-permute-done.16.refs_6_ = bf16[336,128]{1,0:T(8,128)(2,1)S(1)} collective-permute-done((bf16[336,128]{1,0:T(8,128)(2,1)S(1)}, bf16[336,128]{1,0:T(8,128)(2,1)S(1)}, u32[]{:S(2)}, u32[]{:S(2)}) %collective-permute-start.16) | collective-permute-done | bytes 86048 | tf_op jit(solution)/shard_map/ppermute | solution.py:324
  56.8 1.4 %merge.1 = bf16[320,1024]{1,0:T(8,128)(2,1)} custom-call(bf16[144,1024]{1,0:T(8,128)(2,1)S(1)} %collective-permute-done.10.edge_ref, bf16[256,1024]{1,0:T(8,128)(2,1)S(1)} %collective-permute-done.11.inner_ref, bf16[336,128]{1,0:T(8,128)(2,1)S(1)} %collective-permute-done.8.refs_8_.refs_0_, bf16[336,128]{1,0:T(8,128)(2,1)S(1)} %collective-permute-done.9.refs_9_.refs_1_, ...), custom_call_target="tpu_custom_call" | custom-call | bytes 1966080 | tf_op jit(solution)/shard_map/merge/pallas_call | solution.py:400
  (32 shorter events, 0.1 us)
Async XLA Ops:
  0.0 9.9 %copy-start.7 = (s32[1,40,3]{1,0,2:T(1,128)S(1)}, s32[1,40,3]{1,0,2:T(1,128)}, u32[]{:S(2)}) copy-start(s32[1,40,3]{1,0,2:T(1,128)} %param.15) | copy-start | bytes 1444
  0.7 1.1 %copy-start = (bf16[1,320,1024]{2,1,0:T(8,128)(2,1)S(1)}, bf16[1,320,1024]{2,1,0:T(8,128)(2,1)}, u32[]{:S(2)}) copy-start(bf16[1,320,1024]{2,1,0:T(8,128)(2,1)} %param.8) | copy-start | bytes 1966084
  1.8 8.3 %slice-start = ((bf16[1,320,1024]{2,1,0:T(8,128)(2,1)}), bf16[1,128,1024]{2,1,0:T(8,128)(2,1)S(1)}, s32[]{:S(2)}) async-start(bf16[1,320,1024]{2,1,0:T(8,128)(2,1)} %param.9), calls=%async_computation | async-start | bytes 524288 | tf_op jit(solution)/shard_map/slice | solution.py:335
  1.8 8.3 %slice-start.1 = ((bf16[1,320,1024]{2,1,0:T(8,128)(2,1)}), bf16[1,128,1024]{2,1,0:T(8,128)(2,1)S(1)}, s32[]{:S(2)}) async-start(bf16[1,320,1024]{2,1,0:T(8,128)(2,1)} %param.10), calls=%async_computation.1 | async-start | bytes 524288 | tf_op jit(solution)/shard_map/slice | solution.py:335
  2.0 8.1 %collective-permute-start = (bf16[336,128]{1,0:T(8,128)(2,1)S(1)}, bf16[336,128]{1,0:T(8,128)(2,1)S(1)}, u32[]{:S(2)}, u32[]{:S(2)}) collective-permute-start(bf16[336,128]{1,0:T(8,128)(2,1)S(1)} %get-tuple-element.21), channel_id=1, source_target_pairs={{0,7},{1,6},{2,5},{3,4},{4,3},{5,2},{6,1},{7,0},{8,9},{9,8},{10,11... | collective-permute-start | bytes 258056 | tf_op jit(solution)/shard_map/ppermute | solution.py:324
  4.2 6.5 %collective-permute-start.2 = (bf16[336,128]{1,0:T(8,128)(2,1)S(1)}, bf16[336,128]{1,0:T(8,128)(2,1)S(1)}, u32[]{:S(2)}, u32[]{:S(2)}) collective-permute-start(bf16[336,128]{1,0:T(8,128)(2,1)S(1)} %get-tuple-element.22), channel_id=1, source_target_pairs={{0,6},{1,7},{2,4},{3,5},{4,2},{5,3},{6,0},{7,1},{8,10},{9,11},{10,... | collective-permute-start | bytes 258056 | tf_op jit(solution)/shard_map/ppermute | solution.py:324
  5.5 7.3 %collective-permute-start.3 = (bf16[336,128]{1,0:T(8,128)(2,1)S(1)}, bf16[336,128]{1,0:T(8,128)(2,1)S(1)}, u32[]{:S(2)}, u32[]{:S(2)}) collective-permute-start(bf16[336,128]{1,0:T(8,128)(2,1)S(1)} %get-tuple-element.23), channel_id=1, source_target_pairs={{0,5},{1,4},{2,7},{3,6},{4,1},{5,0},{6,3},{7,2},{8,11},{9,10},{10,... | collective-permute-start | bytes 258056 | tf_op jit(solution)/shard_map/ppermute | solution.py:324
  5.5 10.4 %collective-permute-start.4 = (bf16[336,128]{1,0:T(8,128)(2,1)S(1)}, bf16[336,128]{1,0:T(8,128)(2,1)S(1)}, u32[]{:S(2)}, u32[]{:S(2)}) collective-permute-start(bf16[336,128]{1,0:T(8,128)(2,1)S(1)} %get-tuple-element.24), channel_id=1, source_target_pairs={{0,4},{1,5},{2,6},{3,7},{4,0},{5,1},{6,2},{7,3},{8,15},{9,14},{10,... | collective-permute-start | bytes 258056 | tf_op jit(solution)/shard_map/ppermute | solution.py:324
  9.9 6.0 %copy-start.4 = (bf16[1,6144,128]{2,1,0:T(8,128)(2,1)S(1)}, bf16[1,6144,128]{2,1,0:T(8,128)(2,1)}, u32[]{:S(2)}) copy-start(bf16[1,6144,128]{2,1,0:T(8,128)(2,1)} %param.11) | copy-start | bytes 4718596
  9.9 6.0 %copy-start.6 = (s32[1,2]{1,0:T(1,128)S(1)}, s32[1,2]{1,0:T(1,128)}, u32[]{:S(2)}) copy-start(s32[1,2]{1,0:T(1,128)} %param.14) | copy-start | bytes 28
  9.9 6.0 %collective-permute-start.5 = (bf16[336,128]{1,0:T(8,128)(2,1)S(1)}, bf16[336,128]{1,0:T(8,128)(2,1)S(1)}, u32[]{:S(2)}, u32[]{:S(2)}) collective-permute-start(bf16[336,128]{1,0:T(8,128)(2,1)S(1)} %get-tuple-element.25), channel_id=1, source_target_pairs={{0,1},{1,0},{2,3},{3,2},{4,5},{5,4},{6,7},{7,6},{8,14},{9,15},{10,... | collective-permute-start | bytes 258056 | tf_op jit(solution)/shard_map/ppermute | solution.py:324
  10.1 5.8 %copy-start.5 = (bf16[1,6144,128]{2,1,0:T(8,128)(2,1)S(1)}, bf16[1,6144,128]{2,1,0:T(8,128)(2,1)}, u32[]{:S(2)}) copy-start(bf16[1,6144,128]{2,1,0:T(8,128)(2,1)} %param.12) | copy-start | bytes 4718596
  10.2 18.6 %collective-permute-start.6 = (bf16[336,128]{1,0:T(8,128)(2,1)S(1)}, bf16[336,128]{1,0:T(8,128)(2,1)S(1)}, u32[]{:S(2)}, u32[]{:S(2)}) collective-permute-start(bf16[336,128]{1,0:T(8,128)(2,1)S(1)} %get-tuple-element.26), channel_id=1, source_target_pairs={{0,2},{1,3},{2,0},{3,1},{4,6},{5,7},{6,4},{7,5},{8,13},{9,12},{10,... | collective-permute-start | bytes 258056 | tf_op jit(solution)/shard_map/ppermute | solution.py:324
  10.7 18.1 %collective-permute-start.7 = (bf16[336,128]{1,0:T(8,128)(2,1)S(1)}, bf16[336,128]{1,0:T(8,128)(2,1)S(1)}, u32[]{:S(2)}, u32[]{:S(2)}) collective-permute-start(bf16[336,128]{1,0:T(8,128)(2,1)S(1)} %get-tuple-element.27), channel_id=1, source_target_pairs={{0,3},{1,2},{2,1},{3,0},{4,7},{5,6},{6,5},{7,4},{8,12},{9,13},{10,... | collective-permute-start | bytes 258056 | tf_op jit(solution)/shard_map/ppermute | solution.py:324
  12.7 25.4 %collective-permute-start.1 = (bf16[2,128,1024]{2,1,0:T(8,128)(2,1)S(1)}, bf16[2,128,1024]{2,1,0:T(8,128)(2,1)S(1)}, u32[]{:S(2)}, u32[]{:S(2)}) collective-permute-start(bf16[2,128,1024]{2,1,0:T(8,128)(2,1)S(1)} %halo.1), channel_id=1, source_target_pairs={{0,1},{1,2},{2,3},{3,4},{4,5},{5,6},{6,7},{8,9},{9,10},{10,11},{11... | collective-permute-start | bytes 1572872 | tf_op jit(solution)/shard_map/ppermute | solution.py:336
  15.9 12.9 %copy-start.1 = (bf16[1,320,1024]{2,1,0:T(8,128)(2,1)S(1)}, bf16[1,320,1024]{2,1,0:T(8,128)(2,1)}, u32[]{:S(2)}) copy-start(bf16[1,320,1024]{2,1,0:T(8,128)(2,1)} %param.8) | copy-start | bytes 1966084
  15.9 12.9 %copy-start.2 = (bf16[1,320,1024]{2,1,0:T(8,128)(2,1)S(1)}, bf16[1,320,1024]{2,1,0:T(8,128)(2,1)}, u32[]{:S(2)}) copy-start(bf16[1,320,1024]{2,1,0:T(8,128)(2,1)} %param.9) | copy-start | bytes 1966084
  15.9 12.9 %copy-start.3 = (bf16[1,320,1024]{2,1,0:T(8,128)(2,1)S(1)}, bf16[1,320,1024]{2,1,0:T(8,128)(2,1)}, u32[]{:S(2)}) copy-start(bf16[1,320,1024]{2,1,0:T(8,128)(2,1)} %param.10) | copy-start | bytes 1966084
  19.2 12.9 %collective-permute-start.8 = (bf16[336,128]{1,0:T(8,128)(2,1)S(1)}, bf16[336,128]{1,0:T(8,128)(2,1)S(1)}, u32[]{:S(2)}, u32[]{:S(2)}) collective-permute-start(bf16[336,128]{1,0:T(8,128)(2,1)S(1)} %get-tuple-element.29), channel_id=1, source_target_pairs={{0,15},{1,14},{2,13},{3,12},{4,11},{5,10},{6,9},{7,8},{8,17},{9,16... | collective-permute-start | bytes 258056 | tf_op jit(solution)/shard_map/ppermute | solution.py:324
  28.8 8.2 %collective-permute-start.9 = (bf16[336,128]{1,0:T(8,128)(2,1)S(1)}, bf16[336,128]{1,0:T(8,128)(2,1)S(1)}, u32[]{:S(2)}, u32[]{:S(2)}) collective-permute-start(bf16[336,128]{1,0:T(8,128)(2,1)S(1)} %get-tuple-element.30), channel_id=1, source_target_pairs={{0,14},{1,15},{2,12},{3,13},{4,10},{5,11},{6,8},{7,9},{8,18},{9,19... | collective-permute-start | bytes 258056 | tf_op jit(solution)/shard_map/ppermute | solution.py:324
  30.4 26.4 %collective-permute-start.11 = (bf16[256,1024]{1,0:T(8,128)(2,1)S(1)}, bf16[256,1024]{1,0:T(8,128)(2,1)S(1)}, u32[]{:S(2)}, u32[]{:S(2)}) collective-permute-start(bf16[256,1024]{1,0:T(8,128)(2,1)S(1)} %near_inner.1), channel_id=1, source_target_pairs={{0,8},{1,9},{2,10},{3,11},{4,12},{5,13},{6,14},{7,15},{8,16},{9,17... | collective-permute-start | bytes 1572872 | tf_op jit(solution)/shard_map/ppermute | solution.py:324
  31.5 17.8 %collective-permute-start.12 = (bf16[336,128]{1,0:T(8,128)(2,1)S(1)}, bf16[336,128]{1,0:T(8,128)(2,1)S(1)}, u32[]{:S(2)}, u32[]{:S(2)}) collective-permute-start(bf16[336,128]{1,0:T(8,128)(2,1)S(1)} %get-tuple-element.32), channel_id=1, source_target_pairs={{0,13},{1,12},{2,15},{3,14},{4,9},{5,8},{6,11},{7,10},{8,19},{9,18... | collective-permute-start | bytes 258056 | tf_op jit(solution)/shard_map/ppermute | solution.py:324
  32.0 18.8 %collective-permute-start.13 = (bf16[336,128]{1,0:T(8,128)(2,1)S(1)}, bf16[336,128]{1,0:T(8,128)(2,1)S(1)}, u32[]{:S(2)}, u32[]{:S(2)}) collective-permute-start(bf16[336,128]{1,0:T(8,128)(2,1)S(1)} %get-tuple-element.33), channel_id=1, source_target_pairs={{0,12},{1,13},{2,14},{3,15},{4,8},{5,9},{6,10},{7,11},{8,23},{9,22... | collective-permute-start | bytes 258056 | tf_op jit(solution)/shard_map/ppermute | solution.py:324
  37.0 15.1 %collective-permute-start.14 = (bf16[336,128]{1,0:T(8,128)(2,1)S(1)}, bf16[336,128]{1,0:T(8,128)(2,1)S(1)}, u32[]{:S(2)}, u32[]{:S(2)}) collective-permute-start(bf16[336,128]{1,0:T(8,128)(2,1)S(1)} %get-tuple-element.34), channel_id=1, source_target_pairs={{0,9},{1,8},{2,11},{3,10},{4,13},{5,12},{6,15},{7,14},{8,22},{9,23... | collective-permute-start | bytes 258056 | tf_op jit(solution)/shard_map/ppermute | solution.py:324
  39.4 17.3 %collective-permute-start.10 = (bf16[144,1024]{1,0:T(8,128)(2,1)S(1)}, bf16[144,1024]{1,0:T(8,128)(2,1)S(1)}, u32[]{:S(2)}, u32[]{:S(2)}) collective-permute-start(bf16[144,1024]{1,0:T(8,128)(2,1)S(1)} %near_edge.1), channel_id=1, source_target_pairs={{0,8},{1,9},{2,10},{3,11},{4,12},{5,13},{6,14},{7,15},{8,16},{9,17... | collective-permute-start | bytes 884744 | tf_op jit(solution)/shard_map/ppermute | solution.py:324
  49.3 5.4 %collective-permute-start.15 = (bf16[336,128]{1,0:T(8,128)(2,1)S(1)}, bf16[336,128]{1,0:T(8,128)(2,1)S(1)}, u32[]{:S(2)}, u32[]{:S(2)}) collective-permute-start(bf16[336,128]{1,0:T(8,128)(2,1)S(1)} %get-tuple-element.35), channel_id=1, source_target_pairs={{0,10},{1,11},{2,8},{3,9},{4,14},{5,15},{6,12},{7,13},{8,21},{9,20... | collective-permute-start | bytes 258056 | tf_op jit(solution)/shard_map/ppermute | solution.py:324
  50.8 6.0 %collective-permute-start.16 = (bf16[336,128]{1,0:T(8,128)(2,1)S(1)}, bf16[336,128]{1,0:T(8,128)(2,1)S(1)}, u32[]{:S(2)}, u32[]{:S(2)}) collective-permute-start(bf16[336,128]{1,0:T(8,128)(2,1)S(1)} %get-tuple-element.36), channel_id=1, source_target_pairs={{0,11},{1,10},{2,9},{3,8},{4,15},{5,14},{6,13},{7,12},{8,20},{9,21... | collective-permute-start | bytes 258056 | tf_op jit(solution)/shard_map/ppermute | solution.py:324

commit v9 on v8

--- a/solution.py
+++ b/solution.py
@@ -230,9 +230,10 @@
         out_ref[at] = own_ref[index * STAT_ROWS : (index + 1) * STAT_ROWS, :]
 
 
-def near_edge_kernel(there, query_ref, key_ref, value_ref, halo_ref, *refs):
+def near_edge_kernel(there, query_ref, key_ref, value_ref, odd_ref, even_ref, *refs):
     halo = (WMAX - 1) * BLK
-    came_refs, out_ref = refs[: len(there[0])], refs[-1]
+    came_refs, out_ref, halo_ref = refs[: len(there[0])], refs[-2], refs[-1]
+    halo_ref[...] = odd_ref[...] + even_ref[...]
     near_rows(there, 0, halo, query_ref, key_ref, value_ref, halo_ref, came_refs, out_ref)
 
 
@@ -325,16 +326,25 @@
 
     came = [linked(shard, 0, steps) for shard, steps in zip(sent[:-1], zip(*there))]
     came.append(sent[-1])
-    mine = pl.pallas_call(
-        halo_kernel,
-        out_shape=jax.ShapeDtypeStruct((2, halo, wide), bf16),
-        in_specs=[whole_vmem, anywhere],
-        out_specs=whole_vmem,
-        compiler_params=params(queries),
-        name="halo",
-    )(jnp.stack([keys_new[0, rows - halo :], values_new[0, rows - halo :]]), came[0])
-    before = lax.ppermute(mine, "seq", [(i, i + 1) for i in range(seq_count - 1)])
-
+    tails = jnp.stack([keys_new[0, rows - halo :], values_new[0, rows - halo :]])
+
+    def halo_from(parity, after):
+        mine = tails if after is None else pl.pallas_call(
+            halo_kernel,
+            out_shape=jax.ShapeDtypeStruct(tails.shape, bf16),
+            in_specs=[whole_vmem, anywhere],
+            out_specs=whole_vmem,
+            compiler_params=params(queries),
+            name="halo",
+        )(tails, after)
+        pairs = [
+            (s * seq_count + t, s * seq_count + t + 1)
+            for s in range(parity, section_count, 2)
+            for t in range(seq_count - 1)
+        ]
+        return lax.ppermute(mine, ("section", "seq"), pairs)
+
+    halos = [halo_from(1, None), halo_from(0, came[0])]
     picks = random_blocks[0].reshape(-1)
 
     def far_call(chosen):
@@ -368,15 +378,16 @@
     far = [far[at] for at in range(seq_count)]
     handed = [linked(shard, 1, steps) for shard, steps in zip(far[:-1], zip(*there))]
 
-    def near_call(kernel, name, near_part, out_rows, *operands):
+    def near_call(kernel, name, near_part, out_rows, vmem_count, scratch, *operands):
         return pl.pallas_call(
             functools.partial(kernel, there),
             out_shape=jax.ShapeDtypeStruct((out_rows, wide), bf16),
             in_specs=[
-                whole_vmem if index < 4 + seq_count else anywhere
+                whole_vmem if index < 3 + vmem_count else anywhere
                 for index in range(3 + len(operands))
             ],
             out_specs=whole_vmem,
+            scratch_shapes=scratch,
             compiler_params=params(queries),
             cost_estimate=pl.CostEstimate(
                 flops=40 * heads * near_part * 256 * HD * 4,
@@ -389,10 +400,11 @@
     packed_rows = -(-(rows + STAT_ROWS) // (STAT_ROWS * heads)) * STAT_ROWS
     inner_part = near_call(
         near_inner_kernel, "near_inner", rows - halo, rows - halo + STAT_ROWS + packed_rows,
-        far[-1], *came,
+        1 + seq_count, [], far[-1], *came,
     )
     edge_part = near_call(
-        near_edge_kernel, "near_edge", halo, halo + STAT_ROWS, before, *came, *handed[:2]
+        near_edge_kernel, "near_edge", halo, halo + STAT_ROWS,
+        2 + seq_count, [pltpu.VMEM(tails.shape, bf16)], *halos, *came, *handed[:2],
     )
     handed_inner = linked(inner_part, 1, [0, 0])
     handed_edge = linked(edge_part, 1, [0, 0])

time: 58.3 us -> 54.3 us (0.931)
  the two profiles are of different devices: /device:TPU:1 before, /device:TPU:0 now
where the time goes in v9:
time: 54.3 us; the launch traced here: 54.1 us
  starting transfers between devices  31.6 us (58%)
  waiting for transfers between devices  11 us (20%)
  Pallas kernels  9.22 us (17%)
  local copies, waits for them, and re-layouts  1.33 us (2%)
  between operations  0.88 us (2%)
    ppermute x16, starting transfers between devices, linked(): return lax.ppermute(shard, ('section', 'seq'), pairs)  28.6 us
    ppermute x16, waiting for transfers between devices, linked(): return lax.ppermute(shard, ('section', 'seq'), pairs)  11 us
    pallas_call x2, Pallas kernels, far_call(): pl.pallas_call(functools.partial(far_kernel, there, chosen), out_shape=[c...  4.71 us
    ppermute x2, starting transfers between devices, halo_from(): return lax.ppermute(mine, ('section', 'seq'), pairs)  3.06 us
    pallas_call x2, Pallas kernels, near_call(): pl.pallas_call(functools.partial(kernel, there), out_shape=jax.ShapeDtype...  2.84 us
    pallas_call x1, Pallas kernels, per_device(): pl.pallas_call(functools.partial(merge_kernel, there), out_shape=jax.Shap...  1.36 us
    unnamed x17, local copies, waits for them, and re-layouts  1.21 us
  transfers between devices with their start and end apart: 18, of which 5 were waited for; matrix products, arithmetic and copies ran while one was open for 0% of the time, Pallas kernels for 14%

profile of v9, /device:TPU:0, one launch (start us, length us, event | category | flops | bytes accessed | tf_op | source)
XLA Modules:
  0.0 54.1 jit_solution(16145400804303794379)
XLA Ops:
  0.7 1.1 %copy-done = bf16[1,320,1024]{2,1,0:T(8,128)(2,1)S(1)} copy-done((bf16[1,320,1024]{2,1,0:T(8,128)(2,1)S(1)}, bf16[1,320,1024]{2,1,0:T(8,128)(2,1)}, u32[]{:S(2)}) %copy-start) | copy-done | bytes 655384
  1.8 0.3 split.1
  2.0 6.1 %collective-permute-start.1 = (bf16[336,128]{1,0:T(8,128)(2,1)S(1)}, bf16[336,128]{1,0:T(8,128)(2,1)S(1)}, u32[]{:S(2)}, u32[]{:S(2)}) collective-permute-start(bf16[336,128]{1,0:T(8,128)(2,1)S(1)} %get-tuple-element.21), channel_id=1, source_target_pairs={{0,7},{1,6},{2,5},{3,4},{4,3},{5,2},{6,1},{7,0},{8,9},{9,8},{10,11... | collective-permute-start | bytes 258056 | tf_op jit(solution)/shard_map/ppermute | solution.py:325
  8.1 0.2 collective-permute-start.3
  8.3 0.7 %collective-permute-start.4 = (bf16[336,128]{1,0:T(8,128)(2,1)S(1)}, bf16[336,128]{1,0:T(8,128)(2,1)S(1)}, u32[]{:S(2)}, u32[]{:S(2)}) collective-permute-start(bf16[336,128]{1,0:T(8,128)(2,1)S(1)} %get-tuple-element.23), channel_id=1, source_target_pairs={{0,5},{1,4},{2,7},{3,6},{4,1},{5,0},{6,3},{7,2},{8,11},{9,10},{10,... | collective-permute-start | bytes 258056 | tf_op jit(solution)/shard_map/ppermute | solution.py:325
  9.1 2.0 %collective-permute-start.5 = (bf16[336,128]{1,0:T(8,128)(2,1)S(1)}, bf16[336,128]{1,0:T(8,128)(2,1)S(1)}, u32[]{:S(2)}, u32[]{:S(2)}) collective-permute-start(bf16[336,128]{1,0:T(8,128)(2,1)S(1)} %get-tuple-element.24), channel_id=1, source_target_pairs={{0,4},{1,5},{2,6},{3,7},{4,0},{5,1},{6,2},{7,3},{8,15},{9,14},{10,... | collective-permute-start | bytes 258056 | tf_op jit(solution)/shard_map/ppermute | solution.py:325
  11.1 1.6 %collective-permute-start.6 = (bf16[336,128]{1,0:T(8,128)(2,1)S(1)}, bf16[336,128]{1,0:T(8,128)(2,1)S(1)}, u32[]{:S(2)}, u32[]{:S(2)}) collective-permute-start(bf16[336,128]{1,0:T(8,128)(2,1)S(1)} %get-tuple-element.25), channel_id=1, source_target_pairs={{0,1},{1,0},{2,3},{3,2},{4,5},{5,4},{6,7},{7,6},{8,14},{9,15},{10,... | collective-permute-start | bytes 258056 | tf_op jit(solution)/shard_map/ppermute | solution.py:325
  12.7 0.1 copy.10
  12.8 0.1 reshape_squeeze.3.random_ref
  13.0 0.1 pad_maximum_fusion.rows_ref
  13.0 0.8 %collective-permute-start = (bf16[2,128,1024]{2,1,0:T(8,128)(2,1)S(1)}, bf16[2,128,1024]{2,1,0:T(8,128)(2,1)S(1)}, u32[]{:S(2)}, u32[]{:S(2)}) collective-permute-start(bf16[2,128,1024]{2,1,0:T(8,128)(2,1)S(1)} %pad_maximum_fusion.rows_ref), channel_id=1, source_target_pairs={{8,9},{9,10},{10,11},{11,12},{12,13},{13,14},{14,15},{24,25},{25,2... | collective-permute-start | bytes 1572872 | tf_op jit(solution)/shard_map/ppermute | solution.py:345
  13.9 0.6 %collective-permute-done.3.refs_1_ = bf16[336,128]{1,0:T(8,128)(2,1)S(1)} collective-permute-done((bf16[336,128]{1,0:T(8,128)(2,1)S(1)}, bf16[336,128]{1,0:T(8,128)(2,1)S(1)}, u32[]{:S(2)}, u32[]{:S(2)}) %collective-permute-start.3) | collective-permute-done | bytes 86048 | tf_op jit(solution)/shard_map/ppermute | solution.py:325
  14.5 3.7 %collective-permute-start.7 = (bf16[336,128]{1,0:T(8,128)(2,1)S(1)}, bf16[336,128]{1,0:T(8,128)(2,1)S(1)}, u32[]{:S(2)}, u32[]{:S(2)}) collective-permute-start(bf16[336,128]{1,0:T(8,128)(2,1)S(1)} %get-tuple-element.26), channel_id=1, source_target_pairs={{0,2},{1,3},{2,0},{3,1},{4,6},{5,7},{6,4},{7,5},{8,13},{9,12},{10,... | collective-permute-start | bytes 258056 | tf_op jit(solution)/shard_map/ppermute | solution.py:325
  18.2 2.2 %collective-permute-done.4.refs_2_ = bf16[336,128]{1,0:T(8,128)(2,1)S(1)} collective-permute-done((bf16[336,128]{1,0:T(8,128)(2,1)S(1)}, bf16[336,128]{1,0:T(8,128)(2,1)S(1)}, u32[]{:S(2)}, u32[]{:S(2)}) %collective-permute-start.4) | collective-permute-done | bytes 86048 | tf_op jit(solution)/shard_map/ppermute | solution.py:325
  20.3 2.9 %collective-permute-done.5.refs_3_ = bf16[336,128]{1,0:T(8,128)(2,1)S(1)} collective-permute-done((bf16[336,128]{1,0:T(8,128)(2,1)S(1)}, bf16[336,128]{1,0:T(8,128)(2,1)S(1)}, u32[]{:S(2)}, u32[]{:S(2)}) %collective-permute-start.5) | collective-permute-done | bytes 86048 | tf_op jit(solution)/shard_map/ppermute | solution.py:325
  23.2 2.2 %collective-permute-start.2 = (bf16[2,128,1024]{2,1,0:T(8,128)(2,1)S(1)}, bf16[2,128,1024]{2,1,0:T(8,128)(2,1)S(1)}, u32[]{:S(2)}, u32[]{:S(2)}) collective-permute-start(bf16[2,128,1024]{2,1,0:T(8,128)(2,1)S(1)} %halo.1), channel_id=1, source_target_pairs={{0,1},{1,2},{2,3},{3,4},{4,5},{5,6},{6,7},{16,17},{17,18},{18,19},... | collective-permute-start | bytes 1572872 | tf_op jit(solution)/shard_map/ppermute | solution.py:345
  25.6 3.2 %far.2 = (bf16[336,128]{1,0:T(8,128)(2,1)S(1)}, bf16[336,128]{1,0:T(8,128)(2,1)S(1)}, bf16[336,128]{1,0:T(8,128)(2,1)S(1)}, bf16[336,128]{1,0:T(8,128)(2,1)S(1)}...) custom-call(s32[1]{0:T(128)} %bitcast.9.span_ref, s32[2]{0:T(128)S(1)} %bitcast.22, ...), custom_call_target="tpu_custom_call" | custom-call | flops 12582912000 | bytes 4128768 | tf_op jit(solution)/shard_map/far/pallas_call | solution.py:352
  28.8 0.1 collective-permute-start.9
  28.9 2.4 %collective-permute-start.10 = (bf16[336,128]{1,0:T(8,128)(2,1)S(1)}, bf16[336,128]{1,0:T(8,128)(2,1)S(1)}, u32[]{:S(2)}, u32[]{:S(2)}) collective-permute-start(bf16[336,128]{1,0:T(8,128)(2,1)S(1)} %get-tuple-element.30), channel_id=1, source_target_pairs={{0,14},{1,15},{2,12},{3,13},{4,10},{5,11},{6,8},{7,9},{8,18},{9,19... | collective-permute-start | bytes 258056 | tf_op jit(solution)/shard_map/ppermute | solution.py:325
  31.3 1.5 %near_inner.1 = bf16[256,1024]{1,0:T(8,128)(2,1)S(1)} custom-call(bf16[320,1024]{1,0:T(8,128)(2,1)S(1)} %bitcast.12, bf16[320,1024]{1,0:T(8,128)(2,1)S(1)} %bitcast.14, bf16[320,1024]{1,0:T(8,128)(2,1)S(1)} %bitcast.16, bf16[336,128]{1,0:T(8,128)(2,1)S(1)} %get-tuple-element.31.own_ref, bf16[336,128]{1,0:T(8,128)(2,1)S(1)} %collective-permute-done.1._.refs_0_, ...), custom_call_target="tpu_custom_call" | custom-call | flops 8053063680 | bytes 1769472 | tf_op jit(solution)/shard_map/near_inner/pallas_call | solution.py:382
  32.8 0.9 %collective-permute-start.12 = (bf16[256,1024]{1,0:T(8,128)(2,1)S(1)}, bf16[256,1024]{1,0:T(8,128)(2,1)S(1)}, u32[]{:S(2)}, u32[]{:S(2)}) collective-permute-start(bf16[256,1024]{1,0:T(8,128)(2,1)S(1)} %near_inner.1), channel_id=1, source_target_pairs={{0,8},{1,9},{2,10},{3,11},{4,12},{5,13},{6,14},{7,15},{8,16},{9,17... | collective-permute-start | bytes 1572872 | tf_op jit(solution)/shard_map/ppermute | solution.py:325
  33.7 1.3 %collective-permute-start.13 = (bf16[336,128]{1,0:T(8,128)(2,1)S(1)}, bf16[336,128]{1,0:T(8,128)(2,1)S(1)}, u32[]{:S(2)}, u32[]{:S(2)}) collective-permute-start(bf16[336,128]{1,0:T(8,128)(2,1)S(1)} %get-tuple-element.32), channel_id=1, source_target_pairs={{0,13},{1,12},{2,15},{3,14},{4,9},{5,8},{6,11},{7,10},{8,19},{9,18... | collective-permute-start | bytes 258056 | tf_op jit(solution)/shard_map/ppermute | solution.py:325
  35.0 2.5 %collective-permute-start.14 = (bf16[336,128]{1,0:T(8,128)(2,1)S(1)}, bf16[336,128]{1,0:T(8,128)(2,1)S(1)}, u32[]{:S(2)}, u32[]{:S(2)}) collective-permute-start(bf16[336,128]{1,0:T(8,128)(2,1)S(1)} %get-tuple-element.33), channel_id=1, source_target_pairs={{0,12},{1,13},{2,14},{3,15},{4,8},{5,9},{6,10},{7,11},{8,23},{9,22... | collective-permute-start | bytes 258056 | tf_op jit(solution)/shard_map/ppermute | solution.py:325
  37.5 1.2 %collective-permute-start.15 = (bf16[336,128]{1,0:T(8,128)(2,1)S(1)}, bf16[336,128]{1,0:T(8,128)(2,1)S(1)}, u32[]{:S(2)}, u32[]{:S(2)}) collective-permute-start(bf16[336,128]{1,0:T(8,128)(2,1)S(1)} %get-tuple-element.34), channel_id=1, source_target_pairs={{0,9},{1,8},{2,11},{3,10},{4,13},{5,12},{6,15},{7,14},{8,22},{9,23... | collective-permute-start | bytes 258056 | tf_op jit(solution)/shard_map/ppermute | solution.py:325
  38.8 1.3 %near_edge.1 = bf16[144,1024]{1,0:T(8,128)(2,1)S(1)} custom-call(bf16[320,1024]{1,0:T(8,128)(2,1)S(1)} %bitcast.13, bf16[320,1024]{1,0:T(8,128)(2,1)S(1)} %bitcast.15, bf16[320,1024]{1,0:T(8,128)(2,1)S(1)} %bitcast.17, bf16[2,128,1024]{2,1,0:T(8,128)(2,1)S(1)} %collective-permute-done.odd_ref, bf16[2,128,1024]{2,1,0:T(8,128)(2,1)S(1)} %collective-permute-done.2.even_ref, ...), custom_call_target="tpu_custom_call" | custom-call | flops 5368709120 | bytes 1179648 | tf_op jit(solution)/shard_map/near_edge/pallas_call | solution.py:382
  40.1 2.9 %collective-permute-start.11 = (bf16[144,1024]{1,0:T(8,128)(2,1)S(1)}, bf16[144,1024]{1,0:T(8,128)(2,1)S(1)}, u32[]{:S(2)}, u32[]{:S(2)}) collective-permute-start(bf16[144,1024]{1,0:T(8,128)(2,1)S(1)} %near_edge.1), channel_id=1, source_target_pairs={{0,8},{1,9},{2,10},{3,11},{4,12},{5,13},{6,14},{7,15},{8,16},{9,17... | collective-permute-start | bytes 884744 | tf_op jit(solution)/shard_map/ppermute | solution.py:325
  43.0 1.5 %far.3 = (bf16[336,128]{1,0:T(8,128)(2,1)S(1)}, bf16[336,128]{1,0:T(8,128)(2,1)S(1)}) custom-call(s32[1]{0:T(128)} %bitcast.10.span_ref, s32[2]{0:T(128)S(1)} %bitcast.23, s32[120]{0:T(128)S(1)} %reshape_squeeze.3.random_ref, bf16[6144,128]{1,0:T(8,128)(2,1)S(1)} %bitcast.19, bf16[6144,128]{1,0:T(8,128)(2,1)S(1)} %bitcast.21, ...), custom_call_target="tpu_custom_call" | custom-call | flops 4194304000 | bytes 3473408 | tf_op jit(solution)/shard_map/far/pallas_call | solution.py:352
  44.6 0.5 collective-permute-start.16
  45.1 2.4 %collective-permute-start.17 = (bf16[336,128]{1,0:T(8,128)(2,1)S(1)}, bf16[336,128]{1,0:T(8,128)(2,1)S(1)}, u32[]{:S(2)}, u32[]{:S(2)}) collective-permute-start(bf16[336,128]{1,0:T(8,128)(2,1)S(1)} %get-tuple-element.36), channel_id=1, source_target_pairs={{0,11},{1,10},{2,9},{3,8},{4,15},{5,14},{6,13},{7,12},{8,20},{9,21... | collective-permute-start | bytes 258056 | tf_op jit(solution)/shard_map/ppermute | solution.py:325
  47.4 4.2 %collective-permute-done.16.refs_5_ = bf16[336,128]{1,0:T(8,128)(2,1)S(1)} collective-permute-done((bf16[336,128]{1,0:T(8,128)(2,1)S(1)}, bf16[336,128]{1,0:T(8,128)(2,1)S(1)}, u32[]{:S(2)}, u32[]{:S(2)}) %collective-permute-start.16) | collective-permute-done | bytes 86048 | tf_op jit(solution)/shard_map/ppermute | solution.py:325
  51.7 1.1 %collective-permute-done.17.refs_6_ = bf16[336,128]{1,0:T(8,128)(2,1)S(1)} collective-permute-done((bf16[336,128]{1,0:T(8,128)(2,1)S(1)}, bf16[336,128]{1,0:T(8,128)(2,1)S(1)}, u32[]{:S(2)}, u32[]{:S(2)}) %collective-permute-start.17) | collective-permute-done | bytes 86048 | tf_op jit(solution)/shard_map/ppermute | solution.py:325
  52.7 1.4 %merge.1 = bf16[320,1024]{1,0:T(8,128)(2,1)} custom-call(bf16[144,1024]{1,0:T(8,128)(2,1)S(1)} %collective-permute-done.11.edge_ref, bf16[256,1024]{1,0:T(8,128)(2,1)S(1)} %collective-permute-done.12.inner_ref, bf16[336,128]{1,0:T(8,128)(2,1)S(1)} %collective-permute-done.9.refs_8_.refs_0_, bf16[336,128]{1,0:T(8,128)(2,1)S(1)} %collective-permute-done.10.refs_9_.refs_1_, ...), custom_call_target="tpu_custom_call" | custom-call | bytes 1966080 | tf_op jit(solution)/shard_map/merge/pallas_call | solution.py:412
  (34 shorter events, 0.1 us)
Async XLA Ops:
  0.0 12.7 %copy-start.7 = (s32[1,40,3]{1,0,2:T(1,128)S(1)}, s32[1,40,3]{1,0,2:T(1,128)}, u32[]{:S(2)}) copy-start(s32[1,40,3]{1,0,2:T(1,128)} %param.15) | copy-start | bytes 1444
  0.7 1.1 %copy-start = (bf16[1,320,1024]{2,1,0:T(8,128)(2,1)S(1)}, bf16[1,320,1024]{2,1,0:T(8,128)(2,1)}, u32[]{:S(2)}) copy-start(bf16[1,320,1024]{2,1,0:T(8,128)(2,1)} %param.8) | copy-start | bytes 1966084
  1.8 11.2 %slice-start = ((bf16[1,320,1024]{2,1,0:T(8,128)(2,1)}), bf16[1,128,1024]{2,1,0:T(8,128)(2,1)S(1)}, s32[]{:S(2)}) async-start(bf16[1,320,1024]{2,1,0:T(8,128)(2,1)} %param.9), calls=%async_computation | async-start | bytes 524288 | tf_op jit(solution)/shard_map/slice | solution.py:329
  1.8 11.2 %slice-start.1 = ((bf16[1,320,1024]{2,1,0:T(8,128)(2,1)}), bf16[1,128,1024]{2,1,0:T(8,128)(2,1)S(1)}, s32[]{:S(2)}) async-start(bf16[1,320,1024]{2,1,0:T(8,128)(2,1)} %param.10), calls=%async_computation.1 | async-start | bytes 524288 | tf_op jit(solution)/shard_map/slice | solution.py:329
  2.0 11.0 %collective-permute-start.1 = (bf16[336,128]{1,0:T(8,128)(2,1)S(1)}, bf16[336,128]{1,0:T(8,128)(2,1)S(1)}, u32[]{:S(2)}, u32[]{:S(2)}) collective-permute-start(bf16[336,128]{1,0:T(8,128)(2,1)S(1)} %get-tuple-element.21), channel_id=1, source_target_pairs={{0,7},{1,6},{2,5},{3,4},{4,3},{5,2},{6,1},{7,0},{8,9},{9,8},{10,11... | collective-permute-start | bytes 258056 | tf_op jit(solution)/shard_map/ppermute | solution.py:325
  8.1 6.4 %collective-permute-start.3 = (bf16[336,128]{1,0:T(8,128)(2,1)S(1)}, bf16[336,128]{1,0:T(8,128)(2,1)S(1)}, u32[]{:S(2)}, u32[]{:S(2)}) collective-permute-start(bf16[336,128]{1,0:T(8,128)(2,1)S(1)} %get-tuple-element.22), channel_id=1, source_target_pairs={{0,6},{1,7},{2,4},{3,5},{4,2},{5,3},{6,0},{7,1},{8,10},{9,11},{10,... | collective-permute-start | bytes 258056 | tf_op jit(solution)/shard_map/ppermute | solution.py:325
  8.3 12.0 %collective-permute-start.4 = (bf16[336,128]{1,0:T(8,128)(2,1)S(1)}, bf16[336,128]{1,0:T(8,128)(2,1)S(1)}, u32[]{:S(2)}, u32[]{:S(2)}) collective-permute-start(bf16[336,128]{1,0:T(8,128)(2,1)S(1)} %get-tuple-element.23), channel_id=1, source_target_pairs={{0,5},{1,4},{2,7},{3,6},{4,1},{5,0},{6,3},{7,2},{8,11},{9,10},{10,... | collective-permute-start | bytes 258056 | tf_op jit(solution)/shard_map/ppermute | solution.py:325
  9.1 14.2 %collective-permute-start.5 = (bf16[336,128]{1,0:T(8,128)(2,1)S(1)}, bf16[336,128]{1,0:T(8,128)(2,1)S(1)}, u32[]{:S(2)}, u32[]{:S(2)}) collective-permute-start(bf16[336,128]{1,0:T(8,128)(2,1)S(1)} %get-tuple-element.24), channel_id=1, source_target_pairs={{0,4},{1,5},{2,6},{3,7},{4,0},{5,1},{6,2},{7,3},{8,15},{9,14},{10,... | collective-permute-start | bytes 258056 | tf_op jit(solution)/shard_map/ppermute | solution.py:325
  11.1 14.4 %copy-start.4 = (bf16[1,6144,128]{2,1,0:T(8,128)(2,1)S(1)}, bf16[1,6144,128]{2,1,0:T(8,128)(2,1)}, u32[]{:S(2)}) copy-start(bf16[1,6144,128]{2,1,0:T(8,128)(2,1)} %param.11) | copy-start | bytes 4718596
  11.1 14.4 %copy-start.6 = (s32[1,2]{1,0:T(1,128)S(1)}, s32[1,2]{1,0:T(1,128)}, u32[]{:S(2)}) copy-start(s32[1,2]{1,0:T(1,128)} %param.14) | copy-start | bytes 28
  11.1 14.4 %collective-permute-start.6 = (bf16[336,128]{1,0:T(8,128)(2,1)S(1)}, bf16[336,128]{1,0:T(8,128)(2,1)S(1)}, u32[]{:S(2)}, u32[]{:S(2)}) collective-permute-start(bf16[336,128]{1,0:T(8,128)(2,1)S(1)} %get-tuple-element.25), channel_id=1, source_target_pairs={{0,1},{1,0},{2,3},{3,2},{4,5},{5,4},{6,7},{7,6},{8,14},{9,15},{10,... | collective-permute-start | bytes 258056 | tf_op jit(solution)/shard_map/ppermute | solution.py:325
  13.0 12.6 %copy-start.5 = (bf16[1,6144,128]{2,1,0:T(8,128)(2,1)S(1)}, bf16[1,6144,128]{2,1,0:T(8,128)(2,1)}, u32[]{:S(2)}) copy-start(bf16[1,6144,128]{2,1,0:T(8,128)(2,1)} %param.12) | copy-start | bytes 4718596
  13.0 24.5 %collective-permute-start = (bf16[2,128,1024]{2,1,0:T(8,128)(2,1)S(1)}, bf16[2,128,1024]{2,1,0:T(8,128)(2,1)S(1)}, u32[]{:S(2)}, u32[]{:S(2)}) collective-permute-start(bf16[2,128,1024]{2,1,0:T(8,128)(2,1)S(1)} %pad_maximum_fusion.rows_ref), channel_id=1, source_target_pairs={{8,9},{9,10},{10,11},{11,12},{12,13},{13,14},{14,15},{24,25},{25,2... | collective-permute-start | bytes 1572872 | tf_op jit(solution)/shard_map/ppermute | solution.py:345
  14.5 14.4 %collective-permute-start.7 = (bf16[336,128]{1,0:T(8,128)(2,1)S(1)}, bf16[336,128]{1,0:T(8,128)(2,1)S(1)}, u32[]{:S(2)}, u32[]{:S(2)}) collective-permute-start(bf16[336,128]{1,0:T(8,128)(2,1)S(1)} %get-tuple-element.26), channel_id=1, source_target_pairs={{0,2},{1,3},{2,0},{3,1},{4,6},{5,7},{6,4},{7,5},{8,13},{9,12},{10,... | collective-permute-start | bytes 258056 | tf_op jit(solution)/shard_map/ppermute | solution.py:325
  20.3 11.0 %collective-permute-start.8 = (bf16[336,128]{1,0:T(8,128)(2,1)S(1)}, bf16[336,128]{1,0:T(8,128)(2,1)S(1)}, u32[]{:S(2)}, u32[]{:S(2)}) collective-permute-start(bf16[336,128]{1,0:T(8,128)(2,1)S(1)} %get-tuple-element.27), channel_id=1, source_target_pairs={{0,3},{1,2},{2,1},{3,0},{4,7},{5,6},{6,5},{7,4},{8,12},{9,13},{10,... | collective-permute-start | bytes 258056 | tf_op jit(solution)/shard_map/ppermute | solution.py:325
  23.2 15.5 %collective-permute-start.2 = (bf16[2,128,1024]{2,1,0:T(8,128)(2,1)S(1)}, bf16[2,128,1024]{2,1,0:T(8,128)(2,1)S(1)}, u32[]{:S(2)}, u32[]{:S(2)}) collective-permute-start(bf16[2,128,1024]{2,1,0:T(8,128)(2,1)S(1)} %halo.1), channel_id=1, source_target_pairs={{0,1},{1,2},{2,3},{3,4},{4,5},{5,6},{6,7},{16,17},{17,18},{18,19},... | collective-permute-start | bytes 1572872 | tf_op jit(solution)/shard_map/ppermute | solution.py:345
  25.5 5.8 %copy-start.1 = (bf16[1,320,1024]{2,1,0:T(8,128)(2,1)S(1)}, bf16[1,320,1024]{2,1,0:T(8,128)(2,1)}, u32[]{:S(2)}) copy-start(bf16[1,320,1024]{2,1,0:T(8,128)(2,1)} %param.8) | copy-start | bytes 1966084
  25.5 5.8 %copy-start.2 = (bf16[1,320,1024]{2,1,0:T(8,128)(2,1)S(1)}, bf16[1,320,1024]{2,1,0:T(8,128)(2,1)}, u32[]{:S(2)}) copy-start(bf16[1,320,1024]{2,1,0:T(8,128)(2,1)} %param.9) | copy-start | bytes 1966084
  25.6 5.8 %copy-start.3 = (bf16[1,320,1024]{2,1,0:T(8,128)(2,1)S(1)}, bf16[1,320,1024]{2,1,0:T(8,128)(2,1)}, u32[]{:S(2)}) copy-start(bf16[1,320,1024]{2,1,0:T(8,128)(2,1)} %param.10) | copy-start | bytes 1966084
  28.8 4.9 %collective-permute-start.9 = (bf16[336,128]{1,0:T(8,128)(2,1)S(1)}, bf16[336,128]{1,0:T(8,128)(2,1)S(1)}, u32[]{:S(2)}, u32[]{:S(2)}) collective-permute-start(bf16[336,128]{1,0:T(8,128)(2,1)S(1)} %get-tuple-element.29), channel_id=1, source_target_pairs={{0,15},{1,14},{2,13},{3,12},{4,11},{5,10},{6,9},{7,8},{8,17},{9,16... | collective-permute-start | bytes 258056 | tf_op jit(solution)/shard_map/ppermute | solution.py:325
  28.9 6.2 %collective-permute-start.10 = (bf16[336,128]{1,0:T(8,128)(2,1)S(1)}, bf16[336,128]{1,0:T(8,128)(2,1)S(1)}, u32[]{:S(2)}, u32[]{:S(2)}) collective-permute-start(bf16[336,128]{1,0:T(8,128)(2,1)S(1)} %get-tuple-element.30), channel_id=1, source_target_pairs={{0,14},{1,15},{2,12},{3,13},{4,10},{5,11},{6,8},{7,9},{8,18},{9,19... | collective-permute-start | bytes 258056 | tf_op jit(solution)/shard_map/ppermute | solution.py:325
  32.8 19.9 %collective-permute-start.12 = (bf16[256,1024]{1,0:T(8,128)(2,1)S(1)}, bf16[256,1024]{1,0:T(8,128)(2,1)S(1)}, u32[]{:S(2)}, u32[]{:S(2)}) collective-permute-start(bf16[256,1024]{1,0:T(8,128)(2,1)S(1)} %near_inner.1), channel_id=1, source_target_pairs={{0,8},{1,9},{2,10},{3,11},{4,12},{5,13},{6,14},{7,15},{8,16},{9,17... | collective-permute-start | bytes 1572872 | tf_op jit(solution)/shard_map/ppermute | solution.py:325
  33.7 10.9 %collective-permute-start.13 = (bf16[336,128]{1,0:T(8,128)(2,1)S(1)}, bf16[336,128]{1,0:T(8,128)(2,1)S(1)}, u32[]{:S(2)}, u32[]{:S(2)}) collective-permute-start(bf16[336,128]{1,0:T(8,128)(2,1)S(1)} %get-tuple-element.32), channel_id=1, source_target_pairs={{0,13},{1,12},{2,15},{3,14},{4,9},{5,8},{6,11},{7,10},{8,19},{9,18... | collective-permute-start | bytes 258056 | tf_op jit(solution)/shard_map/ppermute | solution.py:325
  35.0 10.0 %collective-permute-start.14 = (bf16[336,128]{1,0:T(8,128)(2,1)S(1)}, bf16[336,128]{1,0:T(8,128)(2,1)S(1)}, u32[]{:S(2)}, u32[]{:S(2)}) collective-permute-start(bf16[336,128]{1,0:T(8,128)(2,1)S(1)} %get-tuple-element.33), channel_id=1, source_target_pairs={{0,12},{1,13},{2,14},{3,15},{4,8},{5,9},{6,10},{7,11},{8,23},{9,22... | collective-permute-start | bytes 258056 | tf_op jit(solution)/shard_map/ppermute | solution.py:325
  37.5 9.9 %collective-permute-start.15 = (bf16[336,128]{1,0:T(8,128)(2,1)S(1)}, bf16[336,128]{1,0:T(8,128)(2,1)S(1)}, u32[]{:S(2)}, u32[]{:S(2)}) collective-permute-start(bf16[336,128]{1,0:T(8,128)(2,1)S(1)} %get-tuple-element.34), channel_id=1, source_target_pairs={{0,9},{1,8},{2,11},{3,10},{4,13},{5,12},{6,15},{7,14},{8,22},{9,23... | collective-permute-start | bytes 258056 | tf_op jit(solution)/shard_map/ppermute | solution.py:325
  40.1 12.6 %collective-permute-start.11 = (bf16[144,1024]{1,0:T(8,128)(2,1)S(1)}, bf16[144,1024]{1,0:T(8,128)(2,1)S(1)}, u32[]{:S(2)}, u32[]{:S(2)}) collective-permute-start(bf16[144,1024]{1,0:T(8,128)(2,1)S(1)} %near_edge.1), channel_id=1, source_target_pairs={{0,8},{1,9},{2,10},{3,11},{4,12},{5,13},{6,14},{7,15},{8,16},{9,17... | collective-permute-start | bytes 884744 | tf_op jit(solution)/shard_map/ppermute | solution.py:325
  44.6 7.1 %collective-permute-start.16 = (bf16[336,128]{1,0:T(8,128)(2,1)S(1)}, bf16[336,128]{1,0:T(8,128)(2,1)S(1)}, u32[]{:S(2)}, u32[]{:S(2)}) collective-permute-start(bf16[336,128]{1,0:T(8,128)(2,1)S(1)} %get-tuple-element.35), channel_id=1, source_target_pairs={{0,10},{1,11},{2,8},{3,9},{4,14},{5,15},{6,12},{7,13},{8,21},{9,20... | collective-permute-start | bytes 258056 | tf_op jit(solution)/shard_map/ppermute | solution.py:325
  45.1 7.7 %collective-permute-start.17 = (bf16[336,128]{1,0:T(8,128)(2,1)S(1)}, bf16[336,128]{1,0:T(8,128)(2,1)S(1)}, u32[]{:S(2)}, u32[]{:S(2)}) collective-permute-start(bf16[336,128]{1,0:T(8,128)(2,1)S(1)} %get-tuple-element.36), channel_id=1, source_target_pairs={{0,11},{1,10},{2,9},{3,8},{4,15},{5,14},{6,13},{7,12},{8,20},{9,21... | collective-permute-start | bytes 258056 | tf_op jit(solution)/shard_map/ppermute | solution.py:325

commit v10 on v9

--- a/solution.py
+++ b/solution.py
@@ -17,6 +17,7 @@
 STAT_ROWS = 16
 MASKED = -1e30
 EXPO_SCALE = math.log2(math.e) / math.sqrt(HD)
+SPLIT_VMEM = 60 * 1024 * 1024
 VMEM_BASE = 12 * 1024 * 1024
 
 whole_vmem = pl.BlockSpec(memory_space=pltpu.VMEM)
@@ -91,21 +92,22 @@
 
 
 def split_kernel(there, span_ref, query_ref, *refs):
-    out_refs, arrived = refs[:-1], refs[-1]
+    out_refs, width_ref, arrived = refs[:-2], refs[-2], refs[-1]
     rows = query_ref.shape[0]
+    width_ref[...] = jnp.full(width_ref.shape, span_ref[0].astype(jnp.float32)).astype(
+        width_ref.dtype
+    )
     copies = []
     for peer, out_ref in zip(peers_of(there, 0), out_refs):
         head = pl.multiple_of(peer * HD, HD)
         copies.append((query_ref.at[:, pl.ds(head, HD)], out_ref.at[:rows]))
+        copies.append((width_ref, out_ref.at[rows:]))
     copies = [
         pltpu.make_async_copy(source, target, arrived.at[index])
         for index, (source, target) in enumerate(copies)
     ]
     for copy in copies:
         copy.start()
-    width = jnp.full((STAT_ROWS, HD), span_ref[0].astype(jnp.float32)).astype(jnp.bfloat16)
-    for out_ref in out_refs:
-        out_ref[rows:, :] = width
     for copy in copies:
         copy.wait()
 
@@ -285,17 +287,23 @@
     bf16 = jnp.bfloat16
     half = max(seq_count // 2, 1)
     inner, outer = list(range(1, half)), list(range(seq_count - 1, half - 1, -1))
-    there = [outer + inner + [0], inner + outer + [0]]
+    outer_first = [step for both in zip(outer, inner) for step in both]
+    outer_first = outer_first[:-1] + outer[len(inner) :] + outer_first[-1:]
+    inner_first = [step for both in zip(inner, outer) for step in both] + outer[len(inner) :]
+    there = [outer_first + [0], inner_first + [0]]
 
     chunk_shape = jax.ShapeDtypeStruct((rows + STAT_ROWS, HD), bf16)
     chunk_shape = jax.ShapeDtypeStruct((rows + STAT_ROWS, HD), bf16)
     sent = pl.pallas_call(
         functools.partial(split_kernel, there),
         out_shape=[chunk_shape] * seq_count,
-        in_specs=[whole_smem, in_hbm],
-        out_specs=[whole_vmem] * seq_count,
-        scratch_shapes=[pltpu.SemaphoreType.DMA((seq_count,))],
-        compiler_params=params(queries),
+        in_specs=[whole_smem, anywhere],
+        out_specs=[anywhere] * seq_count,
+        scratch_shapes=[
+            pltpu.VMEM((STAT_ROWS, HD), bf16),
+            pltpu.SemaphoreType.DMA((2 * seq_count,)),
+        ],
+        compiler_params=pltpu.CompilerParams(vmem_limit_bytes=SPLIT_VMEM),
         cost_estimate=pl.CostEstimate(flops=0, bytes_accessed=5 * rows * wide, transcendentals=0),
         name="split",
     )(window[0], queries[0])

time: 54.3 us -> 78.5 us (1.45)
  Pallas kernels: 9.22 us -> 30.1 us
  starting transfers between devices: 31.6 us -> 37.6 us
  waiting for transfers between devices: 11 us -> 9.37 us
  local copies, waits for them, and re-layouts: 1.33 us -> 0.25 us
    pallas_call x1, Pallas kernels: 0.27 us -> 21.1 us  [per_device(): pl.pallas_call(functools.partial(split_kernel, there), out_shape=[chunk_s...]
    ppermute x16, starting transfers between devices: 28.6 us -> 34.3 us  [linked(): return lax.ppermute(shard, ('section', 'seq'), pairs)]
    ppermute x16, waiting for transfers between devices: 11 us -> 9.36 us  [linked(): return lax.ppermute(shard, ('section', 'seq'), pairs)]
    unnamed x17, local copies, waits for them, and re-layouts: 1.21 us -> 0.13 us
  transfers between devices with their start and end apart: 18 -> 18, of which waited for: 5 -> 4; matrix products, arithmetic and copies ran while one was open for 0% -> 0% of each run, Pallas kernels for 14% -> 10%
where the time goes in v10:
time: 78.5 us; the launch traced here: 78.3 us
  starting transfers between devices  37.6 us (48%)
  Pallas kernels  30.1 us (38%)
  waiting for transfers between devices  9.37 us (12%)
  between operations  0.94 us (1%)
    ppermute x16, starting transfers between devices, linked(): return lax.ppermute(shard, ('section', 'seq'), pairs)  34.3 us
    pallas_call x1, Pallas kernels, per_device(): pl.pallas_call(functools.partial(split_kernel, there), out_shape=[chunk_s...  21.1 us
    ppermute x16, waiting for transfers between devices, linked(): return lax.ppermute(shard, ('section', 'seq'), pairs)  9.36 us
    pallas_call x2, Pallas kernels, far_call(): pl.pallas_call(functools.partial(far_kernel, there, chosen), out_shape=[c...  4.72 us
    ppermute x2, starting transfers between devices, halo_from(): return lax.ppermute(mine, ('section', 'seq'), pairs)  3.27 us
    pallas_call x2, Pallas kernels, near_call(): pl.pallas_call(functools.partial(kernel, there), out_shape=jax.ShapeDtype...  2.84 us
  transfers between devices with their start and end apart: 18, of which 4 were waited for; matrix products, arithmetic and copies ran while one was open for 0% of the time, Pallas kernels for 10%

profile of v10, /device:TPU:0, one launch (start us, length us, event | category | flops | bytes accessed | tf_op | source)
XLA Modules:
  0.0 78.3 jit_solution(17301424411019067804)
XLA Ops:
  0.7 21.1 %split.1 = (bf16[336,128]{1,0:T(8,128)(2,1)}, bf16[336,128]{1,0:T(8,128)(2,1)}, bf16[336,128]{1,0:T(8,128)(2,1)}, bf16[336,128]{1,0:T(8,128)(2,1)}, bf16[336,128...) custom-call(s32[1]{0:T(128)} %bitcast.8.span_ref, ...), custom_call_target="tpu_custom_call" | custom-call | bytes 1638400 | tf_op jit(solution)/shard_map/split/pallas_call | solution.py:297
  21.9 6.1 %collective-permute-start.1 = (bf16[336,128]{1,0:T(8,128)(2,1)}, bf16[336,128]{1,0:T(8,128)(2,1)S(1)}, u32[]{:S(2)}, u32[]{:S(2)}) collective-permute-start(bf16[336,128]{1,0:T(8,128)(2,1)} %get-tuple-element.21), channel_id=1, source_target_pairs={{0,7},{1,6},{2,5},{3,4},{4,3},{5,2},{6,1},{7,0},{8,9},{9,8},{10,11... | collective-permute-start | bytes 258056 | tf_op jit(solution)/shard_map/ppermute | solution.py:333
  27.9 0.5 collective-permute-start.3
  28.4 0.1 collective-permute-start.4
  28.6 5.2 %collective-permute-start.6 = (bf16[336,128]{1,0:T(8,128)(2,1)}, bf16[336,128]{1,0:T(8,128)(2,1)S(1)}, u32[]{:S(2)}, u32[]{:S(2)}) collective-permute-start(bf16[336,128]{1,0:T(8,128)(2,1)} %get-tuple-element.25), channel_id=1, source_target_pairs={{0,5},{1,4},{2,7},{3,6},{4,1},{5,0},{6,3},{7,2},{8,11},{9,10},{10,... | collective-permute-start | bytes 258056 | tf_op jit(solution)/shard_map/ppermute | solution.py:333
  33.8 0.1 copy.10
  33.9 0.1 reshape_squeeze.3.random_ref
  34.0 0.0 copy-start.4
  34.0 0.1 pad_maximum_fusion.rows_ref
  34.1 0.8 %collective-permute-start = (bf16[2,128,1024]{2,1,0:T(8,128)(2,1)S(1)}, bf16[2,128,1024]{2,1,0:T(8,128)(2,1)S(1)}, u32[]{:S(2)}, u32[]{:S(2)}) collective-permute-start(bf16[2,128,1024]{2,1,0:T(8,128)(2,1)S(1)} %pad_maximum_fusion.rows_ref), channel_id=1, source_target_pairs={{8,9},{9,10},{10,11},{11,12},{12,13},{13,14},{14,15},{24,25},{25,2... | collective-permute-start | bytes 1572872 | tf_op jit(solution)/shard_map/ppermute | solution.py:353
  35.0 0.1 collective-permute-start.7
  35.1 0.8 %collective-permute-done.4.refs_2_ = bf16[336,128]{1,0:T(8,128)(2,1)S(1)} collective-permute-done((bf16[336,128]{1,0:T(8,128)(2,1)}, bf16[336,128]{1,0:T(8,128)(2,1)S(1)}, u32[]{:S(2)}, u32[]{:S(2)}) %collective-permute-start.4) | collective-permute-done | bytes 86048 | tf_op jit(solution)/shard_map/ppermute | solution.py:333
  35.9 1.7 %collective-permute-start.8 = (bf16[336,128]{1,0:T(8,128)(2,1)}, bf16[336,128]{1,0:T(8,128)(2,1)S(1)}, u32[]{:S(2)}, u32[]{:S(2)}) collective-permute-start(bf16[336,128]{1,0:T(8,128)(2,1)} %get-tuple-element.27), channel_id=1, source_target_pairs={{0,3},{1,2},{2,1},{3,0},{4,7},{5,6},{6,5},{7,4},{8,12},{9,13},{10,... | collective-permute-start | bytes 258056 | tf_op jit(solution)/shard_map/ppermute | solution.py:333
  37.6 2.4 %collective-permute-start.2 = (bf16[2,128,1024]{2,1,0:T(8,128)(2,1)S(1)}, bf16[2,128,1024]{2,1,0:T(8,128)(2,1)S(1)}, u32[]{:S(2)}, u32[]{:S(2)}) collective-permute-start(bf16[2,128,1024]{2,1,0:T(8,128)(2,1)S(1)} %halo.1), channel_id=1, source_target_pairs={{0,1},{1,2},{2,3},{3,4},{4,5},{5,6},{6,7},{16,17},{17,18},{18,19},... | collective-permute-start | bytes 1572872 | tf_op jit(solution)/shard_map/ppermute | solution.py:353
  40.1 1.3 %collective-permute-done.6.refs_4_ = bf16[336,128]{1,0:T(8,128)(2,1)S(1)} collective-permute-done((bf16[336,128]{1,0:T(8,128)(2,1)}, bf16[336,128]{1,0:T(8,128)(2,1)S(1)}, u32[]{:S(2)}, u32[]{:S(2)}) %collective-permute-start.6) | collective-permute-done | bytes 86048 | tf_op jit(solution)/shard_map/ppermute | solution.py:333
  41.4 0.0 copy-start
  41.4 0.0 copy-start.1
  41.4 3.2 %far.2 = (bf16[336,128]{1,0:T(8,128)(2,1)S(1)}, bf16[336,128]{1,0:T(8,128)(2,1)S(1)}, bf16[336,128]{1,0:T(8,128)(2,1)S(1)}, bf16[336,128]{1,0:T(8,128)(2,1)S(1)}...) custom-call(s32[1]{0:T(128)} %bitcast.9.span_ref, s32[2]{0:T(128)S(1)} %bitcast.22, ...), custom_call_target="tpu_custom_call" | custom-call | flops 12582912000 | bytes 4128768 | tf_op jit(solution)/shard_map/far/pallas_call | solution.py:360
  44.6 0.1 collective-permute-start.9
  44.7 3.4 %collective-permute-start.10 = (bf16[336,128]{1,0:T(8,128)(2,1)S(1)}, bf16[336,128]{1,0:T(8,128)(2,1)S(1)}, u32[]{:S(2)}, u32[]{:S(2)}) collective-permute-start(bf16[336,128]{1,0:T(8,128)(2,1)S(1)} %get-tuple-element.30), channel_id=1, source_target_pairs={{0,9},{1,8},{2,11},{3,10},{4,13},{5,12},{6,15},{7,14},{8,23},{9,22... | collective-permute-start | bytes 258056 | tf_op jit(solution)/shard_map/ppermute | solution.py:333
  48.2 1.5 %near_inner.1 = bf16[256,1024]{1,0:T(8,128)(2,1)S(1)} custom-call(bf16[320,1024]{1,0:T(8,128)(2,1)S(1)} %bitcast.12, bf16[320,1024]{1,0:T(8,128)(2,1)S(1)} %bitcast.14, bf16[320,1024]{1,0:T(8,128)(2,1)S(1)} %bitcast.16, bf16[336,128]{1,0:T(8,128)(2,1)S(1)} %get-tuple-element.31.own_ref, bf16[336,128]{1,0:T(8,128)(2,1)S(1)} %collective-permute-done.1._.refs_0_, ...), custom_call_target="tpu_custom_call" | custom-call | flops 8053063680 | bytes 1769472 | tf_op jit(solution)/shard_map/near_inner/pallas_call | solution.py:390
  49.7 0.6 collective-permute-start.12
  50.3 8.9 %collective-permute-start.13 = (bf16[336,128]{1,0:T(8,128)(2,1)S(1)}, bf16[336,128]{1,0:T(8,128)(2,1)S(1)}, u32[]{:S(2)}, u32[]{:S(2)}) collective-permute-start(bf16[336,128]{1,0:T(8,128)(2,1)S(1)} %get-tuple-element.32), channel_id=1, source_target_pairs={{0,14},{1,15},{2,12},{3,13},{4,10},{5,11},{6,8},{7,9},{8,18},{9,19... | collective-permute-start | bytes 258056 | tf_op jit(solution)/shard_map/ppermute | solution.py:333
  59.2 3.4 %collective-permute-start.15 = (bf16[336,128]{1,0:T(8,128)(2,1)S(1)}, bf16[336,128]{1,0:T(8,128)(2,1)S(1)}, u32[]{:S(2)}, u32[]{:S(2)}) collective-permute-start(bf16[336,128]{1,0:T(8,128)(2,1)S(1)} %get-tuple-element.34), channel_id=1, source_target_pairs={{0,13},{1,12},{2,15},{3,14},{4,9},{5,8},{6,11},{7,10},{8,19},{9,18... | collective-permute-start | bytes 258056 | tf_op jit(solution)/shard_map/ppermute | solution.py:333
  62.6 1.3 %near_edge.1 = bf16[144,1024]{1,0:T(8,128)(2,1)S(1)} custom-call(bf16[320,1024]{1,0:T(8,128)(2,1)S(1)} %bitcast.13, bf16[320,1024]{1,0:T(8,128)(2,1)S(1)} %bitcast.15, bf16[320,1024]{1,0:T(8,128)(2,1)S(1)} %bitcast.17, bf16[2,128,1024]{2,1,0:T(8,128)(2,1)S(1)} %collective-permute-done.odd_ref, bf16[2,128,1024]{2,1,0:T(8,128)(2,1)S(1)} %collective-permute-done.2.even_ref, ...), custom_call_target="tpu_custom_call" | custom-call | flops 5368709120 | bytes 1179648 | tf_op jit(solution)/shard_map/near_edge/pallas_call | solution.py:390
  63.9 0.1 collective-permute-start.11
  64.0 1.5 %far.3 = (bf16[336,128]{1,0:T(8,128)(2,1)S(1)}, bf16[336,128]{1,0:T(8,128)(2,1)S(1)}) custom-call(s32[1]{0:T(128)} %bitcast.10.span_ref, s32[2]{0:T(128)S(1)} %bitcast.23, s32[120]{0:T(128)S(1)} %reshape_squeeze.3.random_ref, bf16[6144,128]{1,0:T(8,128)(2,1)S(1)} %bitcast.19, bf16[6144,128]{1,0:T(8,128)(2,1)S(1)} %bitcast.21, ...), custom_call_target="tpu_custom_call" | custom-call | flops 4194304000 | bytes 3473408 | tf_op jit(solution)/shard_map/far/pallas_call | solution.py:360
  65.5 2.7 %collective-permute-start.16 = (bf16[336,128]{1,0:T(8,128)(2,1)S(1)}, bf16[336,128]{1,0:T(8,128)(2,1)S(1)}, u32[]{:S(2)}, u32[]{:S(2)}) collective-permute-start(bf16[336,128]{1,0:T(8,128)(2,1)S(1)} %get-tuple-element.35), channel_id=1, source_target_pairs={{0,12},{1,13},{2,14},{3,15},{4,8},{5,9},{6,10},{7,11},{8,21},{9,20... | collective-permute-start | bytes 258056 | tf_op jit(solution)/shard_map/ppermute | solution.py:333
  68.2 1.5 %collective-permute-start.17 = (bf16[336,128]{1,0:T(8,128)(2,1)S(1)}, bf16[336,128]{1,0:T(8,128)(2,1)S(1)}, u32[]{:S(2)}, u32[]{:S(2)}) collective-permute-start(bf16[336,128]{1,0:T(8,128)(2,1)S(1)} %get-tuple-element.36), channel_id=1, source_target_pairs={{0,11},{1,10},{2,9},{3,8},{4,15},{5,14},{6,13},{7,12},{8,20},{9,21... | collective-permute-start | bytes 258056 | tf_op jit(solution)/shard_map/ppermute | solution.py:333
  69.7 2.6 %collective-permute-done.16.refs_5_ = bf16[336,128]{1,0:T(8,128)(2,1)S(1)} collective-permute-done((bf16[336,128]{1,0:T(8,128)(2,1)S(1)}, bf16[336,128]{1,0:T(8,128)(2,1)S(1)}, u32[]{:S(2)}, u32[]{:S(2)}) %collective-permute-start.16) | collective-permute-done | bytes 86048 | tf_op jit(solution)/shard_map/ppermute | solution.py:333
  72.3 4.6 %collective-permute-done.17.refs_6_ = bf16[336,128]{1,0:T(8,128)(2,1)S(1)} collective-permute-done((bf16[336,128]{1,0:T(8,128)(2,1)S(1)}, bf16[336,128]{1,0:T(8,128)(2,1)S(1)}, u32[]{:S(2)}, u32[]{:S(2)}) %collective-permute-start.17) | collective-permute-done | bytes 86048 | tf_op jit(solution)/shard_map/ppermute | solution.py:333
  76.9 1.4 %merge.1 = bf16[320,1024]{1,0:T(8,128)(2,1)} custom-call(bf16[144,1024]{1,0:T(8,128)(2,1)S(1)} %collective-permute-done.11.edge_ref, bf16[256,1024]{1,0:T(8,128)(2,1)S(1)} %collective-permute-done.12.inner_ref, bf16[336,128]{1,0:T(8,128)(2,1)S(1)} %collective-permute-done.9.refs_8_.refs_0_, bf16[336,128]{1,0:T(8,128)(2,1)S(1)} %collective-permute-done.10.refs_9_.refs_1_, ...), custom_call_target="tpu_custom_call" | custom-call | bytes 1966080 | tf_op jit(solution)/shard_map/merge/pallas_call | solution.py:420
  (34 shorter events, 0.1 us)
Async XLA Ops:
  0.0 34.0 %slice-start.1 = ((bf16[1,320,1024]{2,1,0:T(8,128)(2,1)}), bf16[1,128,1024]{2,1,0:T(8,128)(2,1)S(1)}, s32[]{:S(2)}) async-start(bf16[1,320,1024]{2,1,0:T(8,128)(2,1)} %param.10), calls=%async_computation.1 | async-start | bytes 524288 | tf_op jit(solution)/shard_map/slice | solution.py:337
  0.0 34.0 %slice-start = ((bf16[1,320,1024]{2,1,0:T(8,128)(2,1)}), bf16[1,128,1024]{2,1,0:T(8,128)(2,1)S(1)}, s32[]{:S(2)}) async-start(bf16[1,320,1024]{2,1,0:T(8,128)(2,1)} %param.9), calls=%async_computation | async-start | bytes 524288 | tf_op jit(solution)/shard_map/slice | solution.py:337
  0.0 33.8 %copy-start.7 = (s32[1,40,3]{1,0,2:T(1,128)S(1)}, s32[1,40,3]{1,0,2:T(1,128)}, u32[]{:S(2)}) copy-start(s32[1,40,3]{1,0,2:T(1,128)} %param.15) | copy-start | bytes 1444
  21.9 12.2 %collective-permute-start.1 = (bf16[336,128]{1,0:T(8,128)(2,1)}, bf16[336,128]{1,0:T(8,128)(2,1)S(1)}, u32[]{:S(2)}, u32[]{:S(2)}) collective-permute-start(bf16[336,128]{1,0:T(8,128)(2,1)} %get-tuple-element.21), channel_id=1, source_target_pairs={{0,7},{1,6},{2,5},{3,4},{4,3},{5,2},{6,1},{7,0},{8,9},{9,8},{10,11... | collective-permute-start | bytes 258056 | tf_op jit(solution)/shard_map/ppermute | solution.py:333
  27.9 7.0 %collective-permute-start.3 = (bf16[336,128]{1,0:T(8,128)(2,1)}, bf16[336,128]{1,0:T(8,128)(2,1)S(1)}, u32[]{:S(2)}, u32[]{:S(2)}) collective-permute-start(bf16[336,128]{1,0:T(8,128)(2,1)} %get-tuple-element.22), channel_id=1, source_target_pairs={{0,1},{1,0},{2,3},{3,2},{4,5},{5,4},{6,7},{7,6},{8,15},{9,14},{10,... | collective-permute-start | bytes 258056 | tf_op jit(solution)/shard_map/ppermute | solution.py:333
  28.4 7.4 %collective-permute-start.4 = (bf16[336,128]{1,0:T(8,128)(2,1)}, bf16[336,128]{1,0:T(8,128)(2,1)S(1)}, u32[]{:S(2)}, u32[]{:S(2)}) collective-permute-start(bf16[336,128]{1,0:T(8,128)(2,1)} %get-tuple-element.23), channel_id=1, source_target_pairs={{0,6},{1,7},{2,4},{3,5},{4,2},{5,3},{6,0},{7,1},{8,10},{9,11},{10,... | collective-permute-start | bytes 258056 | tf_op jit(solution)/shard_map/ppermute | solution.py:333
  28.6 9.1 %collective-permute-start.5 = (bf16[336,128]{1,0:T(8,128)(2,1)}, bf16[336,128]{1,0:T(8,128)(2,1)S(1)}, u32[]{:S(2)}, u32[]{:S(2)}) collective-permute-start(bf16[336,128]{1,0:T(8,128)(2,1)} %get-tuple-element.24), channel_id=1, source_target_pairs={{0,2},{1,3},{2,0},{3,1},{4,6},{5,7},{6,4},{7,5},{8,14},{9,15},{10,... | collective-permute-start | bytes 258056 | tf_op jit(solution)/shard_map/ppermute | solution.py:333
  28.6 12.8 %copy-start.3 = (bf16[1,6144,128]{2,1,0:T(8,128)(2,1)S(1)}, bf16[1,6144,128]{2,1,0:T(8,128)(2,1)}, u32[]{:S(2)}) copy-start(bf16[1,6144,128]{2,1,0:T(8,128)(2,1)} %param.11) | copy-start | bytes 4718596
  28.6 12.8 %copy-start.5 = (bf16[336,128]{1,0:T(8,128)(2,1)S(1)}, bf16[336,128]{1,0:T(8,128)(2,1)}, u32[]{:S(2)}) copy-start(bf16[336,128]{1,0:T(8,128)(2,1)} %get-tuple-element.28.refs_5_.refs_7_) | copy-start | bytes 258052
  28.6 12.8 %copy-start.6 = (s32[1,2]{1,0:T(1,128)S(1)}, s32[1,2]{1,0:T(1,128)}, u32[]{:S(2)}) copy-start(s32[1,2]{1,0:T(1,128)} %param.14) | copy-start | bytes 28
  28.6 12.8 %collective-permute-start.6 = (bf16[336,128]{1,0:T(8,128)(2,1)}, bf16[336,128]{1,0:T(8,128)(2,1)S(1)}, u32[]{:S(2)}, u32[]{:S(2)}) collective-permute-start(bf16[336,128]{1,0:T(8,128)(2,1)} %get-tuple-element.25), channel_id=1, source_target_pairs={{0,5},{1,4},{2,7},{3,6},{4,1},{5,0},{6,3},{7,2},{8,11},{9,10},{10,... | collective-permute-start | bytes 258056 | tf_op jit(solution)/shard_map/ppermute | solution.py:333
  34.0 7.4 %copy-start.4 = (bf16[1,6144,128]{2,1,0:T(8,128)(2,1)S(1)}, bf16[1,6144,128]{2,1,0:T(8,128)(2,1)}, u32[]{:S(2)}) copy-start(bf16[1,6144,128]{2,1,0:T(8,128)(2,1)} %param.12) | copy-start | bytes 4718596
  34.1 25.1 %collective-permute-start = (bf16[2,128,1024]{2,1,0:T(8,128)(2,1)S(1)}, bf16[2,128,1024]{2,1,0:T(8,128)(2,1)S(1)}, u32[]{:S(2)}, u32[]{:S(2)}) collective-permute-start(bf16[2,128,1024]{2,1,0:T(8,128)(2,1)S(1)} %pad_maximum_fusion.rows_ref), channel_id=1, source_target_pairs={{8,9},{9,10},{10,11},{11,12},{12,13},{13,14},{14,15},{24,25},{25,2... | collective-permute-start | bytes 1572872 | tf_op jit(solution)/shard_map/ppermute | solution.py:353
  35.0 9.7 %collective-permute-start.7 = (bf16[336,128]{1,0:T(8,128)(2,1)}, bf16[336,128]{1,0:T(8,128)(2,1)S(1)}, u32[]{:S(2)}, u32[]{:S(2)}) collective-permute-start(bf16[336,128]{1,0:T(8,128)(2,1)} %get-tuple-element.26), channel_id=1, source_target_pairs={{0,4},{1,5},{2,6},{3,7},{4,0},{5,1},{6,2},{7,3},{8,13},{9,12},{10,... | collective-permute-start | bytes 258056 | tf_op jit(solution)/shard_map/ppermute | solution.py:333
  35.9 12.3 %collective-permute-start.8 = (bf16[336,128]{1,0:T(8,128)(2,1)}, bf16[336,128]{1,0:T(8,128)(2,1)S(1)}, u32[]{:S(2)}, u32[]{:S(2)}) collective-permute-start(bf16[336,128]{1,0:T(8,128)(2,1)} %get-tuple-element.27), channel_id=1, source_target_pairs={{0,3},{1,2},{2,1},{3,0},{4,7},{5,6},{6,5},{7,4},{8,12},{9,13},{10,... | collective-permute-start | bytes 258056 | tf_op jit(solution)/shard_map/ppermute | solution.py:333
  37.6 25.0 %collective-permute-start.2 = (bf16[2,128,1024]{2,1,0:T(8,128)(2,1)S(1)}, bf16[2,128,1024]{2,1,0:T(8,128)(2,1)S(1)}, u32[]{:S(2)}, u32[]{:S(2)}) collective-permute-start(bf16[2,128,1024]{2,1,0:T(8,128)(2,1)S(1)} %halo.1), channel_id=1, source_target_pairs={{0,1},{1,2},{2,3},{3,4},{4,5},{5,6},{6,7},{16,17},{17,18},{18,19},... | collective-permute-start | bytes 1572872 | tf_op jit(solution)/shard_map/ppermute | solution.py:353
  41.4 6.8 %copy-start = (bf16[1,320,1024]{2,1,0:T(8,128)(2,1)S(1)}, bf16[1,320,1024]{2,1,0:T(8,128)(2,1)}, u32[]{:S(2)}) copy-start(bf16[1,320,1024]{2,1,0:T(8,128)(2,1)} %param.8) | copy-start | bytes 1966084
  41.4 6.8 %copy-start.1 = (bf16[1,320,1024]{2,1,0:T(8,128)(2,1)S(1)}, bf16[1,320,1024]{2,1,0:T(8,128)(2,1)}, u32[]{:S(2)}) copy-start(bf16[1,320,1024]{2,1,0:T(8,128)(2,1)} %param.9) | copy-start | bytes 1966084
  41.4 6.8 %copy-start.2 = (bf16[1,320,1024]{2,1,0:T(8,128)(2,1)S(1)}, bf16[1,320,1024]{2,1,0:T(8,128)(2,1)}, u32[]{:S(2)}) copy-start(bf16[1,320,1024]{2,1,0:T(8,128)(2,1)} %param.10) | copy-start | bytes 1966084
  44.6 5.6 %collective-permute-start.9 = (bf16[336,128]{1,0:T(8,128)(2,1)S(1)}, bf16[336,128]{1,0:T(8,128)(2,1)S(1)}, u32[]{:S(2)}, u32[]{:S(2)}) collective-permute-start(bf16[336,128]{1,0:T(8,128)(2,1)S(1)} %get-tuple-element.29), channel_id=1, source_target_pairs={{0,15},{1,14},{2,13},{3,12},{4,11},{5,10},{6,9},{7,8},{8,17},{9,16... | collective-permute-start | bytes 258056 | tf_op jit(solution)/shard_map/ppermute | solution.py:333
  44.7 14.5 %collective-permute-start.10 = (bf16[336,128]{1,0:T(8,128)(2,1)S(1)}, bf16[336,128]{1,0:T(8,128)(2,1)S(1)}, u32[]{:S(2)}, u32[]{:S(2)}) collective-permute-start(bf16[336,128]{1,0:T(8,128)(2,1)S(1)} %get-tuple-element.30), channel_id=1, source_target_pairs={{0,9},{1,8},{2,11},{3,10},{4,13},{5,12},{6,15},{7,14},{8,23},{9,22... | collective-permute-start | bytes 258056 | tf_op jit(solution)/shard_map/ppermute | solution.py:333
  49.7 27.2 %collective-permute-start.12 = (bf16[256,1024]{1,0:T(8,128)(2,1)S(1)}, bf16[256,1024]{1,0:T(8,128)(2,1)S(1)}, u32[]{:S(2)}, u32[]{:S(2)}) collective-permute-start(bf16[256,1024]{1,0:T(8,128)(2,1)S(1)} %near_inner.1), channel_id=1, source_target_pairs={{0,8},{1,9},{2,10},{3,11},{4,12},{5,13},{6,14},{7,15},{8,16},{9,17... | collective-permute-start | bytes 1572872 | tf_op jit(solution)/shard_map/ppermute | solution.py:333
  50.3 15.2 %collective-permute-start.13 = (bf16[336,128]{1,0:T(8,128)(2,1)S(1)}, bf16[336,128]{1,0:T(8,128)(2,1)S(1)}, u32[]{:S(2)}, u32[]{:S(2)}) collective-permute-start(bf16[336,128]{1,0:T(8,128)(2,1)S(1)} %get-tuple-element.32), channel_id=1, source_target_pairs={{0,14},{1,15},{2,12},{3,13},{4,10},{5,11},{6,8},{7,9},{8,18},{9,19... | collective-permute-start | bytes 258056 | tf_op jit(solution)/shard_map/ppermute | solution.py:333
  59.2 9.0 %collective-permute-start.14 = (bf16[336,128]{1,0:T(8,128)(2,1)S(1)}, bf16[336,128]{1,0:T(8,128)(2,1)S(1)}, u32[]{:S(2)}, u32[]{:S(2)}) collective-permute-start(bf16[336,128]{1,0:T(8,128)(2,1)S(1)} %get-tuple-element.33), channel_id=1, source_target_pairs={{0,10},{1,11},{2,8},{3,9},{4,14},{5,15},{6,12},{7,13},{8,22},{9,23... | collective-permute-start | bytes 258056 | tf_op jit(solution)/shard_map/ppermute | solution.py:333
  59.2 10.5 %collective-permute-start.15 = (bf16[336,128]{1,0:T(8,128)(2,1)S(1)}, bf16[336,128]{1,0:T(8,128)(2,1)S(1)}, u32[]{:S(2)}, u32[]{:S(2)}) collective-permute-start(bf16[336,128]{1,0:T(8,128)(2,1)S(1)} %get-tuple-element.34), channel_id=1, source_target_pairs={{0,13},{1,12},{2,15},{3,14},{4,9},{5,8},{6,11},{7,10},{8,19},{9,18... | collective-permute-start | bytes 258056 | tf_op jit(solution)/shard_map/ppermute | solution.py:333
  63.9 13.0 %collective-permute-start.11 = (bf16[144,1024]{1,0:T(8,128)(2,1)S(1)}, bf16[144,1024]{1,0:T(8,128)(2,1)S(1)}, u32[]{:S(2)}, u32[]{:S(2)}) collective-permute-start(bf16[144,1024]{1,0:T(8,128)(2,1)S(1)} %near_edge.1), channel_id=1, source_target_pairs={{0,8},{1,9},{2,10},{3,11},{4,12},{5,13},{6,14},{7,15},{8,16},{9,17... | collective-permute-start | bytes 884744 | tf_op jit(solution)/shard_map/ppermute | solution.py:333
  65.5 6.8 %collective-permute-start.16 = (bf16[336,128]{1,0:T(8,128)(2,1)S(1)}, bf16[336,128]{1,0:T(8,128)(2,1)S(1)}, u32[]{:S(2)}, u32[]{:S(2)}) collective-permute-start(bf16[336,128]{1,0:T(8,128)(2,1)S(1)} %get-tuple-element.35), channel_id=1, source_target_pairs={{0,12},{1,13},{2,14},{3,15},{4,8},{5,9},{6,10},{7,11},{8,21},{9,20... | collective-permute-start | bytes 258056 | tf_op jit(solution)/shard_map/ppermute | solution.py:333
  68.2 8.8 %collective-permute-start.17 = (bf16[336,128]{1,0:T(8,128)(2,1)S(1)}, bf16[336,128]{1,0:T(8,128)(2,1)S(1)}, u32[]{:S(2)}, u32[]{:S(2)}) collective-permute-start(bf16[336,128]{1,0:T(8,128)(2,1)S(1)} %get-tuple-element.36), channel_id=1, source_target_pairs={{0,11},{1,10},{2,9},{3,8},{4,15},{5,14},{6,13},{7,12},{8,20},{9,21... | collective-permute-start | bytes 258056 | tf_op jit(solution)/shard_map/ppermute | solution.py:333

commit v11 on v9

--- a/solution.py
+++ b/solution.py
@@ -128,7 +128,7 @@
     glob_keys = [block(key_ref, global_ref[g]) for g in range(GLOB)]
     glob_values = [block(value_ref, global_ref[g]) for g in range(GLOB)]
     peers = [peers_of(there, 0)[at] for at in chosen]
-    query_refs, out_refs = refs[: len(peers)], refs[len(peers) :]
+    query_refs, out_refs = refs[: len(peers)], refs[-len(peers) :]
     rows = query_refs[0].shape[0] - STAT_ROWS
     for chunk, query_ref, out_ref in zip(peers, query_refs, out_refs):
         blocks = rows // BLK
@@ -347,12 +347,12 @@
     halos = [halo_from(1, None), halo_from(0, came[0])]
     picks = random_blocks[0].reshape(-1)
 
-    def far_call(chosen):
+    def far_call(chosen, *after):
         count = len(chosen)
         return pl.pallas_call(
             functools.partial(far_kernel, there, chosen),
             out_shape=[chunk_shape] * count,
-            in_specs=[whole_smem] * 3 + [whole_vmem] * (2 + count),
+            in_specs=[whole_smem] * 3 + [whole_vmem] * (2 + count) + [anywhere] * len(after),
             out_specs=[whole_vmem] * count,
             compiler_params=params(queries),
             cost_estimate=pl.CostEstimate(
@@ -368,13 +368,14 @@
             keys_cache[0],
             values_cache[0],
             *[came[at] for at in chosen],
+            *after,
         )
 
     late = list(range(seq_count - 1 - seq_count // 4, seq_count - 1))
     early = [at for at in range(seq_count) if at not in late]
-    far = dict(zip(early, far_call(early)))
+    far = dict(zip(early, far_call(early, halos[0])))
     if late:
-        far.update(zip(late, far_call(late)))
+        far.update(zip(late, far_call(late, far[early[0]])))
     far = [far[at] for at in range(seq_count)]
     handed = [linked(shard, 1, steps) for shard, steps in zip(far[:-1], zip(*there))]
 

time: 54.3 us -> 60.4 us (1.11)
  local copies, waits for them, and re-layouts: 1.33 us -> 5.6 us
  starting transfers between devices: 31.6 us -> 28.2 us
  Pallas kernels: 9.22 us -> 12.4 us
  waiting for transfers between devices: 11 us -> 12.9 us
    ppermute x16, starting transfers between devices: 28.6 us -> 24.8 us  [linked(): return lax.ppermute(shard, ('section', 'seq'), pairs)]
    slice x4 -> x2, local copies, waits for them, and re-layouts: 0.01 us -> 2 us  [per_device(): tails = jnp.stack([keys_new[0, rows - halo:], values_new[0, rows - halo:]])]
    ppermute x16, waiting for transfers between devices: 11 us -> 12.9 us  [linked(): return lax.ppermute(shard, ('section', 'seq'), pairs)]
    pallas_call x2, Pallas kernels: 2.84 us -> 4.77 us  [near_call(): pl.pallas_call(functools.partial(kernel, there), out_shape=jax.ShapeDtype...]
    unnamed x17 -> x21, local copies, waits for them, and re-layouts: 1.21 us -> 2.76 us
    pallas_call x1, Pallas kernels: 0.27 us -> 1.02 us  [per_device(): pl.pallas_call(functools.partial(split_kernel, there), out_shape=[chunk_s...]
    another operation x1, local copies, waits for them, and re-layouts: 0.11 us -> 0.83 us  [per_device(): picks = random_blocks[0].reshape(-1)]
  transfers between devices with their start and end apart: 18 -> 18, of which waited for: 5 -> 4; matrix products, arithmetic and copies ran while one was open for 0% -> 3% of each run, Pallas kernels for 14% -> 18%
where the time goes in v11:
time: 60.4 us; the launch traced here: 60 us
  starting transfers between devices  28.2 us (47%)
  waiting for transfers between devices  12.9 us (21%)
  Pallas kernels  12.4 us (21%)
  local copies, waits for them, and re-layouts  5.6 us (9%)
  between operations  0.85 us (1%)
    ppermute x16, starting transfers between devices, linked(): return lax.ppermute(shard, ('section', 'seq'), pairs)  24.8 us
    ppermute x16, waiting for transfers between devices, linked(): return lax.ppermute(shard, ('section', 'seq'), pairs)  12.9 us
    pallas_call x2, Pallas kernels, far_call(): pl.pallas_call(functools.partial(far_kernel, there, chosen), out_shape=[c...  5.23 us
    pallas_call x2, Pallas kernels, near_call(): pl.pallas_call(functools.partial(kernel, there), out_shape=jax.ShapeDtype...  4.77 us
    ppermute x2, starting transfers between devices, halo_from(): return lax.ppermute(mine, ('section', 'seq'), pairs)  3.35 us
    unnamed x21, local copies, waits for them, and re-layouts  2.76 us
    slice x2, local copies, waits for them, and re-layouts, per_device(): tails = jnp.stack([keys_new[0, rows - halo:], values_new[0, rows - halo:]])  2 us
    pallas_call x1, Pallas kernels, per_device(): pl.pallas_call(functools.partial(merge_kernel, there), out_shape=jax.Shap...  1.37 us
  transfers between devices with their start and end apart: 18, of which 4 were waited for; matrix products, arithmetic and copies ran while one was open for 3% of the time, Pallas kernels for 18%

profile of v11, /device:TPU:0, one launch (start us, length us, event | category | flops | bytes accessed | tf_op | source)
XLA Modules:
  0.0 60.0 jit_solution(3564577461225101190)
XLA Ops:
  0.0 1.0 %slice.7 = bf16[1,128,1024]{2,1,0:T(8,128)(2,1)S(1)} slice(bf16[1,320,1024]{2,1,0:T(8,128)(2,1)} %param.10), slice={[0:1], [192:320], [0:1024]} | slice | bytes 524288 | tf_op jit(solution)/shard_map/slice | solution.py:329
  1.0 1.0 %slice.6 = bf16[1,128,1024]{2,1,0:T(8,128)(2,1)S(1)} slice(bf16[1,320,1024]{2,1,0:T(8,128)(2,1)} %param.9), slice={[0:1], [192:320], [0:1024]} | slice | bytes 524288 | tf_op jit(solution)/shard_map/slice | solution.py:329
  2.1 0.8 %collective-permute-start = (bf16[2,128,1024]{2,1,0:T(8,128)(2,1)S(1)}, bf16[2,128,1024]{2,1,0:T(8,128)(2,1)S(1)}, u32[]{:S(2)}, u32[]{:S(2)}) collective-permute-start(bf16[2,128,1024]{2,1,0:T(8,128)(2,1)S(1)} %pad_maximum_fusion.rows_ref), channel_id=1, source_target_pairs={{8,9},{9,10},{10,11},{11,12},{12,13},{13,14},{14,15},{24,25},{25,2... | collective-permute-start | bytes 1572872 | tf_op jit(solution)/shard_map/ppermute | solution.py:345
  3.6 1.0 %split.1 = (bf16[336,128]{1,0:T(8,128)(2,1)S(1)}, bf16[336,128]{1,0:T(8,128)(2,1)}, bf16[336,128]{1,0:T(8,128)(2,1)}, bf16[336,128]{1,0:T(8,128)(2,1)}, bf16[336...) custom-call(s32[1]{0:T(128)} %bitcast.8.span_ref, ...), custom_call_target="tpu_custom_call" | custom-call | bytes 1638400 | tf_op jit(solution)/shard_map/split/pallas_call | solution.py:292
  4.6 0.6 %copy-done.6 = bf16[336,128]{1,0:T(8,128)(2,1)} copy-done((bf16[336,128]{1,0:T(8,128)(2,1)}, bf16[336,128]{1,0:T(8,128)(2,1)S(1)}, u32[]{:S(2)}) %copy-start.6) | copy-done | bytes 86040
  5.3 6.0 %collective-permute-start.1 = (bf16[336,128]{1,0:T(8,128)(2,1)S(1)}, bf16[336,128]{1,0:T(8,128)(2,1)S(1)}, u32[]{:S(2)}, u32[]{:S(2)}) collective-permute-start(bf16[336,128]{1,0:T(8,128)(2,1)S(1)} %get-tuple-element.21), channel_id=1, source_target_pairs={{0,7},{1,6},{2,5},{3,4},{4,3},{5,2},{6,1},{7,0},{8,9},{9,8},{10,11... | collective-permute-start | bytes 258056 | tf_op jit(solution)/shard_map/ppermute | solution.py:325
  11.3 0.2 collective-permute-start.3
  11.5 0.7 %collective-permute-start.4 = (bf16[336,128]{1,0:T(8,128)(2,1)}, bf16[336,128]{1,0:T(8,128)(2,1)}, u32[]{:S(2)}, u32[]{:S(2)}) collective-permute-start(bf16[336,128]{1,0:T(8,128)(2,1)} %get-tuple-element.23), channel_id=1, source_target_pairs={{0,5},{1,4},{2,7},{3,6},{4,1},{5,0},{6,3},{7,2},{8,11},{9,10},{10,... | collective-permute-start | bytes 258056 | tf_op jit(solution)/shard_map/ppermute | solution.py:325
  12.2 2.0 %collective-permute-start.5 = (bf16[336,128]{1,0:T(8,128)(2,1)}, bf16[336,128]{1,0:T(8,128)(2,1)}, u32[]{:S(2)}, u32[]{:S(2)}) collective-permute-start(bf16[336,128]{1,0:T(8,128)(2,1)} %get-tuple-element.24), channel_id=1, source_target_pairs={{0,4},{1,5},{2,6},{3,7},{4,0},{5,1},{6,2},{7,3},{8,15},{9,14},{10,... | collective-permute-start | bytes 258056 | tf_op jit(solution)/shard_map/ppermute | solution.py:325
  14.2 1.7 %collective-permute-start.6 = (bf16[336,128]{1,0:T(8,128)(2,1)}, bf16[336,128]{1,0:T(8,128)(2,1)}, u32[]{:S(2)}, u32[]{:S(2)}) collective-permute-start(bf16[336,128]{1,0:T(8,128)(2,1)} %get-tuple-element.25), channel_id=1, source_target_pairs={{0,1},{1,0},{2,3},{3,2},{4,5},{5,4},{6,7},{7,6},{8,14},{9,15},{10,... | collective-permute-start | bytes 258056 | tf_op jit(solution)/shard_map/ppermute | solution.py:325
  15.9 0.7 %copy.10 = s32[1,40,3]{2,1,0:T(8,128)} copy(s32[1,40,3]{1,0,2:T(1,128)S(1)} %copy-done.9) | data formatting | bytes 960 | tf_op args[7]
  16.6 0.8 %reshape_squeeze.3.random_ref = s32[120]{0:T(128)S(1)} reshape(s32[1,40,3]{2,1,0:T(8,128)} %copy.10) | data formatting | bytes 960 | tf_op jit(solution)/shard_map/reshape;squeeze | solution.py:348
  17.5 1.2 %collective-permute-done.3.refs_1_ = bf16[336,128]{1,0:T(8,128)(2,1)S(1)} collective-permute-done((bf16[336,128]{1,0:T(8,128)(2,1)}, bf16[336,128]{1,0:T(8,128)(2,1)S(1)}, u32[]{:S(2)}, u32[]{:S(2)}) %collective-permute-start.3) | collective-permute-done | bytes 86048 | tf_op jit(solution)/shard_map/ppermute | solution.py:325
  18.6 0.2 collective-permute-start.7
  18.8 3.2 %collective-permute-done.4.refs_2_ = bf16[336,128]{1,0:T(8,128)(2,1)} collective-permute-done((bf16[336,128]{1,0:T(8,128)(2,1)}, bf16[336,128]{1,0:T(8,128)(2,1)}, u32[]{:S(2)}, u32[]{:S(2)}) %collective-permute-start.4) | collective-permute-done | bytes 86048 | tf_op jit(solution)/shard_map/ppermute | solution.py:325
  22.0 1.9 %collective-permute-done.5.refs_3_ = bf16[336,128]{1,0:T(8,128)(2,1)} collective-permute-done((bf16[336,128]{1,0:T(8,128)(2,1)}, bf16[336,128]{1,0:T(8,128)(2,1)}, u32[]{:S(2)}, u32[]{:S(2)}) %collective-permute-start.5) | collective-permute-done | bytes 86048 | tf_op jit(solution)/shard_map/ppermute | solution.py:325
  23.9 2.5 %collective-permute-start.2 = (bf16[2,128,1024]{2,1,0:T(8,128)(2,1)S(1)}, bf16[2,128,1024]{2,1,0:T(8,128)(2,1)S(1)}, u32[]{:S(2)}, u32[]{:S(2)}) collective-permute-start(bf16[2,128,1024]{2,1,0:T(8,128)(2,1)S(1)} %halo.1), channel_id=1, source_target_pairs={{0,1},{1,2},{2,3},{3,4},{4,5},{5,6},{6,7},{16,17},{17,18},{18,19},... | collective-permute-start | bytes 1572872 | tf_op jit(solution)/shard_map/ppermute | solution.py:345
  26.5 1.4 %copy-done.4 = bf16[1,6144,128]{2,1,0:T(8,128)(2,1)S(1)} copy-done((bf16[1,6144,128]{2,1,0:T(8,128)(2,1)S(1)}, bf16[1,6144,128]{2,1,0:T(8,128)(2,1)}, u32[]{:S(2)}) %copy-start.4) | copy-done | bytes 1572888
  27.9 3.7 %far.2 = (bf16[336,128]{1,0:T(8,128)(2,1)S(1)}, bf16[336,128]{1,0:T(8,128)(2,1)S(1)}, bf16[336,128]{1,0:T(8,128)(2,1)S(1)}, bf16[336,128]{1,0:T(8,128)(2,1)S(1)}...) custom-call(s32[1]{0:T(128)} %bitcast.9.span_ref, s32[2]{0:T(128)S(1)} %bitcast.22, ...), custom_call_target="tpu_custom_call" | custom-call | flops 12582912000 | bytes 4128768 | tf_op jit(solution)/shard_map/far/pallas_call | solution.py:352
  31.7 0.2 collective-permute-start.9
  31.9 4.9 %collective-permute-start.10 = (bf16[336,128]{1,0:T(8,128)(2,1)S(1)}, bf16[336,128]{1,0:T(8,128)(2,1)S(1)}, u32[]{:S(2)}, u32[]{:S(2)}) collective-permute-start(bf16[336,128]{1,0:T(8,128)(2,1)S(1)} %get-tuple-element.30), channel_id=1, source_target_pairs={{0,14},{1,15},{2,12},{3,13},{4,10},{5,11},{6,8},{7,9},{8,18},{9,19... | collective-permute-start | bytes 258056 | tf_op jit(solution)/shard_map/ppermute | solution.py:325
  36.8 2.5 %near_inner.1 = bf16[256,1024]{1,0:T(8,128)(2,1)S(1)} custom-call(bf16[320,1024]{1,0:T(8,128)(2,1)S(1)} %bitcast.12, bf16[320,1024]{1,0:T(8,128)(2,1)S(1)} %bitcast.14, bf16[320,1024]{1,0:T(8,128)(2,1)S(1)} %bitcast.16, bf16[336,128]{1,0:T(8,128)(2,1)S(1)} %get-tuple-element.31.own_ref, bf16[336,128]{1,0:T(8,128)(2,1)S(1)} %collective-permute-done.1._.refs_0_, ...), custom_call_target="tpu_custom_call" | custom-call | flops 8053063680 | bytes 1769472 | tf_op jit(solution)/shard_map/near_inner/pallas_call | solution.py:383
  39.3 0.3 collective-permute-start.13
  39.6 2.4 %collective-permute-start.14 = (bf16[336,128]{1,0:T(8,128)(2,1)S(1)}, bf16[336,128]{1,0:T(8,128)(2,1)S(1)}, u32[]{:S(2)}, u32[]{:S(2)}) collective-permute-start(bf16[336,128]{1,0:T(8,128)(2,1)S(1)} %get-tuple-element.33), channel_id=1, source_target_pairs={{0,12},{1,13},{2,14},{3,15},{4,8},{5,9},{6,10},{7,11},{8,23},{9,22... | collective-permute-start | bytes 258056 | tf_op jit(solution)/shard_map/ppermute | solution.py:325
  42.0 2.1 %collective-permute-start.15 = (bf16[336,128]{1,0:T(8,128)(2,1)S(1)}, bf16[336,128]{1,0:T(8,128)(2,1)S(1)}, u32[]{:S(2)}, u32[]{:S(2)}) collective-permute-start(bf16[336,128]{1,0:T(8,128)(2,1)S(1)} %get-tuple-element.34), channel_id=1, source_target_pairs={{0,9},{1,8},{2,11},{3,10},{4,13},{5,12},{6,15},{7,14},{8,22},{9,23... | collective-permute-start | bytes 258056 | tf_op jit(solution)/shard_map/ppermute | solution.py:325
  44.1 2.3 %near_edge.1 = bf16[144,1024]{1,0:T(8,128)(2,1)S(1)} custom-call(bf16[320,1024]{1,0:T(8,128)(2,1)S(1)} %bitcast.13, bf16[320,1024]{1,0:T(8,128)(2,1)S(1)} %bitcast.15, bf16[320,1024]{1,0:T(8,128)(2,1)S(1)} %bitcast.17, bf16[2,128,1024]{2,1,0:T(8,128)(2,1)S(1)} %collective-permute-done.refs_6_.odd_ref, ...), custom_call_target="tpu_custom_call" | custom-call | flops 5368709120 | bytes 1179648 | tf_op jit(solution)/shard_map/near_edge/pallas_call | solution.py:383
  46.5 2.5 %collective-permute-start.11 = (bf16[144,1024]{1,0:T(8,128)(2,1)S(1)}, bf16[144,1024]{1,0:T(8,128)(2,1)S(1)}, u32[]{:S(2)}, u32[]{:S(2)}) collective-permute-start(bf16[144,1024]{1,0:T(8,128)(2,1)S(1)} %near_edge.1), channel_id=1, source_target_pairs={{0,8},{1,9},{2,10},{3,11},{4,12},{5,13},{6,14},{7,15},{8,16},{9,17... | collective-permute-start | bytes 884744 | tf_op jit(solution)/shard_map/ppermute | solution.py:325
  48.9 1.5 %far.3 = (bf16[336,128]{1,0:T(8,128)(2,1)S(1)}, bf16[336,128]{1,0:T(8,128)(2,1)S(1)}) custom-call(s32[1]{0:T(128)} %bitcast.10.span_ref, s32[2]{0:T(128)S(1)} %bitcast.23, s32[120]{0:T(128)S(1)} %reshape_squeeze.3.random_ref, bf16[6144,128]{1,0:T(8,128)(2,1)S(1)} %bitcast.19, bf16[6144,128]{1,0:T(8,128)(2,1)S(1)} %bitcast.21, ...), custom_call_target="tpu_custom_call" | custom-call | flops 4194304000 | bytes 3473408 | tf_op jit(solution)/shard_map/far/pallas_call | solution.py:352
  50.5 1.0 %collective-permute-start.16 = (bf16[336,128]{1,0:T(8,128)(2,1)S(1)}, bf16[336,128]{1,0:T(8,128)(2,1)S(1)}, u32[]{:S(2)}, u32[]{:S(2)}) collective-permute-start(bf16[336,128]{1,0:T(8,128)(2,1)S(1)} %get-tuple-element.35), channel_id=1, source_target_pairs={{0,10},{1,11},{2,8},{3,9},{4,14},{5,15},{6,12},{7,13},{8,21},{9,20... | collective-permute-start | bytes 258056 | tf_op jit(solution)/shard_map/ppermute | solution.py:325
  51.4 0.6 collective-permute-start.17
  52.0 6.6 %collective-permute-done.16.refs_5_ = bf16[336,128]{1,0:T(8,128)(2,1)S(1)} collective-permute-done((bf16[336,128]{1,0:T(8,128)(2,1)S(1)}, bf16[336,128]{1,0:T(8,128)(2,1)S(1)}, u32[]{:S(2)}, u32[]{:S(2)}) %collective-permute-start.16) | collective-permute-done | bytes 86048 | tf_op jit(solution)/shard_map/ppermute | solution.py:325
  58.7 1.4 %merge.1 = bf16[320,1024]{1,0:T(8,128)(2,1)} custom-call(bf16[144,1024]{1,0:T(8,128)(2,1)S(1)} %collective-permute-done.11.edge_ref, bf16[256,1024]{1,0:T(8,128)(2,1)S(1)} %collective-permute-done.12.inner_ref, bf16[336,128]{1,0:T(8,128)(2,1)S(1)} %collective-permute-done.9.refs_8_.refs_0_, bf16[336,128]{1,0:T(8,128)(2,1)S(1)} %collective-permute-done.10.refs_9_.refs_1_, ...), custom_call_target="tpu_custom_call" | custom-call | bytes 1966080 | tf_op jit(solution)/shard_map/merge/pallas_call | solution.py:413
  (36 shorter events, 0.2 us)
Async XLA Ops:
  0.0 3.6 %copy-start = (bf16[1,320,1024]{2,1,0:T(8,128)(2,1)S(1)}, bf16[1,320,1024]{2,1,0:T(8,128)(2,1)}, u32[]{:S(2)}) copy-start(bf16[1,320,1024]{2,1,0:T(8,128)(2,1)} %param.8) | copy-start | bytes 1966084
  0.0 15.9 %copy-start.9 = (s32[1,40,3]{1,0,2:T(1,128)S(1)}, s32[1,40,3]{1,0,2:T(1,128)}, u32[]{:S(2)}) copy-start(s32[1,40,3]{1,0,2:T(1,128)} %param.15) | copy-start | bytes 1444
  2.0 24.5 %copy-start.3 = (bf16[1,6144,128]{2,1,0:T(8,128)(2,1)S(1)}, bf16[1,6144,128]{2,1,0:T(8,128)(2,1)}, u32[]{:S(2)}) copy-start(bf16[1,6144,128]{2,1,0:T(8,128)(2,1)} %param.11) | copy-start | bytes 4718596
  2.0 24.5 %copy-start.8 = (s32[1,2]{1,0:T(1,128)S(1)}, s32[1,2]{1,0:T(1,128)}, u32[]{:S(2)}) copy-start(s32[1,2]{1,0:T(1,128)} %param.14) | copy-start | bytes 28
  2.1 24.4 %collective-permute-start = (bf16[2,128,1024]{2,1,0:T(8,128)(2,1)S(1)}, bf16[2,128,1024]{2,1,0:T(8,128)(2,1)S(1)}, u32[]{:S(2)}, u32[]{:S(2)}) collective-permute-start(bf16[2,128,1024]{2,1,0:T(8,128)(2,1)S(1)} %pad_maximum_fusion.rows_ref), channel_id=1, source_target_pairs={{8,9},{9,10},{10,11},{11,12},{12,13},{13,14},{14,15},{24,25},{25,2... | collective-permute-start | bytes 1572872 | tf_op jit(solution)/shard_map/ppermute | solution.py:345
  4.6 0.6 %copy-start.6 = (bf16[336,128]{1,0:T(8,128)(2,1)}, bf16[336,128]{1,0:T(8,128)(2,1)S(1)}, u32[]{:S(2)}) copy-start(bf16[336,128]{1,0:T(8,128)(2,1)S(1)} %get-tuple-element.27) | copy-start | bytes 258052
  5.3 8.9 %copy-start.7 = (bf16[336,128]{1,0:T(8,128)(2,1)}, bf16[336,128]{1,0:T(8,128)(2,1)S(1)}, u32[]{:S(2)}) copy-start(bf16[336,128]{1,0:T(8,128)(2,1)S(1)} %get-tuple-element.26) | copy-start | bytes 258052
  5.3 8.9 %collective-permute-start.1 = (bf16[336,128]{1,0:T(8,128)(2,1)S(1)}, bf16[336,128]{1,0:T(8,128)(2,1)S(1)}, u32[]{:S(2)}, u32[]{:S(2)}) collective-permute-start(bf16[336,128]{1,0:T(8,128)(2,1)S(1)} %get-tuple-element.21), channel_id=1, source_target_pairs={{0,7},{1,6},{2,5},{3,4},{4,3},{5,2},{6,1},{7,0},{8,9},{9,8},{10,11... | collective-permute-start | bytes 258056 | tf_op jit(solution)/shard_map/ppermute | solution.py:325
  11.3 7.4 %collective-permute-start.3 = (bf16[336,128]{1,0:T(8,128)(2,1)}, bf16[336,128]{1,0:T(8,128)(2,1)S(1)}, u32[]{:S(2)}, u32[]{:S(2)}) collective-permute-start(bf16[336,128]{1,0:T(8,128)(2,1)} %get-tuple-element.22), channel_id=1, source_target_pairs={{0,6},{1,7},{2,4},{3,5},{4,2},{5,3},{6,0},{7,1},{8,10},{9,11},{10,... | collective-permute-start | bytes 258056 | tf_op jit(solution)/shard_map/ppermute | solution.py:325
  11.5 10.5 %collective-permute-start.4 = (bf16[336,128]{1,0:T(8,128)(2,1)}, bf16[336,128]{1,0:T(8,128)(2,1)}, u32[]{:S(2)}, u32[]{:S(2)}) collective-permute-start(bf16[336,128]{1,0:T(8,128)(2,1)} %get-tuple-element.23), channel_id=1, source_target_pairs={{0,5},{1,4},{2,7},{3,6},{4,1},{5,0},{6,3},{7,2},{8,11},{9,10},{10,... | collective-permute-start | bytes 258056 | tf_op jit(solution)/shard_map/ppermute | solution.py:325
  12.2 11.7 %collective-permute-start.5 = (bf16[336,128]{1,0:T(8,128)(2,1)}, bf16[336,128]{1,0:T(8,128)(2,1)}, u32[]{:S(2)}, u32[]{:S(2)}) collective-permute-start(bf16[336,128]{1,0:T(8,128)(2,1)} %get-tuple-element.24), channel_id=1, source_target_pairs={{0,4},{1,5},{2,6},{3,7},{4,0},{5,1},{6,2},{7,3},{8,15},{9,14},{10,... | collective-permute-start | bytes 258056 | tf_op jit(solution)/shard_map/ppermute | solution.py:325
  14.2 12.3 %collective-permute-start.6 = (bf16[336,128]{1,0:T(8,128)(2,1)}, bf16[336,128]{1,0:T(8,128)(2,1)}, u32[]{:S(2)}, u32[]{:S(2)}) collective-permute-start(bf16[336,128]{1,0:T(8,128)(2,1)} %get-tuple-element.25), channel_id=1, source_target_pairs={{0,1},{1,0},{2,3},{3,2},{4,5},{5,4},{6,7},{7,6},{8,14},{9,15},{10,... | collective-permute-start | bytes 258056 | tf_op jit(solution)/shard_map/ppermute | solution.py:325
  18.6 18.1 %collective-permute-start.7 = (bf16[336,128]{1,0:T(8,128)(2,1)}, bf16[336,128]{1,0:T(8,128)(2,1)S(1)}, u32[]{:S(2)}, u32[]{:S(2)}) collective-permute-start(bf16[336,128]{1,0:T(8,128)(2,1)} %copy-done.7), channel_id=1, source_target_pairs={{0,2},{1,3},{2,0},{3,1},{4,6},{5,7},{6,4},{7,5},{8,13},{9,12},{10,... | collective-permute-start | bytes 258056 | tf_op jit(solution)/shard_map/ppermute | solution.py:325
  22.0 14.8 %collective-permute-start.8 = (bf16[336,128]{1,0:T(8,128)(2,1)}, bf16[336,128]{1,0:T(8,128)(2,1)S(1)}, u32[]{:S(2)}, u32[]{:S(2)}) collective-permute-start(bf16[336,128]{1,0:T(8,128)(2,1)} %copy-done.6), channel_id=1, source_target_pairs={{0,3},{1,2},{2,1},{3,0},{4,7},{5,6},{6,5},{7,4},{8,12},{9,13},{10,... | collective-permute-start | bytes 258056 | tf_op jit(solution)/shard_map/ppermute | solution.py:325
  23.9 15.7 %collective-permute-start.2 = (bf16[2,128,1024]{2,1,0:T(8,128)(2,1)S(1)}, bf16[2,128,1024]{2,1,0:T(8,128)(2,1)S(1)}, u32[]{:S(2)}, u32[]{:S(2)}) collective-permute-start(bf16[2,128,1024]{2,1,0:T(8,128)(2,1)S(1)} %halo.1), channel_id=1, source_target_pairs={{0,1},{1,2},{2,3},{3,4},{4,5},{5,6},{6,7},{16,17},{17,18},{18,19},... | collective-permute-start | bytes 1572872 | tf_op jit(solution)/shard_map/ppermute | solution.py:345
  26.5 1.4 %copy-start.4 = (bf16[1,6144,128]{2,1,0:T(8,128)(2,1)S(1)}, bf16[1,6144,128]{2,1,0:T(8,128)(2,1)}, u32[]{:S(2)}) copy-start(bf16[1,6144,128]{2,1,0:T(8,128)(2,1)} %param.12) | copy-start | bytes 4718596
  27.9 8.8 %copy-start.1 = (bf16[1,320,1024]{2,1,0:T(8,128)(2,1)S(1)}, bf16[1,320,1024]{2,1,0:T(8,128)(2,1)}, u32[]{:S(2)}) copy-start(bf16[1,320,1024]{2,1,0:T(8,128)(2,1)} %param.9) | copy-start | bytes 1966084
  27.9 8.8 %copy-start.2 = (bf16[1,320,1024]{2,1,0:T(8,128)(2,1)S(1)}, bf16[1,320,1024]{2,1,0:T(8,128)(2,1)}, u32[]{:S(2)}) copy-start(bf16[1,320,1024]{2,1,0:T(8,128)(2,1)} %param.10) | copy-start | bytes 1966084
  31.7 10.4 %collective-permute-start.9 = (bf16[336,128]{1,0:T(8,128)(2,1)S(1)}, bf16[336,128]{1,0:T(8,128)(2,1)S(1)}, u32[]{:S(2)}, u32[]{:S(2)}) collective-permute-start(bf16[336,128]{1,0:T(8,128)(2,1)S(1)} %get-tuple-element.29.refs_2_), channel_id=1, source_target_pairs={{0,15},{1,14},{2,13},{3,12},{4,11},{5,10},{6,9},{7,8},{8,17},{9,16... | collective-permute-start | bytes 258056 | tf_op jit(solution)/shard_map/ppermute | solution.py:325
  31.9 12.3 %collective-permute-start.10 = (bf16[336,128]{1,0:T(8,128)(2,1)S(1)}, bf16[336,128]{1,0:T(8,128)(2,1)S(1)}, u32[]{:S(2)}, u32[]{:S(2)}) collective-permute-start(bf16[336,128]{1,0:T(8,128)(2,1)S(1)} %get-tuple-element.30), channel_id=1, source_target_pairs={{0,14},{1,15},{2,12},{3,13},{4,10},{5,11},{6,8},{7,9},{8,18},{9,19... | collective-permute-start | bytes 258056 | tf_op jit(solution)/shard_map/ppermute | solution.py:325
  39.3 19.4 %collective-permute-start.12 = (bf16[256,1024]{1,0:T(8,128)(2,1)S(1)}, bf16[256,1024]{1,0:T(8,128)(2,1)S(1)}, u32[]{:S(2)}, u32[]{:S(2)}) collective-permute-start(bf16[256,1024]{1,0:T(8,128)(2,1)S(1)} %near_inner.1), channel_id=1, source_target_pairs={{0,8},{1,9},{2,10},{3,11},{4,12},{5,13},{6,14},{7,15},{8,16},{9,17... | collective-permute-start | bytes 1572872 | tf_op jit(solution)/shard_map/ppermute | solution.py:325
  39.3 11.1 %collective-permute-start.13 = (bf16[336,128]{1,0:T(8,128)(2,1)S(1)}, bf16[336,128]{1,0:T(8,128)(2,1)S(1)}, u32[]{:S(2)}, u32[]{:S(2)}) collective-permute-start(bf16[336,128]{1,0:T(8,128)(2,1)S(1)} %get-tuple-element.32), channel_id=1, source_target_pairs={{0,13},{1,12},{2,15},{3,14},{4,9},{5,8},{6,11},{7,10},{8,19},{9,18... | collective-permute-start | bytes 258056 | tf_op jit(solution)/shard_map/ppermute | solution.py:325
  39.6 11.8 %collective-permute-start.14 = (bf16[336,128]{1,0:T(8,128)(2,1)S(1)}, bf16[336,128]{1,0:T(8,128)(2,1)S(1)}, u32[]{:S(2)}, u32[]{:S(2)}) collective-permute-start(bf16[336,128]{1,0:T(8,128)(2,1)S(1)} %get-tuple-element.33), channel_id=1, source_target_pairs={{0,12},{1,13},{2,14},{3,15},{4,8},{5,9},{6,10},{7,11},{8,23},{9,22... | collective-permute-start | bytes 258056 | tf_op jit(solution)/shard_map/ppermute | solution.py:325
  42.0 6.9 %copy-start.5 = (bf16[1,6144,128]{2,1,0:T(8,128)(2,1)S(1)}, bf16[1,6144,128]{2,1,0:T(8,128)(2,1)}, u32[]{:S(2)}) copy-start(bf16[1,6144,128]{2,1,0:T(8,128)(2,1)} %param.12) | copy-start | bytes 4718596
  42.0 10.0 %collective-permute-start.15 = (bf16[336,128]{1,0:T(8,128)(2,1)S(1)}, bf16[336,128]{1,0:T(8,128)(2,1)S(1)}, u32[]{:S(2)}, u32[]{:S(2)}) collective-permute-start(bf16[336,128]{1,0:T(8,128)(2,1)S(1)} %get-tuple-element.34), channel_id=1, source_target_pairs={{0,9},{1,8},{2,11},{3,10},{4,13},{5,12},{6,15},{7,14},{8,22},{9,23... | collective-permute-start | bytes 258056 | tf_op jit(solution)/shard_map/ppermute | solution.py:325
  46.5 12.2 %collective-permute-start.11 = (bf16[144,1024]{1,0:T(8,128)(2,1)S(1)}, bf16[144,1024]{1,0:T(8,128)(2,1)S(1)}, u32[]{:S(2)}, u32[]{:S(2)}) collective-permute-start(bf16[144,1024]{1,0:T(8,128)(2,1)S(1)} %near_edge.1), channel_id=1, source_target_pairs={{0,8},{1,9},{2,10},{3,11},{4,12},{5,13},{6,14},{7,15},{8,16},{9,17... | collective-permute-start | bytes 884744 | tf_op jit(solution)/shard_map/ppermute | solution.py:325
  50.5 8.2 %collective-permute-start.16 = (bf16[336,128]{1,0:T(8,128)(2,1)S(1)}, bf16[336,128]{1,0:T(8,128)(2,1)S(1)}, u32[]{:S(2)}, u32[]{:S(2)}) collective-permute-start(bf16[336,128]{1,0:T(8,128)(2,1)S(1)} %get-tuple-element.35), channel_id=1, source_target_pairs={{0,10},{1,11},{2,8},{3,9},{4,14},{5,15},{6,12},{7,13},{8,21},{9,20... | collective-permute-start | bytes 258056 | tf_op jit(solution)/shard_map/ppermute | solution.py:325
  51.4 7.2 %collective-permute-start.17 = (bf16[336,128]{1,0:T(8,128)(2,1)S(1)}, bf16[336,128]{1,0:T(8,128)(2,1)S(1)}, u32[]{:S(2)}, u32[]{:S(2)}) collective-permute-start(bf16[336,128]{1,0:T(8,128)(2,1)S(1)} %get-tuple-element.36), channel_id=1, source_target_pairs={{0,11},{1,10},{2,9},{3,8},{4,15},{5,14},{6,13},{7,12},{8,20},{9,21... | collective-permute-start | bytes 258056 | tf_op jit(solution)/shard_map/ppermute | solution.py:325

commit v12 on v9

--- a/solution.py
+++ b/solution.py
@@ -179,12 +179,11 @@
         for start, size in zip(starts, sizes)
     ]
     peers = peers_of(there, 0)
-    for begin in range(0, len(peers), 2):
-        pair = range(begin, min(begin + 2, len(peers)))
-        all_lanes = [pl.ds(pl.multiple_of(peers[at] * HD, HD), HD) for at in pair]
+    for peer, came_ref in zip(peers, came_refs):
+        all_lanes = [pl.ds(pl.multiple_of(peer * HD, HD), HD)]
         all_scores, all_values = [], []
-        for at, lanes in zip(pair, all_lanes):
-            width = came_refs[at][rows:, :].astype(jnp.float32)[:1]
+        for lanes in all_lanes:
+            width = came_ref[rows:, :].astype(jnp.float32)[:1]
             width = jnp.concatenate([width] * ((2 * BLK + halo) // LANES), axis=1)
             for start, size, lead in zip(starts, sizes, leads):
                 query = query_ref[start : start + size, lanes]
@@ -344,7 +343,7 @@
         ]
         return lax.ppermute(mine, ("section", "seq"), pairs)
 
-    halos = [halo_from(1, None), halo_from(0, came[0])]
+    halos = [halo_from(0, None), halo_from(1, came[0])]
     picks = random_blocks[0].reshape(-1)
 
     def far_call(chosen):

time: 54.3 us -> 59.5 us (1.096)
  starting transfers between devices: 31.6 us -> 37.9 us
  waiting for transfers between devices: 11 us -> 9.49 us
    ppermute x16, starting transfers between devices: 28.6 us -> 34.7 us  [linked(): return lax.ppermute(shard, ('section', 'seq'), pairs)]
    ppermute x16, waiting for transfers between devices: 11 us -> 9.48 us  [linked(): return lax.ppermute(shard, ('section', 'seq'), pairs)]
where the time goes in v12:
time: 59.5 us; the launch traced here: 59.3 us
  starting transfers between devices  37.9 us (64%)
  Pallas kernels  9.64 us (16%)
  waiting for transfers between devices  9.49 us (16%)
  local copies, waits for them, and re-layouts  1.33 us (2%)
  between operations  0.91 us (2%)
    ppermute x16, starting transfers between devices, linked(): return lax.ppermute(shard, ('section', 'seq'), pairs)  34.7 us
    ppermute x16, waiting for transfers between devices, linked(): return lax.ppermute(shard, ('section', 'seq'), pairs)  9.48 us
    pallas_call x2, Pallas kernels, far_call(): pl.pallas_call(functools.partial(far_kernel, there, chosen), out_shape=[c...  4.71 us
    pallas_call x2, Pallas kernels, near_call(): pl.pallas_call(functools.partial(kernel, there), out_shape=jax.ShapeDtype...  3.26 us
    ppermute x2, starting transfers between devices, halo_from(): return lax.ppermute(mine, ('section', 'seq'), pairs)  3.17 us
    pallas_call x1, Pallas kernels, per_device(): pl.pallas_call(functools.partial(merge_kernel, there), out_shape=jax.Shap...  1.36 us
    unnamed x17, local copies, waits for them, and re-layouts  1.21 us
  transfers between devices with their start and end apart: 18, of which 5 were waited for; matrix products, arithmetic and copies ran while one was open for 0% of the time, Pallas kernels for 14%

profile of v12, /device:TPU:0, one launch (start us, length us, event | category | flops | bytes accessed | tf_op | source)
XLA Modules:
  0.0 59.3 jit_solution(3315628639937792645)
XLA Ops:
  0.7 1.1 %copy-done = bf16[1,320,1024]{2,1,0:T(8,128)(2,1)S(1)} copy-done((bf16[1,320,1024]{2,1,0:T(8,128)(2,1)S(1)}, bf16[1,320,1024]{2,1,0:T(8,128)(2,1)}, u32[]{:S(2)}) %copy-start) | copy-done | bytes 655384
  1.8 0.3 split.1
  2.0 6.1 %collective-permute-start.1 = (bf16[336,128]{1,0:T(8,128)(2,1)S(1)}, bf16[336,128]{1,0:T(8,128)(2,1)S(1)}, u32[]{:S(2)}, u32[]{:S(2)}) collective-permute-start(bf16[336,128]{1,0:T(8,128)(2,1)S(1)} %get-tuple-element.21), channel_id=1, source_target_pairs={{0,7},{1,6},{2,5},{3,4},{4,3},{5,2},{6,1},{7,0},{8,9},{9,8},{10,11... | collective-permute-start | bytes 258056 | tf_op jit(solution)/shard_map/ppermute | solution.py:324
  8.1 0.2 collective-permute-start.3
  8.3 0.7 %collective-permute-start.4 = (bf16[336,128]{1,0:T(8,128)(2,1)S(1)}, bf16[336,128]{1,0:T(8,128)(2,1)S(1)}, u32[]{:S(2)}, u32[]{:S(2)}) collective-permute-start(bf16[336,128]{1,0:T(8,128)(2,1)S(1)} %get-tuple-element.23), channel_id=1, source_target_pairs={{0,5},{1,4},{2,7},{3,6},{4,1},{5,0},{6,3},{7,2},{8,11},{9,10},{10,... | collective-permute-start | bytes 258056 | tf_op jit(solution)/shard_map/ppermute | solution.py:324
  9.1 2.0 %collective-permute-start.5 = (bf16[336,128]{1,0:T(8,128)(2,1)S(1)}, bf16[336,128]{1,0:T(8,128)(2,1)S(1)}, u32[]{:S(2)}, u32[]{:S(2)}) collective-permute-start(bf16[336,128]{1,0:T(8,128)(2,1)S(1)} %get-tuple-element.24), channel_id=1, source_target_pairs={{0,4},{1,5},{2,6},{3,7},{4,0},{5,1},{6,2},{7,3},{8,15},{9,14},{10,... | collective-permute-start | bytes 258056 | tf_op jit(solution)/shard_map/ppermute | solution.py:324
  11.1 1.6 %collective-permute-start.6 = (bf16[336,128]{1,0:T(8,128)(2,1)S(1)}, bf16[336,128]{1,0:T(8,128)(2,1)S(1)}, u32[]{:S(2)}, u32[]{:S(2)}) collective-permute-start(bf16[336,128]{1,0:T(8,128)(2,1)S(1)} %get-tuple-element.25), channel_id=1, source_target_pairs={{0,1},{1,0},{2,3},{3,2},{4,5},{5,4},{6,7},{7,6},{8,14},{9,15},{10,... | collective-permute-start | bytes 258056 | tf_op jit(solution)/shard_map/ppermute | solution.py:324
  12.7 0.1 copy.10
  12.8 0.1 reshape_squeeze.3.random_ref
  13.0 0.1 pad_maximum_fusion.rows_ref
  13.0 2.5 %collective-permute-start = (bf16[2,128,1024]{2,1,0:T(8,128)(2,1)S(1)}, bf16[2,128,1024]{2,1,0:T(8,128)(2,1)S(1)}, u32[]{:S(2)}, u32[]{:S(2)}) collective-permute-start(bf16[2,128,1024]{2,1,0:T(8,128)(2,1)S(1)} %pad_maximum_fusion.rows_ref), channel_id=1, source_target_pairs={{0,1},{1,2},{2,3},{3,4},{4,5},{5,6},{6,7},{16,17},{17,18},{18,19},... | collective-permute-start | bytes 1572872 | tf_op jit(solution)/shard_map/ppermute | solution.py:344
  15.6 4.4 %collective-permute-start.7 = (bf16[336,128]{1,0:T(8,128)(2,1)S(1)}, bf16[336,128]{1,0:T(8,128)(2,1)S(1)}, u32[]{:S(2)}, u32[]{:S(2)}) collective-permute-start(bf16[336,128]{1,0:T(8,128)(2,1)S(1)} %get-tuple-element.26), channel_id=1, source_target_pairs={{0,2},{1,3},{2,0},{3,1},{4,6},{5,7},{6,4},{7,5},{8,13},{9,12},{10,... | collective-permute-start | bytes 258056 | tf_op jit(solution)/shard_map/ppermute | solution.py:324
  20.0 1.2 %collective-permute-done.4.refs_2_ = bf16[336,128]{1,0:T(8,128)(2,1)S(1)} collective-permute-done((bf16[336,128]{1,0:T(8,128)(2,1)S(1)}, bf16[336,128]{1,0:T(8,128)(2,1)S(1)}, u32[]{:S(2)}, u32[]{:S(2)}) %collective-permute-start.4) | collective-permute-done | bytes 86048 | tf_op jit(solution)/shard_map/ppermute | solution.py:324
  21.3 2.0 %collective-permute-done.5.refs_3_ = bf16[336,128]{1,0:T(8,128)(2,1)S(1)} collective-permute-done((bf16[336,128]{1,0:T(8,128)(2,1)S(1)}, bf16[336,128]{1,0:T(8,128)(2,1)S(1)}, u32[]{:S(2)}, u32[]{:S(2)}) %collective-permute-start.5) | collective-permute-done | bytes 86048 | tf_op jit(solution)/shard_map/ppermute | solution.py:324
  23.2 0.7 %collective-permute-start.2 = (bf16[2,128,1024]{2,1,0:T(8,128)(2,1)S(1)}, bf16[2,128,1024]{2,1,0:T(8,128)(2,1)S(1)}, u32[]{:S(2)}, u32[]{:S(2)}) collective-permute-start(bf16[2,128,1024]{2,1,0:T(8,128)(2,1)S(1)} %halo.1), channel_id=1, source_target_pairs={{8,9},{9,10},{10,11},{11,12},{12,13},{13,14},{14,15},{24,25},{25,2... | collective-permute-start | bytes 1572872 | tf_op jit(solution)/shard_map/ppermute | solution.py:344
  24.0 3.2 %far.2 = (bf16[336,128]{1,0:T(8,128)(2,1)S(1)}, bf16[336,128]{1,0:T(8,128)(2,1)S(1)}, bf16[336,128]{1,0:T(8,128)(2,1)S(1)}, bf16[336,128]{1,0:T(8,128)(2,1)S(1)}...) custom-call(s32[1]{0:T(128)} %bitcast.9.span_ref, s32[2]{0:T(128)S(1)} %bitcast.22, ...), custom_call_target="tpu_custom_call" | custom-call | flops 12582912000 | bytes 4128768 | tf_op jit(solution)/shard_map/far/pallas_call | solution.py:351
  27.2 0.1 collective-permute-start.9
  27.3 2.7 %collective-permute-start.10 = (bf16[336,128]{1,0:T(8,128)(2,1)S(1)}, bf16[336,128]{1,0:T(8,128)(2,1)S(1)}, u32[]{:S(2)}, u32[]{:S(2)}) collective-permute-start(bf16[336,128]{1,0:T(8,128)(2,1)S(1)} %get-tuple-element.30), channel_id=1, source_target_pairs={{0,14},{1,15},{2,12},{3,13},{4,10},{5,11},{6,8},{7,9},{8,18},{9,19... | collective-permute-start | bytes 258056 | tf_op jit(solution)/shard_map/ppermute | solution.py:324
  30.0 2.2 %near_inner.1 = bf16[256,1024]{1,0:T(8,128)(2,1)S(1)} custom-call(bf16[320,1024]{1,0:T(8,128)(2,1)S(1)} %bitcast.12, bf16[320,1024]{1,0:T(8,128)(2,1)S(1)} %bitcast.14, bf16[320,1024]{1,0:T(8,128)(2,1)S(1)} %bitcast.16, bf16[336,128]{1,0:T(8,128)(2,1)S(1)} %get-tuple-element.31.own_ref, bf16[336,128]{1,0:T(8,128)(2,1)S(1)} %collective-permute-done.1._.refs_0_, ...), custom_call_target="tpu_custom_call" | custom-call | flops 8053063680 | bytes 1769472 | tf_op jit(solution)/shard_map/near_inner/pallas_call | solution.py:381
  32.3 0.1 collective-permute-start.12
  32.4 11.3 %collective-permute-start.13 = (bf16[336,128]{1,0:T(8,128)(2,1)S(1)}, bf16[336,128]{1,0:T(8,128)(2,1)S(1)}, u32[]{:S(2)}, u32[]{:S(2)}) collective-permute-start(bf16[336,128]{1,0:T(8,128)(2,1)S(1)} %get-tuple-element.32), channel_id=1, source_target_pairs={{0,13},{1,12},{2,15},{3,14},{4,9},{5,8},{6,11},{7,10},{8,19},{9,18... | collective-permute-start | bytes 258056 | tf_op jit(solution)/shard_map/ppermute | solution.py:324
  43.7 0.0 collective-permute-start.14
  43.7 2.4 %collective-permute-start.15 = (bf16[336,128]{1,0:T(8,128)(2,1)S(1)}, bf16[336,128]{1,0:T(8,128)(2,1)S(1)}, u32[]{:S(2)}, u32[]{:S(2)}) collective-permute-start(bf16[336,128]{1,0:T(8,128)(2,1)S(1)} %get-tuple-element.34), channel_id=1, source_target_pairs={{0,9},{1,8},{2,11},{3,10},{4,13},{5,12},{6,15},{7,14},{8,22},{9,23... | collective-permute-start | bytes 258056 | tf_op jit(solution)/shard_map/ppermute | solution.py:324
  46.1 1.0 %near_edge.1 = bf16[144,1024]{1,0:T(8,128)(2,1)S(1)} custom-call(bf16[320,1024]{1,0:T(8,128)(2,1)S(1)} %bitcast.13, bf16[320,1024]{1,0:T(8,128)(2,1)S(1)} %bitcast.15, bf16[320,1024]{1,0:T(8,128)(2,1)S(1)} %bitcast.17, bf16[2,128,1024]{2,1,0:T(8,128)(2,1)S(1)} %collective-permute-done.odd_ref, bf16[2,128,1024]{2,1,0:T(8,128)(2,1)S(1)} %collective-permute-done.2.even_ref, ...), custom_call_target="tpu_custom_call" | custom-call | flops 5368709120 | bytes 1179648 | tf_op jit(solution)/shard_map/near_edge/pallas_call | solution.py:381
  47.1 0.1 collective-permute-start.11
  47.2 1.5 %far.3 = (bf16[336,128]{1,0:T(8,128)(2,1)S(1)}, bf16[336,128]{1,0:T(8,128)(2,1)S(1)}) custom-call(s32[1]{0:T(128)} %bitcast.10.span_ref, s32[2]{0:T(128)S(1)} %bitcast.23, s32[120]{0:T(128)S(1)} %reshape_squeeze.3.random_ref, bf16[6144,128]{1,0:T(8,128)(2,1)S(1)} %bitcast.19, bf16[6144,128]{1,0:T(8,128)(2,1)S(1)} %bitcast.21, ...), custom_call_target="tpu_custom_call" | custom-call | flops 4194304000 | bytes 3473408 | tf_op jit(solution)/shard_map/far/pallas_call | solution.py:351
  48.7 0.9 %collective-permute-start.16 = (bf16[336,128]{1,0:T(8,128)(2,1)S(1)}, bf16[336,128]{1,0:T(8,128)(2,1)S(1)}, u32[]{:S(2)}, u32[]{:S(2)}) collective-permute-start(bf16[336,128]{1,0:T(8,128)(2,1)S(1)} %get-tuple-element.35), channel_id=1, source_target_pairs={{0,10},{1,11},{2,8},{3,9},{4,14},{5,15},{6,12},{7,13},{8,21},{9,20... | collective-permute-start | bytes 258056 | tf_op jit(solution)/shard_map/ppermute | solution.py:324
  49.6 1.7 %collective-permute-done.14.refs_3_ = bf16[336,128]{1,0:T(8,128)(2,1)S(1)} collective-permute-done((bf16[336,128]{1,0:T(8,128)(2,1)S(1)}, bf16[336,128]{1,0:T(8,128)(2,1)S(1)}, u32[]{:S(2)}, u32[]{:S(2)}) %collective-permute-start.14) | collective-permute-done | bytes 86048 | tf_op jit(solution)/shard_map/ppermute | solution.py:324
  51.3 2.1 %collective-permute-start.17 = (bf16[336,128]{1,0:T(8,128)(2,1)S(1)}, bf16[336,128]{1,0:T(8,128)(2,1)S(1)}, u32[]{:S(2)}, u32[]{:S(2)}) collective-permute-start(bf16[336,128]{1,0:T(8,128)(2,1)S(1)} %get-tuple-element.36), channel_id=1, source_target_pairs={{0,11},{1,10},{2,9},{3,8},{4,15},{5,14},{6,13},{7,12},{8,20},{9,21... | collective-permute-start | bytes 258056 | tf_op jit(solution)/shard_map/ppermute | solution.py:324
  53.4 2.8 %collective-permute-done.16.refs_5_ = bf16[336,128]{1,0:T(8,128)(2,1)S(1)} collective-permute-done((bf16[336,128]{1,0:T(8,128)(2,1)S(1)}, bf16[336,128]{1,0:T(8,128)(2,1)S(1)}, u32[]{:S(2)}, u32[]{:S(2)}) %collective-permute-start.16) | collective-permute-done | bytes 86048 | tf_op jit(solution)/shard_map/ppermute | solution.py:324
  56.3 1.7 %collective-permute-done.17.refs_6_ = bf16[336,128]{1,0:T(8,128)(2,1)S(1)} collective-permute-done((bf16[336,128]{1,0:T(8,128)(2,1)S(1)}, bf16[336,128]{1,0:T(8,128)(2,1)S(1)}, u32[]{:S(2)}, u32[]{:S(2)}) %collective-permute-start.17) | collective-permute-done | bytes 86048 | tf_op jit(solution)/shard_map/ppermute | solution.py:324
  58.0 1.4 %merge.1 = bf16[320,1024]{1,0:T(8,128)(2,1)} custom-call(bf16[144,1024]{1,0:T(8,128)(2,1)S(1)} %collective-permute-done.11.edge_ref, bf16[256,1024]{1,0:T(8,128)(2,1)S(1)} %collective-permute-done.12.inner_ref, bf16[336,128]{1,0:T(8,128)(2,1)S(1)} %collective-permute-done.9.refs_8_.refs_0_, bf16[336,128]{1,0:T(8,128)(2,1)S(1)} %collective-permute-done.10.refs_9_.refs_1_, ...), custom_call_target="tpu_custom_call" | custom-call | bytes 1966080 | tf_op jit(solution)/shard_map/merge/pallas_call | solution.py:411
  (34 shorter events, 0.1 us)
Async XLA Ops:
  0.0 12.7 %copy-start.7 = (s32[1,40,3]{1,0,2:T(1,128)S(1)}, s32[1,40,3]{1,0,2:T(1,128)}, u32[]{:S(2)}) copy-start(s32[1,40,3]{1,0,2:T(1,128)} %param.15) | copy-start | bytes 1444
  0.7 1.1 %copy-start = (bf16[1,320,1024]{2,1,0:T(8,128)(2,1)S(1)}, bf16[1,320,1024]{2,1,0:T(8,128)(2,1)}, u32[]{:S(2)}) copy-start(bf16[1,320,1024]{2,1,0:T(8,128)(2,1)} %param.8) | copy-start | bytes 1966084
  1.8 11.2 %slice-start = ((bf16[1,320,1024]{2,1,0:T(8,128)(2,1)}), bf16[1,128,1024]{2,1,0:T(8,128)(2,1)S(1)}, s32[]{:S(2)}) async-start(bf16[1,320,1024]{2,1,0:T(8,128)(2,1)} %param.9), calls=%async_computation | async-start | bytes 524288 | tf_op jit(solution)/shard_map/slice | solution.py:328
  1.8 11.2 %slice-start.1 = ((bf16[1,320,1024]{2,1,0:T(8,128)(2,1)}), bf16[1,128,1024]{2,1,0:T(8,128)(2,1)S(1)}, s32[]{:S(2)}) async-start(bf16[1,320,1024]{2,1,0:T(8,128)(2,1)} %param.10), calls=%async_computation.1 | async-start | bytes 524288 | tf_op jit(solution)/shard_map/slice | solution.py:328
  2.0 11.0 %collective-permute-start.1 = (bf16[336,128]{1,0:T(8,128)(2,1)S(1)}, bf16[336,128]{1,0:T(8,128)(2,1)S(1)}, u32[]{:S(2)}, u32[]{:S(2)}) collective-permute-start(bf16[336,128]{1,0:T(8,128)(2,1)S(1)} %get-tuple-element.21), channel_id=1, source_target_pairs={{0,7},{1,6},{2,5},{3,4},{4,3},{5,2},{6,1},{7,0},{8,9},{9,8},{10,11... | collective-permute-start | bytes 258056 | tf_op jit(solution)/shard_map/ppermute | solution.py:324
  8.1 7.5 %collective-permute-start.3 = (bf16[336,128]{1,0:T(8,128)(2,1)S(1)}, bf16[336,128]{1,0:T(8,128)(2,1)S(1)}, u32[]{:S(2)}, u32[]{:S(2)}) collective-permute-start(bf16[336,128]{1,0:T(8,128)(2,1)S(1)} %get-tuple-element.22), channel_id=1, source_target_pairs={{0,6},{1,7},{2,4},{3,5},{4,2},{5,3},{6,0},{7,1},{8,10},{9,11},{10,... | collective-permute-start | bytes 258056 | tf_op jit(solution)/shard_map/ppermute | solution.py:324
  8.3 12.9 %collective-permute-start.4 = (bf16[336,128]{1,0:T(8,128)(2,1)S(1)}, bf16[336,128]{1,0:T(8,128)(2,1)S(1)}, u32[]{:S(2)}, u32[]{:S(2)}) collective-permute-start(bf16[336,128]{1,0:T(8,128)(2,1)S(1)} %get-tuple-element.23), channel_id=1, source_target_pairs={{0,5},{1,4},{2,7},{3,6},{4,1},{5,0},{6,3},{7,2},{8,11},{9,10},{10,... | collective-permute-start | bytes 258056 | tf_op jit(solution)/shard_map/ppermute | solution.py:324
  9.1 14.2 %collective-permute-start.5 = (bf16[336,128]{1,0:T(8,128)(2,1)S(1)}, bf16[336,128]{1,0:T(8,128)(2,1)S(1)}, u32[]{:S(2)}, u32[]{:S(2)}) collective-permute-start(bf16[336,128]{1,0:T(8,128)(2,1)S(1)} %get-tuple-element.24), channel_id=1, source_target_pairs={{0,4},{1,5},{2,6},{3,7},{4,0},{5,1},{6,2},{7,3},{8,15},{9,14},{10,... | collective-permute-start | bytes 258056 | tf_op jit(solution)/shard_map/ppermute | solution.py:324
  11.1 12.8 %copy-start.4 = (bf16[1,6144,128]{2,1,0:T(8,128)(2,1)S(1)}, bf16[1,6144,128]{2,1,0:T(8,128)(2,1)}, u32[]{:S(2)}) copy-start(bf16[1,6144,128]{2,1,0:T(8,128)(2,1)} %param.11) | copy-start | bytes 4718596
  11.1 12.8 %copy-start.6 = (s32[1,2]{1,0:T(1,128)S(1)}, s32[1,2]{1,0:T(1,128)}, u32[]{:S(2)}) copy-start(s32[1,2]{1,0:T(1,128)} %param.14) | copy-start | bytes 28
  11.1 12.8 %collective-permute-start.6 = (bf16[336,128]{1,0:T(8,128)(2,1)S(1)}, bf16[336,128]{1,0:T(8,128)(2,1)S(1)}, u32[]{:S(2)}, u32[]{:S(2)}) collective-permute-start(bf16[336,128]{1,0:T(8,128)(2,1)S(1)} %get-tuple-element.25), channel_id=1, source_target_pairs={{0,1},{1,0},{2,3},{3,2},{4,5},{5,4},{6,7},{7,6},{8,14},{9,15},{10,... | collective-permute-start | bytes 258056 | tf_op jit(solution)/shard_map/ppermute | solution.py:324
  13.0 11.0 %copy-start.5 = (bf16[1,6144,128]{2,1,0:T(8,128)(2,1)S(1)}, bf16[1,6144,128]{2,1,0:T(8,128)(2,1)}, u32[]{:S(2)}) copy-start(bf16[1,6144,128]{2,1,0:T(8,128)(2,1)} %param.12) | copy-start | bytes 4718596
  13.0 30.7 %collective-permute-start = (bf16[2,128,1024]{2,1,0:T(8,128)(2,1)S(1)}, bf16[2,128,1024]{2,1,0:T(8,128)(2,1)S(1)}, u32[]{:S(2)}, u32[]{:S(2)}) collective-permute-start(bf16[2,128,1024]{2,1,0:T(8,128)(2,1)S(1)} %pad_maximum_fusion.rows_ref), channel_id=1, source_target_pairs={{0,1},{1,2},{2,3},{3,4},{4,5},{5,6},{6,7},{16,17},{17,18},{18,19},... | collective-permute-start | bytes 1572872 | tf_op jit(solution)/shard_map/ppermute | solution.py:344
  15.6 11.7 %collective-permute-start.7 = (bf16[336,128]{1,0:T(8,128)(2,1)S(1)}, bf16[336,128]{1,0:T(8,128)(2,1)S(1)}, u32[]{:S(2)}, u32[]{:S(2)}) collective-permute-start(bf16[336,128]{1,0:T(8,128)(2,1)S(1)} %get-tuple-element.26), channel_id=1, source_target_pairs={{0,2},{1,3},{2,0},{3,1},{4,6},{5,7},{6,4},{7,5},{8,13},{9,12},{10,... | collective-permute-start | bytes 258056 | tf_op jit(solution)/shard_map/ppermute | solution.py:324
  21.2 8.8 %collective-permute-start.8 = (bf16[336,128]{1,0:T(8,128)(2,1)S(1)}, bf16[336,128]{1,0:T(8,128)(2,1)S(1)}, u32[]{:S(2)}, u32[]{:S(2)}) collective-permute-start(bf16[336,128]{1,0:T(8,128)(2,1)S(1)} %get-tuple-element.27), channel_id=1, source_target_pairs={{0,3},{1,2},{2,1},{3,0},{4,7},{5,6},{6,5},{7,4},{8,12},{9,13},{10,... | collective-permute-start | bytes 258056 | tf_op jit(solution)/shard_map/ppermute | solution.py:324
  23.2 22.8 %collective-permute-start.2 = (bf16[2,128,1024]{2,1,0:T(8,128)(2,1)S(1)}, bf16[2,128,1024]{2,1,0:T(8,128)(2,1)S(1)}, u32[]{:S(2)}, u32[]{:S(2)}) collective-permute-start(bf16[2,128,1024]{2,1,0:T(8,128)(2,1)S(1)} %halo.1), channel_id=1, source_target_pairs={{8,9},{9,10},{10,11},{11,12},{12,13},{13,14},{14,15},{24,25},{25,2... | collective-permute-start | bytes 1572872 | tf_op jit(solution)/shard_map/ppermute | solution.py:344
  24.0 6.1 %copy-start.1 = (bf16[1,320,1024]{2,1,0:T(8,128)(2,1)S(1)}, bf16[1,320,1024]{2,1,0:T(8,128)(2,1)}, u32[]{:S(2)}) copy-start(bf16[1,320,1024]{2,1,0:T(8,128)(2,1)} %param.8) | copy-start | bytes 1966084
  24.0 6.0 %copy-start.2 = (bf16[1,320,1024]{2,1,0:T(8,128)(2,1)S(1)}, bf16[1,320,1024]{2,1,0:T(8,128)(2,1)}, u32[]{:S(2)}) copy-start(bf16[1,320,1024]{2,1,0:T(8,128)(2,1)} %param.9) | copy-start | bytes 1966084
  24.0 6.0 %copy-start.3 = (bf16[1,320,1024]{2,1,0:T(8,128)(2,1)S(1)}, bf16[1,320,1024]{2,1,0:T(8,128)(2,1)}, u32[]{:S(2)}) copy-start(bf16[1,320,1024]{2,1,0:T(8,128)(2,1)} %param.10) | copy-start | bytes 1966084
  27.2 5.1 %collective-permute-start.9 = (bf16[336,128]{1,0:T(8,128)(2,1)S(1)}, bf16[336,128]{1,0:T(8,128)(2,1)S(1)}, u32[]{:S(2)}, u32[]{:S(2)}) collective-permute-start(bf16[336,128]{1,0:T(8,128)(2,1)S(1)} %get-tuple-element.29), channel_id=1, source_target_pairs={{0,15},{1,14},{2,13},{3,12},{4,11},{5,10},{6,9},{7,8},{8,17},{9,16... | collective-permute-start | bytes 258056 | tf_op jit(solution)/shard_map/ppermute | solution.py:324
  27.3 16.4 %collective-permute-start.10 = (bf16[336,128]{1,0:T(8,128)(2,1)S(1)}, bf16[336,128]{1,0:T(8,128)(2,1)S(1)}, u32[]{:S(2)}, u32[]{:S(2)}) collective-permute-start(bf16[336,128]{1,0:T(8,128)(2,1)S(1)} %get-tuple-element.30), channel_id=1, source_target_pairs={{0,14},{1,15},{2,12},{3,13},{4,10},{5,11},{6,8},{7,9},{8,18},{9,19... | collective-permute-start | bytes 258056 | tf_op jit(solution)/shard_map/ppermute | solution.py:324
  32.3 25.7 %collective-permute-start.12 = (bf16[256,1024]{1,0:T(8,128)(2,1)S(1)}, bf16[256,1024]{1,0:T(8,128)(2,1)S(1)}, u32[]{:S(2)}, u32[]{:S(2)}) collective-permute-start(bf16[256,1024]{1,0:T(8,128)(2,1)S(1)} %near_inner.1), channel_id=1, source_target_pairs={{0,8},{1,9},{2,10},{3,11},{4,12},{5,13},{6,14},{7,15},{8,16},{9,17... | collective-permute-start | bytes 1572872 | tf_op jit(solution)/shard_map/ppermute | solution.py:324
  32.4 16.3 %collective-permute-start.13 = (bf16[336,128]{1,0:T(8,128)(2,1)S(1)}, bf16[336,128]{1,0:T(8,128)(2,1)S(1)}, u32[]{:S(2)}, u32[]{:S(2)}) collective-permute-start(bf16[336,128]{1,0:T(8,128)(2,1)S(1)} %get-tuple-element.32), channel_id=1, source_target_pairs={{0,13},{1,12},{2,15},{3,14},{4,9},{5,8},{6,11},{7,10},{8,19},{9,18... | collective-permute-start | bytes 258056 | tf_op jit(solution)/shard_map/ppermute | solution.py:324
  43.7 7.6 %collective-permute-start.14 = (bf16[336,128]{1,0:T(8,128)(2,1)S(1)}, bf16[336,128]{1,0:T(8,128)(2,1)S(1)}, u32[]{:S(2)}, u32[]{:S(2)}) collective-permute-start(bf16[336,128]{1,0:T(8,128)(2,1)S(1)} %get-tuple-element.33), channel_id=1, source_target_pairs={{0,12},{1,13},{2,14},{3,15},{4,8},{5,9},{6,10},{7,11},{8,23},{9,22... | collective-permute-start | bytes 258056 | tf_op jit(solution)/shard_map/ppermute | solution.py:324
  43.7 9.7 %collective-permute-start.15 = (bf16[336,128]{1,0:T(8,128)(2,1)S(1)}, bf16[336,128]{1,0:T(8,128)(2,1)S(1)}, u32[]{:S(2)}, u32[]{:S(2)}) collective-permute-start(bf16[336,128]{1,0:T(8,128)(2,1)S(1)} %get-tuple-element.34), channel_id=1, source_target_pairs={{0,9},{1,8},{2,11},{3,10},{4,13},{5,12},{6,15},{7,14},{8,22},{9,23... | collective-permute-start | bytes 258056 | tf_op jit(solution)/shard_map/ppermute | solution.py:324
  47.1 10.9 %collective-permute-start.11 = (bf16[144,1024]{1,0:T(8,128)(2,1)S(1)}, bf16[144,1024]{1,0:T(8,128)(2,1)S(1)}, u32[]{:S(2)}, u32[]{:S(2)}) collective-permute-start(bf16[144,1024]{1,0:T(8,128)(2,1)S(1)} %near_edge.1), channel_id=1, source_target_pairs={{0,8},{1,9},{2,10},{3,11},{4,12},{5,13},{6,14},{7,15},{8,16},{9,17... | collective-permute-start | bytes 884744 | tf_op jit(solution)/shard_map/ppermute | solution.py:324
  48.7 7.6 %collective-permute-start.16 = (bf16[336,128]{1,0:T(8,128)(2,1)S(1)}, bf16[336,128]{1,0:T(8,128)(2,1)S(1)}, u32[]{:S(2)}, u32[]{:S(2)}) collective-permute-start(bf16[336,128]{1,0:T(8,128)(2,1)S(1)} %get-tuple-element.35), channel_id=1, source_target_pairs={{0,10},{1,11},{2,8},{3,9},{4,14},{5,15},{6,12},{7,13},{8,21},{9,20... | collective-permute-start | bytes 258056 | tf_op jit(solution)/shard_map/ppermute | solution.py:324
  51.3 6.7 %collective-permute-start.17 = (bf16[336,128]{1,0:T(8,128)(2,1)S(1)}, bf16[336,128]{1,0:T(8,128)(2,1)S(1)}, u32[]{:S(2)}, u32[]{:S(2)}) collective-permute-start(bf16[336,128]{1,0:T(8,128)(2,1)S(1)} %get-tuple-element.36), channel_id=1, source_target_pairs={{0,11},{1,10},{2,9},{3,8},{4,15},{5,14},{6,13},{7,12},{8,20},{9,21... | collective-permute-start | bytes 258056 | tf_op jit(solution)/shard_map/ppermute | solution.py:324

commit v13 on v9

--- a/solution.py
+++ b/solution.py
@@ -179,8 +179,9 @@
         for start, size in zip(starts, sizes)
     ]
     peers = peers_of(there, 0)
-    for begin in range(0, len(peers), 2):
-        pair = range(begin, min(begin + 2, len(peers)))
+    together = min(len(starts), 2)
+    for begin in range(0, len(peers), together):
+        pair = range(begin, min(begin + together, len(peers)))
         all_lanes = [pl.ds(pl.multiple_of(peers[at] * HD, HD), HD) for at in pair]
         all_scores, all_values = [], []
         for at, lanes in zip(pair, all_lanes):
@@ -285,7 +286,7 @@
     bf16 = jnp.bfloat16
     half = max(seq_count // 2, 1)
     inner, outer = list(range(1, half)), list(range(seq_count - 1, half - 1, -1))
-    there = [outer + inner + [0], inner + outer + [0]]
+    there = [outer[:1] + inner[:1] + outer[1:] + inner[1:] + [0], inner + outer + [0]]
 
     chunk_shape = jax.ShapeDtypeStruct((rows + STAT_ROWS, HD), bf16)
     chunk_shape = jax.ShapeDtypeStruct((rows + STAT_ROWS, HD), bf16)

time: 54.3 us -> 55.4 us (1.020)
  starting transfers between devices: 31.6 us -> 34.6 us
  waiting for transfers between devices: 11 us -> 9.35 us
    ppermute x2, starting transfers between devices: 3.06 us -> 5.12 us  [halo_from(): return lax.ppermute(mine, ('section', 'seq'), pairs)]
    ppermute x16, waiting for transfers between devices: 11 us -> 9.35 us  [linked(): return lax.ppermute(shard, ('section', 'seq'), pairs)]
    ppermute x16, starting transfers between devices: 28.6 us -> 29.5 us  [linked(): return lax.ppermute(shard, ('section', 'seq'), pairs)]
  transfers between devices with their start and end apart: 18 -> 18, of which waited for: 5 -> 4; matrix products, arithmetic and copies ran while one was open for 0% -> 0% of each run, Pallas kernels for 14% -> 13%
where the time goes in v13:
time: 55.4 us; the launch traced here: 55.2 us
  starting transfers between devices  34.6 us (62%)
  waiting for transfers between devices  9.35 us (17%)
  Pallas kernels  8.92 us (16%)
  local copies, waits for them, and re-layouts  1.33 us (2%)
  between operations  0.9 us (2%)
    ppermute x16, starting transfers between devices, linked(): return lax.ppermute(shard, ('section', 'seq'), pairs)  29.5 us
    ppermute x16, waiting for transfers between devices, linked(): return lax.ppermute(shard, ('section', 'seq'), pairs)  9.35 us
    ppermute x2, starting transfers between devices, halo_from(): return lax.ppermute(mine, ('section', 'seq'), pairs)  5.12 us
    pallas_call x2, Pallas kernels, far_call(): pl.pallas_call(functools.partial(far_kernel, there, chosen), out_shape=[c...  4.72 us
    pallas_call x2, Pallas kernels, near_call(): pl.pallas_call(functools.partial(kernel, there), out_shape=jax.ShapeDtype...  2.53 us
    pallas_call x1, Pallas kernels, per_device(): pl.pallas_call(functools.partial(merge_kernel, there), out_shape=jax.Shap...  1.36 us
    unnamed x17, local copies, waits for them, and re-layouts  1.21 us
  transfers between devices with their start and end apart: 18, of which 4 were waited for; matrix products, arithmetic and copies ran while one was open for 0% of the time, Pallas kernels for 13%

profile of v13, /device:TPU:0, one launch (start us, length us, event | category | flops | bytes accessed | tf_op | source)
XLA Modules:
  0.0 55.2 jit_solution(1075398126940281934)
XLA Ops:
  0.7 1.1 %copy-done = bf16[1,320,1024]{2,1,0:T(8,128)(2,1)S(1)} copy-done((bf16[1,320,1024]{2,1,0:T(8,128)(2,1)S(1)}, bf16[1,320,1024]{2,1,0:T(8,128)(2,1)}, u32[]{:S(2)}) %copy-start) | copy-done | bytes 655384
  1.8 0.3 split.1
  2.0 6.1 %collective-permute-start.1 = (bf16[336,128]{1,0:T(8,128)(2,1)S(1)}, bf16[336,128]{1,0:T(8,128)(2,1)S(1)}, u32[]{:S(2)}, u32[]{:S(2)}) collective-permute-start(bf16[336,128]{1,0:T(8,128)(2,1)S(1)} %get-tuple-element.21), channel_id=1, source_target_pairs={{0,7},{1,6},{2,5},{3,4},{4,3},{5,2},{6,1},{7,0},{8,9},{9,8},{10,11... | collective-permute-start | bytes 258056 | tf_op jit(solution)/shard_map/ppermute | solution.py:326
  8.1 0.5 collective-permute-start.3
  8.6 0.1 collective-permute-start.4
  8.8 1.8 %collective-permute-start.5 = (bf16[336,128]{1,0:T(8,128)(2,1)S(1)}, bf16[336,128]{1,0:T(8,128)(2,1)S(1)}, u32[]{:S(2)}, u32[]{:S(2)}) collective-permute-start(bf16[336,128]{1,0:T(8,128)(2,1)S(1)} %get-tuple-element.24), channel_id=1, source_target_pairs={{0,5},{1,4},{2,7},{3,6},{4,1},{5,0},{6,3},{7,2},{8,15},{9,14},{10,... | collective-permute-start | bytes 258056 | tf_op jit(solution)/shard_map/ppermute | solution.py:326
  10.6 2.1 %collective-permute-start.6 = (bf16[336,128]{1,0:T(8,128)(2,1)S(1)}, bf16[336,128]{1,0:T(8,128)(2,1)S(1)}, u32[]{:S(2)}, u32[]{:S(2)}) collective-permute-start(bf16[336,128]{1,0:T(8,128)(2,1)S(1)} %get-tuple-element.25), channel_id=1, source_target_pairs={{0,4},{1,5},{2,6},{3,7},{4,0},{5,1},{6,2},{7,3},{8,14},{9,15},{10,... | collective-permute-start | bytes 258056 | tf_op jit(solution)/shard_map/ppermute | solution.py:326
  12.7 0.1 copy.10
  12.8 0.1 reshape_squeeze.3.random_ref
  13.0 0.1 pad_maximum_fusion.rows_ref
  13.0 0.8 %collective-permute-start = (bf16[2,128,1024]{2,1,0:T(8,128)(2,1)S(1)}, bf16[2,128,1024]{2,1,0:T(8,128)(2,1)S(1)}, u32[]{:S(2)}, u32[]{:S(2)}) collective-permute-start(bf16[2,128,1024]{2,1,0:T(8,128)(2,1)S(1)} %pad_maximum_fusion.rows_ref), channel_id=1, source_target_pairs={{8,9},{9,10},{10,11},{11,12},{12,13},{13,14},{14,15},{24,25},{25,2... | collective-permute-start | bytes 1572872 | tf_op jit(solution)/shard_map/ppermute | solution.py:346
  13.9 1.3 %collective-permute-start.7 = (bf16[336,128]{1,0:T(8,128)(2,1)S(1)}, bf16[336,128]{1,0:T(8,128)(2,1)S(1)}, u32[]{:S(2)}, u32[]{:S(2)}) collective-permute-start(bf16[336,128]{1,0:T(8,128)(2,1)S(1)} %get-tuple-element.26), channel_id=1, source_target_pairs={{0,2},{1,3},{2,0},{3,1},{4,6},{5,7},{6,4},{7,5},{8,13},{9,12},{10,... | collective-permute-start | bytes 258056 | tf_op jit(solution)/shard_map/ppermute | solution.py:326
  15.2 2.2 %collective-permute-start.8 = (bf16[336,128]{1,0:T(8,128)(2,1)S(1)}, bf16[336,128]{1,0:T(8,128)(2,1)S(1)}, u32[]{:S(2)}, u32[]{:S(2)}) collective-permute-start(bf16[336,128]{1,0:T(8,128)(2,1)S(1)} %get-tuple-element.27), channel_id=1, source_target_pairs={{0,3},{1,2},{2,1},{3,0},{4,7},{5,6},{6,5},{7,4},{8,12},{9,13},{10,... | collective-permute-start | bytes 258056 | tf_op jit(solution)/shard_map/ppermute | solution.py:326
  17.5 3.4 %collective-permute-done.5.refs_3_ = bf16[336,128]{1,0:T(8,128)(2,1)S(1)} collective-permute-done((bf16[336,128]{1,0:T(8,128)(2,1)S(1)}, bf16[336,128]{1,0:T(8,128)(2,1)S(1)}, u32[]{:S(2)}, u32[]{:S(2)}) %collective-permute-start.5) | collective-permute-done | bytes 86048 | tf_op jit(solution)/shard_map/ppermute | solution.py:326
  20.8 4.3 %collective-permute-start.2 = (bf16[2,128,1024]{2,1,0:T(8,128)(2,1)S(1)}, bf16[2,128,1024]{2,1,0:T(8,128)(2,1)S(1)}, u32[]{:S(2)}, u32[]{:S(2)}) collective-permute-start(bf16[2,128,1024]{2,1,0:T(8,128)(2,1)S(1)} %halo.1), channel_id=1, source_target_pairs={{0,1},{1,2},{2,3},{3,4},{4,5},{5,6},{6,7},{16,17},{17,18},{18,19},... | collective-permute-start | bytes 1572872 | tf_op jit(solution)/shard_map/ppermute | solution.py:346
  25.2 3.2 %far.2 = (bf16[336,128]{1,0:T(8,128)(2,1)S(1)}, bf16[336,128]{1,0:T(8,128)(2,1)S(1)}, bf16[336,128]{1,0:T(8,128)(2,1)S(1)}, bf16[336,128]{1,0:T(8,128)(2,1)S(1)}...) custom-call(s32[1]{0:T(128)} %bitcast.9.span_ref, s32[2]{0:T(128)S(1)} %bitcast.22, ...), custom_call_target="tpu_custom_call" | custom-call | flops 12582912000 | bytes 4128768 | tf_op jit(solution)/shard_map/far/pallas_call | solution.py:353
  28.4 0.1 collective-permute-start.9
  28.5 2.7 %collective-permute-start.10 = (bf16[336,128]{1,0:T(8,128)(2,1)S(1)}, bf16[336,128]{1,0:T(8,128)(2,1)S(1)}, u32[]{:S(2)}, u32[]{:S(2)}) collective-permute-start(bf16[336,128]{1,0:T(8,128)(2,1)S(1)} %get-tuple-element.30), channel_id=1, source_target_pairs={{0,9},{1,8},{2,11},{3,10},{4,13},{5,12},{6,15},{7,14},{8,18},{9,19... | collective-permute-start | bytes 258056 | tf_op jit(solution)/shard_map/ppermute | solution.py:326
  31.2 1.5 %near_inner.1 = bf16[256,1024]{1,0:T(8,128)(2,1)S(1)} custom-call(bf16[320,1024]{1,0:T(8,128)(2,1)S(1)} %bitcast.12, bf16[320,1024]{1,0:T(8,128)(2,1)S(1)} %bitcast.14, bf16[320,1024]{1,0:T(8,128)(2,1)S(1)} %bitcast.16, bf16[336,128]{1,0:T(8,128)(2,1)S(1)} %get-tuple-element.31.own_ref, bf16[336,128]{1,0:T(8,128)(2,1)S(1)} %collective-permute-done.1._.refs_0_, ...), custom_call_target="tpu_custom_call" | custom-call | flops 8053063680 | bytes 1769472 | tf_op jit(solution)/shard_map/near_inner/pallas_call | solution.py:383
  32.7 0.1 collective-permute-start.12
  32.8 0.6 %collective-permute-done.9.refs_8_.refs_0_ = bf16[336,128]{1,0:T(8,128)(2,1)S(1)} collective-permute-done((bf16[336,128]{1,0:T(8,128)(2,1)S(1)}, bf16[336,128]{1,0:T(8,128)(2,1)S(1)}, u32[]{:S(2)}, u32[]{:S(2)}) %collective-permute-start.9) | collective-permute-done | bytes 86048 | tf_op jit(solution)/shard_map/ppermute | solution.py:326
  33.4 5.3 %collective-permute-start.13 = (bf16[336,128]{1,0:T(8,128)(2,1)S(1)}, bf16[336,128]{1,0:T(8,128)(2,1)S(1)}, u32[]{:S(2)}, u32[]{:S(2)}) collective-permute-start(bf16[336,128]{1,0:T(8,128)(2,1)S(1)} %get-tuple-element.32), channel_id=1, source_target_pairs={{0,14},{1,15},{2,12},{3,13},{4,10},{5,11},{6,8},{7,9},{8,19},{9,18... | collective-permute-start | bytes 258056 | tf_op jit(solution)/shard_map/ppermute | solution.py:326
  38.7 1.0 %collective-permute-start.14 = (bf16[336,128]{1,0:T(8,128)(2,1)S(1)}, bf16[336,128]{1,0:T(8,128)(2,1)S(1)}, u32[]{:S(2)}, u32[]{:S(2)}) collective-permute-start(bf16[336,128]{1,0:T(8,128)(2,1)S(1)} %get-tuple-element.33), channel_id=1, source_target_pairs={{0,13},{1,12},{2,15},{3,14},{4,9},{5,8},{6,11},{7,10},{8,23},{9,22... | collective-permute-start | bytes 258056 | tf_op jit(solution)/shard_map/ppermute | solution.py:326
  39.6 1.0 %collective-permute-start.15 = (bf16[336,128]{1,0:T(8,128)(2,1)S(1)}, bf16[336,128]{1,0:T(8,128)(2,1)S(1)}, u32[]{:S(2)}, u32[]{:S(2)}) collective-permute-start(bf16[336,128]{1,0:T(8,128)(2,1)S(1)} %get-tuple-element.34), channel_id=1, source_target_pairs={{0,12},{1,13},{2,14},{3,15},{4,8},{5,9},{6,10},{7,11},{8,22},{9,23... | collective-permute-start | bytes 258056 | tf_op jit(solution)/shard_map/ppermute | solution.py:326
  40.7 1.0 %near_edge.1 = bf16[144,1024]{1,0:T(8,128)(2,1)S(1)} custom-call(bf16[320,1024]{1,0:T(8,128)(2,1)S(1)} %bitcast.13, bf16[320,1024]{1,0:T(8,128)(2,1)S(1)} %bitcast.15, bf16[320,1024]{1,0:T(8,128)(2,1)S(1)} %bitcast.17, bf16[2,128,1024]{2,1,0:T(8,128)(2,1)S(1)} %collective-permute-done.odd_ref, bf16[2,128,1024]{2,1,0:T(8,128)(2,1)S(1)} %collective-permute-done.2.even_ref, ...), custom_call_target="tpu_custom_call" | custom-call | flops 5368709120 | bytes 1179648 | tf_op jit(solution)/shard_map/near_edge/pallas_call | solution.py:383
  41.7 0.1 collective-permute-start.11
  41.8 1.5 %far.3 = (bf16[336,128]{1,0:T(8,128)(2,1)S(1)}, bf16[336,128]{1,0:T(8,128)(2,1)S(1)}) custom-call(s32[1]{0:T(128)} %bitcast.10.span_ref, s32[2]{0:T(128)S(1)} %bitcast.23, s32[120]{0:T(128)S(1)} %reshape_squeeze.3.random_ref, bf16[6144,128]{1,0:T(8,128)(2,1)S(1)} %bitcast.19, bf16[6144,128]{1,0:T(8,128)(2,1)S(1)} %bitcast.21, ...), custom_call_target="tpu_custom_call" | custom-call | flops 4194304000 | bytes 3473408 | tf_op jit(solution)/shard_map/far/pallas_call | solution.py:353
  43.3 4.5 %collective-permute-start.16 = (bf16[336,128]{1,0:T(8,128)(2,1)S(1)}, bf16[336,128]{1,0:T(8,128)(2,1)S(1)}, u32[]{:S(2)}, u32[]{:S(2)}) collective-permute-start(bf16[336,128]{1,0:T(8,128)(2,1)S(1)} %get-tuple-element.35), channel_id=1, source_target_pairs={{0,10},{1,11},{2,8},{3,9},{4,14},{5,15},{6,12},{7,13},{8,21},{9,20... | collective-permute-start | bytes 258056 | tf_op jit(solution)/shard_map/ppermute | solution.py:326
  47.7 0.7 %collective-permute-start.17 = (bf16[336,128]{1,0:T(8,128)(2,1)S(1)}, bf16[336,128]{1,0:T(8,128)(2,1)S(1)}, u32[]{:S(2)}, u32[]{:S(2)}) collective-permute-start(bf16[336,128]{1,0:T(8,128)(2,1)S(1)} %get-tuple-element.36), channel_id=1, source_target_pairs={{0,11},{1,10},{2,9},{3,8},{4,15},{5,14},{6,13},{7,12},{8,20},{9,21... | collective-permute-start | bytes 258056 | tf_op jit(solution)/shard_map/ppermute | solution.py:326
  48.5 3.6 %collective-permute-done.16.refs_5_ = bf16[336,128]{1,0:T(8,128)(2,1)S(1)} collective-permute-done((bf16[336,128]{1,0:T(8,128)(2,1)S(1)}, bf16[336,128]{1,0:T(8,128)(2,1)S(1)}, u32[]{:S(2)}, u32[]{:S(2)}) %collective-permute-start.16) | collective-permute-done | bytes 86048 | tf_op jit(solution)/shard_map/ppermute | solution.py:326
  52.1 1.8 %collective-permute-done.17.refs_6_ = bf16[336,128]{1,0:T(8,128)(2,1)S(1)} collective-permute-done((bf16[336,128]{1,0:T(8,128)(2,1)S(1)}, bf16[336,128]{1,0:T(8,128)(2,1)S(1)}, u32[]{:S(2)}, u32[]{:S(2)}) %collective-permute-start.17) | collective-permute-done | bytes 86048 | tf_op jit(solution)/shard_map/ppermute | solution.py:326
  53.8 1.4 %merge.1 = bf16[320,1024]{1,0:T(8,128)(2,1)} custom-call(bf16[144,1024]{1,0:T(8,128)(2,1)S(1)} %collective-permute-done.11.edge_ref, bf16[256,1024]{1,0:T(8,128)(2,1)S(1)} %collective-permute-done.12.inner_ref, bf16[336,128]{1,0:T(8,128)(2,1)S(1)} %collective-permute-done.9.refs_8_.refs_0_, bf16[336,128]{1,0:T(8,128)(2,1)S(1)} %collective-permute-done.10.refs_9_.refs_1_, ...), custom_call_target="tpu_custom_call" | custom-call | bytes 1966080 | tf_op jit(solution)/shard_map/merge/pallas_call | solution.py:413
  (34 shorter events, 0.1 us)
Async XLA Ops:
  0.0 12.7 %copy-start.7 = (s32[1,40,3]{1,0,2:T(1,128)S(1)}, s32[1,40,3]{1,0,2:T(1,128)}, u32[]{:S(2)}) copy-start(s32[1,40,3]{1,0,2:T(1,128)} %param.15) | copy-start | bytes 1444
  0.7 1.1 %copy-start = (bf16[1,320,1024]{2,1,0:T(8,128)(2,1)S(1)}, bf16[1,320,1024]{2,1,0:T(8,128)(2,1)}, u32[]{:S(2)}) copy-start(bf16[1,320,1024]{2,1,0:T(8,128)(2,1)} %param.8) | copy-start | bytes 1966084
  1.8 11.2 %slice-start = ((bf16[1,320,1024]{2,1,0:T(8,128)(2,1)}), bf16[1,128,1024]{2,1,0:T(8,128)(2,1)S(1)}, s32[]{:S(2)}) async-start(bf16[1,320,1024]{2,1,0:T(8,128)(2,1)} %param.9), calls=%async_computation | async-start | bytes 524288 | tf_op jit(solution)/shard_map/slice | solution.py:330
  1.8 11.2 %slice-start.1 = ((bf16[1,320,1024]{2,1,0:T(8,128)(2,1)}), bf16[1,128,1024]{2,1,0:T(8,128)(2,1)S(1)}, s32[]{:S(2)}) async-start(bf16[1,320,1024]{2,1,0:T(8,128)(2,1)} %param.10), calls=%async_computation.1 | async-start | bytes 524288 | tf_op jit(solution)/shard_map/slice | solution.py:330
  2.0 11.0 %collective-permute-start.1 = (bf16[336,128]{1,0:T(8,128)(2,1)S(1)}, bf16[336,128]{1,0:T(8,128)(2,1)S(1)}, u32[]{:S(2)}, u32[]{:S(2)}) collective-permute-start(bf16[336,128]{1,0:T(8,128)(2,1)S(1)} %get-tuple-element.21), channel_id=1, source_target_pairs={{0,7},{1,6},{2,5},{3,4},{4,3},{5,2},{6,1},{7,0},{8,9},{9,8},{10,11... | collective-permute-start | bytes 258056 | tf_op jit(solution)/shard_map/ppermute | solution.py:326
  8.1 5.8 %collective-permute-start.3 = (bf16[336,128]{1,0:T(8,128)(2,1)S(1)}, bf16[336,128]{1,0:T(8,128)(2,1)S(1)}, u32[]{:S(2)}, u32[]{:S(2)}) collective-permute-start(bf16[336,128]{1,0:T(8,128)(2,1)S(1)} %get-tuple-element.22), channel_id=1, source_target_pairs={{0,1},{1,0},{2,3},{3,2},{4,5},{5,4},{6,7},{7,6},{8,10},{9,11},{10,... | collective-permute-start | bytes 258056 | tf_op jit(solution)/shard_map/ppermute | solution.py:326
  8.6 6.6 %collective-permute-start.4 = (bf16[336,128]{1,0:T(8,128)(2,1)S(1)}, bf16[336,128]{1,0:T(8,128)(2,1)S(1)}, u32[]{:S(2)}, u32[]{:S(2)}) collective-permute-start(bf16[336,128]{1,0:T(8,128)(2,1)S(1)} %get-tuple-element.23), channel_id=1, source_target_pairs={{0,6},{1,7},{2,4},{3,5},{4,2},{5,3},{6,0},{7,1},{8,11},{9,10},{10,... | collective-permute-start | bytes 258056 | tf_op jit(solution)/shard_map/ppermute | solution.py:326
  8.8 12.1 %collective-permute-start.5 = (bf16[336,128]{1,0:T(8,128)(2,1)S(1)}, bf16[336,128]{1,0:T(8,128)(2,1)S(1)}, u32[]{:S(2)}, u32[]{:S(2)}) collective-permute-start(bf16[336,128]{1,0:T(8,128)(2,1)S(1)} %get-tuple-element.24), channel_id=1, source_target_pairs={{0,5},{1,4},{2,7},{3,6},{4,1},{5,0},{6,3},{7,2},{8,15},{9,14},{10,... | collective-permute-start | bytes 258056 | tf_op jit(solution)/shard_map/ppermute | solution.py:326
  10.6 14.6 %copy-start.4 = (bf16[1,6144,128]{2,1,0:T(8,128)(2,1)S(1)}, bf16[1,6144,128]{2,1,0:T(8,128)(2,1)}, u32[]{:S(2)}) copy-start(bf16[1,6144,128]{2,1,0:T(8,128)(2,1)} %param.11) | copy-start | bytes 4718596
  10.6 14.6 %copy-start.6 = (s32[1,2]{1,0:T(1,128)S(1)}, s32[1,2]{1,0:T(1,128)}, u32[]{:S(2)}) copy-start(s32[1,2]{1,0:T(1,128)} %param.14) | copy-start | bytes 28
  10.6 14.5 %collective-permute-start.6 = (bf16[336,128]{1,0:T(8,128)(2,1)S(1)}, bf16[336,128]{1,0:T(8,128)(2,1)S(1)}, u32[]{:S(2)}, u32[]{:S(2)}) collective-permute-start(bf16[336,128]{1,0:T(8,128)(2,1)S(1)} %get-tuple-element.25), channel_id=1, source_target_pairs={{0,4},{1,5},{2,6},{3,7},{4,0},{5,1},{6,2},{7,3},{8,14},{9,15},{10,... | collective-permute-start | bytes 258056 | tf_op jit(solution)/shard_map/ppermute | solution.py:326
  13.0 12.2 %copy-start.5 = (bf16[1,6144,128]{2,1,0:T(8,128)(2,1)S(1)}, bf16[1,6144,128]{2,1,0:T(8,128)(2,1)}, u32[]{:S(2)}) copy-start(bf16[1,6144,128]{2,1,0:T(8,128)(2,1)} %param.12) | copy-start | bytes 4718596
  13.0 26.6 %collective-permute-start = (bf16[2,128,1024]{2,1,0:T(8,128)(2,1)S(1)}, bf16[2,128,1024]{2,1,0:T(8,128)(2,1)S(1)}, u32[]{:S(2)}, u32[]{:S(2)}) collective-permute-start(bf16[2,128,1024]{2,1,0:T(8,128)(2,1)S(1)} %pad_maximum_fusion.rows_ref), channel_id=1, source_target_pairs={{8,9},{9,10},{10,11},{11,12},{12,13},{13,14},{14,15},{24,25},{25,2... | collective-permute-start | bytes 1572872 | tf_op jit(solution)/shard_map/ppermute | solution.py:346
  13.9 14.6 %collective-permute-start.7 = (bf16[336,128]{1,0:T(8,128)(2,1)S(1)}, bf16[336,128]{1,0:T(8,128)(2,1)S(1)}, u32[]{:S(2)}, u32[]{:S(2)}) collective-permute-start(bf16[336,128]{1,0:T(8,128)(2,1)S(1)} %get-tuple-element.26), channel_id=1, source_target_pairs={{0,2},{1,3},{2,0},{3,1},{4,6},{5,7},{6,4},{7,5},{8,13},{9,12},{10,... | collective-permute-start | bytes 258056 | tf_op jit(solution)/shard_map/ppermute | solution.py:326
  15.2 15.9 %collective-permute-start.8 = (bf16[336,128]{1,0:T(8,128)(2,1)S(1)}, bf16[336,128]{1,0:T(8,128)(2,1)S(1)}, u32[]{:S(2)}, u32[]{:S(2)}) collective-permute-start(bf16[336,128]{1,0:T(8,128)(2,1)S(1)} %get-tuple-element.27), channel_id=1, source_target_pairs={{0,3},{1,2},{2,1},{3,0},{4,7},{5,6},{6,5},{7,4},{8,12},{9,13},{10,... | collective-permute-start | bytes 258056 | tf_op jit(solution)/shard_map/ppermute | solution.py:326
  20.8 19.8 %collective-permute-start.2 = (bf16[2,128,1024]{2,1,0:T(8,128)(2,1)S(1)}, bf16[2,128,1024]{2,1,0:T(8,128)(2,1)S(1)}, u32[]{:S(2)}, u32[]{:S(2)}) collective-permute-start(bf16[2,128,1024]{2,1,0:T(8,128)(2,1)S(1)} %halo.1), channel_id=1, source_target_pairs={{0,1},{1,2},{2,3},{3,4},{4,5},{5,6},{6,7},{16,17},{17,18},{18,19},... | collective-permute-start | bytes 1572872 | tf_op jit(solution)/shard_map/ppermute | solution.py:346
  25.2 6.0 %copy-start.1 = (bf16[1,320,1024]{2,1,0:T(8,128)(2,1)S(1)}, bf16[1,320,1024]{2,1,0:T(8,128)(2,1)}, u32[]{:S(2)}) copy-start(bf16[1,320,1024]{2,1,0:T(8,128)(2,1)} %param.8) | copy-start | bytes 1966084
  25.2 6.0 %copy-start.2 = (bf16[1,320,1024]{2,1,0:T(8,128)(2,1)S(1)}, bf16[1,320,1024]{2,1,0:T(8,128)(2,1)}, u32[]{:S(2)}) copy-start(bf16[1,320,1024]{2,1,0:T(8,128)(2,1)} %param.9) | copy-start | bytes 1966084
  25.2 6.0 %copy-start.3 = (bf16[1,320,1024]{2,1,0:T(8,128)(2,1)S(1)}, bf16[1,320,1024]{2,1,0:T(8,128)(2,1)}, u32[]{:S(2)}) copy-start(bf16[1,320,1024]{2,1,0:T(8,128)(2,1)} %param.10) | copy-start | bytes 1966084
  28.4 4.9 %collective-permute-start.9 = (bf16[336,128]{1,0:T(8,128)(2,1)S(1)}, bf16[336,128]{1,0:T(8,128)(2,1)S(1)}, u32[]{:S(2)}, u32[]{:S(2)}) collective-permute-start(bf16[336,128]{1,0:T(8,128)(2,1)S(1)} %get-tuple-element.29), channel_id=1, source_target_pairs={{0,15},{1,14},{2,13},{3,12},{4,11},{5,10},{6,9},{7,8},{8,17},{9,16... | collective-permute-start | bytes 258056 | tf_op jit(solution)/shard_map/ppermute | solution.py:326
  28.5 10.2 %collective-permute-start.10 = (bf16[336,128]{1,0:T(8,128)(2,1)S(1)}, bf16[336,128]{1,0:T(8,128)(2,1)S(1)}, u32[]{:S(2)}, u32[]{:S(2)}) collective-permute-start(bf16[336,128]{1,0:T(8,128)(2,1)S(1)} %get-tuple-element.30), channel_id=1, source_target_pairs={{0,9},{1,8},{2,11},{3,10},{4,13},{5,12},{6,15},{7,14},{8,18},{9,19... | collective-permute-start | bytes 258056 | tf_op jit(solution)/shard_map/ppermute | solution.py:326
  32.7 21.1 %collective-permute-start.12 = (bf16[256,1024]{1,0:T(8,128)(2,1)S(1)}, bf16[256,1024]{1,0:T(8,128)(2,1)S(1)}, u32[]{:S(2)}, u32[]{:S(2)}) collective-permute-start(bf16[256,1024]{1,0:T(8,128)(2,1)S(1)} %near_inner.1), channel_id=1, source_target_pairs={{0,8},{1,9},{2,10},{3,11},{4,12},{5,13},{6,14},{7,15},{8,16},{9,17... | collective-permute-start | bytes 1572872 | tf_op jit(solution)/shard_map/ppermute | solution.py:326
  33.4 9.9 %collective-permute-start.13 = (bf16[336,128]{1,0:T(8,128)(2,1)S(1)}, bf16[336,128]{1,0:T(8,128)(2,1)S(1)}, u32[]{:S(2)}, u32[]{:S(2)}) collective-permute-start(bf16[336,128]{1,0:T(8,128)(2,1)S(1)} %get-tuple-element.32), channel_id=1, source_target_pairs={{0,14},{1,15},{2,12},{3,13},{4,10},{5,11},{6,8},{7,9},{8,19},{9,18... | collective-permute-start | bytes 258056 | tf_op jit(solution)/shard_map/ppermute | solution.py:326
  38.7 9.1 %collective-permute-start.14 = (bf16[336,128]{1,0:T(8,128)(2,1)S(1)}, bf16[336,128]{1,0:T(8,128)(2,1)S(1)}, u32[]{:S(2)}, u32[]{:S(2)}) collective-permute-start(bf16[336,128]{1,0:T(8,128)(2,1)S(1)} %get-tuple-element.33), channel_id=1, source_target_pairs={{0,13},{1,12},{2,15},{3,14},{4,9},{5,8},{6,11},{7,10},{8,23},{9,22... | collective-permute-start | bytes 258056 | tf_op jit(solution)/shard_map/ppermute | solution.py:326
  39.6 8.8 %collective-permute-start.15 = (bf16[336,128]{1,0:T(8,128)(2,1)S(1)}, bf16[336,128]{1,0:T(8,128)(2,1)S(1)}, u32[]{:S(2)}, u32[]{:S(2)}) collective-permute-start(bf16[336,128]{1,0:T(8,128)(2,1)S(1)} %get-tuple-element.34), channel_id=1, source_target_pairs={{0,12},{1,13},{2,14},{3,15},{4,8},{5,9},{6,10},{7,11},{8,22},{9,23... | collective-permute-start | bytes 258056 | tf_op jit(solution)/shard_map/ppermute | solution.py:326
  41.7 12.1 %collective-permute-start.11 = (bf16[144,1024]{1,0:T(8,128)(2,1)S(1)}, bf16[144,1024]{1,0:T(8,128)(2,1)S(1)}, u32[]{:S(2)}, u32[]{:S(2)}) collective-permute-start(bf16[144,1024]{1,0:T(8,128)(2,1)S(1)} %near_edge.1), channel_id=1, source_target_pairs={{0,8},{1,9},{2,10},{3,11},{4,12},{5,13},{6,14},{7,15},{8,16},{9,17... | collective-permute-start | bytes 884744 | tf_op jit(solution)/shard_map/ppermute | solution.py:326
  43.3 8.8 %collective-permute-start.16 = (bf16[336,128]{1,0:T(8,128)(2,1)S(1)}, bf16[336,128]{1,0:T(8,128)(2,1)S(1)}, u32[]{:S(2)}, u32[]{:S(2)}) collective-permute-start(bf16[336,128]{1,0:T(8,128)(2,1)S(1)} %get-tuple-element.35), channel_id=1, source_target_pairs={{0,10},{1,11},{2,8},{3,9},{4,14},{5,15},{6,12},{7,13},{8,21},{9,20... | collective-permute-start | bytes 258056 | tf_op jit(solution)/shard_map/ppermute | solution.py:326
  47.7 6.1 %collective-permute-start.17 = (bf16[336,128]{1,0:T(8,128)(2,1)S(1)}, bf16[336,128]{1,0:T(8,128)(2,1)S(1)}, u32[]{:S(2)}, u32[]{:S(2)}) collective-permute-start(bf16[336,128]{1,0:T(8,128)(2,1)S(1)} %get-tuple-element.36), channel_id=1, source_target_pairs={{0,11},{1,10},{2,9},{3,8},{4,15},{5,14},{6,13},{7,12},{8,20},{9,21... | collective-permute-start | bytes 258056 | tf_op jit(solution)/shard_map/ppermute | solution.py:326

commit v14 on v13

--- a/solution.py
+++ b/solution.py
@@ -125,35 +125,50 @@
             return ref[at * BLK : (at + 1) * BLK, :]
         return ref[pl.ds(pl.multiple_of(at * BLK, BLK), BLK), :]
 
-    glob_keys = [block(key_ref, global_ref[g]) for g in range(GLOB)]
-    glob_values = [block(value_ref, global_ref[g]) for g in range(GLOB)]
+    glob_keys = jnp.concatenate([block(key_ref, global_ref[g]) for g in range(GLOB)], axis=0)
+    glob_values = jnp.concatenate([block(value_ref, global_ref[g]) for g in range(GLOB)], axis=0)
     peers = [peers_of(there, 0)[at] for at in chosen]
     query_refs, out_refs = refs[: len(peers)], refs[len(peers) :]
     rows = query_refs[0].shape[0] - STAT_ROWS
     for chunk, query_ref, out_ref in zip(peers, query_refs, out_refs):
         blocks = rows // BLK
         first = chunk == 0
-        all_scores, all_picks = [], []
+        glob_scores = scores_of(query_ref[:rows, :], glob_keys)
+        all_scores, all_values = [], []
         for b in range(blocks):
-            query = query_ref[b * BLK : (b + 1) * BLK, :]
             base = (chunk * blocks + b) * RAND
-            picks = [random_ref[base + r] for r in range(RAND)]
-            keys = glob_keys + [block(key_ref, pick) for pick in picks]
-            known = len(keys) * BLK
             spare = [last + 1 + b - w for w in range(b + 1, WMAX)]
-            keys = keys + [block(key_ref, at) for at in spare]
-            scores = scores_of(query, jnp.concatenate(keys, axis=0))
+            picks = [random_ref[base + r] for r in range(RAND)] + spare
+            keys = jnp.concatenate([block(key_ref, pick) for pick in picks], axis=0)
+            scores = scores_of(query_ref[b * BLK : (b + 1) * BLK, :], keys)
             if spare:
                 open_slots = jnp.where(first, jnp.clip(span - (b + 1), 0, len(spare)), 0)
                 lane_at = lax.broadcasted_iota(jnp.int32, scores.shape, 1)
-                scores = jnp.where(lane_at < known + open_slots * BLK, scores, MASKED)
-            all_scores.append(scores)
-            all_picks.append(picks + spare)
-        all_values = [
-            jnp.concatenate(glob_values + [block(value_ref, at) for at in picks], axis=0)
-            for picks in all_picks
+                scores = jnp.where(lane_at < (RAND + open_slots) * BLK, scores, MASKED)
+            glob = glob_scores[b * BLK : (b + 1) * BLK, :]
+            all_scores.append(jnp.concatenate([glob, scores], axis=1))
+            all_values.append(
+                jnp.concatenate([block(value_ref, pick) for pick in picks], axis=0)
+            )
+        tops = [jnp.max(scores, axis=1, keepdims=True) for scores in all_scores]
+        expos = [
+            jnp.exp2((scores - top) * EXPO_SCALE) for scores, top in zip(all_scores, tops)
         ]
-        parts, lses = softmax_parts(all_scores, all_values)
+        totals = [jnp.sum(expo, axis=1, keepdims=True) for expo in expos]
+        weights = [expo.astype(jnp.bfloat16) for expo in expos]
+        shared = GLOB * BLK
+        glob_mixed = jnp.dot(
+            jnp.concatenate([weight[:, :shared] for weight in weights], axis=0),
+            glob_values,
+            preferred_element_type=jnp.float32,
+        )
+        mixed = [
+            glob_mixed[b * BLK : (b + 1) * BLK, :]
+            + jnp.dot(weight[:, shared:], value, preferred_element_type=jnp.float32)
+            for b, (weight, value) in enumerate(zip(weights, all_values))
+        ]
+        parts = [(mix * (1.0 / total)).astype(jnp.bfloat16) for mix, total in zip(mixed, totals)]
+        lses = [top * EXPO_SCALE + jnp.log2(total) for top, total in zip(tops, totals)]
         stats = []
         for b in range(blocks):
             row = as_row(lses[b], (b * BLK) % LANES)
@@ -286,7 +301,7 @@
     bf16 = jnp.bfloat16
     half = max(seq_count // 2, 1)
     inner, outer = list(range(1, half)), list(range(seq_count - 1, half - 1, -1))
-    there = [outer[:1] + inner[:1] + outer[1:] + inner[1:] + [0], inner + outer + [0]]
+    there = [outer + inner + [0], inner + outer + [0]]
 
     chunk_shape = jax.ShapeDtypeStruct((rows + STAT_ROWS, HD), bf16)
     chunk_shape = jax.ShapeDtypeStruct((rows + STAT_ROWS, HD), bf16)

time: 55.4 us -> 54.2 us (0.978)
  the two profiles are of different devices: /device:TPU:0 before, /device:TPU:1 now
where the time goes in v14:
time: 54.2 us; the launch traced here: 54 us
  starting transfers between devices  38.7 us (71%)
  Pallas kernels  9.31 us (17%)
  waiting for transfers between devices  3.75 us (7%)
  local copies, waits for them, and re-layouts  1.33 us (2%)
  between operations  0.89 us (2%)
    ppermute x16, starting transfers between devices, linked(): return lax.ppermute(shard, ('section', 'seq'), pairs)  35.6 us
    pallas_call x2, Pallas kernels, far_call(): pl.pallas_call(functools.partial(far_kernel, there, chosen), out_shape=[c...  5.13 us
    ppermute x16, waiting for transfers between devices, linked(): return lax.ppermute(shard, ('section', 'seq'), pairs)  3.74 us
    ppermute x2, starting transfers between devices, halo_from(): return lax.ppermute(mine, ('section', 'seq'), pairs)  3.04 us
    pallas_call x2, Pallas kernels, near_call(): pl.pallas_call(functools.partial(kernel, there), out_shape=jax.ShapeDtype...  2.52 us
    pallas_call x1, Pallas kernels, per_device(): pl.pallas_call(functools.partial(merge_kernel, there), out_shape=jax.Shap...  1.36 us
    unnamed x17, local copies, waits for them, and re-layouts  1.21 us
  transfers between devices with their start and end apart: 18, of which 3 were waited for; matrix products, arithmetic and copies ran while one was open for 0% of the time, Pallas kernels for 14%

profile of v14, /device:TPU:1, one launch (start us, length us, event | category | flops | bytes accessed | tf_op | source)
XLA Modules:
  0.0 54.0 jit_solution(7140294781467729878)
XLA Ops:
  0.7 0.0 copy-start
  0.7 1.1 %copy-done = bf16[1,320,1024]{2,1,0:T(8,128)(2,1)S(1)} copy-done((bf16[1,320,1024]{2,1,0:T(8,128)(2,1)S(1)}, bf16[1,320,1024]{2,1,0:T(8,128)(2,1)}, u32[]{:S(2)}) %copy-start) | copy-done | bytes 655384
  1.8 0.3 split.1
  2.0 2.1 %collective-permute-start.1 = (bf16[336,128]{1,0:T(8,128)(2,1)S(1)}, bf16[336,128]{1,0:T(8,128)(2,1)S(1)}, u32[]{:S(2)}, u32[]{:S(2)}) collective-permute-start(bf16[336,128]{1,0:T(8,128)(2,1)S(1)} %get-tuple-element.21), channel_id=1, source_target_pairs={{0,7},{1,6},{2,5},{3,4},{4,3},{5,2},{6,1},{7,0},{8,9},{9,8},{10,11... | collective-permute-start | bytes 258056 | tf_op jit(solution)/shard_map/ppermute | solution.py:341
  4.2 1.3 %collective-permute-start.3 = (bf16[336,128]{1,0:T(8,128)(2,1)S(1)}, bf16[336,128]{1,0:T(8,128)(2,1)S(1)}, u32[]{:S(2)}, u32[]{:S(2)}) collective-permute-start(bf16[336,128]{1,0:T(8,128)(2,1)S(1)} %get-tuple-element.22), channel_id=1, source_target_pairs={{0,6},{1,7},{2,4},{3,5},{4,2},{5,3},{6,0},{7,1},{8,10},{9,11},{10,... | collective-permute-start | bytes 258056 | tf_op jit(solution)/shard_map/ppermute | solution.py:341
  5.5 4.4 %collective-permute-start.5 = (bf16[336,128]{1,0:T(8,128)(2,1)S(1)}, bf16[336,128]{1,0:T(8,128)(2,1)S(1)}, u32[]{:S(2)}, u32[]{:S(2)}) collective-permute-start(bf16[336,128]{1,0:T(8,128)(2,1)S(1)} %get-tuple-element.24), channel_id=1, source_target_pairs={{0,4},{1,5},{2,6},{3,7},{4,0},{5,1},{6,2},{7,3},{8,15},{9,14},{10,... | collective-permute-start | bytes 258056 | tf_op jit(solution)/shard_map/ppermute | solution.py:341
  9.9 0.1 copy.10
  10.0 0.1 reshape_squeeze.3.random_ref
  10.1 0.0 copy-start.5
  10.1 0.1 pad_maximum_fusion.rows_ref
  10.2 2.3 %collective-permute-start = (bf16[2,128,1024]{2,1,0:T(8,128)(2,1)S(1)}, bf16[2,128,1024]{2,1,0:T(8,128)(2,1)S(1)}, u32[]{:S(2)}, u32[]{:S(2)}) collective-permute-start(bf16[2,128,1024]{2,1,0:T(8,128)(2,1)S(1)} %pad_maximum_fusion.rows_ref), channel_id=1, source_target_pairs={{8,9},{9,10},{10,11},{11,12},{12,13},{13,14},{14,15},{24,25},{25,2... | collective-permute-start | bytes 1572872 | tf_op jit(solution)/shard_map/ppermute | solution.py:361
  12.6 4.2 %collective-permute-start.7 = (bf16[336,128]{1,0:T(8,128)(2,1)S(1)}, bf16[336,128]{1,0:T(8,128)(2,1)S(1)}, u32[]{:S(2)}, u32[]{:S(2)}) collective-permute-start(bf16[336,128]{1,0:T(8,128)(2,1)S(1)} %get-tuple-element.26), channel_id=1, source_target_pairs={{0,2},{1,3},{2,0},{3,1},{4,6},{5,7},{6,4},{7,5},{8,13},{9,12},{10,... | collective-permute-start | bytes 258056 | tf_op jit(solution)/shard_map/ppermute | solution.py:341
  16.8 0.7 %collective-permute-start.2 = (bf16[2,128,1024]{2,1,0:T(8,128)(2,1)S(1)}, bf16[2,128,1024]{2,1,0:T(8,128)(2,1)S(1)}, u32[]{:S(2)}, u32[]{:S(2)}) collective-permute-start(bf16[2,128,1024]{2,1,0:T(8,128)(2,1)S(1)} %halo.1), channel_id=1, source_target_pairs={{0,1},{1,2},{2,3},{3,4},{4,5},{5,6},{6,7},{16,17},{17,18},{18,19},... | collective-permute-start | bytes 1572872 | tf_op jit(solution)/shard_map/ppermute | solution.py:361
  17.5 0.0 copy-start.1
  17.6 0.0 copy-start.2
  17.6 0.0 copy-start.3
  17.6 3.5 %far.2 = (bf16[336,128]{1,0:T(8,128)(2,1)S(1)}, bf16[336,128]{1,0:T(8,128)(2,1)S(1)}, bf16[336,128]{1,0:T(8,128)(2,1)S(1)}, bf16[336,128]{1,0:T(8,128)(2,1)S(1)}...) custom-call(s32[1]{0:T(128)} %bitcast.9.span_ref, s32[2]{0:T(128)S(1)} %bitcast.22, ...), custom_call_target="tpu_custom_call" | custom-call | flops 12582912000 | bytes 4128768 | tf_op jit(solution)/shard_map/far/pallas_call | solution.py:368
  21.1 10.8 %collective-permute-start.9 = (bf16[336,128]{1,0:T(8,128)(2,1)S(1)}, bf16[336,128]{1,0:T(8,128)(2,1)S(1)}, u32[]{:S(2)}, u32[]{:S(2)}) collective-permute-start(bf16[336,128]{1,0:T(8,128)(2,1)S(1)} %get-tuple-element.29), channel_id=1, source_target_pairs={{0,15},{1,14},{2,13},{3,12},{4,11},{5,10},{6,9},{7,8},{8,17},{9,16... | collective-permute-start | bytes 258056 | tf_op jit(solution)/shard_map/ppermute | solution.py:341
  32.0 1.5 %near_inner.1 = bf16[256,1024]{1,0:T(8,128)(2,1)S(1)} custom-call(bf16[320,1024]{1,0:T(8,128)(2,1)S(1)} %bitcast.12, bf16[320,1024]{1,0:T(8,128)(2,1)S(1)} %bitcast.14, bf16[320,1024]{1,0:T(8,128)(2,1)S(1)} %bitcast.16, bf16[336,128]{1,0:T(8,128)(2,1)S(1)} %get-tuple-element.31.own_ref, bf16[336,128]{1,0:T(8,128)(2,1)S(1)} %collective-permute-done.1._.refs_0_, ...), custom_call_target="tpu_custom_call" | custom-call | flops 8053063680 | bytes 1769472 | tf_op jit(solution)/shard_map/near_inner/pallas_call | solution.py:398
  33.5 0.7 %collective-permute-start.12 = (bf16[256,1024]{1,0:T(8,128)(2,1)S(1)}, bf16[256,1024]{1,0:T(8,128)(2,1)S(1)}, u32[]{:S(2)}, u32[]{:S(2)}) collective-permute-start(bf16[256,1024]{1,0:T(8,128)(2,1)S(1)} %near_inner.1), channel_id=1, source_target_pairs={{0,8},{1,9},{2,10},{3,11},{4,12},{5,13},{6,14},{7,15},{8,16},{9,17... | collective-permute-start | bytes 1572872 | tf_op jit(solution)/shard_map/ppermute | solution.py:341
  34.1 2.7 %collective-permute-start.13 = (bf16[336,128]{1,0:T(8,128)(2,1)S(1)}, bf16[336,128]{1,0:T(8,128)(2,1)S(1)}, u32[]{:S(2)}, u32[]{:S(2)}) collective-permute-start(bf16[336,128]{1,0:T(8,128)(2,1)S(1)} %get-tuple-element.32), channel_id=1, source_target_pairs={{0,13},{1,12},{2,15},{3,14},{4,9},{5,8},{6,11},{7,10},{8,19},{9,18... | collective-permute-start | bytes 258056 | tf_op jit(solution)/shard_map/ppermute | solution.py:341
  36.9 0.8 %collective-permute-done.10.refs_9_.refs_1_ = bf16[336,128]{1,0:T(8,128)(2,1)S(1)} collective-permute-done((bf16[336,128]{1,0:T(8,128)(2,1)S(1)}, bf16[336,128]{1,0:T(8,128)(2,1)S(1)}, u32[]{:S(2)}, u32[]{:S(2)}) %collective-permute-start.10) | collective-permute-done | bytes 86048 | tf_op jit(solution)/shard_map/ppermute | solution.py:341
  37.6 1.7 %collective-permute-start.14 = (bf16[336,128]{1,0:T(8,128)(2,1)S(1)}, bf16[336,128]{1,0:T(8,128)(2,1)S(1)}, u32[]{:S(2)}, u32[]{:S(2)}) collective-permute-start(bf16[336,128]{1,0:T(8,128)(2,1)S(1)} %get-tuple-element.33), channel_id=1, source_target_pairs={{0,12},{1,13},{2,14},{3,15},{4,8},{5,9},{6,10},{7,11},{8,23},{9,22... | collective-permute-start | bytes 258056 | tf_op jit(solution)/shard_map/ppermute | solution.py:341
  39.3 1.9 %collective-permute-start.15 = (bf16[336,128]{1,0:T(8,128)(2,1)S(1)}, bf16[336,128]{1,0:T(8,128)(2,1)S(1)}, u32[]{:S(2)}, u32[]{:S(2)}) collective-permute-start(bf16[336,128]{1,0:T(8,128)(2,1)S(1)} %get-tuple-element.34), channel_id=1, source_target_pairs={{0,9},{1,8},{2,11},{3,10},{4,13},{5,12},{6,15},{7,14},{8,22},{9,23... | collective-permute-start | bytes 258056 | tf_op jit(solution)/shard_map/ppermute | solution.py:341
  41.2 1.0 %near_edge.1 = bf16[144,1024]{1,0:T(8,128)(2,1)S(1)} custom-call(bf16[320,1024]{1,0:T(8,128)(2,1)S(1)} %bitcast.13, bf16[320,1024]{1,0:T(8,128)(2,1)S(1)} %bitcast.15, bf16[320,1024]{1,0:T(8,128)(2,1)S(1)} %bitcast.17, bf16[2,128,1024]{2,1,0:T(8,128)(2,1)S(1)} %collective-permute-done.odd_ref, bf16[2,128,1024]{2,1,0:T(8,128)(2,1)S(1)} %collective-permute-done.2.even_ref, ...), custom_call_target="tpu_custom_call" | custom-call | flops 5368709120 | bytes 1179648 | tf_op jit(solution)/shard_map/near_edge/pallas_call | solution.py:398
  42.2 0.1 collective-permute-start.11
  42.3 1.6 %far.3 = (bf16[336,128]{1,0:T(8,128)(2,1)S(1)}, bf16[336,128]{1,0:T(8,128)(2,1)S(1)}) custom-call(s32[1]{0:T(128)} %bitcast.10.span_ref, s32[2]{0:T(128)S(1)} %bitcast.23, s32[120]{0:T(128)S(1)} %reshape_squeeze.3.random_ref, bf16[6144,128]{1,0:T(8,128)(2,1)S(1)} %bitcast.19, bf16[6144,128]{1,0:T(8,128)(2,1)S(1)} %bitcast.21, ...), custom_call_target="tpu_custom_call" | custom-call | flops 4194304000 | bytes 3473408 | tf_op jit(solution)/shard_map/far/pallas_call | solution.py:368
  43.9 3.9 %collective-permute-start.16 = (bf16[336,128]{1,0:T(8,128)(2,1)S(1)}, bf16[336,128]{1,0:T(8,128)(2,1)S(1)}, u32[]{:S(2)}, u32[]{:S(2)}) collective-permute-start(bf16[336,128]{1,0:T(8,128)(2,1)S(1)} %get-tuple-element.35), channel_id=1, source_target_pairs={{0,10},{1,11},{2,8},{3,9},{4,14},{5,15},{6,12},{7,13},{8,21},{9,20... | collective-permute-start | bytes 258056 | tf_op jit(solution)/shard_map/ppermute | solution.py:341
  47.8 1.9 %collective-permute-start.17 = (bf16[336,128]{1,0:T(8,128)(2,1)S(1)}, bf16[336,128]{1,0:T(8,128)(2,1)S(1)}, u32[]{:S(2)}, u32[]{:S(2)}) collective-permute-start(bf16[336,128]{1,0:T(8,128)(2,1)S(1)} %get-tuple-element.36), channel_id=1, source_target_pairs={{0,11},{1,10},{2,9},{3,8},{4,15},{5,14},{6,13},{7,12},{8,20},{9,21... | collective-permute-start | bytes 258056 | tf_op jit(solution)/shard_map/ppermute | solution.py:341
  49.7 0.3 collective-permute-done.16.refs_5_
  50.0 2.6 %collective-permute-done.17.refs_6_ = bf16[336,128]{1,0:T(8,128)(2,1)S(1)} collective-permute-done((bf16[336,128]{1,0:T(8,128)(2,1)S(1)}, bf16[336,128]{1,0:T(8,128)(2,1)S(1)}, u32[]{:S(2)}, u32[]{:S(2)}) %collective-permute-start.17) | collective-permute-done | bytes 86048 | tf_op jit(solution)/shard_map/ppermute | solution.py:341
  52.6 1.4 %merge.1 = bf16[320,1024]{1,0:T(8,128)(2,1)} custom-call(bf16[144,1024]{1,0:T(8,128)(2,1)S(1)} %collective-permute-done.11.edge_ref, bf16[256,1024]{1,0:T(8,128)(2,1)S(1)} %collective-permute-done.12.inner_ref, bf16[336,128]{1,0:T(8,128)(2,1)S(1)} %collective-permute-done.9.refs_8_.refs_0_, bf16[336,128]{1,0:T(8,128)(2,1)S(1)} %collective-permute-done.10.refs_9_.refs_1_, ...), custom_call_target="tpu_custom_call" | custom-call | bytes 1966080 | tf_op jit(solution)/shard_map/merge/pallas_call | solution.py:428
  (34 shorter events, 0.1 us)
Async XLA Ops:
  0.0 9.9 %copy-start.7 = (s32[1,40,3]{1,0,2:T(1,128)S(1)}, s32[1,40,3]{1,0,2:T(1,128)}, u32[]{:S(2)}) copy-start(s32[1,40,3]{1,0,2:T(1,128)} %param.15) | copy-start | bytes 1444
  0.7 1.1 %copy-start = (bf16[1,320,1024]{2,1,0:T(8,128)(2,1)S(1)}, bf16[1,320,1024]{2,1,0:T(8,128)(2,1)}, u32[]{:S(2)}) copy-start(bf16[1,320,1024]{2,1,0:T(8,128)(2,1)} %param.8) | copy-start | bytes 1966084
  1.8 8.3 %slice-start = ((bf16[1,320,1024]{2,1,0:T(8,128)(2,1)}), bf16[1,128,1024]{2,1,0:T(8,128)(2,1)S(1)}, s32[]{:S(2)}) async-start(bf16[1,320,1024]{2,1,0:T(8,128)(2,1)} %param.9), calls=%async_computation | async-start | bytes 524288 | tf_op jit(solution)/shard_map/slice | solution.py:345
  1.8 8.3 %slice-start.1 = ((bf16[1,320,1024]{2,1,0:T(8,128)(2,1)}), bf16[1,128,1024]{2,1,0:T(8,128)(2,1)S(1)}, s32[]{:S(2)}) async-start(bf16[1,320,1024]{2,1,0:T(8,128)(2,1)} %param.10), calls=%async_computation.1 | async-start | bytes 524288 | tf_op jit(solution)/shard_map/slice | solution.py:345
  2.0 8.1 %collective-permute-start.1 = (bf16[336,128]{1,0:T(8,128)(2,1)S(1)}, bf16[336,128]{1,0:T(8,128)(2,1)S(1)}, u32[]{:S(2)}, u32[]{:S(2)}) collective-permute-start(bf16[336,128]{1,0:T(8,128)(2,1)S(1)} %get-tuple-element.21), channel_id=1, source_target_pairs={{0,7},{1,6},{2,5},{3,4},{4,3},{5,2},{6,1},{7,0},{8,9},{9,8},{10,11... | collective-permute-start | bytes 258056 | tf_op jit(solution)/shard_map/ppermute | solution.py:341
  4.2 8.4 %collective-permute-start.3 = (bf16[336,128]{1,0:T(8,128)(2,1)S(1)}, bf16[336,128]{1,0:T(8,128)(2,1)S(1)}, u32[]{:S(2)}, u32[]{:S(2)}) collective-permute-start(bf16[336,128]{1,0:T(8,128)(2,1)S(1)} %get-tuple-element.22), channel_id=1, source_target_pairs={{0,6},{1,7},{2,4},{3,5},{4,2},{5,3},{6,0},{7,1},{8,10},{9,11},{10,... | collective-permute-start | bytes 258056 | tf_op jit(solution)/shard_map/ppermute | solution.py:341
  5.5 11.3 %collective-permute-start.4 = (bf16[336,128]{1,0:T(8,128)(2,1)S(1)}, bf16[336,128]{1,0:T(8,128)(2,1)S(1)}, u32[]{:S(2)}, u32[]{:S(2)}) collective-permute-start(bf16[336,128]{1,0:T(8,128)(2,1)S(1)} %get-tuple-element.23), channel_id=1, source_target_pairs={{0,5},{1,4},{2,7},{3,6},{4,1},{5,0},{6,3},{7,2},{8,11},{9,10},{10,... | collective-permute-start | bytes 258056 | tf_op jit(solution)/shard_map/ppermute | solution.py:341
  5.5 11.3 %collective-permute-start.5 = (bf16[336,128]{1,0:T(8,128)(2,1)S(1)}, bf16[336,128]{1,0:T(8,128)(2,1)S(1)}, u32[]{:S(2)}, u32[]{:S(2)}) collective-permute-start(bf16[336,128]{1,0:T(8,128)(2,1)S(1)} %get-tuple-element.24), channel_id=1, source_target_pairs={{0,4},{1,5},{2,6},{3,7},{4,0},{5,1},{6,2},{7,3},{8,15},{9,14},{10,... | collective-permute-start | bytes 258056 | tf_op jit(solution)/shard_map/ppermute | solution.py:341
  9.9 7.7 %copy-start.4 = (bf16[1,6144,128]{2,1,0:T(8,128)(2,1)S(1)}, bf16[1,6144,128]{2,1,0:T(8,128)(2,1)}, u32[]{:S(2)}) copy-start(bf16[1,6144,128]{2,1,0:T(8,128)(2,1)} %param.11) | copy-start | bytes 4718596
  9.9 7.7 %copy-start.6 = (s32[1,2]{1,0:T(1,128)S(1)}, s32[1,2]{1,0:T(1,128)}, u32[]{:S(2)}) copy-start(s32[1,2]{1,0:T(1,128)} %param.14) | copy-start | bytes 28
  9.9 7.6 %collective-permute-start.6 = (bf16[336,128]{1,0:T(8,128)(2,1)S(1)}, bf16[336,128]{1,0:T(8,128)(2,1)S(1)}, u32[]{:S(2)}, u32[]{:S(2)}) collective-permute-start(bf16[336,128]{1,0:T(8,128)(2,1)S(1)} %get-tuple-element.25), channel_id=1, source_target_pairs={{0,1},{1,0},{2,3},{3,2},{4,5},{5,4},{6,7},{7,6},{8,14},{9,15},{10,... | collective-permute-start | bytes 258056 | tf_op jit(solution)/shard_map/ppermute | solution.py:341
  10.1 7.4 %copy-start.5 = (bf16[1,6144,128]{2,1,0:T(8,128)(2,1)S(1)}, bf16[1,6144,128]{2,1,0:T(8,128)(2,1)}, u32[]{:S(2)}) copy-start(bf16[1,6144,128]{2,1,0:T(8,128)(2,1)} %param.12) | copy-start | bytes 4718596
  10.2 29.2 %collective-permute-start = (bf16[2,128,1024]{2,1,0:T(8,128)(2,1)S(1)}, bf16[2,128,1024]{2,1,0:T(8,128)(2,1)S(1)}, u32[]{:S(2)}, u32[]{:S(2)}) collective-permute-start(bf16[2,128,1024]{2,1,0:T(8,128)(2,1)S(1)} %pad_maximum_fusion.rows_ref), channel_id=1, source_target_pairs={{8,9},{9,10},{10,11},{11,12},{12,13},{13,14},{14,15},{24,25},{25,2... | collective-permute-start | bytes 1572872 | tf_op jit(solution)/shard_map/ppermute | solution.py:361
  12.6 19.3 %collective-permute-start.7 = (bf16[336,128]{1,0:T(8,128)(2,1)S(1)}, bf16[336,128]{1,0:T(8,128)(2,1)S(1)}, u32[]{:S(2)}, u32[]{:S(2)}) collective-permute-start(bf16[336,128]{1,0:T(8,128)(2,1)S(1)} %get-tuple-element.26), channel_id=1, source_target_pairs={{0,2},{1,3},{2,0},{3,1},{4,6},{5,7},{6,4},{7,5},{8,13},{9,12},{10,... | collective-permute-start | bytes 258056 | tf_op jit(solution)/shard_map/ppermute | solution.py:341
  16.8 15.1 %collective-permute-start.8 = (bf16[336,128]{1,0:T(8,128)(2,1)S(1)}, bf16[336,128]{1,0:T(8,128)(2,1)S(1)}, u32[]{:S(2)}, u32[]{:S(2)}) collective-permute-start(bf16[336,128]{1,0:T(8,128)(2,1)S(1)} %get-tuple-element.27), channel_id=1, source_target_pairs={{0,3},{1,2},{2,1},{3,0},{4,7},{5,6},{6,5},{7,4},{8,12},{9,13},{10,... | collective-permute-start | bytes 258056 | tf_op jit(solution)/shard_map/ppermute | solution.py:341
  16.8 24.4 %collective-permute-start.2 = (bf16[2,128,1024]{2,1,0:T(8,128)(2,1)S(1)}, bf16[2,128,1024]{2,1,0:T(8,128)(2,1)S(1)}, u32[]{:S(2)}, u32[]{:S(2)}) collective-permute-start(bf16[2,128,1024]{2,1,0:T(8,128)(2,1)S(1)} %halo.1), channel_id=1, source_target_pairs={{0,1},{1,2},{2,3},{3,4},{4,5},{5,6},{6,7},{16,17},{17,18},{18,19},... | collective-permute-start | bytes 1572872 | tf_op jit(solution)/shard_map/ppermute | solution.py:361
  17.5 14.4 %copy-start.1 = (bf16[1,320,1024]{2,1,0:T(8,128)(2,1)S(1)}, bf16[1,320,1024]{2,1,0:T(8,128)(2,1)}, u32[]{:S(2)}) copy-start(bf16[1,320,1024]{2,1,0:T(8,128)(2,1)} %param.8) | copy-start | bytes 1966084
  17.6 14.4 %copy-start.2 = (bf16[1,320,1024]{2,1,0:T(8,128)(2,1)S(1)}, bf16[1,320,1024]{2,1,0:T(8,128)(2,1)}, u32[]{:S(2)}) copy-start(bf16[1,320,1024]{2,1,0:T(8,128)(2,1)} %param.9) | copy-start | bytes 1966084
  17.6 14.4 %copy-start.3 = (bf16[1,320,1024]{2,1,0:T(8,128)(2,1)S(1)}, bf16[1,320,1024]{2,1,0:T(8,128)(2,1)}, u32[]{:S(2)}) copy-start(bf16[1,320,1024]{2,1,0:T(8,128)(2,1)} %param.10) | copy-start | bytes 1966084
  21.1 13.1 %collective-permute-start.9 = (bf16[336,128]{1,0:T(8,128)(2,1)S(1)}, bf16[336,128]{1,0:T(8,128)(2,1)S(1)}, u32[]{:S(2)}, u32[]{:S(2)}) collective-permute-start(bf16[336,128]{1,0:T(8,128)(2,1)S(1)} %get-tuple-element.29), channel_id=1, source_target_pairs={{0,15},{1,14},{2,13},{3,12},{4,11},{5,10},{6,9},{7,8},{8,17},{9,16... | collective-permute-start | bytes 258056 | tf_op jit(solution)/shard_map/ppermute | solution.py:341
  31.9 5.7 %collective-permute-start.10 = (bf16[336,128]{1,0:T(8,128)(2,1)S(1)}, bf16[336,128]{1,0:T(8,128)(2,1)S(1)}, u32[]{:S(2)}, u32[]{:S(2)}) collective-permute-start(bf16[336,128]{1,0:T(8,128)(2,1)S(1)} %get-tuple-element.30), channel_id=1, source_target_pairs={{0,14},{1,15},{2,12},{3,13},{4,10},{5,11},{6,8},{7,9},{8,18},{9,19... | collective-permute-start | bytes 258056 | tf_op jit(solution)/shard_map/ppermute | solution.py:341
  33.5 19.1 %collective-permute-start.12 = (bf16[256,1024]{1,0:T(8,128)(2,1)S(1)}, bf16[256,1024]{1,0:T(8,128)(2,1)S(1)}, u32[]{:S(2)}, u32[]{:S(2)}) collective-permute-start(bf16[256,1024]{1,0:T(8,128)(2,1)S(1)} %near_inner.1), channel_id=1, source_target_pairs={{0,8},{1,9},{2,10},{3,11},{4,12},{5,13},{6,14},{7,15},{8,16},{9,17... | collective-permute-start | bytes 1572872 | tf_op jit(solution)/shard_map/ppermute | solution.py:341
  34.1 9.8 %collective-permute-start.13 = (bf16[336,128]{1,0:T(8,128)(2,1)S(1)}, bf16[336,128]{1,0:T(8,128)(2,1)S(1)}, u32[]{:S(2)}, u32[]{:S(2)}) collective-permute-start(bf16[336,128]{1,0:T(8,128)(2,1)S(1)} %get-tuple-element.32), channel_id=1, source_target_pairs={{0,13},{1,12},{2,15},{3,14},{4,9},{5,8},{6,11},{7,10},{8,19},{9,18... | collective-permute-start | bytes 258056 | tf_op jit(solution)/shard_map/ppermute | solution.py:341
  37.6 10.2 %collective-permute-start.14 = (bf16[336,128]{1,0:T(8,128)(2,1)S(1)}, bf16[336,128]{1,0:T(8,128)(2,1)S(1)}, u32[]{:S(2)}, u32[]{:S(2)}) collective-permute-start(bf16[336,128]{1,0:T(8,128)(2,1)S(1)} %get-tuple-element.33), channel_id=1, source_target_pairs={{0,12},{1,13},{2,14},{3,15},{4,8},{5,9},{6,10},{7,11},{8,23},{9,22... | collective-permute-start | bytes 258056 | tf_op jit(solution)/shard_map/ppermute | solution.py:341
  39.3 10.3 %collective-permute-start.15 = (bf16[336,128]{1,0:T(8,128)(2,1)S(1)}, bf16[336,128]{1,0:T(8,128)(2,1)S(1)}, u32[]{:S(2)}, u32[]{:S(2)}) collective-permute-start(bf16[336,128]{1,0:T(8,128)(2,1)S(1)} %get-tuple-element.34), channel_id=1, source_target_pairs={{0,9},{1,8},{2,11},{3,10},{4,13},{5,12},{6,15},{7,14},{8,22},{9,23... | collective-permute-start | bytes 258056 | tf_op jit(solution)/shard_map/ppermute | solution.py:341
  42.2 10.4 %collective-permute-start.11 = (bf16[144,1024]{1,0:T(8,128)(2,1)S(1)}, bf16[144,1024]{1,0:T(8,128)(2,1)S(1)}, u32[]{:S(2)}, u32[]{:S(2)}) collective-permute-start(bf16[144,1024]{1,0:T(8,128)(2,1)S(1)} %near_edge.1), channel_id=1, source_target_pairs={{0,8},{1,9},{2,10},{3,11},{4,12},{5,13},{6,14},{7,15},{8,16},{9,17... | collective-permute-start | bytes 884744 | tf_op jit(solution)/shard_map/ppermute | solution.py:341
  43.9 6.1 %collective-permute-start.16 = (bf16[336,128]{1,0:T(8,128)(2,1)S(1)}, bf16[336,128]{1,0:T(8,128)(2,1)S(1)}, u32[]{:S(2)}, u32[]{:S(2)}) collective-permute-start(bf16[336,128]{1,0:T(8,128)(2,1)S(1)} %get-tuple-element.35), channel_id=1, source_target_pairs={{0,10},{1,11},{2,8},{3,9},{4,14},{5,15},{6,12},{7,13},{8,21},{9,20... | collective-permute-start | bytes 258056 | tf_op jit(solution)/shard_map/ppermute | solution.py:341
  47.8 4.8 %collective-permute-start.17 = (bf16[336,128]{1,0:T(8,128)(2,1)S(1)}, bf16[336,128]{1,0:T(8,128)(2,1)S(1)}, u32[]{:S(2)}, u32[]{:S(2)}) collective-permute-start(bf16[336,128]{1,0:T(8,128)(2,1)S(1)} %get-tuple-element.36), channel_id=1, source_target_pairs={{0,11},{1,10},{2,9},{3,8},{4,15},{5,14},{6,13},{7,12},{8,20},{9,21... | collective-permute-start | bytes 258056 | tf_op jit(solution)/shard_map/ppermute | solution.py:341

commit v15 on v13

--- a/solution.py
+++ b/solution.py
@@ -115,7 +115,7 @@
 
 
 def far_kernel(
-    there, chosen, span_ref, global_ref, random_ref, key_ref, value_ref, *refs
+    there, back, chosen, span_ref, global_ref, random_ref, key_ref, value_ref, *refs
 ):
     span = span_ref[0]
     last = key_ref.shape[0] // BLK - 1
@@ -127,10 +127,23 @@
 
     glob_keys = [block(key_ref, global_ref[g]) for g in range(GLOB)]
     glob_values = [block(value_ref, global_ref[g]) for g in range(GLOB)]
-    peers = [peers_of(there, 0)[at] for at in chosen]
-    query_refs, out_refs = refs[: len(peers)], refs[len(peers) :]
+    count = len(chosen)
+    query_refs, out_refs, held_ref = refs[:count], refs[count:-1], refs[-1]
     rows = query_refs[0].shape[0] - STAT_ROWS
-    for chunk, query_ref, out_ref in zip(peers, query_refs, out_refs):
+    odd = lax.rem(lax.axis_index("section"), 2) == 1
+    moved = any(steps != others for steps, others in zip(there, back))
+    if moved:
+        for index, query_ref in enumerate(query_refs):
+            held_ref[index] = query_ref[:rows, :]
+    for index, (at, out_ref) in enumerate(zip(chosen, out_refs)):
+        chunk = peers_of(back, 0)[at]
+        if moved:
+            even_at, odd_at = (
+                chosen.index(steps.index(others[at])) for steps, others in zip(there, back)
+            )
+            query_ref = held_ref.at[jnp.where(odd, odd_at, even_at)]
+        else:
+            query_ref = query_refs[index]
         blocks = rows // BLK
         first = chunk == 0
         all_scores, all_picks = [], []
@@ -287,6 +300,7 @@
     half = max(seq_count // 2, 1)
     inner, outer = list(range(1, half)), list(range(seq_count - 1, half - 1, -1))
     there = [outer[:1] + inner[:1] + outer[1:] + inner[1:] + [0], inner + outer + [0]]
+    back = [outer + inner + [0], inner + outer + [0]]
 
     chunk_shape = jax.ShapeDtypeStruct((rows + STAT_ROWS, HD), bf16)
     chunk_shape = jax.ShapeDtypeStruct((rows + STAT_ROWS, HD), bf16)
@@ -325,8 +339,6 @@
         ]
         return lax.ppermute(shard, ("section", "seq"), pairs)
 
-    came = [linked(shard, 0, steps) for shard, steps in zip(sent[:-1], zip(*there))]
-    came.append(sent[-1])
     tails = jnp.stack([keys_new[0, rows - halo :], values_new[0, rows - halo :]])
 
     def halo_from(parity, after):
@@ -350,11 +362,13 @@
 
     def far_call(chosen):
         count = len(chosen)
+        moved = any(steps[at] != others[at] for steps, others in zip(there, back) for at in chosen)
         return pl.pallas_call(
-            functools.partial(far_kernel, there, chosen),
+            functools.partial(far_kernel, there, back if moved else there, chosen),
             out_shape=[chunk_shape] * count,
             in_specs=[whole_smem] * 3 + [whole_vmem] * (2 + count),
             out_specs=[whole_vmem] * count,
+            scratch_shapes=[pltpu.VMEM((count, rows, HD), bf16)],
             compiler_params=params(queries),
             cost_estimate=pl.CostEstimate(
                 flops=40 * count * rows * 320 * HD * 4,
@@ -377,7 +391,7 @@
     if late:
         far.update(zip(late, far_call(late)))
     far = [far[at] for at in range(seq_count)]
-    handed = [linked(shard, 1, steps) for shard, steps in zip(far[:-1], zip(*there))]
+    handed = [linked(shard, 1, steps) for shard, steps in zip(far[:-1], zip(*back))]
 
     def near_call(kernel, name, near_part, out_rows, vmem_count, scratch, *operands):
         return pl.pallas_call(
@@ -411,7 +425,7 @@
     handed_edge = linked(edge_part, 1, [0, 0])
 
     merged = pl.pallas_call(
-        functools.partial(merge_kernel, there),
+        functools.partial(merge_kernel, back),
         out_shape=jax.ShapeDtypeStruct((rows, wide), bf16),
         in_specs=[whole_vmem] * (1 + seq_count),
         out_specs=whole_vmem,

time: 55.4 us -> 55.7 us (level)
  starting transfers between devices: 34.6 us -> 36.7 us
  waiting for transfers between devices: 9.35 us -> 7.59 us
    ppermute x16, starting transfers between devices: 29.5 us -> 31.6 us  [linked(): return lax.ppermute(shard, ('section', 'seq'), pairs)]
    ppermute x16, waiting for transfers between devices: 9.35 us -> 7.58 us  [linked(): return lax.ppermute(shard, ('section', 'seq'), pairs)]
where the time goes in v15:
time: 55.7 us; the launch traced here: 55.5 us
  starting transfers between devices  36.7 us (66%)
  Pallas kernels  8.93 us (16%)
  waiting for transfers between devices  7.59 us (14%)
  local copies, waits for them, and re-layouts  1.33 us (2%)
  between operations  0.91 us (2%)
    ppermute x16, starting transfers between devices, linked(): return lax.ppermute(shard, ('section', 'seq'), pairs)  31.6 us
    ppermute x16, waiting for transfers between devices, linked(): return lax.ppermute(shard, ('section', 'seq'), pairs)  7.58 us
    ppermute x2, starting transfers between devices, halo_from(): return lax.ppermute(mine, ('section', 'seq'), pairs)  5.12 us
    pallas_call x2, Pallas kernels, far_call(): pl.pallas_call(functools.partial(far_kernel, there, back if moved else th...  4.73 us
    pallas_call x2, Pallas kernels, near_call(): pl.pallas_call(functools.partial(kernel, there), out_shape=jax.ShapeDtype...  2.53 us
    pallas_call x1, Pallas kernels, per_device(): pl.pallas_call(functools.partial(merge_kernel, back), out_shape=jax.Shape...  1.36 us
    unnamed x17, local copies, waits for them, and re-layouts  1.21 us
  transfers between devices with their start and end apart: 18, of which 4 were waited for; matrix products, arithmetic and copies ran while one was open for 0% of the time, Pallas kernels for 13%

profile of v15, /device:TPU:0, one launch (start us, length us, event | category | flops | bytes accessed | tf_op | source)
XLA Modules:
  0.0 55.5 jit_solution(7118327241924212110)
XLA Ops:
  0.7 1.1 %copy-done = bf16[1,320,1024]{2,1,0:T(8,128)(2,1)S(1)} copy-done((bf16[1,320,1024]{2,1,0:T(8,128)(2,1)S(1)}, bf16[1,320,1024]{2,1,0:T(8,128)(2,1)}, u32[]{:S(2)}) %copy-start) | copy-done | bytes 655384
  1.8 0.3 split.1
  2.0 6.1 %collective-permute-start.1 = (bf16[336,128]{1,0:T(8,128)(2,1)S(1)}, bf16[336,128]{1,0:T(8,128)(2,1)S(1)}, u32[]{:S(2)}, u32[]{:S(2)}) collective-permute-start(bf16[336,128]{1,0:T(8,128)(2,1)S(1)} %get-tuple-element.21), channel_id=1, source_target_pairs={{0,7},{1,6},{2,5},{3,4},{4,3},{5,2},{6,1},{7,0},{8,9},{9,8},{10,11... | collective-permute-start | bytes 258056 | tf_op jit(solution)/shard_map/ppermute | solution.py:327
  8.1 0.5 collective-permute-start.3
  8.6 0.1 collective-permute-start.4
  8.8 1.8 %collective-permute-start.5 = (bf16[336,128]{1,0:T(8,128)(2,1)S(1)}, bf16[336,128]{1,0:T(8,128)(2,1)S(1)}, u32[]{:S(2)}, u32[]{:S(2)}) collective-permute-start(bf16[336,128]{1,0:T(8,128)(2,1)S(1)} %get-tuple-element.24), channel_id=1, source_target_pairs={{0,5},{1,4},{2,7},{3,6},{4,1},{5,0},{6,3},{7,2},{8,15},{9,14},{10,... | collective-permute-start | bytes 258056 | tf_op jit(solution)/shard_map/ppermute | solution.py:327
  10.6 2.1 %collective-permute-start.6 = (bf16[336,128]{1,0:T(8,128)(2,1)S(1)}, bf16[336,128]{1,0:T(8,128)(2,1)S(1)}, u32[]{:S(2)}, u32[]{:S(2)}) collective-permute-start(bf16[336,128]{1,0:T(8,128)(2,1)S(1)} %get-tuple-element.25), channel_id=1, source_target_pairs={{0,4},{1,5},{2,6},{3,7},{4,0},{5,1},{6,2},{7,3},{8,14},{9,15},{10,... | collective-permute-start | bytes 258056 | tf_op jit(solution)/shard_map/ppermute | solution.py:327
  12.7 0.1 copy.10
  12.8 0.1 reshape_squeeze.3.random_ref
  13.0 0.1 pad_maximum_fusion.rows_ref
  13.0 0.8 %collective-permute-start = (bf16[2,128,1024]{2,1,0:T(8,128)(2,1)S(1)}, bf16[2,128,1024]{2,1,0:T(8,128)(2,1)S(1)}, u32[]{:S(2)}, u32[]{:S(2)}) collective-permute-start(bf16[2,128,1024]{2,1,0:T(8,128)(2,1)S(1)} %pad_maximum_fusion.rows_ref), channel_id=1, source_target_pairs={{8,9},{9,10},{10,11},{11,12},{12,13},{13,14},{14,15},{24,25},{25,2... | collective-permute-start | bytes 1572872 | tf_op jit(solution)/shard_map/ppermute | solution.py:358
  13.9 1.3 %collective-permute-start.7 = (bf16[336,128]{1,0:T(8,128)(2,1)S(1)}, bf16[336,128]{1,0:T(8,128)(2,1)S(1)}, u32[]{:S(2)}, u32[]{:S(2)}) collective-permute-start(bf16[336,128]{1,0:T(8,128)(2,1)S(1)} %get-tuple-element.26), channel_id=1, source_target_pairs={{0,2},{1,3},{2,0},{3,1},{4,6},{5,7},{6,4},{7,5},{8,13},{9,12},{10,... | collective-permute-start | bytes 258056 | tf_op jit(solution)/shard_map/ppermute | solution.py:327
  15.2 2.2 %collective-permute-start.8 = (bf16[336,128]{1,0:T(8,128)(2,1)S(1)}, bf16[336,128]{1,0:T(8,128)(2,1)S(1)}, u32[]{:S(2)}, u32[]{:S(2)}) collective-permute-start(bf16[336,128]{1,0:T(8,128)(2,1)S(1)} %get-tuple-element.27), channel_id=1, source_target_pairs={{0,3},{1,2},{2,1},{3,0},{4,7},{5,6},{6,5},{7,4},{8,12},{9,13},{10,... | collective-permute-start | bytes 258056 | tf_op jit(solution)/shard_map/ppermute | solution.py:327
  17.5 3.4 %collective-permute-done.5.refs_3_ = bf16[336,128]{1,0:T(8,128)(2,1)S(1)} collective-permute-done((bf16[336,128]{1,0:T(8,128)(2,1)S(1)}, bf16[336,128]{1,0:T(8,128)(2,1)S(1)}, u32[]{:S(2)}, u32[]{:S(2)}) %collective-permute-start.5) | collective-permute-done | bytes 86048 | tf_op jit(solution)/shard_map/ppermute | solution.py:327
  20.8 4.3 %collective-permute-start.2 = (bf16[2,128,1024]{2,1,0:T(8,128)(2,1)S(1)}, bf16[2,128,1024]{2,1,0:T(8,128)(2,1)S(1)}, u32[]{:S(2)}, u32[]{:S(2)}) collective-permute-start(bf16[2,128,1024]{2,1,0:T(8,128)(2,1)S(1)} %halo.1), channel_id=1, source_target_pairs={{0,1},{1,2},{2,3},{3,4},{4,5},{5,6},{6,7},{16,17},{17,18},{18,19},... | collective-permute-start | bytes 1572872 | tf_op jit(solution)/shard_map/ppermute | solution.py:358
  25.2 3.2 %far.2 = (bf16[336,128]{1,0:T(8,128)(2,1)S(1)}, bf16[336,128]{1,0:T(8,128)(2,1)S(1)}, bf16[336,128]{1,0:T(8,128)(2,1)S(1)}, bf16[336,128]{1,0:T(8,128)(2,1)S(1)}...) custom-call(s32[1]{0:T(128)} %bitcast.9.span_ref, s32[2]{0:T(128)S(1)} %bitcast.22, ...), custom_call_target="tpu_custom_call" | custom-call | flops 12582912000 | bytes 4128768 | tf_op jit(solution)/shard_map/far/pallas_call | solution.py:366
  28.4 0.1 collective-permute-start.9
  28.5 7.0 %collective-permute-start.10 = (bf16[336,128]{1,0:T(8,128)(2,1)S(1)}, bf16[336,128]{1,0:T(8,128)(2,1)S(1)}, u32[]{:S(2)}, u32[]{:S(2)}) collective-permute-start(bf16[336,128]{1,0:T(8,128)(2,1)S(1)} %get-tuple-element.30), channel_id=1, source_target_pairs={{0,14},{1,15},{2,12},{3,13},{4,10},{5,11},{6,8},{7,9},{8,18},{9,19... | collective-permute-start | bytes 258056 | tf_op jit(solution)/shard_map/ppermute | solution.py:340
  35.5 1.5 %near_inner.1 = bf16[256,1024]{1,0:T(8,128)(2,1)S(1)} custom-call(bf16[320,1024]{1,0:T(8,128)(2,1)S(1)} %bitcast.12, bf16[320,1024]{1,0:T(8,128)(2,1)S(1)} %bitcast.14, bf16[320,1024]{1,0:T(8,128)(2,1)S(1)} %bitcast.16, bf16[336,128]{1,0:T(8,128)(2,1)S(1)} %get-tuple-element.31.own_ref, bf16[336,128]{1,0:T(8,128)(2,1)S(1)} %collective-permute-done.1._.refs_0_, ...), custom_call_target="tpu_custom_call" | custom-call | flops 8053063680 | bytes 1769472 | tf_op jit(solution)/shard_map/near_inner/pallas_call | solution.py:397
  37.1 0.1 collective-permute-start.12
  37.1 0.1 collective-permute-start.13
  37.2 0.4 collective-permute-done.10.refs_9_.refs_1_
  37.6 3.2 %collective-permute-start.14 = (bf16[336,128]{1,0:T(8,128)(2,1)S(1)}, bf16[336,128]{1,0:T(8,128)(2,1)S(1)}, u32[]{:S(2)}, u32[]{:S(2)}) collective-permute-start(bf16[336,128]{1,0:T(8,128)(2,1)S(1)} %get-tuple-element.33), channel_id=1, source_target_pairs={{0,12},{1,13},{2,14},{3,15},{4,8},{5,9},{6,10},{7,11},{8,23},{9,22... | collective-permute-start | bytes 258056 | tf_op jit(solution)/shard_map/ppermute | solution.py:340
  40.8 0.1 collective-permute-start.15
  40.9 1.0 %near_edge.1 = bf16[144,1024]{1,0:T(8,128)(2,1)S(1)} custom-call(bf16[320,1024]{1,0:T(8,128)(2,1)S(1)} %bitcast.13, bf16[320,1024]{1,0:T(8,128)(2,1)S(1)} %bitcast.15, bf16[320,1024]{1,0:T(8,128)(2,1)S(1)} %bitcast.17, bf16[2,128,1024]{2,1,0:T(8,128)(2,1)S(1)} %collective-permute-done.odd_ref, bf16[2,128,1024]{2,1,0:T(8,128)(2,1)S(1)} %collective-permute-done.2.even_ref, ...), custom_call_target="tpu_custom_call" | custom-call | flops 5368709120 | bytes 1179648 | tf_op jit(solution)/shard_map/near_edge/pallas_call | solution.py:397
  41.9 0.1 collective-permute-start.11
  42.0 1.5 %far.3 = (bf16[336,128]{1,0:T(8,128)(2,1)S(1)}, bf16[336,128]{1,0:T(8,128)(2,1)S(1)}) custom-call(s32[1]{0:T(128)} %bitcast.10.span_ref, s32[2]{0:T(128)S(1)} %bitcast.23, s32[120]{0:T(128)S(1)} %reshape_squeeze.3.random_ref, bf16[6144,128]{1,0:T(8,128)(2,1)S(1)} %bitcast.19, bf16[6144,128]{1,0:T(8,128)(2,1)S(1)} %bitcast.21, ...), custom_call_target="tpu_custom_call" | custom-call | flops 4194304000 | bytes 3473408 | tf_op jit(solution)/shard_map/far/pallas_call | solution.py:366
  43.5 2.5 %collective-permute-start.16 = (bf16[336,128]{1,0:T(8,128)(2,1)S(1)}, bf16[336,128]{1,0:T(8,128)(2,1)S(1)}, u32[]{:S(2)}, u32[]{:S(2)}) collective-permute-start(bf16[336,128]{1,0:T(8,128)(2,1)S(1)} %get-tuple-element.35), channel_id=1, source_target_pairs={{0,10},{1,11},{2,8},{3,9},{4,14},{5,15},{6,12},{7,13},{8,21},{9,20... | collective-permute-start | bytes 258056 | tf_op jit(solution)/shard_map/ppermute | solution.py:340
  46.0 4.4 %collective-permute-start.17 = (bf16[336,128]{1,0:T(8,128)(2,1)S(1)}, bf16[336,128]{1,0:T(8,128)(2,1)S(1)}, u32[]{:S(2)}, u32[]{:S(2)}) collective-permute-start(bf16[336,128]{1,0:T(8,128)(2,1)S(1)} %get-tuple-element.36), channel_id=1, source_target_pairs={{0,11},{1,10},{2,9},{3,8},{4,15},{5,14},{6,13},{7,12},{8,20},{9,21... | collective-permute-start | bytes 258056 | tf_op jit(solution)/shard_map/ppermute | solution.py:340
  50.4 0.8 %collective-permute-done.16.refs_5_ = bf16[336,128]{1,0:T(8,128)(2,1)S(1)} collective-permute-done((bf16[336,128]{1,0:T(8,128)(2,1)S(1)}, bf16[336,128]{1,0:T(8,128)(2,1)S(1)}, u32[]{:S(2)}, u32[]{:S(2)}) %collective-permute-start.16) | collective-permute-done | bytes 86048 | tf_op jit(solution)/shard_map/ppermute | solution.py:340
  51.2 3.0 %collective-permute-done.17.refs_6_ = bf16[336,128]{1,0:T(8,128)(2,1)S(1)} collective-permute-done((bf16[336,128]{1,0:T(8,128)(2,1)S(1)}, bf16[336,128]{1,0:T(8,128)(2,1)S(1)}, u32[]{:S(2)}, u32[]{:S(2)}) %collective-permute-start.17) | collective-permute-done | bytes 86048 | tf_op jit(solution)/shard_map/ppermute | solution.py:340
  54.2 1.4 %merge.1 = bf16[320,1024]{1,0:T(8,128)(2,1)} custom-call(bf16[144,1024]{1,0:T(8,128)(2,1)S(1)} %collective-permute-done.11.edge_ref, bf16[256,1024]{1,0:T(8,128)(2,1)S(1)} %collective-permute-done.12.inner_ref, bf16[336,128]{1,0:T(8,128)(2,1)S(1)} %collective-permute-done.9.refs_8_.refs_0_, bf16[336,128]{1,0:T(8,128)(2,1)S(1)} %collective-permute-done.10.refs_9_.refs_1_, ...), custom_call_target="tpu_custom_call" | custom-call | bytes 1966080 | tf_op jit(solution)/shard_map/merge/pallas_call | solution.py:427
  (34 shorter events, 0.1 us)
Async XLA Ops:
  0.0 12.7 %copy-start.7 = (s32[1,40,3]{1,0,2:T(1,128)S(1)}, s32[1,40,3]{1,0,2:T(1,128)}, u32[]{:S(2)}) copy-start(s32[1,40,3]{1,0,2:T(1,128)} %param.15) | copy-start | bytes 1444
  0.7 1.1 %copy-start = (bf16[1,320,1024]{2,1,0:T(8,128)(2,1)S(1)}, bf16[1,320,1024]{2,1,0:T(8,128)(2,1)}, u32[]{:S(2)}) copy-start(bf16[1,320,1024]{2,1,0:T(8,128)(2,1)} %param.8) | copy-start | bytes 1966084
  1.8 11.2 %slice-start = ((bf16[1,320,1024]{2,1,0:T(8,128)(2,1)}), bf16[1,128,1024]{2,1,0:T(8,128)(2,1)S(1)}, s32[]{:S(2)}) async-start(bf16[1,320,1024]{2,1,0:T(8,128)(2,1)} %param.9), calls=%async_computation | async-start | bytes 524288 | tf_op jit(solution)/shard_map/slice | solution.py:342
  1.8 11.2 %slice-start.1 = ((bf16[1,320,1024]{2,1,0:T(8,128)(2,1)}), bf16[1,128,1024]{2,1,0:T(8,128)(2,1)S(1)}, s32[]{:S(2)}) async-start(bf16[1,320,1024]{2,1,0:T(8,128)(2,1)} %param.10), calls=%async_computation.1 | async-start | bytes 524288 | tf_op jit(solution)/shard_map/slice | solution.py:342
  2.0 11.0 %collective-permute-start.1 = (bf16[336,128]{1,0:T(8,128)(2,1)S(1)}, bf16[336,128]{1,0:T(8,128)(2,1)S(1)}, u32[]{:S(2)}, u32[]{:S(2)}) collective-permute-start(bf16[336,128]{1,0:T(8,128)(2,1)S(1)} %get-tuple-element.21), channel_id=1, source_target_pairs={{0,7},{1,6},{2,5},{3,4},{4,3},{5,2},{6,1},{7,0},{8,9},{9,8},{10,11... | collective-permute-start | bytes 258056 | tf_op jit(solution)/shard_map/ppermute | solution.py:327
  8.1 5.8 %collective-permute-start.3 = (bf16[336,128]{1,0:T(8,128)(2,1)S(1)}, bf16[336,128]{1,0:T(8,128)(2,1)S(1)}, u32[]{:S(2)}, u32[]{:S(2)}) collective-permute-start(bf16[336,128]{1,0:T(8,128)(2,1)S(1)} %get-tuple-element.22), channel_id=1, source_target_pairs={{0,1},{1,0},{2,3},{3,2},{4,5},{5,4},{6,7},{7,6},{8,10},{9,11},{10,... | collective-permute-start | bytes 258056 | tf_op jit(solution)/shard_map/ppermute | solution.py:327
  8.6 6.6 %collective-permute-start.4 = (bf16[336,128]{1,0:T(8,128)(2,1)S(1)}, bf16[336,128]{1,0:T(8,128)(2,1)S(1)}, u32[]{:S(2)}, u32[]{:S(2)}) collective-permute-start(bf16[336,128]{1,0:T(8,128)(2,1)S(1)} %get-tuple-element.23), channel_id=1, source_target_pairs={{0,6},{1,7},{2,4},{3,5},{4,2},{5,3},{6,0},{7,1},{8,11},{9,10},{10,... | collective-permute-start | bytes 258056 | tf_op jit(solution)/shard_map/ppermute | solution.py:327
  8.8 12.1 %collective-permute-start.5 = (bf16[336,128]{1,0:T(8,128)(2,1)S(1)}, bf16[336,128]{1,0:T(8,128)(2,1)S(1)}, u32[]{:S(2)}, u32[]{:S(2)}) collective-permute-start(bf16[336,128]{1,0:T(8,128)(2,1)S(1)} %get-tuple-element.24), channel_id=1, source_target_pairs={{0,5},{1,4},{2,7},{3,6},{4,1},{5,0},{6,3},{7,2},{8,15},{9,14},{10,... | collective-permute-start | bytes 258056 | tf_op jit(solution)/shard_map/ppermute | solution.py:327
  10.6 14.6 %copy-start.4 = (bf16[1,6144,128]{2,1,0:T(8,128)(2,1)S(1)}, bf16[1,6144,128]{2,1,0:T(8,128)(2,1)}, u32[]{:S(2)}) copy-start(bf16[1,6144,128]{2,1,0:T(8,128)(2,1)} %param.11) | copy-start | bytes 4718596
  10.6 14.6 %copy-start.6 = (s32[1,2]{1,0:T(1,128)S(1)}, s32[1,2]{1,0:T(1,128)}, u32[]{:S(2)}) copy-start(s32[1,2]{1,0:T(1,128)} %param.14) | copy-start | bytes 28
  10.6 14.5 %collective-permute-start.6 = (bf16[336,128]{1,0:T(8,128)(2,1)S(1)}, bf16[336,128]{1,0:T(8,128)(2,1)S(1)}, u32[]{:S(2)}, u32[]{:S(2)}) collective-permute-start(bf16[336,128]{1,0:T(8,128)(2,1)S(1)} %get-tuple-element.25), channel_id=1, source_target_pairs={{0,4},{1,5},{2,6},{3,7},{4,0},{5,1},{6,2},{7,3},{8,14},{9,15},{10,... | collective-permute-start | bytes 258056 | tf_op jit(solution)/shard_map/ppermute | solution.py:327
  13.0 12.2 %copy-start.5 = (bf16[1,6144,128]{2,1,0:T(8,128)(2,1)S(1)}, bf16[1,6144,128]{2,1,0:T(8,128)(2,1)}, u32[]{:S(2)}) copy-start(bf16[1,6144,128]{2,1,0:T(8,128)(2,1)} %param.12) | copy-start | bytes 4718596
  13.0 27.8 %collective-permute-start = (bf16[2,128,1024]{2,1,0:T(8,128)(2,1)S(1)}, bf16[2,128,1024]{2,1,0:T(8,128)(2,1)S(1)}, u32[]{:S(2)}, u32[]{:S(2)}) collective-permute-start(bf16[2,128,1024]{2,1,0:T(8,128)(2,1)S(1)} %pad_maximum_fusion.rows_ref), channel_id=1, source_target_pairs={{8,9},{9,10},{10,11},{11,12},{12,13},{13,14},{14,15},{24,25},{25,2... | collective-permute-start | bytes 1572872 | tf_op jit(solution)/shard_map/ppermute | solution.py:358
  13.9 14.6 %collective-permute-start.7 = (bf16[336,128]{1,0:T(8,128)(2,1)S(1)}, bf16[336,128]{1,0:T(8,128)(2,1)S(1)}, u32[]{:S(2)}, u32[]{:S(2)}) collective-permute-start(bf16[336,128]{1,0:T(8,128)(2,1)S(1)} %get-tuple-element.26), channel_id=1, source_target_pairs={{0,2},{1,3},{2,0},{3,1},{4,6},{5,7},{6,4},{7,5},{8,13},{9,12},{10,... | collective-permute-start | bytes 258056 | tf_op jit(solution)/shard_map/ppermute | solution.py:327
  15.2 20.3 %collective-permute-start.8 = (bf16[336,128]{1,0:T(8,128)(2,1)S(1)}, bf16[336,128]{1,0:T(8,128)(2,1)S(1)}, u32[]{:S(2)}, u32[]{:S(2)}) collective-permute-start(bf16[336,128]{1,0:T(8,128)(2,1)S(1)} %get-tuple-element.27), channel_id=1, source_target_pairs={{0,3},{1,2},{2,1},{3,0},{4,7},{5,6},{6,5},{7,4},{8,12},{9,13},{10,... | collective-permute-start | bytes 258056 | tf_op jit(solution)/shard_map/ppermute | solution.py:327
  20.8 20.1 %collective-permute-start.2 = (bf16[2,128,1024]{2,1,0:T(8,128)(2,1)S(1)}, bf16[2,128,1024]{2,1,0:T(8,128)(2,1)S(1)}, u32[]{:S(2)}, u32[]{:S(2)}) collective-permute-start(bf16[2,128,1024]{2,1,0:T(8,128)(2,1)S(1)} %halo.1), channel_id=1, source_target_pairs={{0,1},{1,2},{2,3},{3,4},{4,5},{5,6},{6,7},{16,17},{17,18},{18,19},... | collective-permute-start | bytes 1572872 | tf_op jit(solution)/shard_map/ppermute | solution.py:358
  25.2 10.4 %copy-start.1 = (bf16[1,320,1024]{2,1,0:T(8,128)(2,1)S(1)}, bf16[1,320,1024]{2,1,0:T(8,128)(2,1)}, u32[]{:S(2)}) copy-start(bf16[1,320,1024]{2,1,0:T(8,128)(2,1)} %param.8) | copy-start | bytes 1966084
  25.2 10.3 %copy-start.2 = (bf16[1,320,1024]{2,1,0:T(8,128)(2,1)S(1)}, bf16[1,320,1024]{2,1,0:T(8,128)(2,1)}, u32[]{:S(2)}) copy-start(bf16[1,320,1024]{2,1,0:T(8,128)(2,1)} %param.9) | copy-start | bytes 1966084
  25.2 10.3 %copy-start.3 = (bf16[1,320,1024]{2,1,0:T(8,128)(2,1)S(1)}, bf16[1,320,1024]{2,1,0:T(8,128)(2,1)}, u32[]{:S(2)}) copy-start(bf16[1,320,1024]{2,1,0:T(8,128)(2,1)} %param.10) | copy-start | bytes 1966084
  28.4 8.7 %collective-permute-start.9 = (bf16[336,128]{1,0:T(8,128)(2,1)S(1)}, bf16[336,128]{1,0:T(8,128)(2,1)S(1)}, u32[]{:S(2)}, u32[]{:S(2)}) collective-permute-start(bf16[336,128]{1,0:T(8,128)(2,1)S(1)} %get-tuple-element.29), channel_id=1, source_target_pairs={{0,15},{1,14},{2,13},{3,12},{4,11},{5,10},{6,9},{7,8},{8,17},{9,16... | collective-permute-start | bytes 258056 | tf_op jit(solution)/shard_map/ppermute | solution.py:340
  28.5 9.1 %collective-permute-start.10 = (bf16[336,128]{1,0:T(8,128)(2,1)S(1)}, bf16[336,128]{1,0:T(8,128)(2,1)S(1)}, u32[]{:S(2)}, u32[]{:S(2)}) collective-permute-start(bf16[336,128]{1,0:T(8,128)(2,1)S(1)} %get-tuple-element.30), channel_id=1, source_target_pairs={{0,14},{1,15},{2,12},{3,13},{4,10},{5,11},{6,8},{7,9},{8,18},{9,19... | collective-permute-start | bytes 258056 | tf_op jit(solution)/shard_map/ppermute | solution.py:340
  37.1 17.1 %collective-permute-start.12 = (bf16[256,1024]{1,0:T(8,128)(2,1)S(1)}, bf16[256,1024]{1,0:T(8,128)(2,1)S(1)}, u32[]{:S(2)}, u32[]{:S(2)}) collective-permute-start(bf16[256,1024]{1,0:T(8,128)(2,1)S(1)} %near_inner.1), channel_id=1, source_target_pairs={{0,8},{1,9},{2,10},{3,11},{4,12},{5,13},{6,14},{7,15},{8,16},{9,17... | collective-permute-start | bytes 1572872 | tf_op jit(solution)/shard_map/ppermute | solution.py:340
  37.1 6.4 %collective-permute-start.13 = (bf16[336,128]{1,0:T(8,128)(2,1)S(1)}, bf16[336,128]{1,0:T(8,128)(2,1)S(1)}, u32[]{:S(2)}, u32[]{:S(2)}) collective-permute-start(bf16[336,128]{1,0:T(8,128)(2,1)S(1)} %get-tuple-element.32), channel_id=1, source_target_pairs={{0,13},{1,12},{2,15},{3,14},{4,9},{5,8},{6,11},{7,10},{8,19},{9,18... | collective-permute-start | bytes 258056 | tf_op jit(solution)/shard_map/ppermute | solution.py:340
  37.6 8.4 %collective-permute-start.14 = (bf16[336,128]{1,0:T(8,128)(2,1)S(1)}, bf16[336,128]{1,0:T(8,128)(2,1)S(1)}, u32[]{:S(2)}, u32[]{:S(2)}) collective-permute-start(bf16[336,128]{1,0:T(8,128)(2,1)S(1)} %get-tuple-element.33), channel_id=1, source_target_pairs={{0,12},{1,13},{2,14},{3,15},{4,8},{5,9},{6,10},{7,11},{8,23},{9,22... | collective-permute-start | bytes 258056 | tf_op jit(solution)/shard_map/ppermute | solution.py:340
  40.8 9.6 %collective-permute-start.15 = (bf16[336,128]{1,0:T(8,128)(2,1)S(1)}, bf16[336,128]{1,0:T(8,128)(2,1)S(1)}, u32[]{:S(2)}, u32[]{:S(2)}) collective-permute-start(bf16[336,128]{1,0:T(8,128)(2,1)S(1)} %get-tuple-element.34), channel_id=1, source_target_pairs={{0,9},{1,8},{2,11},{3,10},{4,13},{5,12},{6,15},{7,14},{8,22},{9,23... | collective-permute-start | bytes 258056 | tf_op jit(solution)/shard_map/ppermute | solution.py:340
  41.9 12.2 %collective-permute-start.11 = (bf16[144,1024]{1,0:T(8,128)(2,1)S(1)}, bf16[144,1024]{1,0:T(8,128)(2,1)S(1)}, u32[]{:S(2)}, u32[]{:S(2)}) collective-permute-start(bf16[144,1024]{1,0:T(8,128)(2,1)S(1)} %near_edge.1), channel_id=1, source_target_pairs={{0,8},{1,9},{2,10},{3,11},{4,12},{5,13},{6,14},{7,15},{8,16},{9,17... | collective-permute-start | bytes 884744 | tf_op jit(solution)/shard_map/ppermute | solution.py:340
  43.5 7.7 %collective-permute-start.16 = (bf16[336,128]{1,0:T(8,128)(2,1)S(1)}, bf16[336,128]{1,0:T(8,128)(2,1)S(1)}, u32[]{:S(2)}, u32[]{:S(2)}) collective-permute-start(bf16[336,128]{1,0:T(8,128)(2,1)S(1)} %get-tuple-element.35), channel_id=1, source_target_pairs={{0,10},{1,11},{2,8},{3,9},{4,14},{5,15},{6,12},{7,13},{8,21},{9,20... | collective-permute-start | bytes 258056 | tf_op jit(solution)/shard_map/ppermute | solution.py:340
  46.0 8.2 %collective-permute-start.17 = (bf16[336,128]{1,0:T(8,128)(2,1)S(1)}, bf16[336,128]{1,0:T(8,128)(2,1)S(1)}, u32[]{:S(2)}, u32[]{:S(2)}) collective-permute-start(bf16[336,128]{1,0:T(8,128)(2,1)S(1)} %get-tuple-element.36), channel_id=1, source_target_pairs={{0,11},{1,10},{2,9},{3,8},{4,15},{5,14},{6,13},{7,12},{8,20},{9,21... | collective-permute-start | bytes 258056 | tf_op jit(solution)/shard_map/ppermute | solution.py:340

commit v16 on v13

--- a/solution.py
+++ b/solution.py
@@ -286,7 +286,7 @@
     bf16 = jnp.bfloat16
     half = max(seq_count // 2, 1)
     inner, outer = list(range(1, half)), list(range(seq_count - 1, half - 1, -1))
-    there = [outer[:1] + inner[:1] + outer[1:] + inner[1:] + [0], inner + outer + [0]]
+    there = [outer + inner + [0], inner + outer + [0]]
 
     chunk_shape = jax.ShapeDtypeStruct((rows + STAT_ROWS, HD), bf16)
     chunk_shape = jax.ShapeDtypeStruct((rows + STAT_ROWS, HD), bf16)
@@ -301,19 +301,6 @@
         name="split",
     )(window[0], queries[0])
 
-    def linked(shard, by, steps):
-        pairs = [
-            (
-                s * seq_count + t,
-                (s + by) % section_count * seq_count + (t ^ steps[s % 2]),
-            )
-            for s in range(section_count)
-            for t in range(seq_count)
-        ]
-        return lax.ppermute(shard, ("section", "seq"), pairs)
-
-    came = [linked(shard, 0, steps) for shard, steps in zip(sent[:-1], zip(*there))]
-    came.append(sent[-1])
     def linked(shard, by, steps):
         pairs = [
             (
@@ -405,7 +392,7 @@
     )
     edge_part = near_call(
         near_edge_kernel, "near_edge", halo, halo + STAT_ROWS,
-        2 + seq_count, [pltpu.VMEM(tails.shape, bf16)], *halos, *came, *handed[:2],
+        2 + seq_count, [pltpu.VMEM(tails.shape, bf16)], *halos, *came, *handed[:1],
     )
     handed_inner = linked(inner_part, 1, [0, 0])
     handed_edge = linked(edge_part, 1, [0, 0])

time: 55.4 us -> 56.3 us (1.016)
  waiting for transfers between devices: 9.35 us -> 12.4 us
  starting transfers between devices: 34.6 us -> 32.5 us
    ppermute x16, waiting for transfers between devices: 9.35 us -> 12.4 us  [linked(): return lax.ppermute(shard, ('section', 'seq'), pairs)]
    ppermute x2, starting transfers between devices: 5.12 us -> 3.06 us  [halo_from(): return lax.ppermute(mine, ('section', 'seq'), pairs)]
  transfers between devices with their start and end apart: 18 -> 18, of which waited for: 4 -> 6; matrix products, arithmetic and copies ran while one was open for 0% -> 0% of each run, Pallas kernels for 13% -> 13%
where the time goes in v16:
time: 56.3 us; the launch traced here: 56.1 us
  starting transfers between devices  32.5 us (58%)
  waiting for transfers between devices  12.4 us (22%)
  Pallas kernels  8.9 us (16%)
  local copies, waits for them, and re-layouts  1.33 us (2%)
  between operations  0.9 us (2%)
    ppermute x16, starting transfers between devices, linked(): return lax.ppermute(shard, ('section', 'seq'), pairs)  29.4 us
    ppermute x16, waiting for transfers between devices, linked(): return lax.ppermute(shard, ('section', 'seq'), pairs)  12.4 us
    pallas_call x2, Pallas kernels, far_call(): pl.pallas_call(functools.partial(far_kernel, there, chosen), out_shape=[c...  4.7 us
    ppermute x2, starting transfers between devices, halo_from(): return lax.ppermute(mine, ('section', 'seq'), pairs)  3.06 us
    pallas_call x2, Pallas kernels, near_call(): pl.pallas_call(functools.partial(kernel, there), out_shape=jax.ShapeDtype...  2.53 us
    pallas_call x1, Pallas kernels, per_device(): pl.pallas_call(functools.partial(merge_kernel, there), out_shape=jax.Shap...  1.37 us
    unnamed x17, local copies, waits for them, and re-layouts  1.21 us
  transfers between devices with their start and end apart: 18, of which 6 were waited for; matrix products, arithmetic and copies ran while one was open for 0% of the time, Pallas kernels for 13%

profile of v16, /device:TPU:0, one launch (start us, length us, event | category | flops | bytes accessed | tf_op | source)
XLA Modules:
  0.0 56.1 jit_solution(10782200363230917487)
XLA Ops:
  0.7 0.0 copy-start
  0.7 1.1 %copy-done = bf16[1,320,1024]{2,1,0:T(8,128)(2,1)S(1)} copy-done((bf16[1,320,1024]{2,1,0:T(8,128)(2,1)S(1)}, bf16[1,320,1024]{2,1,0:T(8,128)(2,1)}, u32[]{:S(2)}) %copy-start) | copy-done | bytes 655384
  1.8 0.3 split.1
  2.0 6.1 %collective-permute-start.1 = (bf16[336,128]{1,0:T(8,128)(2,1)S(1)}, bf16[336,128]{1,0:T(8,128)(2,1)S(1)}, u32[]{:S(2)}, u32[]{:S(2)}) collective-permute-start(bf16[336,128]{1,0:T(8,128)(2,1)S(1)} %get-tuple-element.21), channel_id=1, source_target_pairs={{0,7},{1,6},{2,5},{3,4},{4,3},{5,2},{6,1},{7,0},{8,9},{9,8},{10,11... | collective-permute-start | bytes 258056 | tf_op jit(solution)/shard_map/ppermute | solution.py:313
  8.1 0.2 collective-permute-start.3
  8.3 0.7 %collective-permute-start.4 = (bf16[336,128]{1,0:T(8,128)(2,1)S(1)}, bf16[336,128]{1,0:T(8,128)(2,1)S(1)}, u32[]{:S(2)}, u32[]{:S(2)}) collective-permute-start(bf16[336,128]{1,0:T(8,128)(2,1)S(1)} %get-tuple-element.23), channel_id=1, source_target_pairs={{0,5},{1,4},{2,7},{3,6},{4,1},{5,0},{6,3},{7,2},{8,11},{9,10},{10,... | collective-permute-start | bytes 258056 | tf_op jit(solution)/shard_map/ppermute | solution.py:313
  9.1 2.0 %collective-permute-start.5 = (bf16[336,128]{1,0:T(8,128)(2,1)S(1)}, bf16[336,128]{1,0:T(8,128)(2,1)S(1)}, u32[]{:S(2)}, u32[]{:S(2)}) collective-permute-start(bf16[336,128]{1,0:T(8,128)(2,1)S(1)} %get-tuple-element.24), channel_id=1, source_target_pairs={{0,4},{1,5},{2,6},{3,7},{4,0},{5,1},{6,2},{7,3},{8,15},{9,14},{10,... | collective-permute-start | bytes 258056 | tf_op jit(solution)/shard_map/ppermute | solution.py:313
  11.1 1.6 %collective-permute-start.6 = (bf16[336,128]{1,0:T(8,128)(2,1)S(1)}, bf16[336,128]{1,0:T(8,128)(2,1)S(1)}, u32[]{:S(2)}, u32[]{:S(2)}) collective-permute-start(bf16[336,128]{1,0:T(8,128)(2,1)S(1)} %get-tuple-element.25), channel_id=1, source_target_pairs={{0,1},{1,0},{2,3},{3,2},{4,5},{5,4},{6,7},{7,6},{8,14},{9,15},{10,... | collective-permute-start | bytes 258056 | tf_op jit(solution)/shard_map/ppermute | solution.py:313
  12.7 0.1 copy.10
  12.8 0.1 reshape_squeeze.3.random_ref
  13.0 0.1 pad_maximum_fusion.rows_ref
  13.0 0.8 %collective-permute-start = (bf16[2,128,1024]{2,1,0:T(8,128)(2,1)S(1)}, bf16[2,128,1024]{2,1,0:T(8,128)(2,1)S(1)}, u32[]{:S(2)}, u32[]{:S(2)}) collective-permute-start(bf16[2,128,1024]{2,1,0:T(8,128)(2,1)S(1)} %pad_maximum_fusion.rows_ref), channel_id=1, source_target_pairs={{8,9},{9,10},{10,11},{11,12},{12,13},{13,14},{14,15},{24,25},{25,2... | collective-permute-start | bytes 1572872 | tf_op jit(solution)/shard_map/ppermute | solution.py:333
  13.9 0.6 %collective-permute-done.3.refs_1_ = bf16[336,128]{1,0:T(8,128)(2,1)S(1)} collective-permute-done((bf16[336,128]{1,0:T(8,128)(2,1)S(1)}, bf16[336,128]{1,0:T(8,128)(2,1)S(1)}, u32[]{:S(2)}, u32[]{:S(2)}) %collective-permute-start.3) | collective-permute-done | bytes 86048 | tf_op jit(solution)/shard_map/ppermute | solution.py:313
  14.5 3.7 %collective-permute-start.7 = (bf16[336,128]{1,0:T(8,128)(2,1)S(1)}, bf16[336,128]{1,0:T(8,128)(2,1)S(1)}, u32[]{:S(2)}, u32[]{:S(2)}) collective-permute-start(bf16[336,128]{1,0:T(8,128)(2,1)S(1)} %get-tuple-element.26), channel_id=1, source_target_pairs={{0,2},{1,3},{2,0},{3,1},{4,6},{5,7},{6,4},{7,5},{8,13},{9,12},{10,... | collective-permute-start | bytes 258056 | tf_op jit(solution)/shard_map/ppermute | solution.py:313
  18.2 2.2 %collective-permute-done.4.refs_2_ = bf16[336,128]{1,0:T(8,128)(2,1)S(1)} collective-permute-done((bf16[336,128]{1,0:T(8,128)(2,1)S(1)}, bf16[336,128]{1,0:T(8,128)(2,1)S(1)}, u32[]{:S(2)}, u32[]{:S(2)}) %collective-permute-start.4) | collective-permute-done | bytes 86048 | tf_op jit(solution)/shard_map/ppermute | solution.py:313
  20.3 2.9 %collective-permute-done.5.refs_3_ = bf16[336,128]{1,0:T(8,128)(2,1)S(1)} collective-permute-done((bf16[336,128]{1,0:T(8,128)(2,1)S(1)}, bf16[336,128]{1,0:T(8,128)(2,1)S(1)}, u32[]{:S(2)}, u32[]{:S(2)}) %collective-permute-start.5) | collective-permute-done | bytes 86048 | tf_op jit(solution)/shard_map/ppermute | solution.py:313
  23.2 2.2 %collective-permute-start.2 = (bf16[2,128,1024]{2,1,0:T(8,128)(2,1)S(1)}, bf16[2,128,1024]{2,1,0:T(8,128)(2,1)S(1)}, u32[]{:S(2)}, u32[]{:S(2)}) collective-permute-start(bf16[2,128,1024]{2,1,0:T(8,128)(2,1)S(1)} %halo.1), channel_id=1, source_target_pairs={{0,1},{1,2},{2,3},{3,4},{4,5},{5,6},{6,7},{16,17},{17,18},{18,19},... | collective-permute-start | bytes 1572872 | tf_op jit(solution)/shard_map/ppermute | solution.py:333
  25.6 3.2 %far.2 = (bf16[336,128]{1,0:T(8,128)(2,1)S(1)}, bf16[336,128]{1,0:T(8,128)(2,1)S(1)}, bf16[336,128]{1,0:T(8,128)(2,1)S(1)}, bf16[336,128]{1,0:T(8,128)(2,1)S(1)}...) custom-call(s32[1]{0:T(128)} %bitcast.9.span_ref, s32[2]{0:T(128)S(1)} %bitcast.22, ...), custom_call_target="tpu_custom_call" | custom-call | flops 12582912000 | bytes 4128768 | tf_op jit(solution)/shard_map/far/pallas_call | solution.py:340
  28.8 0.1 collective-permute-start.9
  28.9 1.5 %near_inner.1 = bf16[256,1024]{1,0:T(8,128)(2,1)S(1)} custom-call(bf16[320,1024]{1,0:T(8,128)(2,1)S(1)} %bitcast.12, bf16[320,1024]{1,0:T(8,128)(2,1)S(1)} %bitcast.14, bf16[320,1024]{1,0:T(8,128)(2,1)S(1)} %bitcast.16, bf16[336,128]{1,0:T(8,128)(2,1)S(1)} %get-tuple-element.30.own_ref, bf16[336,128]{1,0:T(8,128)(2,1)S(1)} %collective-permute-done.1._.refs_0_, ...), custom_call_target="tpu_custom_call" | custom-call | flops 8053063680 | bytes 1769472 | tf_op jit(solution)/shard_map/near_inner/pallas_call | solution.py:370
  30.4 3.3 %collective-permute-start.11 = (bf16[256,1024]{1,0:T(8,128)(2,1)S(1)}, bf16[256,1024]{1,0:T(8,128)(2,1)S(1)}, u32[]{:S(2)}, u32[]{:S(2)}) collective-permute-start(bf16[256,1024]{1,0:T(8,128)(2,1)S(1)} %near_inner.1), channel_id=1, source_target_pairs={{0,8},{1,9},{2,10},{3,11},{4,12},{5,13},{6,14},{7,15},{8,16},{9,17... | collective-permute-start | bytes 1572872 | tf_op jit(solution)/shard_map/ppermute | solution.py:313
  33.7 2.8 %collective-permute-start.13 = (bf16[336,128]{1,0:T(8,128)(2,1)S(1)}, bf16[336,128]{1,0:T(8,128)(2,1)S(1)}, u32[]{:S(2)}, u32[]{:S(2)}) collective-permute-start(bf16[336,128]{1,0:T(8,128)(2,1)S(1)} %get-tuple-element.32), channel_id=1, source_target_pairs={{0,13},{1,12},{2,15},{3,14},{4,9},{5,8},{6,11},{7,10},{8,19},{9,18... | collective-permute-start | bytes 258056 | tf_op jit(solution)/shard_map/ppermute | solution.py:313
  36.4 1.1 %collective-permute-start.14 = (bf16[336,128]{1,0:T(8,128)(2,1)S(1)}, bf16[336,128]{1,0:T(8,128)(2,1)S(1)}, u32[]{:S(2)}, u32[]{:S(2)}) collective-permute-start(bf16[336,128]{1,0:T(8,128)(2,1)S(1)} %get-tuple-element.33), channel_id=1, source_target_pairs={{0,12},{1,13},{2,14},{3,15},{4,8},{5,9},{6,10},{7,11},{8,23},{9,22... | collective-permute-start | bytes 258056 | tf_op jit(solution)/shard_map/ppermute | solution.py:313
  37.5 1.0 %near_edge.1 = bf16[144,1024]{1,0:T(8,128)(2,1)S(1)} custom-call(bf16[320,1024]{1,0:T(8,128)(2,1)S(1)} %bitcast.13, bf16[320,1024]{1,0:T(8,128)(2,1)S(1)} %bitcast.15, bf16[320,1024]{1,0:T(8,128)(2,1)S(1)} %bitcast.17, bf16[2,128,1024]{2,1,0:T(8,128)(2,1)S(1)} %collective-permute-done.odd_ref, bf16[2,128,1024]{2,1,0:T(8,128)(2,1)S(1)} %collective-permute-done.2.even_ref, ...), custom_call_target="tpu_custom_call" | custom-call | flops 5368709120 | bytes 1179648 | tf_op jit(solution)/shard_map/near_edge/pallas_call | solution.py:370
  38.6 2.5 %collective-permute-start.10 = (bf16[144,1024]{1,0:T(8,128)(2,1)S(1)}, bf16[144,1024]{1,0:T(8,128)(2,1)S(1)}, u32[]{:S(2)}, u32[]{:S(2)}) collective-permute-start(bf16[144,1024]{1,0:T(8,128)(2,1)S(1)} %near_edge.1), channel_id=1, source_target_pairs={{0,8},{1,9},{2,10},{3,11},{4,12},{5,13},{6,14},{7,15},{8,16},{9,17... | collective-permute-start | bytes 884744 | tf_op jit(solution)/shard_map/ppermute | solution.py:313
  41.1 1.5 %far.3 = (bf16[336,128]{1,0:T(8,128)(2,1)S(1)}, bf16[336,128]{1,0:T(8,128)(2,1)S(1)}) custom-call(s32[1]{0:T(128)} %bitcast.10.span_ref, s32[2]{0:T(128)S(1)} %bitcast.23, s32[120]{0:T(128)S(1)} %reshape_squeeze.3.random_ref, bf16[6144,128]{1,0:T(8,128)(2,1)S(1)} %bitcast.19, bf16[6144,128]{1,0:T(8,128)(2,1)S(1)} %bitcast.21, ...), custom_call_target="tpu_custom_call" | custom-call | flops 4194304000 | bytes 3473408 | tf_op jit(solution)/shard_map/far/pallas_call | solution.py:340
  42.6 0.5 collective-permute-start.15
  43.1 4.9 %collective-permute-start.16 = (bf16[336,128]{1,0:T(8,128)(2,1)S(1)}, bf16[336,128]{1,0:T(8,128)(2,1)S(1)}, u32[]{:S(2)}, u32[]{:S(2)}) collective-permute-start(bf16[336,128]{1,0:T(8,128)(2,1)S(1)} %get-tuple-element.35), channel_id=1, source_target_pairs={{0,10},{1,11},{2,8},{3,9},{4,14},{5,15},{6,12},{7,13},{8,21},{9,20... | collective-permute-start | bytes 258056 | tf_op jit(solution)/shard_map/ppermute | solution.py:313
  48.0 1.4 %collective-permute-done.15.refs_4_ = bf16[336,128]{1,0:T(8,128)(2,1)S(1)} collective-permute-done((bf16[336,128]{1,0:T(8,128)(2,1)S(1)}, bf16[336,128]{1,0:T(8,128)(2,1)S(1)}, u32[]{:S(2)}, u32[]{:S(2)}) %collective-permute-start.15) | collective-permute-done | bytes 86048 | tf_op jit(solution)/shard_map/ppermute | solution.py:313
  49.4 1.3 %collective-permute-done.16.refs_5_ = bf16[336,128]{1,0:T(8,128)(2,1)S(1)} collective-permute-done((bf16[336,128]{1,0:T(8,128)(2,1)S(1)}, bf16[336,128]{1,0:T(8,128)(2,1)S(1)}, u32[]{:S(2)}, u32[]{:S(2)}) %collective-permute-start.16) | collective-permute-done | bytes 86048 | tf_op jit(solution)/shard_map/ppermute | solution.py:313
  50.7 4.1 %collective-permute-done.17.refs_6_ = bf16[336,128]{1,0:T(8,128)(2,1)S(1)} collective-permute-done((bf16[336,128]{1,0:T(8,128)(2,1)S(1)}, bf16[336,128]{1,0:T(8,128)(2,1)S(1)}, u32[]{:S(2)}, u32[]{:S(2)}) %collective-permute-start.17) | collective-permute-done | bytes 86048 | tf_op jit(solution)/shard_map/ppermute | solution.py:313
  54.7 1.4 %merge.1 = bf16[320,1024]{1,0:T(8,128)(2,1)} custom-call(bf16[144,1024]{1,0:T(8,128)(2,1)S(1)} %collective-permute-done.10.edge_ref, bf16[256,1024]{1,0:T(8,128)(2,1)S(1)} %collective-permute-done.11.inner_ref, bf16[336,128]{1,0:T(8,128)(2,1)S(1)} %collective-permute-done.9.refs_8_.refs_0_, bf16[336,128]{1,0:T(8,128)(2,1)S(1)} %collective-permute-done.12.refs_1_, ...), custom_call_target="tpu_custom_call" | custom-call | bytes 1966080 | tf_op jit(solution)/shard_map/merge/pallas_call | solution.py:400
  (34 shorter events, 0.1 us)
Async XLA Ops:
  0.0 12.7 %copy-start.7 = (s32[1,40,3]{1,0,2:T(1,128)S(1)}, s32[1,40,3]{1,0,2:T(1,128)}, u32[]{:S(2)}) copy-start(s32[1,40,3]{1,0,2:T(1,128)} %param.15) | copy-start | bytes 1444
  0.7 1.1 %copy-start = (bf16[1,320,1024]{2,1,0:T(8,128)(2,1)S(1)}, bf16[1,320,1024]{2,1,0:T(8,128)(2,1)}, u32[]{:S(2)}) copy-start(bf16[1,320,1024]{2,1,0:T(8,128)(2,1)} %param.8) | copy-start | bytes 1966084
  1.8 11.2 %slice-start = ((bf16[1,320,1024]{2,1,0:T(8,128)(2,1)}), bf16[1,128,1024]{2,1,0:T(8,128)(2,1)S(1)}, s32[]{:S(2)}) async-start(bf16[1,320,1024]{2,1,0:T(8,128)(2,1)} %param.9), calls=%async_computation | async-start | bytes 524288 | tf_op jit(solution)/shard_map/slice | solution.py:317
  1.8 11.2 %slice-start.1 = ((bf16[1,320,1024]{2,1,0:T(8,128)(2,1)}), bf16[1,128,1024]{2,1,0:T(8,128)(2,1)S(1)}, s32[]{:S(2)}) async-start(bf16[1,320,1024]{2,1,0:T(8,128)(2,1)} %param.10), calls=%async_computation.1 | async-start | bytes 524288 | tf_op jit(solution)/shard_map/slice | solution.py:317
  2.0 11.0 %collective-permute-start.1 = (bf16[336,128]{1,0:T(8,128)(2,1)S(1)}, bf16[336,128]{1,0:T(8,128)(2,1)S(1)}, u32[]{:S(2)}, u32[]{:S(2)}) collective-permute-start(bf16[336,128]{1,0:T(8,128)(2,1)S(1)} %get-tuple-element.21), channel_id=1, source_target_pairs={{0,7},{1,6},{2,5},{3,4},{4,3},{5,2},{6,1},{7,0},{8,9},{9,8},{10,11... | collective-permute-start | bytes 258056 | tf_op jit(solution)/shard_map/ppermute | solution.py:313
  8.1 6.4 %collective-permute-start.3 = (bf16[336,128]{1,0:T(8,128)(2,1)S(1)}, bf16[336,128]{1,0:T(8,128)(2,1)S(1)}, u32[]{:S(2)}, u32[]{:S(2)}) collective-permute-start(bf16[336,128]{1,0:T(8,128)(2,1)S(1)} %get-tuple-element.22), channel_id=1, source_target_pairs={{0,6},{1,7},{2,4},{3,5},{4,2},{5,3},{6,0},{7,1},{8,10},{9,11},{10,... | collective-permute-start | bytes 258056 | tf_op jit(solution)/shard_map/ppermute | solution.py:313
  8.3 12.0 %collective-permute-start.4 = (bf16[336,128]{1,0:T(8,128)(2,1)S(1)}, bf16[336,128]{1,0:T(8,128)(2,1)S(1)}, u32[]{:S(2)}, u32[]{:S(2)}) collective-permute-start(bf16[336,128]{1,0:T(8,128)(2,1)S(1)} %get-tuple-element.23), channel_id=1, source_target_pairs={{0,5},{1,4},{2,7},{3,6},{4,1},{5,0},{6,3},{7,2},{8,11},{9,10},{10,... | collective-permute-start | bytes 258056 | tf_op jit(solution)/shard_map/ppermute | solution.py:313
  9.1 14.2 %collective-permute-start.5 = (bf16[336,128]{1,0:T(8,128)(2,1)S(1)}, bf16[336,128]{1,0:T(8,128)(2,1)S(1)}, u32[]{:S(2)}, u32[]{:S(2)}) collective-permute-start(bf16[336,128]{1,0:T(8,128)(2,1)S(1)} %get-tuple-element.24), channel_id=1, source_target_pairs={{0,4},{1,5},{2,6},{3,7},{4,0},{5,1},{6,2},{7,3},{8,15},{9,14},{10,... | collective-permute-start | bytes 258056 | tf_op jit(solution)/shard_map/ppermute | solution.py:313
  11.1 14.4 %copy-start.4 = (bf16[1,6144,128]{2,1,0:T(8,128)(2,1)S(1)}, bf16[1,6144,128]{2,1,0:T(8,128)(2,1)}, u32[]{:S(2)}) copy-start(bf16[1,6144,128]{2,1,0:T(8,128)(2,1)} %param.11) | copy-start | bytes 4718596
  11.1 14.4 %copy-start.6 = (s32[1,2]{1,0:T(1,128)S(1)}, s32[1,2]{1,0:T(1,128)}, u32[]{:S(2)}) copy-start(s32[1,2]{1,0:T(1,128)} %param.14) | copy-start | bytes 28
  11.1 14.4 %collective-permute-start.6 = (bf16[336,128]{1,0:T(8,128)(2,1)S(1)}, bf16[336,128]{1,0:T(8,128)(2,1)S(1)}, u32[]{:S(2)}, u32[]{:S(2)}) collective-permute-start(bf16[336,128]{1,0:T(8,128)(2,1)S(1)} %get-tuple-element.25), channel_id=1, source_target_pairs={{0,1},{1,0},{2,3},{3,2},{4,5},{5,4},{6,7},{7,6},{8,14},{9,15},{10,... | collective-permute-start | bytes 258056 | tf_op jit(solution)/shard_map/ppermute | solution.py:313
  13.0 12.6 %copy-start.5 = (bf16[1,6144,128]{2,1,0:T(8,128)(2,1)S(1)}, bf16[1,6144,128]{2,1,0:T(8,128)(2,1)}, u32[]{:S(2)}) copy-start(bf16[1,6144,128]{2,1,0:T(8,128)(2,1)} %param.12) | copy-start | bytes 4718596
  13.0 23.4 %collective-permute-start = (bf16[2,128,1024]{2,1,0:T(8,128)(2,1)S(1)}, bf16[2,128,1024]{2,1,0:T(8,128)(2,1)S(1)}, u32[]{:S(2)}, u32[]{:S(2)}) collective-permute-start(bf16[2,128,1024]{2,1,0:T(8,128)(2,1)S(1)} %pad_maximum_fusion.rows_ref), channel_id=1, source_target_pairs={{8,9},{9,10},{10,11},{11,12},{12,13},{13,14},{14,15},{24,25},{25,2... | collective-permute-start | bytes 1572872 | tf_op jit(solution)/shard_map/ppermute | solution.py:333
  14.5 14.3 %collective-permute-start.7 = (bf16[336,128]{1,0:T(8,128)(2,1)S(1)}, bf16[336,128]{1,0:T(8,128)(2,1)S(1)}, u32[]{:S(2)}, u32[]{:S(2)}) collective-permute-start(bf16[336,128]{1,0:T(8,128)(2,1)S(1)} %get-tuple-element.26), channel_id=1, source_target_pairs={{0,2},{1,3},{2,0},{3,1},{4,6},{5,7},{6,4},{7,5},{8,13},{9,12},{10,... | collective-permute-start | bytes 258056 | tf_op jit(solution)/shard_map/ppermute | solution.py:313
  20.3 8.5 %collective-permute-start.8 = (bf16[336,128]{1,0:T(8,128)(2,1)S(1)}, bf16[336,128]{1,0:T(8,128)(2,1)S(1)}, u32[]{:S(2)}, u32[]{:S(2)}) collective-permute-start(bf16[336,128]{1,0:T(8,128)(2,1)S(1)} %get-tuple-element.27), channel_id=1, source_target_pairs={{0,3},{1,2},{2,1},{3,0},{4,7},{5,6},{6,5},{7,4},{8,12},{9,13},{10,... | collective-permute-start | bytes 258056 | tf_op jit(solution)/shard_map/ppermute | solution.py:313
  23.2 14.3 %collective-permute-start.2 = (bf16[2,128,1024]{2,1,0:T(8,128)(2,1)S(1)}, bf16[2,128,1024]{2,1,0:T(8,128)(2,1)S(1)}, u32[]{:S(2)}, u32[]{:S(2)}) collective-permute-start(bf16[2,128,1024]{2,1,0:T(8,128)(2,1)S(1)} %halo.1), channel_id=1, source_target_pairs={{0,1},{1,2},{2,3},{3,4},{4,5},{5,6},{6,7},{16,17},{17,18},{18,19},... | collective-permute-start | bytes 1572872 | tf_op jit(solution)/shard_map/ppermute | solution.py:333
  25.5 3.3 %copy-start.1 = (bf16[1,320,1024]{2,1,0:T(8,128)(2,1)S(1)}, bf16[1,320,1024]{2,1,0:T(8,128)(2,1)}, u32[]{:S(2)}) copy-start(bf16[1,320,1024]{2,1,0:T(8,128)(2,1)} %param.8) | copy-start | bytes 1966084
  25.5 3.3 %copy-start.2 = (bf16[1,320,1024]{2,1,0:T(8,128)(2,1)S(1)}, bf16[1,320,1024]{2,1,0:T(8,128)(2,1)}, u32[]{:S(2)}) copy-start(bf16[1,320,1024]{2,1,0:T(8,128)(2,1)} %param.9) | copy-start | bytes 1966084
  25.6 3.3 %copy-start.3 = (bf16[1,320,1024]{2,1,0:T(8,128)(2,1)S(1)}, bf16[1,320,1024]{2,1,0:T(8,128)(2,1)}, u32[]{:S(2)}) copy-start(bf16[1,320,1024]{2,1,0:T(8,128)(2,1)} %param.10) | copy-start | bytes 1966084
  28.8 4.9 %collective-permute-start.9 = (bf16[336,128]{1,0:T(8,128)(2,1)S(1)}, bf16[336,128]{1,0:T(8,128)(2,1)S(1)}, u32[]{:S(2)}, u32[]{:S(2)}) collective-permute-start(bf16[336,128]{1,0:T(8,128)(2,1)S(1)} %get-tuple-element.29), channel_id=1, source_target_pairs={{0,15},{1,14},{2,13},{3,12},{4,11},{5,10},{6,9},{7,8},{8,17},{9,16... | collective-permute-start | bytes 258056 | tf_op jit(solution)/shard_map/ppermute | solution.py:313
  30.4 24.3 %collective-permute-start.11 = (bf16[256,1024]{1,0:T(8,128)(2,1)S(1)}, bf16[256,1024]{1,0:T(8,128)(2,1)S(1)}, u32[]{:S(2)}, u32[]{:S(2)}) collective-permute-start(bf16[256,1024]{1,0:T(8,128)(2,1)S(1)} %near_inner.1), channel_id=1, source_target_pairs={{0,8},{1,9},{2,10},{3,11},{4,12},{5,13},{6,14},{7,15},{8,16},{9,17... | collective-permute-start | bytes 1572872 | tf_op jit(solution)/shard_map/ppermute | solution.py:313
  33.7 8.9 %collective-permute-start.12 = (bf16[336,128]{1,0:T(8,128)(2,1)S(1)}, bf16[336,128]{1,0:T(8,128)(2,1)S(1)}, u32[]{:S(2)}, u32[]{:S(2)}) collective-permute-start(bf16[336,128]{1,0:T(8,128)(2,1)S(1)} %get-tuple-element.31), channel_id=1, source_target_pairs={{0,14},{1,15},{2,12},{3,13},{4,10},{5,11},{6,8},{7,9},{8,18},{9,19... | collective-permute-start | bytes 258056 | tf_op jit(solution)/shard_map/ppermute | solution.py:313
  33.7 9.4 %collective-permute-start.13 = (bf16[336,128]{1,0:T(8,128)(2,1)S(1)}, bf16[336,128]{1,0:T(8,128)(2,1)S(1)}, u32[]{:S(2)}, u32[]{:S(2)}) collective-permute-start(bf16[336,128]{1,0:T(8,128)(2,1)S(1)} %get-tuple-element.32), channel_id=1, source_target_pairs={{0,13},{1,12},{2,15},{3,14},{4,9},{5,8},{6,11},{7,10},{8,19},{9,18... | collective-permute-start | bytes 258056 | tf_op jit(solution)/shard_map/ppermute | solution.py:313
  36.4 11.5 %collective-permute-start.14 = (bf16[336,128]{1,0:T(8,128)(2,1)S(1)}, bf16[336,128]{1,0:T(8,128)(2,1)S(1)}, u32[]{:S(2)}, u32[]{:S(2)}) collective-permute-start(bf16[336,128]{1,0:T(8,128)(2,1)S(1)} %get-tuple-element.33), channel_id=1, source_target_pairs={{0,12},{1,13},{2,14},{3,15},{4,8},{5,9},{6,10},{7,11},{8,23},{9,22... | collective-permute-start | bytes 258056 | tf_op jit(solution)/shard_map/ppermute | solution.py:313
  38.6 16.2 %collective-permute-start.10 = (bf16[144,1024]{1,0:T(8,128)(2,1)S(1)}, bf16[144,1024]{1,0:T(8,128)(2,1)S(1)}, u32[]{:S(2)}, u32[]{:S(2)}) collective-permute-start(bf16[144,1024]{1,0:T(8,128)(2,1)S(1)} %near_edge.1), channel_id=1, source_target_pairs={{0,8},{1,9},{2,10},{3,11},{4,12},{5,13},{6,14},{7,15},{8,16},{9,17... | collective-permute-start | bytes 884744 | tf_op jit(solution)/shard_map/ppermute | solution.py:313
  42.6 6.7 %collective-permute-start.15 = (bf16[336,128]{1,0:T(8,128)(2,1)S(1)}, bf16[336,128]{1,0:T(8,128)(2,1)S(1)}, u32[]{:S(2)}, u32[]{:S(2)}) collective-permute-start(bf16[336,128]{1,0:T(8,128)(2,1)S(1)} %get-tuple-element.34), channel_id=1, source_target_pairs={{0,9},{1,8},{2,11},{3,10},{4,13},{5,12},{6,15},{7,14},{8,22},{9,23... | collective-permute-start | bytes 258056 | tf_op jit(solution)/shard_map/ppermute | solution.py:313
  43.1 7.6 %collective-permute-start.16 = (bf16[336,128]{1,0:T(8,128)(2,1)S(1)}, bf16[336,128]{1,0:T(8,128)(2,1)S(1)}, u32[]{:S(2)}, u32[]{:S(2)}) collective-permute-start(bf16[336,128]{1,0:T(8,128)(2,1)S(1)} %get-tuple-element.35), channel_id=1, source_target_pairs={{0,10},{1,11},{2,8},{3,9},{4,14},{5,15},{6,12},{7,13},{8,21},{9,20... | collective-permute-start | bytes 258056 | tf_op jit(solution)/shard_map/ppermute | solution.py:313
  48.0 6.8 %collective-permute-start.17 = (bf16[336,128]{1,0:T(8,128)(2,1)S(1)}, bf16[336,128]{1,0:T(8,128)(2,1)S(1)}, u32[]{:S(2)}, u32[]{:S(2)}) collective-permute-start(bf16[336,128]{1,0:T(8,128)(2,1)S(1)} %get-tuple-element.36), channel_id=1, source_target_pairs={{0,11},{1,10},{2,9},{3,8},{4,15},{5,14},{6,13},{7,12},{8,20},{9,21... | collective-permute-start | bytes 258056 | tf_op jit(solution)/shard_map/ppermute | solution.py:313

commit v17 on v16

--- a/solution.py
+++ b/solution.py
@@ -392,7 +392,7 @@
     )
     edge_part = near_call(
         near_edge_kernel, "near_edge", halo, halo + STAT_ROWS,
-        2 + seq_count, [pltpu.VMEM(tails.shape, bf16)], *halos, *came, *handed[:1],
+        2 + seq_count, [pltpu.VMEM(tails.shape, bf16)], *halos, *came, *handed[:2],
     )
     handed_inner = linked(inner_part, 1, [0, 0])
     handed_edge = linked(edge_part, 1, [0, 0])

time: 56.3 us -> 53.9 us (0.957)
  the two profiles are of different devices: /device:TPU:0 before, /device:TPU:1 now
where the time goes in v17:
time: 53.9 us; the launch traced here: 53.8 us
  starting transfers between devices  38.9 us (72%)
  Pallas kernels  8.9 us (17%)
  waiting for transfers between devices  3.66 us (7%)
  local copies, waits for them, and re-layouts  1.33 us (2%)
  between operations  0.9 us (2%)
    ppermute x16, starting transfers between devices, linked(): return lax.ppermute(shard, ('section', 'seq'), pairs)  35.9 us
    pallas_call x2, Pallas kernels, far_call(): pl.pallas_call(functools.partial(far_kernel, there, chosen), out_shape=[c...  4.71 us
    ppermute x16, waiting for transfers between devices, linked(): return lax.ppermute(shard, ('section', 'seq'), pairs)  3.66 us
    ppermute x2, starting transfers between devices, halo_from(): return lax.ppermute(mine, ('section', 'seq'), pairs)  3.04 us
    pallas_call x2, Pallas kernels, near_call(): pl.pallas_call(functools.partial(kernel, there), out_shape=jax.ShapeDtype...  2.52 us
    pallas_call x1, Pallas kernels, per_device(): pl.pallas_call(functools.partial(merge_kernel, there), out_shape=jax.Shap...  1.36 us
    unnamed x17, local copies, waits for them, and re-layouts  1.21 us
  transfers between devices with their start and end apart: 18, of which 3 were waited for; matrix products, arithmetic and copies ran while one was open for 0% of the time, Pallas kernels for 14%

profile of v17, /device:TPU:1, one launch (start us, length us, event | category | flops | bytes accessed | tf_op | source)
XLA Modules:
  0.0 53.8 jit_solution(2437198760575481414)
XLA Ops:
  0.7 0.0 copy-start
  0.7 1.1 %copy-done = bf16[1,320,1024]{2,1,0:T(8,128)(2,1)S(1)} copy-done((bf16[1,320,1024]{2,1,0:T(8,128)(2,1)S(1)}, bf16[1,320,1024]{2,1,0:T(8,128)(2,1)}, u32[]{:S(2)}) %copy-start) | copy-done | bytes 655384
  1.8 0.3 split.1
  2.0 2.1 %collective-permute-start.1 = (bf16[336,128]{1,0:T(8,128)(2,1)S(1)}, bf16[336,128]{1,0:T(8,128)(2,1)S(1)}, u32[]{:S(2)}, u32[]{:S(2)}) collective-permute-start(bf16[336,128]{1,0:T(8,128)(2,1)S(1)} %get-tuple-element.21), channel_id=1, source_target_pairs={{0,7},{1,6},{2,5},{3,4},{4,3},{5,2},{6,1},{7,0},{8,9},{9,8},{10,11... | collective-permute-start | bytes 258056 | tf_op jit(solution)/shard_map/ppermute | solution.py:313
  4.2 1.3 %collective-permute-start.3 = (bf16[336,128]{1,0:T(8,128)(2,1)S(1)}, bf16[336,128]{1,0:T(8,128)(2,1)S(1)}, u32[]{:S(2)}, u32[]{:S(2)}) collective-permute-start(bf16[336,128]{1,0:T(8,128)(2,1)S(1)} %get-tuple-element.22), channel_id=1, source_target_pairs={{0,6},{1,7},{2,4},{3,5},{4,2},{5,3},{6,0},{7,1},{8,10},{9,11},{10,... | collective-permute-start | bytes 258056 | tf_op jit(solution)/shard_map/ppermute | solution.py:313
  5.5 4.4 %collective-permute-start.5 = (bf16[336,128]{1,0:T(8,128)(2,1)S(1)}, bf16[336,128]{1,0:T(8,128)(2,1)S(1)}, u32[]{:S(2)}, u32[]{:S(2)}) collective-permute-start(bf16[336,128]{1,0:T(8,128)(2,1)S(1)} %get-tuple-element.24), channel_id=1, source_target_pairs={{0,4},{1,5},{2,6},{3,7},{4,0},{5,1},{6,2},{7,3},{8,15},{9,14},{10,... | collective-permute-start | bytes 258056 | tf_op jit(solution)/shard_map/ppermute | solution.py:313
  9.9 0.1 copy.10
  10.0 0.1 reshape_squeeze.3.random_ref
  10.1 0.0 copy-start.5
  10.1 0.1 pad_maximum_fusion.rows_ref
  10.2 2.3 %collective-permute-start = (bf16[2,128,1024]{2,1,0:T(8,128)(2,1)S(1)}, bf16[2,128,1024]{2,1,0:T(8,128)(2,1)S(1)}, u32[]{:S(2)}, u32[]{:S(2)}) collective-permute-start(bf16[2,128,1024]{2,1,0:T(8,128)(2,1)S(1)} %pad_maximum_fusion.rows_ref), channel_id=1, source_target_pairs={{8,9},{9,10},{10,11},{11,12},{12,13},{13,14},{14,15},{24,25},{25,2... | collective-permute-start | bytes 1572872 | tf_op jit(solution)/shard_map/ppermute | solution.py:333
  12.6 4.2 %collective-permute-start.7 = (bf16[336,128]{1,0:T(8,128)(2,1)S(1)}, bf16[336,128]{1,0:T(8,128)(2,1)S(1)}, u32[]{:S(2)}, u32[]{:S(2)}) collective-permute-start(bf16[336,128]{1,0:T(8,128)(2,1)S(1)} %get-tuple-element.26), channel_id=1, source_target_pairs={{0,2},{1,3},{2,0},{3,1},{4,6},{5,7},{6,4},{7,5},{8,13},{9,12},{10,... | collective-permute-start | bytes 258056 | tf_op jit(solution)/shard_map/ppermute | solution.py:313
  16.8 0.7 %collective-permute-start.2 = (bf16[2,128,1024]{2,1,0:T(8,128)(2,1)S(1)}, bf16[2,128,1024]{2,1,0:T(8,128)(2,1)S(1)}, u32[]{:S(2)}, u32[]{:S(2)}) collective-permute-start(bf16[2,128,1024]{2,1,0:T(8,128)(2,1)S(1)} %halo.1), channel_id=1, source_target_pairs={{0,1},{1,2},{2,3},{3,4},{4,5},{5,6},{6,7},{16,17},{17,18},{18,19},... | collective-permute-start | bytes 1572872 | tf_op jit(solution)/shard_map/ppermute | solution.py:333
  17.5 0.0 copy-start.1
  17.6 0.0 copy-start.2
  17.6 0.0 copy-start.3
  17.6 3.2 %far.2 = (bf16[336,128]{1,0:T(8,128)(2,1)S(1)}, bf16[336,128]{1,0:T(8,128)(2,1)S(1)}, bf16[336,128]{1,0:T(8,128)(2,1)S(1)}, bf16[336,128]{1,0:T(8,128)(2,1)S(1)}...) custom-call(s32[1]{0:T(128)} %bitcast.9.span_ref, s32[2]{0:T(128)S(1)} %bitcast.22, ...), custom_call_target="tpu_custom_call" | custom-call | flops 12582912000 | bytes 4128768 | tf_op jit(solution)/shard_map/far/pallas_call | solution.py:340
  20.8 10.8 %collective-permute-start.9 = (bf16[336,128]{1,0:T(8,128)(2,1)S(1)}, bf16[336,128]{1,0:T(8,128)(2,1)S(1)}, u32[]{:S(2)}, u32[]{:S(2)}) collective-permute-start(bf16[336,128]{1,0:T(8,128)(2,1)S(1)} %get-tuple-element.29), channel_id=1, source_target_pairs={{0,15},{1,14},{2,13},{3,12},{4,11},{5,10},{6,9},{7,8},{8,17},{9,16... | collective-permute-start | bytes 258056 | tf_op jit(solution)/shard_map/ppermute | solution.py:313
  31.7 1.5 %near_inner.1 = bf16[256,1024]{1,0:T(8,128)(2,1)S(1)} custom-call(bf16[320,1024]{1,0:T(8,128)(2,1)S(1)} %bitcast.12, bf16[320,1024]{1,0:T(8,128)(2,1)S(1)} %bitcast.14, bf16[320,1024]{1,0:T(8,128)(2,1)S(1)} %bitcast.16, bf16[336,128]{1,0:T(8,128)(2,1)S(1)} %get-tuple-element.31.own_ref, bf16[336,128]{1,0:T(8,128)(2,1)S(1)} %collective-permute-done.1._.refs_0_, ...), custom_call_target="tpu_custom_call" | custom-call | flops 8053063680 | bytes 1769472 | tf_op jit(solution)/shard_map/near_inner/pallas_call | solution.py:370
  33.2 0.9 %collective-permute-start.12 = (bf16[256,1024]{1,0:T(8,128)(2,1)S(1)}, bf16[256,1024]{1,0:T(8,128)(2,1)S(1)}, u32[]{:S(2)}, u32[]{:S(2)}) collective-permute-start(bf16[256,1024]{1,0:T(8,128)(2,1)S(1)} %near_inner.1), channel_id=1, source_target_pairs={{0,8},{1,9},{2,10},{3,11},{4,12},{5,13},{6,14},{7,15},{8,16},{9,17... | collective-permute-start | bytes 1572872 | tf_op jit(solution)/shard_map/ppermute | solution.py:313
  34.1 2.6 %collective-permute-start.13 = (bf16[336,128]{1,0:T(8,128)(2,1)S(1)}, bf16[336,128]{1,0:T(8,128)(2,1)S(1)}, u32[]{:S(2)}, u32[]{:S(2)}) collective-permute-start(bf16[336,128]{1,0:T(8,128)(2,1)S(1)} %get-tuple-element.32), channel_id=1, source_target_pairs={{0,13},{1,12},{2,15},{3,14},{4,9},{5,8},{6,11},{7,10},{8,19},{9,18... | collective-permute-start | bytes 258056 | tf_op jit(solution)/shard_map/ppermute | solution.py:313
  36.7 0.6 %collective-permute-done.10.refs_9_.refs_1_ = bf16[336,128]{1,0:T(8,128)(2,1)S(1)} collective-permute-done((bf16[336,128]{1,0:T(8,128)(2,1)S(1)}, bf16[336,128]{1,0:T(8,128)(2,1)S(1)}, u32[]{:S(2)}, u32[]{:S(2)}) %collective-permute-start.10) | collective-permute-done | bytes 86048 | tf_op jit(solution)/shard_map/ppermute | solution.py:313
  37.4 1.7 %collective-permute-start.14 = (bf16[336,128]{1,0:T(8,128)(2,1)S(1)}, bf16[336,128]{1,0:T(8,128)(2,1)S(1)}, u32[]{:S(2)}, u32[]{:S(2)}) collective-permute-start(bf16[336,128]{1,0:T(8,128)(2,1)S(1)} %get-tuple-element.33), channel_id=1, source_target_pairs={{0,12},{1,13},{2,14},{3,15},{4,8},{5,9},{6,10},{7,11},{8,23},{9,22... | collective-permute-start | bytes 258056 | tf_op jit(solution)/shard_map/ppermute | solution.py:313
  39.1 2.1 %collective-permute-start.15 = (bf16[336,128]{1,0:T(8,128)(2,1)S(1)}, bf16[336,128]{1,0:T(8,128)(2,1)S(1)}, u32[]{:S(2)}, u32[]{:S(2)}) collective-permute-start(bf16[336,128]{1,0:T(8,128)(2,1)S(1)} %get-tuple-element.34), channel_id=1, source_target_pairs={{0,9},{1,8},{2,11},{3,10},{4,13},{5,12},{6,15},{7,14},{8,22},{9,23... | collective-permute-start | bytes 258056 | tf_op jit(solution)/shard_map/ppermute | solution.py:313
  41.2 1.0 %near_edge.1 = bf16[144,1024]{1,0:T(8,128)(2,1)S(1)} custom-call(bf16[320,1024]{1,0:T(8,128)(2,1)S(1)} %bitcast.13, bf16[320,1024]{1,0:T(8,128)(2,1)S(1)} %bitcast.15, bf16[320,1024]{1,0:T(8,128)(2,1)S(1)} %bitcast.17, bf16[2,128,1024]{2,1,0:T(8,128)(2,1)S(1)} %collective-permute-done.odd_ref, bf16[2,128,1024]{2,1,0:T(8,128)(2,1)S(1)} %collective-permute-done.2.even_ref, ...), custom_call_target="tpu_custom_call" | custom-call | flops 5368709120 | bytes 1179648 | tf_op jit(solution)/shard_map/near_edge/pallas_call | solution.py:370
  42.2 0.1 collective-permute-start.11
  42.3 1.5 %far.3 = (bf16[336,128]{1,0:T(8,128)(2,1)S(1)}, bf16[336,128]{1,0:T(8,128)(2,1)S(1)}) custom-call(s32[1]{0:T(128)} %bitcast.10.span_ref, s32[2]{0:T(128)S(1)} %bitcast.23, s32[120]{0:T(128)S(1)} %reshape_squeeze.3.random_ref, bf16[6144,128]{1,0:T(8,128)(2,1)S(1)} %bitcast.19, bf16[6144,128]{1,0:T(8,128)(2,1)S(1)} %bitcast.21, ...), custom_call_target="tpu_custom_call" | custom-call | flops 4194304000 | bytes 3473408 | tf_op jit(solution)/shard_map/far/pallas_call | solution.py:340
  43.8 3.8 %collective-permute-start.16 = (bf16[336,128]{1,0:T(8,128)(2,1)S(1)}, bf16[336,128]{1,0:T(8,128)(2,1)S(1)}, u32[]{:S(2)}, u32[]{:S(2)}) collective-permute-start(bf16[336,128]{1,0:T(8,128)(2,1)S(1)} %get-tuple-element.35), channel_id=1, source_target_pairs={{0,10},{1,11},{2,8},{3,9},{4,14},{5,15},{6,12},{7,13},{8,21},{9,20... | collective-permute-start | bytes 258056 | tf_op jit(solution)/shard_map/ppermute | solution.py:313
  47.6 1.8 %collective-permute-start.17 = (bf16[336,128]{1,0:T(8,128)(2,1)S(1)}, bf16[336,128]{1,0:T(8,128)(2,1)S(1)}, u32[]{:S(2)}, u32[]{:S(2)}) collective-permute-start(bf16[336,128]{1,0:T(8,128)(2,1)S(1)} %get-tuple-element.36), channel_id=1, source_target_pairs={{0,11},{1,10},{2,9},{3,8},{4,15},{5,14},{6,13},{7,12},{8,20},{9,21... | collective-permute-start | bytes 258056 | tf_op jit(solution)/shard_map/ppermute | solution.py:313
  49.4 0.5 collective-permute-done.16.refs_5_
  49.9 2.5 %collective-permute-done.17.refs_6_ = bf16[336,128]{1,0:T(8,128)(2,1)S(1)} collective-permute-done((bf16[336,128]{1,0:T(8,128)(2,1)S(1)}, bf16[336,128]{1,0:T(8,128)(2,1)S(1)}, u32[]{:S(2)}, u32[]{:S(2)}) %collective-permute-start.17) | collective-permute-done | bytes 86048 | tf_op jit(solution)/shard_map/ppermute | solution.py:313
  52.4 1.4 %merge.1 = bf16[320,1024]{1,0:T(8,128)(2,1)} custom-call(bf16[144,1024]{1,0:T(8,128)(2,1)S(1)} %collective-permute-done.11.edge_ref, bf16[256,1024]{1,0:T(8,128)(2,1)S(1)} %collective-permute-done.12.inner_ref, bf16[336,128]{1,0:T(8,128)(2,1)S(1)} %collective-permute-done.9.refs_8_.refs_0_, bf16[336,128]{1,0:T(8,128)(2,1)S(1)} %collective-permute-done.10.refs_9_.refs_1_, ...), custom_call_target="tpu_custom_call" | custom-call | bytes 1966080 | tf_op jit(solution)/shard_map/merge/pallas_call | solution.py:400
  (34 shorter events, 0.1 us)
Async XLA Ops:
  0.0 9.9 %copy-start.7 = (s32[1,40,3]{1,0,2:T(1,128)S(1)}, s32[1,40,3]{1,0,2:T(1,128)}, u32[]{:S(2)}) copy-start(s32[1,40,3]{1,0,2:T(1,128)} %param.15) | copy-start | bytes 1444
  0.7 1.1 %copy-start = (bf16[1,320,1024]{2,1,0:T(8,128)(2,1)S(1)}, bf16[1,320,1024]{2,1,0:T(8,128)(2,1)}, u32[]{:S(2)}) copy-start(bf16[1,320,1024]{2,1,0:T(8,128)(2,1)} %param.8) | copy-start | bytes 1966084
  1.8 8.3 %slice-start = ((bf16[1,320,1024]{2,1,0:T(8,128)(2,1)}), bf16[1,128,1024]{2,1,0:T(8,128)(2,1)S(1)}, s32[]{:S(2)}) async-start(bf16[1,320,1024]{2,1,0:T(8,128)(2,1)} %param.9), calls=%async_computation | async-start | bytes 524288 | tf_op jit(solution)/shard_map/slice | solution.py:317
  1.8 8.3 %slice-start.1 = ((bf16[1,320,1024]{2,1,0:T(8,128)(2,1)}), bf16[1,128,1024]{2,1,0:T(8,128)(2,1)S(1)}, s32[]{:S(2)}) async-start(bf16[1,320,1024]{2,1,0:T(8,128)(2,1)} %param.10), calls=%async_computation.1 | async-start | bytes 524288 | tf_op jit(solution)/shard_map/slice | solution.py:317
  2.0 8.1 %collective-permute-start.1 = (bf16[336,128]{1,0:T(8,128)(2,1)S(1)}, bf16[336,128]{1,0:T(8,128)(2,1)S(1)}, u32[]{:S(2)}, u32[]{:S(2)}) collective-permute-start(bf16[336,128]{1,0:T(8,128)(2,1)S(1)} %get-tuple-element.21), channel_id=1, source_target_pairs={{0,7},{1,6},{2,5},{3,4},{4,3},{5,2},{6,1},{7,0},{8,9},{9,8},{10,11... | collective-permute-start | bytes 258056 | tf_op jit(solution)/shard_map/ppermute | solution.py:313
  4.2 8.4 %collective-permute-start.3 = (bf16[336,128]{1,0:T(8,128)(2,1)S(1)}, bf16[336,128]{1,0:T(8,128)(2,1)S(1)}, u32[]{:S(2)}, u32[]{:S(2)}) collective-permute-start(bf16[336,128]{1,0:T(8,128)(2,1)S(1)} %get-tuple-element.22), channel_id=1, source_target_pairs={{0,6},{1,7},{2,4},{3,5},{4,2},{5,3},{6,0},{7,1},{8,10},{9,11},{10,... | collective-permute-start | bytes 258056 | tf_op jit(solution)/shard_map/ppermute | solution.py:313
  5.5 11.3 %collective-permute-start.4 = (bf16[336,128]{1,0:T(8,128)(2,1)S(1)}, bf16[336,128]{1,0:T(8,128)(2,1)S(1)}, u32[]{:S(2)}, u32[]{:S(2)}) collective-permute-start(bf16[336,128]{1,0:T(8,128)(2,1)S(1)} %get-tuple-element.23), channel_id=1, source_target_pairs={{0,5},{1,4},{2,7},{3,6},{4,1},{5,0},{6,3},{7,2},{8,11},{9,10},{10,... | collective-permute-start | bytes 258056 | tf_op jit(solution)/shard_map/ppermute | solution.py:313
  5.5 11.3 %collective-permute-start.5 = (bf16[336,128]{1,0:T(8,128)(2,1)S(1)}, bf16[336,128]{1,0:T(8,128)(2,1)S(1)}, u32[]{:S(2)}, u32[]{:S(2)}) collective-permute-start(bf16[336,128]{1,0:T(8,128)(2,1)S(1)} %get-tuple-element.24), channel_id=1, source_target_pairs={{0,4},{1,5},{2,6},{3,7},{4,0},{5,1},{6,2},{7,3},{8,15},{9,14},{10,... | collective-permute-start | bytes 258056 | tf_op jit(solution)/shard_map/ppermute | solution.py:313
  9.9 7.7 %copy-start.4 = (bf16[1,6144,128]{2,1,0:T(8,128)(2,1)S(1)}, bf16[1,6144,128]{2,1,0:T(8,128)(2,1)}, u32[]{:S(2)}) copy-start(bf16[1,6144,128]{2,1,0:T(8,128)(2,1)} %param.11) | copy-start | bytes 4718596
  9.9 7.7 %copy-start.6 = (s32[1,2]{1,0:T(1,128)S(1)}, s32[1,2]{1,0:T(1,128)}, u32[]{:S(2)}) copy-start(s32[1,2]{1,0:T(1,128)} %param.14) | copy-start | bytes 28
  9.9 7.6 %collective-permute-start.6 = (bf16[336,128]{1,0:T(8,128)(2,1)S(1)}, bf16[336,128]{1,0:T(8,128)(2,1)S(1)}, u32[]{:S(2)}, u32[]{:S(2)}) collective-permute-start(bf16[336,128]{1,0:T(8,128)(2,1)S(1)} %get-tuple-element.25), channel_id=1, source_target_pairs={{0,1},{1,0},{2,3},{3,2},{4,5},{5,4},{6,7},{7,6},{8,14},{9,15},{10,... | collective-permute-start | bytes 258056 | tf_op jit(solution)/shard_map/ppermute | solution.py:313
  10.1 7.4 %copy-start.5 = (bf16[1,6144,128]{2,1,0:T(8,128)(2,1)S(1)}, bf16[1,6144,128]{2,1,0:T(8,128)(2,1)}, u32[]{:S(2)}) copy-start(bf16[1,6144,128]{2,1,0:T(8,128)(2,1)} %param.12) | copy-start | bytes 4718596
  10.2 28.9 %collective-permute-start = (bf16[2,128,1024]{2,1,0:T(8,128)(2,1)S(1)}, bf16[2,128,1024]{2,1,0:T(8,128)(2,1)S(1)}, u32[]{:S(2)}, u32[]{:S(2)}) collective-permute-start(bf16[2,128,1024]{2,1,0:T(8,128)(2,1)S(1)} %pad_maximum_fusion.rows_ref), channel_id=1, source_target_pairs={{8,9},{9,10},{10,11},{11,12},{12,13},{13,14},{14,15},{24,25},{25,2... | collective-permute-start | bytes 1572872 | tf_op jit(solution)/shard_map/ppermute | solution.py:333
  12.6 19.1 %collective-permute-start.7 = (bf16[336,128]{1,0:T(8,128)(2,1)S(1)}, bf16[336,128]{1,0:T(8,128)(2,1)S(1)}, u32[]{:S(2)}, u32[]{:S(2)}) collective-permute-start(bf16[336,128]{1,0:T(8,128)(2,1)S(1)} %get-tuple-element.26), channel_id=1, source_target_pairs={{0,2},{1,3},{2,0},{3,1},{4,6},{5,7},{6,4},{7,5},{8,13},{9,12},{10,... | collective-permute-start | bytes 258056 | tf_op jit(solution)/shard_map/ppermute | solution.py:313
  16.8 14.9 %collective-permute-start.8 = (bf16[336,128]{1,0:T(8,128)(2,1)S(1)}, bf16[336,128]{1,0:T(8,128)(2,1)S(1)}, u32[]{:S(2)}, u32[]{:S(2)}) collective-permute-start(bf16[336,128]{1,0:T(8,128)(2,1)S(1)} %get-tuple-element.27), channel_id=1, source_target_pairs={{0,3},{1,2},{2,1},{3,0},{4,7},{5,6},{6,5},{7,4},{8,12},{9,13},{10,... | collective-permute-start | bytes 258056 | tf_op jit(solution)/shard_map/ppermute | solution.py:313
  16.8 24.4 %collective-permute-start.2 = (bf16[2,128,1024]{2,1,0:T(8,128)(2,1)S(1)}, bf16[2,128,1024]{2,1,0:T(8,128)(2,1)S(1)}, u32[]{:S(2)}, u32[]{:S(2)}) collective-permute-start(bf16[2,128,1024]{2,1,0:T(8,128)(2,1)S(1)} %halo.1), channel_id=1, source_target_pairs={{0,1},{1,2},{2,3},{3,4},{4,5},{5,6},{6,7},{16,17},{17,18},{18,19},... | collective-permute-start | bytes 1572872 | tf_op jit(solution)/shard_map/ppermute | solution.py:333
  17.5 14.1 %copy-start.1 = (bf16[1,320,1024]{2,1,0:T(8,128)(2,1)S(1)}, bf16[1,320,1024]{2,1,0:T(8,128)(2,1)}, u32[]{:S(2)}) copy-start(bf16[1,320,1024]{2,1,0:T(8,128)(2,1)} %param.8) | copy-start | bytes 1966084
  17.6 14.1 %copy-start.2 = (bf16[1,320,1024]{2,1,0:T(8,128)(2,1)S(1)}, bf16[1,320,1024]{2,1,0:T(8,128)(2,1)}, u32[]{:S(2)}) copy-start(bf16[1,320,1024]{2,1,0:T(8,128)(2,1)} %param.9) | copy-start | bytes 1966084
  17.6 14.1 %copy-start.3 = (bf16[1,320,1024]{2,1,0:T(8,128)(2,1)S(1)}, bf16[1,320,1024]{2,1,0:T(8,128)(2,1)}, u32[]{:S(2)}) copy-start(bf16[1,320,1024]{2,1,0:T(8,128)(2,1)} %param.10) | copy-start | bytes 1966084
  20.8 13.3 %collective-permute-start.9 = (bf16[336,128]{1,0:T(8,128)(2,1)S(1)}, bf16[336,128]{1,0:T(8,128)(2,1)S(1)}, u32[]{:S(2)}, u32[]{:S(2)}) collective-permute-start(bf16[336,128]{1,0:T(8,128)(2,1)S(1)} %get-tuple-element.29), channel_id=1, source_target_pairs={{0,15},{1,14},{2,13},{3,12},{4,11},{5,10},{6,9},{7,8},{8,17},{9,16... | collective-permute-start | bytes 258056 | tf_op jit(solution)/shard_map/ppermute | solution.py:313
  31.6 5.7 %collective-permute-start.10 = (bf16[336,128]{1,0:T(8,128)(2,1)S(1)}, bf16[336,128]{1,0:T(8,128)(2,1)S(1)}, u32[]{:S(2)}, u32[]{:S(2)}) collective-permute-start(bf16[336,128]{1,0:T(8,128)(2,1)S(1)} %get-tuple-element.30), channel_id=1, source_target_pairs={{0,14},{1,15},{2,12},{3,13},{4,10},{5,11},{6,8},{7,9},{8,18},{9,19... | collective-permute-start | bytes 258056 | tf_op jit(solution)/shard_map/ppermute | solution.py:313
  33.2 19.2 %collective-permute-start.12 = (bf16[256,1024]{1,0:T(8,128)(2,1)S(1)}, bf16[256,1024]{1,0:T(8,128)(2,1)S(1)}, u32[]{:S(2)}, u32[]{:S(2)}) collective-permute-start(bf16[256,1024]{1,0:T(8,128)(2,1)S(1)} %near_inner.1), channel_id=1, source_target_pairs={{0,8},{1,9},{2,10},{3,11},{4,12},{5,13},{6,14},{7,15},{8,16},{9,17... | collective-permute-start | bytes 1572872 | tf_op jit(solution)/shard_map/ppermute | solution.py:313
  34.1 9.7 %collective-permute-start.13 = (bf16[336,128]{1,0:T(8,128)(2,1)S(1)}, bf16[336,128]{1,0:T(8,128)(2,1)S(1)}, u32[]{:S(2)}, u32[]{:S(2)}) collective-permute-start(bf16[336,128]{1,0:T(8,128)(2,1)S(1)} %get-tuple-element.32), channel_id=1, source_target_pairs={{0,13},{1,12},{2,15},{3,14},{4,9},{5,8},{6,11},{7,10},{8,19},{9,18... | collective-permute-start | bytes 258056 | tf_op jit(solution)/shard_map/ppermute | solution.py:313
  37.4 10.2 %collective-permute-start.14 = (bf16[336,128]{1,0:T(8,128)(2,1)S(1)}, bf16[336,128]{1,0:T(8,128)(2,1)S(1)}, u32[]{:S(2)}, u32[]{:S(2)}) collective-permute-start(bf16[336,128]{1,0:T(8,128)(2,1)S(1)} %get-tuple-element.33), channel_id=1, source_target_pairs={{0,12},{1,13},{2,14},{3,15},{4,8},{5,9},{6,10},{7,11},{8,23},{9,22... | collective-permute-start | bytes 258056 | tf_op jit(solution)/shard_map/ppermute | solution.py:313
  39.1 10.3 %collective-permute-start.15 = (bf16[336,128]{1,0:T(8,128)(2,1)S(1)}, bf16[336,128]{1,0:T(8,128)(2,1)S(1)}, u32[]{:S(2)}, u32[]{:S(2)}) collective-permute-start(bf16[336,128]{1,0:T(8,128)(2,1)S(1)} %get-tuple-element.34), channel_id=1, source_target_pairs={{0,9},{1,8},{2,11},{3,10},{4,13},{5,12},{6,15},{7,14},{8,22},{9,23... | collective-permute-start | bytes 258056 | tf_op jit(solution)/shard_map/ppermute | solution.py:313
  42.2 10.2 %collective-permute-start.11 = (bf16[144,1024]{1,0:T(8,128)(2,1)S(1)}, bf16[144,1024]{1,0:T(8,128)(2,1)S(1)}, u32[]{:S(2)}, u32[]{:S(2)}) collective-permute-start(bf16[144,1024]{1,0:T(8,128)(2,1)S(1)} %near_edge.1), channel_id=1, source_target_pairs={{0,8},{1,9},{2,10},{3,11},{4,12},{5,13},{6,14},{7,15},{8,16},{9,17... | collective-permute-start | bytes 884744 | tf_op jit(solution)/shard_map/ppermute | solution.py:313
  43.8 6.1 %collective-permute-start.16 = (bf16[336,128]{1,0:T(8,128)(2,1)S(1)}, bf16[336,128]{1,0:T(8,128)(2,1)S(1)}, u32[]{:S(2)}, u32[]{:S(2)}) collective-permute-start(bf16[336,128]{1,0:T(8,128)(2,1)S(1)} %get-tuple-element.35), channel_id=1, source_target_pairs={{0,10},{1,11},{2,8},{3,9},{4,14},{5,15},{6,12},{7,13},{8,21},{9,20... | collective-permute-start | bytes 258056 | tf_op jit(solution)/shard_map/ppermute | solution.py:313
  47.6 4.8 %collective-permute-start.17 = (bf16[336,128]{1,0:T(8,128)(2,1)S(1)}, bf16[336,128]{1,0:T(8,128)(2,1)S(1)}, u32[]{:S(2)}, u32[]{:S(2)}) collective-permute-start(bf16[336,128]{1,0:T(8,128)(2,1)S(1)} %get-tuple-element.36), channel_id=1, source_target_pairs={{0,11},{1,10},{2,9},{3,8},{4,15},{5,14},{6,13},{7,12},{8,20},{9,21... | collective-permute-start | bytes 258056 | tf_op jit(solution)/shard_map/ppermute | solution.py:313

commit v18 on v17

--- a/solution.py
+++ b/solution.py
@@ -179,7 +179,7 @@
         for start, size in zip(starts, sizes)
     ]
     peers = peers_of(there, 0)
-    together = min(len(starts), 2)
+    together = 4 if len(starts) > 1 else 1
     for begin in range(0, len(peers), together):
         pair = range(begin, min(begin + together, len(peers)))
         all_lanes = [pl.ds(pl.multiple_of(peers[at] * HD, HD), HD) for at in pair]

time: 53.9 us -> 53.9 us (level)
  transfers between devices with their start and end apart: 18 -> 18, of which waited for: 3 -> 3; matrix products, arithmetic and copies ran while one was open for 0% -> 0% of each run, Pallas kernels for 14% -> 13%
where the time goes in v18:
time: 53.9 us; the launch traced here: 53.8 us
  starting transfers between devices  39.2 us (73%)
  Pallas kernels  8.64 us (16%)
  waiting for transfers between devices  3.66 us (7%)
  local copies, waits for them, and re-layouts  1.33 us (2%)
  between operations  0.9 us (2%)
    ppermute x16, starting transfers between devices, linked(): return lax.ppermute(shard, ('section', 'seq'), pairs)  36.1 us
    pallas_call x2, Pallas kernels, far_call(): pl.pallas_call(functools.partial(far_kernel, there, chosen), out_shape=[c...  4.71 us
    ppermute x16, waiting for transfers between devices, linked(): return lax.ppermute(shard, ('section', 'seq'), pairs)  3.66 us
    ppermute x2, starting transfers between devices, halo_from(): return lax.ppermute(mine, ('section', 'seq'), pairs)  3.04 us
    pallas_call x2, Pallas kernels, near_call(): pl.pallas_call(functools.partial(kernel, there), out_shape=jax.ShapeDtype...  2.26 us
    pallas_call x1, Pallas kernels, per_device(): pl.pallas_call(functools.partial(merge_kernel, there), out_shape=jax.Shap...  1.36 us
    unnamed x17, local copies, waits for them, and re-layouts  1.21 us
  transfers between devices with their start and end apart: 18, of which 3 were waited for; matrix products, arithmetic and copies ran while one was open for 0% of the time, Pallas kernels for 13%

profile of v18, /device:TPU:1, one launch (start us, length us, event | category | flops | bytes accessed | tf_op | source)
XLA Modules:
  0.0 53.8 jit_solution(11372900648150950610)
XLA Ops:
  0.7 0.0 copy-start
  0.7 1.1 %copy-done = bf16[1,320,1024]{2,1,0:T(8,128)(2,1)S(1)} copy-done((bf16[1,320,1024]{2,1,0:T(8,128)(2,1)S(1)}, bf16[1,320,1024]{2,1,0:T(8,128)(2,1)}, u32[]{:S(2)}) %copy-start) | copy-done | bytes 655384
  1.8 0.3 split.1
  2.0 2.1 %collective-permute-start.1 = (bf16[336,128]{1,0:T(8,128)(2,1)S(1)}, bf16[336,128]{1,0:T(8,128)(2,1)S(1)}, u32[]{:S(2)}, u32[]{:S(2)}) collective-permute-start(bf16[336,128]{1,0:T(8,128)(2,1)S(1)} %get-tuple-element.21), channel_id=1, source_target_pairs={{0,7},{1,6},{2,5},{3,4},{4,3},{5,2},{6,1},{7,0},{8,9},{9,8},{10,11... | collective-permute-start | bytes 258056 | tf_op jit(solution)/shard_map/ppermute | solution.py:313
  4.2 1.3 %collective-permute-start.3 = (bf16[336,128]{1,0:T(8,128)(2,1)S(1)}, bf16[336,128]{1,0:T(8,128)(2,1)S(1)}, u32[]{:S(2)}, u32[]{:S(2)}) collective-permute-start(bf16[336,128]{1,0:T(8,128)(2,1)S(1)} %get-tuple-element.22), channel_id=1, source_target_pairs={{0,6},{1,7},{2,4},{3,5},{4,2},{5,3},{6,0},{7,1},{8,10},{9,11},{10,... | collective-permute-start | bytes 258056 | tf_op jit(solution)/shard_map/ppermute | solution.py:313
  5.5 4.4 %collective-permute-start.5 = (bf16[336,128]{1,0:T(8,128)(2,1)S(1)}, bf16[336,128]{1,0:T(8,128)(2,1)S(1)}, u32[]{:S(2)}, u32[]{:S(2)}) collective-permute-start(bf16[336,128]{1,0:T(8,128)(2,1)S(1)} %get-tuple-element.24), channel_id=1, source_target_pairs={{0,4},{1,5},{2,6},{3,7},{4,0},{5,1},{6,2},{7,3},{8,15},{9,14},{10,... | collective-permute-start | bytes 258056 | tf_op jit(solution)/shard_map/ppermute | solution.py:313
  9.9 0.1 copy.10
  10.0 0.1 reshape_squeeze.3.random_ref
  10.1 0.0 copy-start.5
  10.1 0.1 pad_maximum_fusion.rows_ref
  10.2 2.3 %collective-permute-start = (bf16[2,128,1024]{2,1,0:T(8,128)(2,1)S(1)}, bf16[2,128,1024]{2,1,0:T(8,128)(2,1)S(1)}, u32[]{:S(2)}, u32[]{:S(2)}) collective-permute-start(bf16[2,128,1024]{2,1,0:T(8,128)(2,1)S(1)} %pad_maximum_fusion.rows_ref), channel_id=1, source_target_pairs={{8,9},{9,10},{10,11},{11,12},{12,13},{13,14},{14,15},{24,25},{25,2... | collective-permute-start | bytes 1572872 | tf_op jit(solution)/shard_map/ppermute | solution.py:333
  12.6 4.2 %collective-permute-start.7 = (bf16[336,128]{1,0:T(8,128)(2,1)S(1)}, bf16[336,128]{1,0:T(8,128)(2,1)S(1)}, u32[]{:S(2)}, u32[]{:S(2)}) collective-permute-start(bf16[336,128]{1,0:T(8,128)(2,1)S(1)} %get-tuple-element.26), channel_id=1, source_target_pairs={{0,2},{1,3},{2,0},{3,1},{4,6},{5,7},{6,4},{7,5},{8,13},{9,12},{10,... | collective-permute-start | bytes 258056 | tf_op jit(solution)/shard_map/ppermute | solution.py:313
  16.8 0.7 %collective-permute-start.2 = (bf16[2,128,1024]{2,1,0:T(8,128)(2,1)S(1)}, bf16[2,128,1024]{2,1,0:T(8,128)(2,1)S(1)}, u32[]{:S(2)}, u32[]{:S(2)}) collective-permute-start(bf16[2,128,1024]{2,1,0:T(8,128)(2,1)S(1)} %halo.1), channel_id=1, source_target_pairs={{0,1},{1,2},{2,3},{3,4},{4,5},{5,6},{6,7},{16,17},{17,18},{18,19},... | collective-permute-start | bytes 1572872 | tf_op jit(solution)/shard_map/ppermute | solution.py:333
  17.5 0.0 copy-start.1
  17.6 0.0 copy-start.2
  17.6 0.0 copy-start.3
  17.6 3.2 %far.2 = (bf16[336,128]{1,0:T(8,128)(2,1)S(1)}, bf16[336,128]{1,0:T(8,128)(2,1)S(1)}, bf16[336,128]{1,0:T(8,128)(2,1)S(1)}, bf16[336,128]{1,0:T(8,128)(2,1)S(1)}...) custom-call(s32[1]{0:T(128)} %bitcast.9.span_ref, s32[2]{0:T(128)S(1)} %bitcast.22, ...), custom_call_target="tpu_custom_call" | custom-call | flops 12582912000 | bytes 4128768 | tf_op jit(solution)/shard_map/far/pallas_call | solution.py:340
  20.8 10.8 %collective-permute-start.9 = (bf16[336,128]{1,0:T(8,128)(2,1)S(1)}, bf16[336,128]{1,0:T(8,128)(2,1)S(1)}, u32[]{:S(2)}, u32[]{:S(2)}) collective-permute-start(bf16[336,128]{1,0:T(8,128)(2,1)S(1)} %get-tuple-element.29), channel_id=1, source_target_pairs={{0,15},{1,14},{2,13},{3,12},{4,11},{5,10},{6,9},{7,8},{8,17},{9,16... | collective-permute-start | bytes 258056 | tf_op jit(solution)/shard_map/ppermute | solution.py:313
  31.7 1.2 %near_inner.1 = bf16[256,1024]{1,0:T(8,128)(2,1)S(1)} custom-call(bf16[320,1024]{1,0:T(8,128)(2,1)S(1)} %bitcast.12, bf16[320,1024]{1,0:T(8,128)(2,1)S(1)} %bitcast.14, bf16[320,1024]{1,0:T(8,128)(2,1)S(1)} %bitcast.16, bf16[336,128]{1,0:T(8,128)(2,1)S(1)} %get-tuple-element.31.own_ref, bf16[336,128]{1,0:T(8,128)(2,1)S(1)} %collective-permute-done.1._.refs_0_, ...), custom_call_target="tpu_custom_call" | custom-call | flops 8053063680 | bytes 1769472 | tf_op jit(solution)/shard_map/near_inner/pallas_call | solution.py:370
  32.9 0.9 %collective-permute-start.12 = (bf16[256,1024]{1,0:T(8,128)(2,1)S(1)}, bf16[256,1024]{1,0:T(8,128)(2,1)S(1)}, u32[]{:S(2)}, u32[]{:S(2)}) collective-permute-start(bf16[256,1024]{1,0:T(8,128)(2,1)S(1)} %near_inner.1), channel_id=1, source_target_pairs={{0,8},{1,9},{2,10},{3,11},{4,12},{5,13},{6,14},{7,15},{8,16},{9,17... | collective-permute-start | bytes 1572872 | tf_op jit(solution)/shard_map/ppermute | solution.py:313
  33.9 2.8 %collective-permute-start.13 = (bf16[336,128]{1,0:T(8,128)(2,1)S(1)}, bf16[336,128]{1,0:T(8,128)(2,1)S(1)}, u32[]{:S(2)}, u32[]{:S(2)}) collective-permute-start(bf16[336,128]{1,0:T(8,128)(2,1)S(1)} %get-tuple-element.32), channel_id=1, source_target_pairs={{0,13},{1,12},{2,15},{3,14},{4,9},{5,8},{6,11},{7,10},{8,19},{9,18... | collective-permute-start | bytes 258056 | tf_op jit(solution)/shard_map/ppermute | solution.py:313
  36.7 0.6 %collective-permute-done.10.refs_9_.refs_1_ = bf16[336,128]{1,0:T(8,128)(2,1)S(1)} collective-permute-done((bf16[336,128]{1,0:T(8,128)(2,1)S(1)}, bf16[336,128]{1,0:T(8,128)(2,1)S(1)}, u32[]{:S(2)}, u32[]{:S(2)}) %collective-permute-start.10) | collective-permute-done | bytes 86048 | tf_op jit(solution)/shard_map/ppermute | solution.py:313
  37.4 1.7 %collective-permute-start.14 = (bf16[336,128]{1,0:T(8,128)(2,1)S(1)}, bf16[336,128]{1,0:T(8,128)(2,1)S(1)}, u32[]{:S(2)}, u32[]{:S(2)}) collective-permute-start(bf16[336,128]{1,0:T(8,128)(2,1)S(1)} %get-tuple-element.33), channel_id=1, source_target_pairs={{0,12},{1,13},{2,14},{3,15},{4,8},{5,9},{6,10},{7,11},{8,23},{9,22... | collective-permute-start | bytes 258056 | tf_op jit(solution)/shard_map/ppermute | solution.py:313
  39.1 2.1 %collective-permute-start.15 = (bf16[336,128]{1,0:T(8,128)(2,1)S(1)}, bf16[336,128]{1,0:T(8,128)(2,1)S(1)}, u32[]{:S(2)}, u32[]{:S(2)}) collective-permute-start(bf16[336,128]{1,0:T(8,128)(2,1)S(1)} %get-tuple-element.34), channel_id=1, source_target_pairs={{0,9},{1,8},{2,11},{3,10},{4,13},{5,12},{6,15},{7,14},{8,22},{9,23... | collective-permute-start | bytes 258056 | tf_op jit(solution)/shard_map/ppermute | solution.py:313
  41.2 1.0 %near_edge.1 = bf16[144,1024]{1,0:T(8,128)(2,1)S(1)} custom-call(bf16[320,1024]{1,0:T(8,128)(2,1)S(1)} %bitcast.13, bf16[320,1024]{1,0:T(8,128)(2,1)S(1)} %bitcast.15, bf16[320,1024]{1,0:T(8,128)(2,1)S(1)} %bitcast.17, bf16[2,128,1024]{2,1,0:T(8,128)(2,1)S(1)} %collective-permute-done.odd_ref, bf16[2,128,1024]{2,1,0:T(8,128)(2,1)S(1)} %collective-permute-done.2.even_ref, ...), custom_call_target="tpu_custom_call" | custom-call | flops 5368709120 | bytes 1179648 | tf_op jit(solution)/shard_map/near_edge/pallas_call | solution.py:370
  42.2 0.1 collective-permute-start.11
  42.3 1.5 %far.3 = (bf16[336,128]{1,0:T(8,128)(2,1)S(1)}, bf16[336,128]{1,0:T(8,128)(2,1)S(1)}) custom-call(s32[1]{0:T(128)} %bitcast.10.span_ref, s32[2]{0:T(128)S(1)} %bitcast.23, s32[120]{0:T(128)S(1)} %reshape_squeeze.3.random_ref, bf16[6144,128]{1,0:T(8,128)(2,1)S(1)} %bitcast.19, bf16[6144,128]{1,0:T(8,128)(2,1)S(1)} %bitcast.21, ...), custom_call_target="tpu_custom_call" | custom-call | flops 4194304000 | bytes 3473408 | tf_op jit(solution)/shard_map/far/pallas_call | solution.py:340
  43.8 3.8 %collective-permute-start.16 = (bf16[336,128]{1,0:T(8,128)(2,1)S(1)}, bf16[336,128]{1,0:T(8,128)(2,1)S(1)}, u32[]{:S(2)}, u32[]{:S(2)}) collective-permute-start(bf16[336,128]{1,0:T(8,128)(2,1)S(1)} %get-tuple-element.35), channel_id=1, source_target_pairs={{0,10},{1,11},{2,8},{3,9},{4,14},{5,15},{6,12},{7,13},{8,21},{9,20... | collective-permute-start | bytes 258056 | tf_op jit(solution)/shard_map/ppermute | solution.py:313
  47.6 1.8 %collective-permute-start.17 = (bf16[336,128]{1,0:T(8,128)(2,1)S(1)}, bf16[336,128]{1,0:T(8,128)(2,1)S(1)}, u32[]{:S(2)}, u32[]{:S(2)}) collective-permute-start(bf16[336,128]{1,0:T(8,128)(2,1)S(1)} %get-tuple-element.36), channel_id=1, source_target_pairs={{0,11},{1,10},{2,9},{3,8},{4,15},{5,14},{6,13},{7,12},{8,20},{9,21... | collective-permute-start | bytes 258056 | tf_op jit(solution)/shard_map/ppermute | solution.py:313
  49.4 0.5 collective-permute-done.16.refs_5_
  49.9 2.5 %collective-permute-done.17.refs_6_ = bf16[336,128]{1,0:T(8,128)(2,1)S(1)} collective-permute-done((bf16[336,128]{1,0:T(8,128)(2,1)S(1)}, bf16[336,128]{1,0:T(8,128)(2,1)S(1)}, u32[]{:S(2)}, u32[]{:S(2)}) %collective-permute-start.17) | collective-permute-done | bytes 86048 | tf_op jit(solution)/shard_map/ppermute | solution.py:313
  52.4 1.4 %merge.1 = bf16[320,1024]{1,0:T(8,128)(2,1)} custom-call(bf16[144,1024]{1,0:T(8,128)(2,1)S(1)} %collective-permute-done.11.edge_ref, bf16[256,1024]{1,0:T(8,128)(2,1)S(1)} %collective-permute-done.12.inner_ref, bf16[336,128]{1,0:T(8,128)(2,1)S(1)} %collective-permute-done.9.refs_8_.refs_0_, bf16[336,128]{1,0:T(8,128)(2,1)S(1)} %collective-permute-done.10.refs_9_.refs_1_, ...), custom_call_target="tpu_custom_call" | custom-call | bytes 1966080 | tf_op jit(solution)/shard_map/merge/pallas_call | solution.py:400
  (34 shorter events, 0.1 us)
Async XLA Ops:
  0.0 9.9 %copy-start.7 = (s32[1,40,3]{1,0,2:T(1,128)S(1)}, s32[1,40,3]{1,0,2:T(1,128)}, u32[]{:S(2)}) copy-start(s32[1,40,3]{1,0,2:T(1,128)} %param.15) | copy-start | bytes 1444
  0.7 1.1 %copy-start = (bf16[1,320,1024]{2,1,0:T(8,128)(2,1)S(1)}, bf16[1,320,1024]{2,1,0:T(8,128)(2,1)}, u32[]{:S(2)}) copy-start(bf16[1,320,1024]{2,1,0:T(8,128)(2,1)} %param.8) | copy-start | bytes 1966084
  1.8 8.3 %slice-start = ((bf16[1,320,1024]{2,1,0:T(8,128)(2,1)}), bf16[1,128,1024]{2,1,0:T(8,128)(2,1)S(1)}, s32[]{:S(2)}) async-start(bf16[1,320,1024]{2,1,0:T(8,128)(2,1)} %param.9), calls=%async_computation | async-start | bytes 524288 | tf_op jit(solution)/shard_map/slice | solution.py:317
  1.8 8.3 %slice-start.1 = ((bf16[1,320,1024]{2,1,0:T(8,128)(2,1)}), bf16[1,128,1024]{2,1,0:T(8,128)(2,1)S(1)}, s32[]{:S(2)}) async-start(bf16[1,320,1024]{2,1,0:T(8,128)(2,1)} %param.10), calls=%async_computation.1 | async-start | bytes 524288 | tf_op jit(solution)/shard_map/slice | solution.py:317
  2.0 8.1 %collective-permute-start.1 = (bf16[336,128]{1,0:T(8,128)(2,1)S(1)}, bf16[336,128]{1,0:T(8,128)(2,1)S(1)}, u32[]{:S(2)}, u32[]{:S(2)}) collective-permute-start(bf16[336,128]{1,0:T(8,128)(2,1)S(1)} %get-tuple-element.21), channel_id=1, source_target_pairs={{0,7},{1,6},{2,5},{3,4},{4,3},{5,2},{6,1},{7,0},{8,9},{9,8},{10,11... | collective-permute-start | bytes 258056 | tf_op jit(solution)/shard_map/ppermute | solution.py:313
  4.2 8.4 %collective-permute-start.3 = (bf16[336,128]{1,0:T(8,128)(2,1)S(1)}, bf16[336,128]{1,0:T(8,128)(2,1)S(1)}, u32[]{:S(2)}, u32[]{:S(2)}) collective-permute-start(bf16[336,128]{1,0:T(8,128)(2,1)S(1)} %get-tuple-element.22), channel_id=1, source_target_pairs={{0,6},{1,7},{2,4},{3,5},{4,2},{5,3},{6,0},{7,1},{8,10},{9,11},{10,... | collective-permute-start | bytes 258056 | tf_op jit(solution)/shard_map/ppermute | solution.py:313
  5.5 11.3 %collective-permute-start.4 = (bf16[336,128]{1,0:T(8,128)(2,1)S(1)}, bf16[336,128]{1,0:T(8,128)(2,1)S(1)}, u32[]{:S(2)}, u32[]{:S(2)}) collective-permute-start(bf16[336,128]{1,0:T(8,128)(2,1)S(1)} %get-tuple-element.23), channel_id=1, source_target_pairs={{0,5},{1,4},{2,7},{3,6},{4,1},{5,0},{6,3},{7,2},{8,11},{9,10},{10,... | collective-permute-start | bytes 258056 | tf_op jit(solution)/shard_map/ppermute | solution.py:313
  5.5 11.3 %collective-permute-start.5 = (bf16[336,128]{1,0:T(8,128)(2,1)S(1)}, bf16[336,128]{1,0:T(8,128)(2,1)S(1)}, u32[]{:S(2)}, u32[]{:S(2)}) collective-permute-start(bf16[336,128]{1,0:T(8,128)(2,1)S(1)} %get-tuple-element.24), channel_id=1, source_target_pairs={{0,4},{1,5},{2,6},{3,7},{4,0},{5,1},{6,2},{7,3},{8,15},{9,14},{10,... | collective-permute-start | bytes 258056 | tf_op jit(solution)/shard_map/ppermute | solution.py:313
  9.9 7.7 %copy-start.4 = (bf16[1,6144,128]{2,1,0:T(8,128)(2,1)S(1)}, bf16[1,6144,128]{2,1,0:T(8,128)(2,1)}, u32[]{:S(2)}) copy-start(bf16[1,6144,128]{2,1,0:T(8,128)(2,1)} %param.11) | copy-start | bytes 4718596
  9.9 7.7 %copy-start.6 = (s32[1,2]{1,0:T(1,128)S(1)}, s32[1,2]{1,0:T(1,128)}, u32[]{:S(2)}) copy-start(s32[1,2]{1,0:T(1,128)} %param.14) | copy-start | bytes 28
  9.9 7.6 %collective-permute-start.6 = (bf16[336,128]{1,0:T(8,128)(2,1)S(1)}, bf16[336,128]{1,0:T(8,128)(2,1)S(1)}, u32[]{:S(2)}, u32[]{:S(2)}) collective-permute-start(bf16[336,128]{1,0:T(8,128)(2,1)S(1)} %get-tuple-element.25), channel_id=1, source_target_pairs={{0,1},{1,0},{2,3},{3,2},{4,5},{5,4},{6,7},{7,6},{8,14},{9,15},{10,... | collective-permute-start | bytes 258056 | tf_op jit(solution)/shard_map/ppermute | solution.py:313
  10.1 7.4 %copy-start.5 = (bf16[1,6144,128]{2,1,0:T(8,128)(2,1)S(1)}, bf16[1,6144,128]{2,1,0:T(8,128)(2,1)}, u32[]{:S(2)}) copy-start(bf16[1,6144,128]{2,1,0:T(8,128)(2,1)} %param.12) | copy-start | bytes 4718596
  10.2 28.9 %collective-permute-start = (bf16[2,128,1024]{2,1,0:T(8,128)(2,1)S(1)}, bf16[2,128,1024]{2,1,0:T(8,128)(2,1)S(1)}, u32[]{:S(2)}, u32[]{:S(2)}) collective-permute-start(bf16[2,128,1024]{2,1,0:T(8,128)(2,1)S(1)} %pad_maximum_fusion.rows_ref), channel_id=1, source_target_pairs={{8,9},{9,10},{10,11},{11,12},{12,13},{13,14},{14,15},{24,25},{25,2... | collective-permute-start | bytes 1572872 | tf_op jit(solution)/shard_map/ppermute | solution.py:333
  12.6 19.1 %collective-permute-start.7 = (bf16[336,128]{1,0:T(8,128)(2,1)S(1)}, bf16[336,128]{1,0:T(8,128)(2,1)S(1)}, u32[]{:S(2)}, u32[]{:S(2)}) collective-permute-start(bf16[336,128]{1,0:T(8,128)(2,1)S(1)} %get-tuple-element.26), channel_id=1, source_target_pairs={{0,2},{1,3},{2,0},{3,1},{4,6},{5,7},{6,4},{7,5},{8,13},{9,12},{10,... | collective-permute-start | bytes 258056 | tf_op jit(solution)/shard_map/ppermute | solution.py:313
  16.8 14.9 %collective-permute-start.8 = (bf16[336,128]{1,0:T(8,128)(2,1)S(1)}, bf16[336,128]{1,0:T(8,128)(2,1)S(1)}, u32[]{:S(2)}, u32[]{:S(2)}) collective-permute-start(bf16[336,128]{1,0:T(8,128)(2,1)S(1)} %get-tuple-element.27), channel_id=1, source_target_pairs={{0,3},{1,2},{2,1},{3,0},{4,7},{5,6},{6,5},{7,4},{8,12},{9,13},{10,... | collective-permute-start | bytes 258056 | tf_op jit(solution)/shard_map/ppermute | solution.py:313
  16.8 24.4 %collective-permute-start.2 = (bf16[2,128,1024]{2,1,0:T(8,128)(2,1)S(1)}, bf16[2,128,1024]{2,1,0:T(8,128)(2,1)S(1)}, u32[]{:S(2)}, u32[]{:S(2)}) collective-permute-start(bf16[2,128,1024]{2,1,0:T(8,128)(2,1)S(1)} %halo.1), channel_id=1, source_target_pairs={{0,1},{1,2},{2,3},{3,4},{4,5},{5,6},{6,7},{16,17},{17,18},{18,19},... | collective-permute-start | bytes 1572872 | tf_op jit(solution)/shard_map/ppermute | solution.py:333
  17.5 14.1 %copy-start.1 = (bf16[1,320,1024]{2,1,0:T(8,128)(2,1)S(1)}, bf16[1,320,1024]{2,1,0:T(8,128)(2,1)}, u32[]{:S(2)}) copy-start(bf16[1,320,1024]{2,1,0:T(8,128)(2,1)} %param.8) | copy-start | bytes 1966084
  17.6 14.1 %copy-start.2 = (bf16[1,320,1024]{2,1,0:T(8,128)(2,1)S(1)}, bf16[1,320,1024]{2,1,0:T(8,128)(2,1)}, u32[]{:S(2)}) copy-start(bf16[1,320,1024]{2,1,0:T(8,128)(2,1)} %param.9) | copy-start | bytes 1966084
  17.6 14.1 %copy-start.3 = (bf16[1,320,1024]{2,1,0:T(8,128)(2,1)S(1)}, bf16[1,320,1024]{2,1,0:T(8,128)(2,1)}, u32[]{:S(2)}) copy-start(bf16[1,320,1024]{2,1,0:T(8,128)(2,1)} %param.10) | copy-start | bytes 1966084
  20.8 13.1 %collective-permute-start.9 = (bf16[336,128]{1,0:T(8,128)(2,1)S(1)}, bf16[336,128]{1,0:T(8,128)(2,1)S(1)}, u32[]{:S(2)}, u32[]{:S(2)}) collective-permute-start(bf16[336,128]{1,0:T(8,128)(2,1)S(1)} %get-tuple-element.29), channel_id=1, source_target_pairs={{0,15},{1,14},{2,13},{3,12},{4,11},{5,10},{6,9},{7,8},{8,17},{9,16... | collective-permute-start | bytes 258056 | tf_op jit(solution)/shard_map/ppermute | solution.py:313
  31.6 5.7 %collective-permute-start.10 = (bf16[336,128]{1,0:T(8,128)(2,1)S(1)}, bf16[336,128]{1,0:T(8,128)(2,1)S(1)}, u32[]{:S(2)}, u32[]{:S(2)}) collective-permute-start(bf16[336,128]{1,0:T(8,128)(2,1)S(1)} %get-tuple-element.30), channel_id=1, source_target_pairs={{0,14},{1,15},{2,12},{3,13},{4,10},{5,11},{6,8},{7,9},{8,18},{9,19... | collective-permute-start | bytes 258056 | tf_op jit(solution)/shard_map/ppermute | solution.py:313
  32.9 19.5 %collective-permute-start.12 = (bf16[256,1024]{1,0:T(8,128)(2,1)S(1)}, bf16[256,1024]{1,0:T(8,128)(2,1)S(1)}, u32[]{:S(2)}, u32[]{:S(2)}) collective-permute-start(bf16[256,1024]{1,0:T(8,128)(2,1)S(1)} %near_inner.1), channel_id=1, source_target_pairs={{0,8},{1,9},{2,10},{3,11},{4,12},{5,13},{6,14},{7,15},{8,16},{9,17... | collective-permute-start | bytes 1572872 | tf_op jit(solution)/shard_map/ppermute | solution.py:313
  33.9 9.9 %collective-permute-start.13 = (bf16[336,128]{1,0:T(8,128)(2,1)S(1)}, bf16[336,128]{1,0:T(8,128)(2,1)S(1)}, u32[]{:S(2)}, u32[]{:S(2)}) collective-permute-start(bf16[336,128]{1,0:T(8,128)(2,1)S(1)} %get-tuple-element.32), channel_id=1, source_target_pairs={{0,13},{1,12},{2,15},{3,14},{4,9},{5,8},{6,11},{7,10},{8,19},{9,18... | collective-permute-start | bytes 258056 | tf_op jit(solution)/shard_map/ppermute | solution.py:313
  37.4 10.2 %collective-permute-start.14 = (bf16[336,128]{1,0:T(8,128)(2,1)S(1)}, bf16[336,128]{1,0:T(8,128)(2,1)S(1)}, u32[]{:S(2)}, u32[]{:S(2)}) collective-permute-start(bf16[336,128]{1,0:T(8,128)(2,1)S(1)} %get-tuple-element.33), channel_id=1, source_target_pairs={{0,12},{1,13},{2,14},{3,15},{4,8},{5,9},{6,10},{7,11},{8,23},{9,22... | collective-permute-start | bytes 258056 | tf_op jit(solution)/shard_map/ppermute | solution.py:313
  39.1 10.3 %collective-permute-start.15 = (bf16[336,128]{1,0:T(8,128)(2,1)S(1)}, bf16[336,128]{1,0:T(8,128)(2,1)S(1)}, u32[]{:S(2)}, u32[]{:S(2)}) collective-permute-start(bf16[336,128]{1,0:T(8,128)(2,1)S(1)} %get-tuple-element.34), channel_id=1, source_target_pairs={{0,9},{1,8},{2,11},{3,10},{4,13},{5,12},{6,15},{7,14},{8,22},{9,23... | collective-permute-start | bytes 258056 | tf_op jit(solution)/shard_map/ppermute | solution.py:313
  42.2 10.2 %collective-permute-start.11 = (bf16[144,1024]{1,0:T(8,128)(2,1)S(1)}, bf16[144,1024]{1,0:T(8,128)(2,1)S(1)}, u32[]{:S(2)}, u32[]{:S(2)}) collective-permute-start(bf16[144,1024]{1,0:T(8,128)(2,1)S(1)} %near_edge.1), channel_id=1, source_target_pairs={{0,8},{1,9},{2,10},{3,11},{4,12},{5,13},{6,14},{7,15},{8,16},{9,17... | collective-permute-start | bytes 884744 | tf_op jit(solution)/shard_map/ppermute | solution.py:313
  43.8 6.1 %collective-permute-start.16 = (bf16[336,128]{1,0:T(8,128)(2,1)S(1)}, bf16[336,128]{1,0:T(8,128)(2,1)S(1)}, u32[]{:S(2)}, u32[]{:S(2)}) collective-permute-start(bf16[336,128]{1,0:T(8,128)(2,1)S(1)} %get-tuple-element.35), channel_id=1, source_target_pairs={{0,10},{1,11},{2,8},{3,9},{4,14},{5,15},{6,12},{7,13},{8,21},{9,20... | collective-permute-start | bytes 258056 | tf_op jit(solution)/shard_map/ppermute | solution.py:313
  47.6 4.8 %collective-permute-start.17 = (bf16[336,128]{1,0:T(8,128)(2,1)S(1)}, bf16[336,128]{1,0:T(8,128)(2,1)S(1)}, u32[]{:S(2)}, u32[]{:S(2)}) collective-permute-start(bf16[336,128]{1,0:T(8,128)(2,1)S(1)} %get-tuple-element.36), channel_id=1, source_target_pairs={{0,11},{1,10},{2,9},{3,8},{4,15},{5,14},{6,13},{7,12},{8,20},{9,21... | collective-permute-start | bytes 258056 | tf_op jit(solution)/shard_map/ppermute | solution.py:313
